TPU v7x, 32 devices: a whole 2x2x4 slice. The times are simulated.
32 devices in a mesh: shard: 4 (over z), ctx: 2 (over y), tp: 4 (over x, core).
Axes of the slice: x: 2, y: 2, z: 4, core: 2. Of those that a mesh axis runs over, the one named last changes fastest.
Arguments:
- frames: bfloat16 [4, 1536, 768], P('shard', 'ctx'), may hold values from -6 to 6
- cotangent: bfloat16 [4, 1536, 768], P('shard', 'ctx'), may hold values from -6 to 6
- w_qkv: bfloat16 [2, 768, 12, 192], P(None, 'shard', 'tp'), may hold values from -2 to 2
- qv_bias: bfloat16 [2, 12, 128], P(None, 'tp', 'shard'), may hold values from -3 to 3
- w_out: bfloat16 [2, 12, 64, 768], P(None, 'tp', None, 'shard'), may hold values from -0.375 to 0.375
- w_up: bfloat16 [2, 768, 3072], P(None, 'shard', 'tp'), may hold values from -0.21875 to 0.21875
- up_bias: bfloat16 [2, 48, 64], P(None, 'tp', 'shard'), may hold values from -3 to 3
- w_down: bfloat16 [2, 3072, 768], P(None, 'tp', 'shard'), may hold values from -0.109375 to 0.109375
- norm_gains: bfloat16 [2, 2, 768], P(None, None, 'shard'), may hold values from 0.099609375 to 1.8984375
- shifts: bfloat16 [2, 4, 768], P(None, None, 'shard'), may hold values from -3 to 3
Outputs:
- out_frames: bfloat16 [4, 1536, 768], P('shard', 'ctx')
- frames_grad: bfloat16 [4, 1536, 768], P('shard', 'ctx')
- grad_w_qkv: float32 [2, 768, 12, 192], P(None, 'shard', 'tp')
- grad_qv_bias: float32 [2, 12, 128], P(None, 'tp', 'shard')
- grad_w_out: float32 [2, 12, 64, 768], P(None, 'tp', None, 'shard')
- grad_w_up: float32 [2, 768, 3072], P(None, 'shard', 'tp')
- grad_up_bias: float32 [2, 48, 64], P(None, 'tp', 'shard')
- grad_w_down: float32 [2, 3072, 768], P(None, 'tp', 'shard')
- grad_norm_gains: float32 [2, 2, 768], P(None, None, 'shard')
- grad_shifts: float32 [2, 4, 768], P(None, None, 'shard')
All inputs are finite; a program needn't handle non-finite values.
Results may differ from a plain program's by a relative error of at most 0.015.
Values may be sent and summed in bfloat16 or wider, within the bound.
No kernel may reach another device: no remote copies, remote signals or barrier semaphores. Data moves between devices by JAX's collectives and lax.ppermute only.
A program may use at most 192 MiB of HBM per device.

v0:
```python
from functools import partial

import jax
import jax.numpy as jnp
from jax import lax
from jax.sharding import PartitionSpec as P

epsilon = 1e-05


def normalize(values, gain, shift):
    centre = jnp.mean(values, -1, keepdims=True)
    centred = values - centre
    spread = jnp.mean(centred * centred, -1, keepdims=True)
    return centred * lax.rsqrt(spread + epsilon) * gain + shift


def fetch_layer(w_qkv, qv_bias, w_out, w_up, up_bias, w_down, norm_gains, shifts, layer_idx):
    return (
        lax.all_gather(w_qkv[layer_idx], "shard", axis=0, tiled=True),
        lax.all_gather(qv_bias[layer_idx], "shard", axis=1, tiled=True),
        lax.all_gather(w_out[layer_idx], "shard", axis=2, tiled=True),
        lax.all_gather(w_up[layer_idx], "shard", axis=0, tiled=True),
        lax.all_gather(up_bias[layer_idx], "shard", axis=1, tiled=True),
        lax.all_gather(w_down[layer_idx], "shard", axis=1, tiled=True),
        lax.all_gather(norm_gains[layer_idx], "shard", axis=1, tiled=True),
        lax.all_gather(shifts[layer_idx], "shard", axis=1, tiled=True),
    )


def branch_reduce(partial_sum):
    return lax.psum(partial_sum, "tp")


def input_reduce(partial_sum):
    return lax.psum(partial_sum, "tp")


def norm_grad_total(gain_grads, shift_grads):
    return (gain_grads, shift_grads)


def attend(pieces):
    queries, keys_values = pieces
    head_size = queries.shape[-1]
    scores = jnp.einsum(
        "qhe,khe->hqk", queries, keys_values[..., :head_size], preferred_element_type=jnp.float32
    ) * head_size ** (-0.5)
    row_max = jnp.max(scores, -1, keepdims=True)
    log_total = row_max + jnp.log(jnp.sum(jnp.exp(scores - row_max), -1, keepdims=True))
    probs_low = jnp.exp(scores - log_total).astype(jnp.bfloat16)
    attended = jnp.einsum(
        "hqk,khe->qhe", probs_low, keys_values[..., head_size:], preferred_element_type=jnp.float32
    )
    return (attended.astype(jnp.bfloat16), log_total)


def back_attend(pieces):
    queries, keys_values, log_total, grad_out = pieces
    head_size = queries.shape[-1]
    scale = head_size ** (-0.5)
    keys_only = keys_values[..., :head_size]
    values_only = keys_values[..., head_size:]
    scores = (
        jnp.einsum("qhe,khe->hqk", queries, keys_only, preferred_element_type=jnp.float32) * scale
    )
    probs = jnp.exp(scores - log_total)
    grad_probs = jnp.einsum(
        "qhe,khe->hqk", grad_out, values_only, preferred_element_type=jnp.float32
    )
    grad_values = jnp.einsum(
        "hqk,qhe->khe", probs.astype(jnp.bfloat16), grad_out, preferred_element_type=jnp.float32
    )
    grad_scores = (probs * (grad_probs - jnp.sum(probs * grad_probs, -1, keepdims=True))).astype(
        jnp.bfloat16
    )
    grad_queries = (
        jnp.einsum("hqk,khe->qhe", grad_scores, keys_only, preferred_element_type=jnp.float32)
        * scale
    )
    grad_keys = (
        jnp.einsum("hqk,qhe->khe", grad_scores, queries, preferred_element_type=jnp.float32) * scale
    )
    return (grad_queries, jnp.concatenate([grad_keys, grad_values], -1))


def forward_layer(stream, weights, clip_count):
    w_qkv, qv_bias, w_out, w_up, up_bias, w_down, norm_gains, shifts = weights
    model_width = stream.shape[1]
    head_count = w_qkv.shape[1]
    head_size = qv_bias.shape[1] // 2
    gains = norm_gains.astype(jnp.float32)
    offsets = shifts.astype(jnp.float32)
    normed_in = normalize(stream, gains[0], offsets[0]).astype(jnp.bfloat16)
    row_count = normed_in.shape[0]
    half_len = row_count // clip_count
    projected = jnp.dot(
        normed_in, w_qkv.reshape(model_width, -1), preferred_element_type=jnp.float32
    )
    projected = projected.reshape(clip_count, half_len, head_count, 3 * head_size)
    bias_full = qv_bias.astype(jnp.float32)
    queries = (projected[..., :head_size] + bias_full[:, :head_size]).astype(jnp.bfloat16)
    kv_bias = jnp.concatenate(
        [jnp.zeros((head_count, head_size), jnp.float32), bias_full[:, head_size:]], 1
    )
    local_kv = (projected[..., head_size:] + kv_bias).astype(jnp.bfloat16)
    keys_values = lax.all_gather(local_kv, "ctx", axis=1, tiled=True)
    attended, log_total = lax.map(attend, (queries, keys_values))
    flat_att = attended.reshape(row_count, head_count * head_size)
    branch = (
        branch_reduce(
            jnp.dot(
                flat_att,
                w_out.reshape(head_count * head_size, model_width),
                preferred_element_type=jnp.float32,
            )
        )
        + offsets[1]
    )
    middle = stream + branch
    normed_mid = normalize(middle, gains[1], offsets[2]).astype(jnp.bfloat16)
    pre_act = jnp.dot(normed_mid, w_up, preferred_element_type=jnp.float32) + up_bias.astype(
        jnp.float32
    ).reshape(-1)
    hidden = jax.nn.gelu(pre_act, approximate=False).astype(jnp.bfloat16)
    result = middle + (
        branch_reduce(jnp.dot(hidden, w_down, preferred_element_type=jnp.float32)) + offsets[3]
    )
    kept = (
        stream,
        normed_in,
        queries,
        keys_values,
        attended,
        log_total,
        middle,
        normed_mid,
        pre_act,
        hidden,
    )
    return (result, kept)


def backward_layer(gradient, kept, weights, clip_count):
    (
        stream,
        normed_in,
        queries,
        keys_values,
        attended,
        log_total,
        middle,
        normed_mid,
        pre_act,
        hidden,
    ) = kept
    w_qkv, qv_bias, w_out, w_up, up_bias, w_down, norm_gains, shifts = weights
    row_count, model_width = normed_in.shape
    half_len = row_count // clip_count
    head_count = w_qkv.shape[1]
    head_size = qv_bias.shape[1] // 2
    gains = norm_gains.astype(jnp.float32)
    offsets = shifts.astype(jnp.float32)
    grad_mlp = gradient.astype(jnp.bfloat16)
    grad_down = jnp.dot(hidden.T, grad_mlp, preferred_element_type=jnp.float32)
    grad_hidden = jnp.dot(grad_mlp, w_down.T, preferred_element_type=jnp.float32)
    _, gelu_back = jax.vjp(partial(jax.nn.gelu, approximate=False), pre_act)
    grad_pre = gelu_back(grad_hidden)[0].astype(jnp.bfloat16)
    grad_up = jnp.dot(normed_mid.T, grad_pre, preferred_element_type=jnp.float32)
    grad_up_bias = jnp.sum(grad_pre.astype(jnp.float32), 0).reshape(up_bias.shape[0], -1)
    grad_normed_mid = input_reduce(jnp.dot(grad_pre, w_up.T, preferred_element_type=jnp.float32))
    _, norm_back_mid = jax.vjp(normalize, middle, gains[1], offsets[2])
    grad_middle_norm, grad_gain_two, grad_shift_two = norm_back_mid(grad_normed_mid)
    grad_middle = gradient + grad_middle_norm
    grad_branch = grad_middle.astype(jnp.bfloat16)
    flat_att = attended.reshape(row_count, head_count * head_size)
    grad_w_out = jnp.dot(flat_att.T, grad_branch, preferred_element_type=jnp.float32)
    grad_w_out = grad_w_out.reshape(head_count, head_size, model_width)
    grad_att = jnp.dot(
        grad_branch,
        w_out.reshape(head_count * head_size, model_width).T,
        preferred_element_type=jnp.float32,
    ).astype(jnp.bfloat16)
    grad_att = grad_att.reshape(clip_count, half_len, head_count, head_size)
    grad_queries, grad_kv_all = lax.map(back_attend, (queries, keys_values, log_total, grad_att))
    grad_kv = lax.psum_scatter(grad_kv_all, "ctx", scatter_dimension=1, tiled=True).astype(
        jnp.bfloat16
    )
    grad_q_low = grad_queries.astype(jnp.bfloat16)
    grad_proj = jnp.concatenate([grad_q_low, grad_kv], -1).reshape(
        row_count, head_count * 3 * head_size
    )
    grad_w_qkv = jnp.dot(normed_in.T, grad_proj, preferred_element_type=jnp.float32)
    grad_w_qkv = grad_w_qkv.reshape(model_width, head_count, 3 * head_size)
    grad_qv = jnp.concatenate(
        [
            jnp.sum(grad_q_low.astype(jnp.float32), (0, 1)),
            jnp.sum(grad_kv[..., head_size:].astype(jnp.float32), (0, 1)),
        ],
        -1,
    )
    grad_normed_in = input_reduce(
        jnp.dot(grad_proj, w_qkv.reshape(model_width, -1).T, preferred_element_type=jnp.float32)
    )
    _, norm_back_in = jax.vjp(normalize, stream, gains[0], offsets[0])
    grad_stream_norm, grad_gain_one, grad_shift_one = norm_back_in(grad_normed_in)
    grad_stream = grad_middle + grad_stream_norm
    gain_grads, shift_grads = norm_grad_total(
        jnp.stack([grad_gain_one, grad_gain_two]), jnp.stack([grad_shift_one, grad_shift_two])
    )
    grad_shift_branch = jnp.sum(grad_branch.astype(jnp.float32), 0)
    grad_shift_mlp = jnp.sum(grad_mlp.astype(jnp.float32), 0)
    grads = (
        grad_w_qkv,
        grad_qv,
        grad_w_out,
        grad_up,
        grad_up_bias,
        grad_down,
        gain_grads,
        jnp.stack([shift_grads[0], grad_shift_branch, shift_grads[1], grad_shift_mlp]),
    )
    return (grad_stream, grads)


def reduce_grads(grads):
    totals = lax.psum(
        (grads[0], grads[1], grads[2], grads[3], grads[4], grads[5], grads[6], grads[7]), "ctx"
    )
    return (
        lax.psum_scatter(totals[0], "shard", scatter_dimension=0, tiled=True),
        lax.psum_scatter(totals[1], "shard", scatter_dimension=1, tiled=True),
        lax.psum_scatter(totals[2], "shard", scatter_dimension=2, tiled=True),
        lax.psum_scatter(totals[3], "shard", scatter_dimension=0, tiled=True),
        lax.psum_scatter(totals[4], "shard", scatter_dimension=1, tiled=True),
        lax.psum_scatter(totals[5], "shard", scatter_dimension=1, tiled=True),
        lax.psum_scatter(totals[6], "shard", scatter_dimension=1, tiled=True),
        lax.psum_scatter(totals[7], "shard", scatter_dimension=1, tiled=True),
    )


def local(frames, cotangent, w_qkv, qv_bias, w_out, w_up, up_bias, w_down, norm_gains, shifts):
    layer_count = w_qkv.shape[0]
    clip_count, half_len, model_width = frames.shape
    stream = frames.astype(jnp.float32).reshape(clip_count * half_len, model_width)
    fetched = []
    stored = []
    for layer_idx in range(layer_count):
        weights = fetch_layer(
            w_qkv, qv_bias, w_out, w_up, up_bias, w_down, norm_gains, shifts, layer_idx
        )
        fetched.append(weights)
        stream, kept = forward_layer(stream, weights, clip_count)
        stored.append(kept)
    out_frames = stream.astype(jnp.bfloat16).reshape(frames.shape)
    gradient = cotangent.astype(jnp.float32).reshape(clip_count * half_len, model_width)
    reduced = [None] * layer_count
    for layer_idx in reversed(range(layer_count)):
        weights = fetch_layer(
            w_qkv, qv_bias, w_out, w_up, up_bias, w_down, norm_gains, shifts, layer_idx
        )
        gradient, grads = backward_layer(gradient, stored[layer_idx], weights, clip_count)
        reduced[layer_idx] = reduce_grads(grads)
    stacked = [
        jnp.stack([reduced[layer_idx][position] for layer_idx in range(layer_count)])
        for position in range(8)
    ]
    frames_grad = gradient.astype(jnp.bfloat16).reshape(frames.shape)
    return (
        out_frames,
        frames_grad,
        stacked[0],
        stacked[1],
        stacked[2],
        stacked[3],
        stacked[4],
        stacked[5],
        stacked[6],
        stacked[7],
    )


def solution(mesh):
    in_specs = (
        P("shard", "ctx", None),
        P("shard", "ctx", None),
        P(None, "shard", "tp", None),
        P(None, "tp", "shard"),
        P(None, "tp", None, "shard"),
        P(None, "shard", "tp"),
        P(None, "tp", "shard"),
        P(None, "tp", "shard"),
        P(None, None, "shard"),
        P(None, None, "shard"),
    )
    out_specs = (
        P("shard", "ctx", None),
        P("shard", "ctx", None),
        P(None, "shard", "tp", None),
        P(None, "tp", "shard"),
        P(None, "tp", None, "shard"),
        P(None, "shard", "tp"),
        P(None, "tp", "shard"),
        P(None, "tp", "shard"),
        P(None, None, "shard"),
        P(None, None, "shard"),
    )
    return jax.shard_map(local, mesh=mesh, in_specs=in_specs, out_specs=out_specs, check_vma=False)
```

profile of v0, /device:TPU:0, one launch (start us, length us, event | category | flops | bytes accessed | tf_op | source)
XLA Modules:
  0.0 1324.6 jit_solution(14729889293801708188)
XLA Ops:
  14.7 14.9 %all-gather.3 = bf16[1,3,128]{1,0,2:T(2,128)(2,1)S(1)} all-gather(bf16[1,3,32]{1,0,2:T(2,128)(2,1)S(1)} %copy.131), channel_id=5, replica_groups=mesh['shard'=4,'ctx'=2,'tp'=4] {'shard'}, dimensions={2}, use_global_device_ids=true | all-gather | bytes 960 | tf_op jit(solution)/shard_map/all_gather | solution.py:21
  30.1 15.2 %all-gather = bf16[1,2,768]{1,0,2:T(2,128)(2,1)S(1)} all-gather(bf16[1,2,192]{1,0,2:T(2,128)(2,1)S(1)} %copy.133), channel_id=2, replica_groups=mesh['shard'=4,'ctx'=2,'tp'=4] {'shard'}, dimensions={2}, use_global_device_ids=true | all-gather | bytes 3840 | tf_op jit(solution)/shard_map/all_gather | solution.py:26
  50.3 14.6 %all-gather.1 = bf16[1,4,768]{1,0,2:T(2,128)(2,1)S(1)} all-gather(bf16[1,4,192]{1,0,2:T(2,128)(2,1)S(1)} %copy.134), channel_id=3, replica_groups=mesh['shard'=4,'ctx'=2,'tp'=4] {'shard'}, dimensions={2}, use_global_device_ids=true | all-gather | bytes 7680 | tf_op jit(solution)/shard_map/all_gather | solution.py:27
  65.4 10.8 slice_reduce_fusion.6
  77.2 24.6 %all-gather.2 = bf16[1,768,3,192]{3,2,0,1:T(4,128)(2,1)S(1)} all-gather(bf16[1,192,3,192]{3,2,0,1:T(4,128)(2,1)S(1)} %copy.135), channel_id=4, replica_groups=mesh['shard'=4,'ctx'=2,'tp'=4] {'shard'}, dimensions={1}, use_global_device_ids=true | all-gather | bytes 1105920 | tf_op jit(solution)/shard_map/all_gather | solution.py:20
  108.2 16.8 %all-gather.4 = bf16[1,3,64,768]{2,1,0,3:T(4,128)(2,1)} all-gather(bf16[1,3,64,192]{2,1,0,3:T(4,128)(2,1)S(1)} %copy.136), channel_id=6, replica_groups=mesh['shard'=4,'ctx'=2,'tp'=4] {'shard'}, dimensions={3}, use_global_device_ids=true | all-gather | bytes 368640 | tf_op jit(solution)/shard_map/all_gather | solution.py:22
  130.1 8.2 multiply_reduce_fusion.3
  138.3 7.5 exponential_reduce_fusion.1
  145.9 7.6 convolution_convert_fusion.3
  158.3 13.2 %all-gather.6 = bf16[1,12,64]{1,0,2:T(2,128)(2,1)S(1)} all-gather(bf16[1,12,16]{1,0,2:T(2,128)(2,1)S(1)} %copy.137), channel_id=8, replica_groups=mesh['shard'=4,'ctx'=2,'tp'=4] {'shard'}, dimensions={2}, use_global_device_ids=true | all-gather | bytes 1920 | tf_op jit(solution)/shard_map/all_gather | solution.py:24
  172.3 39.1 %all-reduce.14.cloned.1.call-done = f32[768,768]{1,0:T(8,128)} async-done(((f32[768,768]{1,0:T(8,128)}), f32[768,768]{1,0:T(8,128)}) %all-reduce.14.cloned.1.call-update) | async-done | bytes 2359312 | tf_op jit(solution)/shard_map/psum | solution.py:32
  214.2 8.9 multiply_convert_fusion.3
  228.1 13.3 %all-gather.11 = bf16[1,3,128]{1,0,2:T(2,128)(2,1)S(1)} all-gather(bf16[1,3,32]{1,0,2:T(2,128)(2,1)S(1)} %copy.132), channel_id=13, replica_groups=mesh['shard'=4,'ctx'=2,'tp'=4] {'shard'}, dimensions={2}, use_global_device_ids=true | all-gather | bytes 960 | tf_op jit(solution)/shard_map/all_gather | solution.py:21
  242.5 15.2 %all-gather.8 = bf16[1,2,768]{1,0,2:T(2,128)(2,1)S(1)} all-gather(bf16[1,2,192]{1,0,2:T(2,128)(2,1)S(1)} %copy.138), channel_id=10, replica_groups=mesh['shard'=4,'ctx'=2,'tp'=4] {'shard'}, dimensions={2}, use_global_device_ids=true | all-gather | bytes 3840 | tf_op jit(solution)/shard_map/all_gather | solution.py:26
  258.1 15.2 %all-gather.9 = bf16[1,4,768]{1,0,2:T(2,128)(2,1)S(1)} all-gather(bf16[1,4,192]{1,0,2:T(2,128)(2,1)S(1)} %copy.139), channel_id=11, replica_groups=mesh['shard'=4,'ctx'=2,'tp'=4] {'shard'}, dimensions={2}, use_global_device_ids=true | all-gather | bytes 7680 | tf_op jit(solution)/shard_map/all_gather | solution.py:27
  274.0 25.0 %all-gather.10 = bf16[1,768,3,192]{3,2,0,1:T(4,128)(2,1)} all-gather(bf16[1,192,3,192]{3,2,0,1:T(4,128)(2,1)S(1)} %copy.140), channel_id=12, replica_groups=mesh['shard'=4,'ctx'=2,'tp'=4] {'shard'}, dimensions={1}, use_global_device_ids=true | all-gather | bytes 1105920 | tf_op jit(solution)/shard_map/all_gather | solution.py:20
  307.2 11.0 slice_reduce_fusion
  324.5 15.7 %all-gather.12 = bf16[1,3,64,768]{2,1,0,3:T(4,128)(2,1)S(1)} all-gather(bf16[1,3,64,192]{2,1,0,3:T(4,128)(2,1)S(1)} %copy.141), channel_id=14, replica_groups=mesh['shard'=4,'ctx'=2,'tp'=4] {'shard'}, dimensions={3}, use_global_device_ids=true | all-gather | bytes 368640 | tf_op jit(solution)/shard_map/all_gather | solution.py:22
  345.7 8.2 multiply_reduce_fusion.2
  353.9 7.5 exponential_reduce_fusion
  361.5 7.6 convolution_convert_fusion.2
  373.4 13.3 %all-gather.14 = bf16[1,12,64]{1,0,2:T(2,128)(2,1)S(1)} all-gather(bf16[1,12,16]{1,0,2:T(2,128)(2,1)S(1)} %copy.142), channel_id=16, replica_groups=mesh['shard'=4,'ctx'=2,'tp'=4] {'shard'}, dimensions={2}, use_global_device_ids=true | all-gather | bytes 1920 | tf_op jit(solution)/shard_map/all_gather | solution.py:24
  387.4 40.3 %all-reduce.18.cloned.1.call-done = f32[768,768]{1,0:T(8,128)} async-done(((f32[768,768]{1,0:T(8,128)}), f32[768,768]{1,0:T(8,128)}) %all-reduce.18.cloned.1.call-update) | async-done | bytes 2359312 | tf_op jit(solution)/shard_map/psum | solution.py:32
  431.5 9.3 multiply_convert_fusion.2
  449.6 55.8 %all-reduce.20.cloned.1.call-done = f32[768,768]{1,0:T(8,128)} async-done(((f32[768,768]{1,0:T(8,128)}), f32[768,768]{1,0:T(8,128)}) %all-reduce.20.cloned.1.call-update) | async-done | bytes 2359312 | tf_op jit(solution)/shard_map/psum | solution.py:36
  520.2 6.9 multiply_reduce_fusion.1
  527.1 7.0 multiply_convert_fusion.1
  545.6 28.0 %reduce-scatter.39.cloned.1.call-done = f32[1,768,3,128]{1,3,2,0:T(8,128)} async-done(((f32[1,1536,3,128]{1,3,2,0:T(8,128)}), f32[1,768,3,128]{1,3,2,0:T(8,128)}) %reduce-scatter.39.cloned.1.call-update) | async-done | bytes 1179664 | tf_op jit(solution)/shard_map/reduce_scatter | solution.py:186
  579.5 55.7 %all-reduce.22.cloned.1.call-done = f32[768,768]{1,0:T(8,128)} async-done(((f32[768,768]{1,0:T(8,128)}), f32[768,768]{1,0:T(8,128)}) %all-reduce.22.cloned.1.call-update) | async-done | bytes 2359312 | tf_op jit(solution)/shard_map/psum | solution.py:36
  651.1 55.6 %all-reduce.24.cloned.1.call-done = f32[768,768]{1,0:T(8,128)} async-done(((f32[768,768]{1,0:T(8,128)}), f32[768,768]{1,0:T(8,128)}) %all-reduce.24.cloned.1.call-update) | async-done | bytes 2359312 | tf_op jit(solution)/shard_map/psum | solution.py:36
  722.6 6.8 multiply_reduce_fusion
  729.4 7.0 multiply_convert_fusion
  748.9 27.0 %reduce-scatter.41.cloned.1.call-done = f32[1,768,3,128]{1,3,2,0:T(8,128)} async-done(((f32[1,1536,3,128]{1,3,2,0:T(8,128)}), f32[1,768,3,128]{1,3,2,0:T(8,128)}) %reduce-scatter.41.cloned.1.call-update) | async-done | bytes 1179664 | tf_op jit(solution)/shard_map/reduce_scatter | solution.py:186
  860.2 15.9 %all-reduce.26.cloned.1.call-done = (f32[768,768]{1,0:T(8,128)}, f32[768,768]{1,0:T(8,128)}) async-done(((f32[768,768]{1,0:T(8,128)}, f32[768,768]{1,0:T(8,128)}), (f32[768,768]{1,0:T(8,128)}, f32[768,768]{1,0:T(8,128)})) %all-reduce.26.cloned.1.call-update) | async-done | bytes 4718608 | tf_op jit(solution)/shard_map/psum | solution.py:32
  894.4 42.1 %reduce-scatter.53.cloned.1.call-done = f32[768,192]{0,1:T(8,128)} async-done(((f32[768,768]{0,1:T(8,128)}), f32[768,192]{0,1:T(8,128)}) %reduce-scatter.53.cloned.1.call-update) | async-done | bytes 589840 | tf_op jit(solution)/shard_map/reduce_scatter | solution.py:236
  936.5 49.2 %reduce-scatter.45.cloned.1.call-done = f32[192,3,192]{2,0,1:T(8,128)} async-done(((f32[768,3,192]{2,0,1:T(8,128)}), f32[192,3,192]{2,0,1:T(8,128)}) %reduce-scatter.45.cloned.1.call-update) | async-done | bytes 442384 | tf_op jit(solution)/shard_map/reduce_scatter | solution.py:231
  985.7 49.6 %reduce-scatter.47.cloned.1.call-done = f32[192,768]{1,0:T(8,128)} async-done(((f32[768,768]{1,0:T(8,128)}), f32[192,768]{1,0:T(8,128)}) %reduce-scatter.47.cloned.1.call-update) | async-done | bytes 589840 | tf_op jit(solution)/shard_map/reduce_scatter | solution.py:234
  1035.4 49.4 %reduce-scatter.51.cloned.1.call-done = f32[768,192]{0,1:T(8,128)} async-done(((f32[768,768]{0,1:T(8,128)}), f32[768,192]{0,1:T(8,128)}) %reduce-scatter.51.cloned.1.call-update) | async-done | bytes 589840 | tf_op jit(solution)/shard_map/reduce_scatter | solution.py:236
  1084.7 49.4 %reduce-scatter.43.cloned.1.call-done = f32[192,3,192]{2,0,1:T(8,128)} async-done(((f32[768,3,192]{2,0,1:T(8,128)}), f32[192,3,192]{2,0,1:T(8,128)}) %reduce-scatter.43.cloned.1.call-update) | async-done | bytes 442384 | tf_op jit(solution)/shard_map/reduce_scatter | solution.py:231
  1134.1 20.6 %reduce-scatter.65.cloned.1.call-done = f32[16,12]{1,0:T(8,128)} async-done(((f32[64,12]{1,0:T(8,128)}), f32[16,12]{1,0:T(8,128)}) %reduce-scatter.65.cloned.1.call-update) | async-done | bytes 784
  1156.1 18.7 %reduce-scatter.57.cloned.1.call-done = f32[32,3]{1,0:T(8,128)} async-done(((f32[128,3]{1,0:T(8,128)}), f32[32,3]{1,0:T(8,128)}) %reduce-scatter.57.cloned.1.call-update) | async-done | bytes 400
  1176.2 18.0 %reduce-scatter.63.cloned.1.call-done = f32[16,12]{1,0:T(8,128)} async-done(((f32[64,12]{1,0:T(8,128)}), f32[16,12]{1,0:T(8,128)}) %reduce-scatter.63.cloned.1.call-update) | async-done | bytes 784
  1195.6 20.3 %reduce-scatter.69.cloned.1.call-done = f32[192,2]{1,0:T(8,128)} async-done(((f32[768,2]{1,0:T(8,128)}), f32[192,2]{1,0:T(8,128)}) %reduce-scatter.69.cloned.1.call-update) | async-done | bytes 1552
  1217.4 20.1 %reduce-scatter.73.cloned.1.call-done = f32[192,4]{1,0:T(8,128)} async-done(((f32[768,4]{1,0:T(8,128)}), f32[192,4]{1,0:T(8,128)}) %reduce-scatter.73.cloned.1.call-update) | async-done | bytes 3088
  1239.1 17.8 %reduce-scatter.55.cloned.1.call-done = f32[32,3]{1,0:T(8,128)} async-done(((f32[128,3]{1,0:T(8,128)}), f32[32,3]{1,0:T(8,128)}) %reduce-scatter.55.cloned.1.call-update) | async-done | bytes 400
  1265.5 13.0 reduce-scatter.67.cloned.1.call-done
  1279.5 20.0 %reduce-scatter.71.cloned.1.call-done = f32[192,4]{1,0:T(8,128)} async-done(((f32[768,4]{1,0:T(8,128)}), f32[192,4]{1,0:T(8,128)}) %reduce-scatter.71.cloned.1.call-update) | async-done | bytes 3088
  1300.5 8.2 all-reduce.3
  (540 shorter events, 281.2 us)
Async XLA Ops:
  8.0 122.1 %all-gather.23.cloned.1.call-start = ((), (), s32[]{:S(2)}) async-start(), calls=%async_computation.18 | async-start | bytes 1769472 | tf_op jit(solution)/shard_map/all_gather | solution.py:107
  12.2 91.8 %copy-start.61 = (f32[768]{0:T(1024)}, f32[768]{0:T(1024)S(1)}, u32[]{:S(2)}) copy-start(f32[768]{0:T(1024)S(1)} %broadcast_multiply_fusion.3) | copy-start | bytes 9220
  14.0 90.0 %copy-start.81 = (f32[768]{0:T(1024)}, f32[768]{0:T(1024)S(1)}, u32[]{:S(2)}) copy-start(f32[768]{0:T(1024)S(1)} %fusion.101) | copy-start | bytes 9220
  29.8 100.4 %copy-start.59 = (f32[3,64]{1,0:T(4,128)}, f32[3,64]{1,0:T(4,128)S(1)}, u32[]{:S(2)}) copy-start(f32[3,64]{1,0:T(4,128)S(1)} %get-tuple-element.214) | copy-start | bytes 2308
  30.1 46.0 %copy-start.48 = (bf16[2,192,3,192]{3,1,2,0:T(8,128)(2,1)S(1)}, bf16[2,192,3,192]{3,1,2,0:T(8,128)(2,1)}, u32[]{:S(2)}) copy-start(bf16[2,192,3,192]{3,1,2,0:T(8,128)(2,1)} %param.12) | copy-start | bytes 1327108
  50.3 53.7 %copy-start.63 = (f32[768]{0:T(1024)}, f32[768]{0:T(1024)S(1)}, u32[]{:S(2)}) copy-start(f32[768]{0:T(1024)S(1)} %get-tuple-element.156) | copy-start | bytes 9220
  50.3 163.7 %copy-start.73 = (f32[768]{0:T(1024)}, f32[768]{0:T(1024)S(1)}, u32[]{:S(2)}) copy-start(f32[768]{0:T(1024)S(1)} %get-tuple-element.155) | copy-start | bytes 9220
  107.2 104.2 %all-reduce.14.cloned.1.call-start = ((), (), s32[]{:S(2)}) async-start(), calls=%async_computation.19 | async-start | bytes 4718592 | tf_op jit(solution)/shard_map/psum | solution.py:32
  155.6 58.4 %all-gather.27.cloned.1.call-start = ((), (), s32[]{:S(2)}) async-start(), calls=%async_computation.28 | async-start | bytes 1474560 | tf_op jit(solution)/shard_map/all_gather | solution.py:23
  156.5 66.6 %all-gather.29.cloned.1.call-start = ((), (), s32[]{:S(2)}) async-start(), calls=%async_computation.29 | async-start | bytes 1474560 | tf_op jit(solution)/shard_map/all_gather | solution.py:25
  157.5 160.7 %all-reduce.16.cloned.1.call-start = ((), (), s32[]{:S(2)}) async-start(), calls=%async_computation.20 | async-start | bytes 4718592 | tf_op jit(solution)/shard_map/psum | solution.py:32
  213.5 104.8 %copy-start.3 = (f32[768,768]{1,0:T(8,128)}, f32[768,768]{1,0:T(8,128)S(1)}, u32[]{:S(2)}) copy-start(f32[768,768]{1,0:T(8,128)S(1)} %get-tuple-element.196) | copy-start | bytes 7077892
  227.3 46.5 %copy-start.42 = (bf16[1,192,3,192]{3,1,2,0:T(8,128)(2,1)S(1)}, bf16[1,192,3,192]{3,1,2,0:T(8,128)(2,1)}, u32[]{:S(2)}) copy-start(bf16[1,192,3,192]{3,1,2,0:T(8,128)(2,1)} %get-tuple-element.202) | copy-start | bytes 663556
  227.3 118.4 %all-gather.25.cloned.1.call-start = ((), (), s32[]{:S(2)}) async-start(), calls=%async_computation.21 | async-start | bytes 1769472 | tf_op jit(solution)/shard_map/all_gather | solution.py:107
  324.2 103.5 %all-reduce.18.cloned.1.call-start = ((), (), s32[]{:S(2)}) async-start(), calls=%async_computation.22 | async-start | bytes 4718592 | tf_op jit(solution)/shard_map/psum | solution.py:32
  371.9 59.6 %all-gather.31.cloned.1.call-start = ((), (), s32[]{:S(2)}) async-start(), calls=%async_computation.30 | async-start | bytes 1474560 | tf_op jit(solution)/shard_map/all_gather | solution.py:23
  372.5 68.3 %all-gather.33.cloned.1.call-start = ((), (), s32[]{:S(2)}) async-start(), calls=%async_computation.31 | async-start | bytes 1474560 | tf_op jit(solution)/shard_map/all_gather | solution.py:25
  373.2 132.2 %all-reduce.20.cloned.1.call-start = ((), (), s32[]{:S(2)}) async-start(), calls=%async_computation.23 | async-start | bytes 4718592 | tf_op jit(solution)/shard_map/psum | solution.py:36
  449.5 55.9 %copy-start.71 = (f32[768]{0:T(1024)S(1)}, f32[768]{0:T(1024)}, u32[]{:S(2)}) copy-start(f32[768]{0:T(1024)} %copy-done.70) | copy-start | bytes 9220
  449.5 55.9 %copy-start.79 = (f32[768]{0:T(1024)S(1)}, f32[768]{0:T(1024)}, u32[]{:S(2)}) copy-start(f32[768]{0:T(1024)} %get-tuple-element.149) | copy-start | bytes 9220
  449.5 55.9 %copy-start.89 = (f32[768]{0:T(1024)S(1)}, f32[768]{0:T(1024)}, u32[]{:S(2)}) copy-start(f32[768]{0:T(1024)} %fusion.104) | copy-start | bytes 9220
  449.5 59.2 %copy-start.99 = (f32[768]{0:T(1024)S(1)}, f32[768]{0:T(1024)}, u32[]{:S(2)}) copy-start(f32[768]{0:T(1024)} %copy-done.98) | copy-start | bytes 9220
  449.5 124.1 %reduce-scatter.39.cloned.1.call-start = ((), (), s32[]{:S(2)}) async-start(), calls=%async_computation.24 | async-start | bytes 3538944 | tf_op jit(solution)/shard_map/reduce_scatter | solution.py:186
  538.7 96.6 %all-reduce.22.cloned.1.call-start = ((), (), s32[]{:S(2)}) async-start(), calls=%async_computation.25 | async-start | bytes 4718592 | tf_op jit(solution)/shard_map/psum | solution.py:36
  579.4 55.8 %copy-start.68 = (f32[768]{0:T(1024)S(1)}, f32[768]{0:T(1024)}, u32[]{:S(2)}) copy-start(f32[768]{0:T(1024)} %copy-done.67) | copy-start | bytes 9220
  579.4 127.2 %all-reduce.24.cloned.1.call-start = ((), (), s32[]{:S(2)}) async-start(), calls=%async_computation.26 | async-start | bytes 4718592 | tf_op jit(solution)/shard_map/psum | solution.py:36
  650.8 55.9 %copy-start.66 = (f32[768]{0:T(1024)S(1)}, f32[768]{0:T(1024)}, u32[]{:S(2)}) copy-start(f32[768]{0:T(1024)} %copy-done.65) | copy-start | bytes 9220
  650.8 125.1 %reduce-scatter.41.cloned.1.call-start = ((), (), s32[]{:S(2)}) async-start(), calls=%async_computation.27 | async-start | bytes 3538944 | tf_op jit(solution)/shard_map/reduce_scatter | solution.py:186
  740.9 135.1 %all-reduce.26.cloned.1.call-start = ((), (), s32[]{:S(2)}) async-start(), calls=%async_computation.48 | async-start | bytes 9437184 | tf_op jit(solution)/shard_map/psum | solution.py:32
  781.6 105.4 %reduce-scatter.61.cloned.1.call-start = ((), (), s32[]{:S(2)}) async-start(), calls=%async_computation.41 | async-start | bytes 983040
  789.3 101.4 %reduce-scatter.59.cloned.1.call-start = ((), (), s32[]{:S(2)}) async-start(), calls=%async_computation.40 | async-start | bytes 983040
  797.0 97.3 %reduce-scatter.49.cloned.1.call-start = ((), (), s32[]{:S(2)}) async-start(), calls=%async_computation.35 | async-start | bytes 2949120 | tf_op jit(solution)/shard_map/reduce_scatter | solution.py:234
  801.3 135.2 %reduce-scatter.53.cloned.1.call-start = ((), (), s32[]{:S(2)}) async-start(), calls=%async_computation.37 | async-start | bytes 2949120 | tf_op jit(solution)/shard_map/reduce_scatter | solution.py:236
  806.5 179.3 %reduce-scatter.45.cloned.1.call-start = ((), (), s32[]{:S(2)}) async-start(), calls=%async_computation.33 | async-start | bytes 2949120 | tf_op jit(solution)/shard_map/reduce_scatter | solution.py:231
  812.2 223.2 %reduce-scatter.47.cloned.1.call-start = ((), (), s32[]{:S(2)}) async-start(), calls=%async_computation.34 | async-start | bytes 2949120 | tf_op jit(solution)/shard_map/reduce_scatter | solution.py:234
  818.0 266.7 %reduce-scatter.51.cloned.1.call-start = ((), (), s32[]{:S(2)}) async-start(), calls=%async_computation.36 | async-start | bytes 2949120 | tf_op jit(solution)/shard_map/reduce_scatter | solution.py:236
  823.5 310.5 %reduce-scatter.43.cloned.1.call-start = ((), (), s32[]{:S(2)}) async-start(), calls=%async_computation.32 | async-start | bytes 2949120 | tf_op jit(solution)/shard_map/reduce_scatter | solution.py:231
  828.9 325.9 %reduce-scatter.65.cloned.1.call-start = ((), (), s32[]{:S(2)}) async-start(), calls=%async_computation.43 | async-start | bytes 40960
  831.7 343.1 %reduce-scatter.57.cloned.1.call-start = ((), (), s32[]{:S(2)}) async-start(), calls=%async_computation.39 | async-start | bytes 81920
  835.6 358.6 %reduce-scatter.63.cloned.1.call-start = ((), (), s32[]{:S(2)}) async-start(), calls=%async_computation.42 | async-start | bytes 40960
  842.3 373.6 %reduce-scatter.69.cloned.1.call-start = ((), (), s32[]{:S(2)}) async-start(), calls=%async_computation.45 | async-start | bytes 491520
  847.8 389.7 %reduce-scatter.73.cloned.1.call-start = ((), (), s32[]{:S(2)}) async-start(), calls=%async_computation.47 | async-start | bytes 491520
  852.1 404.8 %reduce-scatter.55.cloned.1.call-start = ((), (), s32[]{:S(2)}) async-start(), calls=%async_computation.38 | async-start | bytes 81920
  859.8 418.7 %reduce-scatter.67.cloned.1.call-start = ((), (), s32[]{:S(2)}) async-start(), calls=%async_computation.44 | async-start | bytes 491520
  883.9 415.6 %reduce-scatter.71.cloned.1.call-start = ((), (), s32[]{:S(2)}) async-start(), calls=%async_computation.46 | async-start | bytes 491520
  887.0 424.1 %all-reduce.28.cloned.1.call-start = ((), (), s32[]{:S(2)}) async-start(), calls=%async_computation.49 | async-start | bytes 7864320 | tf_op jit(solution)/shard_map/psum | solution.py:227
  1262.1 38.3 %copy-start.102 = (f32[12,16]{1,0:T(8,128)S(1)}, f32[12,16]{1,0:T(8,128)}, u32[]{:S(2)}) copy-start(f32[12,16]{1,0:T(8,128)} %copy.120) | copy-start | bytes 2308
  1262.1 38.3 %copy-start.103 = (f32[12,16]{1,0:T(8,128)S(1)}, f32[12,16]{1,0:T(8,128)}, u32[]{:S(2)}) copy-start(f32[12,16]{1,0:T(8,128)} %copy.118) | copy-start | bytes 2308
  (128 other events, 798.0 us)
Sparse Core Ops, SparseCore 0:
  107.3 22.7 all-gather.22
  155.7 55.6 all-reduce.13
  227.4 55.7 all-reduce.15
  324.4 21.3 all-gather.24
  372.0 55.6 all-reduce.17
  449.6 55.7 all-reduce.19
  538.8 34.7 reduce-scatter.38
  579.6 55.6 all-reduce.21
  650.9 55.7 all-reduce.23
  741.0 34.7 reduce-scatter.40
  781.8 94.2 all-reduce.25
  1134.2 103.6 all-reduce.27
Sparse Core Ops, SparseCore 1:
  158.2 30.2 all-gather.26
  190.5 29.4 all-gather.28
  374.5 30.3 all-gather.30
  407.1 29.3 all-gather.32
  789.4 22.9 reduce-scatter.60
  815.2 22.5 reduce-scatter.58
  839.9 47.1 reduce-scatter.48
  889.2 47.2 reduce-scatter.52
  938.7 47.0 reduce-scatter.44
  988.1 47.2 reduce-scatter.46
  1037.5 47.1 reduce-scatter.50
  1087.0 47.0 reduce-scatter.42
  1136.3 18.4 reduce-scatter.64
  1157.6 17.1 reduce-scatter.56
  1177.2 17.0 reduce-scatter.62
  1197.1 18.7 reduce-scatter.68
  1218.8 18.7 reduce-scatter.72
  1239.8 17.0 reduce-scatter.54
  1259.7 18.7 reduce-scatter.66
  1280.8 18.6 reduce-scatter.70
where the time goes:
time: 1330 us; the launch traced here: 1320 us
  waiting for transfers between devices  716 us (54%)
  blocking collectives  205 us (15%)
  matrix products  157 us (12%)
  local copies, waits for them, and re-layouts  125 us (9%)
  other arithmetic  99.9 us (8%)
  between operations  18.1 us (1%)
    psum x3, waiting for transfers between devices, input_reduce(): return lax.psum(partial_sum, 'tp')  167 us
    unnamed x42, waiting for transfers between devices  150 us
    reduce_scatter x2, waiting for transfers between devices, reduce_grads(): lax.psum_scatter(totals[0], 'shard', scatter_dimension=0, tiled=True)  98.6 us
    psum x4, waiting for transfers between devices, branch_reduce(): return lax.psum(partial_sum, 'tp')  95.3 us
    reduce_scatter x2, waiting for transfers between devices, reduce_grads(): lax.psum_scatter(totals[5], 'shard', scatter_dimension=1, tiled=True)  91.5 us
    unnamed x328, local copies, waits for them, and re-layouts  62.9 us
    reduce_scatter x2, waiting for transfers between devices, backward_layer(): lax.psum_scatter(grad_kv_all, 'ctx', scatter_dimension=1, tiled=True)  55 us
    all_gather x2, blocking collectives, fetch_layer(): lax.all_gather(w_qkv[layer_idx], 'shard', axis=0, tiled=True)  49.6 us
  transfers between devices with their start and end apart: 32, of which 23 were waited for; matrix products, arithmetic and copies ran while one was open for 13% of the time, Pallas kernels for 0%

commit v1 on v0

v1 whole, which is shorter than its diff:
```python
import math

import jax
import jax.numpy as jnp
from jax import lax
from jax.experimental import pallas as pl
from jax.experimental.pallas import tpu as pltpu
from jax.sharding import PartitionSpec as P

f32 = jnp.float32
bf16 = jnp.bfloat16
EPSILON = 1e-05
NN = (((1,), (0,)), ((), ()))
NT = (((1,), (1,)), ((), ()))
TN = (((0,), (0,)), ((), ()))
VMEM_BYTES = 40 * 1024 * 1024
WIDE = 128


def mm(a, b, dims=NN):
    return lax.dot_general(a, b, dims, preferred_element_type=f32)


def core_swap(x):
    return lax.ppermute(x, "tp", [(i, i ^ 1) for i in range(4)])


def x_swap(x):
    return lax.ppermute(x, "tp", [(i, i ^ 2) for i in range(4)])


def y_swap(x):
    return lax.ppermute(x, "ctx", [(0, 1), (1, 0)])


def gather_rows(x, shards):
    if shards != 4:
        return [lax.all_gather(x, "shard", axis=0, tiled=True)]
    up = [(i, (i + 1) % 4) for i in range(4)]
    down = [(i, (i - 1) % 4) for i in range(4)]
    half = x.shape[0] // 2
    below = lax.ppermute(x, "shard", up)
    above = lax.ppermute(x, "shard", down)
    far_low = lax.ppermute(below[:half], "shard", up)
    far_high = lax.ppermute(above[half:], "shard", down)
    return [x, below, above, far_low, far_high]


def piece_offsets(rows, shards):
    if shards != 4:
        return [jnp.int32(0)]
    me = lax.axis_index("shard").astype(jnp.int32)
    far = ((me + 2) % 4) * rows
    return [me * rows, ((me + 3) % 4) * rows, ((me + 1) % 4) * rows, far, far + rows // 2]


def vmem():
    return pl.BlockSpec(memory_space=pltpu.VMEM)


def run(kernel, ins, outs, scratch=(), pieces=(), scalars=None, flops=0, name=None):
    specs = [vmem() for _ in ins] + [pl.BlockSpec(memory_space=pl.ANY) for _ in pieces]
    args = list(ins) + list(pieces)
    if scalars is not None:
        specs = [pl.BlockSpec(memory_space=pltpu.SMEM)] + specs
        args = [scalars] + args
    size = sum(a.size * a.dtype.itemsize for a in args)
    size += sum(math.prod(s) * jnp.dtype(d).itemsize for s, d in outs)
    return pl.pallas_call(
        kernel,
        out_shape=[jax.ShapeDtypeStruct(s, d) for s, d in outs],
        in_specs=specs,
        out_specs=[vmem() for _ in outs],
        scratch_shapes=list(scratch),
        compiler_params=pltpu.CompilerParams(vmem_limit_bytes=VMEM_BYTES),
        cost_estimate=pl.CostEstimate(flops=int(flops), bytes_accessed=int(size), transcendentals=0),
        name=name,
    )(*args)


def weight_copies(scal, pieces, columns, dest, sems, by_parity):
    count = len(pieces) // 2
    copies = []
    for pair in range(2):
        if by_parity:
            slot = scal[8] if pair == 0 else 1 - scal[8]
        else:
            slot = pair
        for j in range(count):
            piece = pieces[pair * count + j]
            rows = piece.shape[0]
            start = pl.multiple_of(scal[j], 16)
            copies.append(
                pltpu.make_async_copy(
                    piece.at[:, columns],
                    dest.at[slot, pl.ds(start, rows), :],
                    sems.at[pair * count + j],
                )
            )
    return copies


def start_all(copies):
    for c in copies:
        c.start()


def wait_all(copies):
    for c in copies:
        c.wait()


def ln_parts(x):
    centred = x - jnp.mean(x, -1, keepdims=True)
    inv = lax.rsqrt(jnp.mean(centred * centred, -1, keepdims=True) + EPSILON)
    return centred * inv, inv


def ln_back(x, gain, dn):
    hat, inv = ln_parts(x)
    dhat = dn * gain
    dx = inv * (
        dhat
        - jnp.mean(dhat, -1, keepdims=True)
        - hat * jnp.mean(dhat * hat, -1, keepdims=True)
    )
    return dx, jnp.sum(dn * hat, 0, keepdims=True), jnp.sum(dn, 0, keepdims=True)


def split3(v):
    a = v.astype(bf16)
    r = v - a.astype(f32)
    b = r.astype(bf16)
    c = (r - b.astype(f32)).astype(bf16)
    return a, b, c


def beside(wide, column):
    a, b, c = split3(column)
    rows, size = wide.shape[0], wide.shape[1]
    return jnp.concatenate([wide, a, b, c, jnp.zeros((rows, WIDE - size - 3), bf16)], 1)


class Sizes:
    def __init__(self, mesh, frames, w_qkv, w_up):
        self.shards = mesh.shape["shard"]
        self.layers = w_qkv.shape[0]
        self.width = frames.shape[-1]
        self.rows = frames.shape[1] // 2
        self.heads = w_qkv.shape[2]
        self.hd = w_qkv.shape[3] // 3
        self.att = self.heads * self.hd
        self.hidden = w_up.shape[2]
        self.m = w_qkv.shape[1]
        self.a_cols = 4 * self.att
        self.b_cols = 2 * self.hidden


def make(z):
    R, D, A, H, HD, F = z.rows, z.width, z.att, z.heads, z.hd, z.hidden
    coef = HD ** (-0.5) / math.log(2.0)
    scale = HD ** (-0.5)
    dma = pltpu.SemaphoreType.DMA

    def proj(scal, x, vec, qb, pieces, first, prev=None):
        n = len(pieces)
        cols = pl.ds(0, z.a_cols)

        def kernel(*refs):
            it = iter(refs)
            scal_r, x_r, vec_r, qb_r = (next(it) for _ in range(4))
            extra = [] if first else [next(it) for _ in range(3)]
            piece_r = [next(it) for _ in range(n)]
            x_o = None if first else next(it)
            n_o, q0, q1, kv0, kv1, w_s, sems = (next(it) for _ in range(7))
            copies = weight_copies(scal_r, piece_r, cols, w_s, sems, True)
            start_all(copies)
            xv = x_r[...].astype(f32)
            if not first:
                xv = xv + (extra[0][...].astype(f32) + extra[1][...].astype(f32) + extra[2][5:6, :])
                x_o[...] = xv
            hat, _ = ln_parts(xv)
            nv = (hat * vec_r[0:1, :] + vec_r[2:3, :]).astype(bf16)
            n_o[...] = nv
            wait_all(copies)
            for e, (q_o, kv_o) in enumerate(((q0, kv0), (q1, kv1))):
                p = (mm(nv, w_s[e, :, : 3 * A]) + qb_r[e : e + 1, :]).astype(bf16)
                q_o[...] = p[:, :A]
                kv_o[...] = p[:, A:]

        ins = [x, vec, qb] + ([] if first else list(prev))
        outs = ([] if first else [((R, D), f32)]) + [((R, D), bf16)]
        outs += [((R, A), bf16)] * 2 + [((R, 2 * A), bf16)] * 2
        return run(
            kernel,
            ins,
            outs,
            [pltpu.VMEM((2, D, z.a_cols), bf16), dma((n,))],
            pieces,
            scal,
            4 * R * D * 3 * A,
            "project",
        )

    def aug(block, offset, fill):
        return jnp.concatenate([block[:, offset : offset + HD], fill], 1)

    def attend(q, kvs, last=False, scal=None, o_prev=None, pieces=()):
        K = 4 * R
        n = len(pieces)

        def kernel(*refs):
            it = iter(refs)
            if last:
                scal_r = next(it)
            q_r = next(it)
            kv_r = [next(it) for _ in range(4)]
            if last:
                op_r = next(it)
                piece_r = [next(it) for _ in range(n)]
            o_o, qa_o = next(it), next(it)
            if last:
                own_o, snd_o, part_o = (next(it) for _ in range(3))
            q_s, k_s, v_s, o_s = (next(it) for _ in range(4))
            if last:
                w_s, sems = next(it), next(it)
                copies = weight_copies(scal_r, piece_r, pl.ds(z.a_cols - 256, 256), w_s, sems, True)
                start_all(copies)
            ones = jnp.ones((R, HD), bf16)
            zeros = jnp.zeros((R, HD), bf16)
            for h in range(H):
                q_s[h] = aug(q_r[...], h * HD, zeros)
                for b in range(4):
                    blk = kv_r[b][...]
                    k_s[h, b * R : (b + 1) * R, :] = aug(blk, h * HD, ones)
                    v_s[h, b * R : (b + 1) * R, :] = aug(blk, A + h * HD, ones)

            def head(h, carry):
                s = mm(q_s[h], k_s[h], NT)
                top = jnp.max(s, -1, keepdims=True)
                p = jnp.exp2((s - top) * coef).astype(bf16)
                oe = mm(p, v_s[h])
                total = oe[:, HD : HD + 1]
                o_s[h] = (oe[:, :HD] / total).astype(bf16)
                lse = top + jnp.log2(total) * (1.0 / coef)
                qa_o[h] = beside(q_s[h][:, :HD], -lse)
                return carry

            lax.fori_loop(0, H, head, 0)
            o_new = jnp.concatenate([o_s[h] for h in range(H)], 1)
            o_o[...] = o_new
            if last:
                o_old = op_r[...]
                odd = scal_r[8] == 1
                own_o[...] = jnp.where(odd, o_new, o_old)
                snd_o[...] = jnp.where(odd, o_old, o_new)
                wait_all(copies)
                part = mm(o_old, w_s[0, :, 256 - A :], NT) + mm(o_new, w_s[1, :, 256 - A :], NT)
                part_o[...] = part.astype(bf16)

        ins = [q] + list(kvs) + ([o_prev] if last else [])
        outs = [((R, A), bf16), ((H, R, WIDE), bf16)]
        scratch = [
            pltpu.VMEM((H, R, WIDE), bf16),
            pltpu.VMEM((H, K, WIDE), bf16),
            pltpu.VMEM((H, K, WIDE), bf16),
            pltpu.VMEM((H, R, HD), bf16),
        ]
        if last:
            outs += [((R, A), bf16)] * 2 + [((R, D), bf16)]
            scratch += [pltpu.VMEM((2, D, 256), bf16), dma((n,))]
        return run(kernel, ins, outs, scratch, pieces, scal, 4 * H * R * K * 128, "attend")

    def feed(scal, x, pa, pb, vec, upb, pieces, cols):
        n = len(pieces)

        def kernel(scal_r, x_r, pa_r, pb_r, vec_r, upb_r, *refs):
            piece_r = refs[:n]
            y_o, swap_o, hid_o, gp_o, part_o, w_s, sems = refs[n:]
            copies = weight_copies(scal_r, piece_r, cols, w_s, sems, False)
            start_all(copies)
            y = x_r[...] + (pa_r[...].astype(f32) + pb_r[...].astype(f32) + vec_r[3:4, :])
            y_o[...] = y
            hat, _ = ln_parts(y)
            nv = (hat * vec_r[1:2, :] + vec_r[4:5, :]).astype(bf16)
            swap_o[:, :D] = nv
            wait_all(copies)
            part = None
            for s in range(2):
                u = mm(nv, w_s[s, :, :F]) + upb_r[s : s + 1, :]
                cdf = 0.5 * (1.0 + lax.erf(u * (0.5**0.5)))
                pdf = jnp.exp(-0.5 * u * u) * (1.0 / math.sqrt(2.0 * math.pi))
                hidden = (u * cdf).astype(bf16)
                gp_o[s] = (cdf + u * pdf).astype(bf16)
                if s == 0:
                    hid_o[...] = hidden
                else:
                    swap_o[:, D:] = hidden
                t = mm(hidden, w_s[s, :, F:], NT)
                part = t if part is None else part + t
            part_o[...] = part.astype(bf16)

        outs = [
            ((R, D), f32),
            ((R, D + F), bf16),
            ((R, F), bf16),
            ((2, R, F), bf16),
            ((R, D), bf16),
        ]
        return run(
            kernel,
            [x, pa, pb, vec, upb],
            outs,
            [pltpu.VMEM((2, D, 2 * F), bf16), dma((n,))],
            pieces,
            scal,
            8 * R * D * F,
            "feed",
        )

    def finish(y, pa, pb, vec):
        def kernel(y_r, pa_r, pb_r, vec_r, o):
            v = y_r[...] + (pa_r[...].astype(f32) + pb_r[...].astype(f32) + vec_r[5:6, :])
            o[...] = v.astype(bf16)

        return run(kernel, [y, pa, pb, vec], [((R, D), bf16)], name="finish")[0]

    def feed_back(scal, grad, gp, pieces, cols, before=None):
        n = len(pieces)

        def kernel(*refs):
            it = iter(refs)
            scal_r = next(it)
            if before is None:
                g_r = next(it)
            else:
                x_r, dy_r, pa_r, pb_r, vec_r = (next(it) for _ in range(5))
            gp_r = next(it)
            piece_r = [next(it) for _ in range(n)]
            swap_o, du_o, part_o, sums_o = (next(it) for _ in range(4))
            if before is not None:
                g_o, pre_o = next(it), next(it)
            w_s, sems = next(it), next(it)
            copies = weight_copies(scal_r, piece_r, cols, w_s, sems, False)
            start_all(copies)
            if before is None:
                g = g_r[...].astype(f32)
            else:
                dn = pa_r[...].astype(f32) + pb_r[...].astype(f32)
                dx, dgain, dshift = ln_back(x_r[...], vec_r[0:1, :], dn)
                g = dy_r[...] + dx
                g_o[...] = g
                pre_o[0:1, :] = dgain
                pre_o[1:2, :] = dshift
            g2 = g.astype(bf16)
            swap_o[:, :D] = g2
            sums_o[...] = jnp.sum(g2.astype(f32), 0, keepdims=True)
            wait_all(copies)
            part = None
            for s in range(2):
                dh = mm(g2, w_s[s, :, F:])
                du = (gp_r[s].astype(f32) * dh).astype(bf16)
                if s == 0:
                    du_o[...] = du
                else:
                    swap_o[:, D:] = du
                t = mm(du, w_s[s, :, :F], NT)
                part = t if part is None else part + t
            part_o[...] = part.astype(bf16)

        ins = ([grad] if before is None else list(before)) + [gp]
        outs = [((R, D + F), bf16), ((R, F), bf16), ((R, D), bf16), ((1, D), f32)]
        if before is not None:
            outs += [((R, D), f32), ((2, D), f32)]
        return run(
            kernel,
            ins,
            outs,
            [pltpu.VMEM((2, D, 2 * F), bf16), dma((n,))],
            pieces,
            scal,
            8 * R * D * F,
            "feed_back",
        )

    def feed_grads(swap_f, recv_f, hid, swap_b, recv_b, du):
        def kernel(sf, rf, h_r, sb, rb, du_r, g_o, b_o):
            g_o[:, :F] = (mm(sf[:, :D], du_r[...], TN) + mm(rf[:, :D], rb[:, D:], TN)).astype(bf16)
            g_o[:, F:] = (mm(sb[:, :D], h_r[...], TN) + mm(rb[:, :D], rf[:, D:], TN)).astype(bf16)
            b_o[...] = jnp.sum(du_r[...].astype(f32), 0, keepdims=True) + jnp.sum(
                rb[:, D:].astype(f32), 0, keepdims=True
            )

        return run(
            kernel,
            [swap_f, recv_f, hid, swap_b, recv_b, du],
            [((D, 2 * F), bf16), ((1, F), f32)],
            flops=8 * R * D * F,
            name="feed_grads",
        )

    def middle_back(scal, y, g, pa, pb, vec, o0, o1, pieces):
        n = len(pieces)

        def kernel(scal_r, y_r, g_r, pa_r, pb_r, vec_r, o0_r, o1_r, *refs):
            piece_r = refs[:n]
            dy_o, g1_o, d0_o, d1_o, sums_o, w_s, sems = refs[n:]
            copies = weight_copies(scal_r, piece_r, pl.ds(z.a_cols - 256, 256), w_s, sems, True)
            start_all(copies)
            dn = pa_r[...].astype(f32) + pb_r[...].astype(f32)
            dx, dgain, dshift = ln_back(y_r[...], vec_r[1:2, :], dn)
            dy = g_r[...].astype(f32) + dx
            dy_o[...] = dy
            g1 = dy.astype(bf16)
            g1_o[...] = g1
            sums_o[0:1, :] = dgain
            sums_o[1:2, :] = jnp.sum(g1.astype(f32), 0, keepdims=True)
            sums_o[2:3, :] = dshift
            wait_all(copies)
            for e, (o_r, d_o) in enumerate(((o0_r, d0_o), (o1_r, d1_o))):
                do = mm(g1, w_s[e, :, 256 - A :]).astype(bf16)
                prod = do.astype(f32) * o_r[...].astype(f32)
                for h in range(H):
                    lanes = slice(h * HD, (h + 1) * HD)
                    d_o[h] = beside(do[:, lanes], -jnp.sum(prod[:, lanes], -1, keepdims=True))

        outs = [((R, D), f32), ((R, D), bf16)] + [((H, R, WIDE), bf16)] * 2 + [((3, D), f32)]
        return run(
            kernel,
            [y, g, pa, pb, vec, o0, o1],
            outs,
            [pltpu.VMEM((2, D, 256), bf16), dma((n,))],
            pieces,
            scal,
            4 * R * D * A,
            "middle_back",
        )

    def attend_back(qa, kvs, da):
        K = 4 * R

        def kernel(qa_r, k0, k1, k2, k3, da_r, dq_o, e0, e1, e2, e3, k_s, v_s, dk_s, dv_s, dq_s):
            ones = jnp.ones((R, HD), bf16)
            for h in range(H):
                for b, kv_r in enumerate((k0, k1, k2, k3)):
                    blk = kv_r[...]
                    k_s[h, b * R : (b + 1) * R, :] = aug(blk, h * HD, ones)
                    v_s[h, b * R : (b + 1) * R, :] = aug(blk, A + h * HD, ones)

            def head(h, carry):
                qv = qa_r[h]
                dv_in = da_r[h]
                dqt = jnp.zeros((WIDE, R), f32)
                for b in range(4):
                    at = slice(b * R, (b + 1) * R)
                    kb = k_s[h, at, :]
                    p = jnp.exp2(mm(kb, qv, NT) * coef)
                    ds = (p * mm(v_s[h, at, :], dv_in, NT)).astype(bf16)
                    dv_s[h, at, :] = mm(p.astype(bf16), dv_in).astype(bf16)
                    dk_s[h, at, :] = (mm(ds, qv) * scale).astype(bf16)
                    dqt = dqt + mm(kb, ds, TN)
                dq_s[h] = (dqt.T * scale).astype(bf16)
                return carry

            lax.fori_loop(0, H, head, 0)
            dq_o[...] = jnp.concatenate([dq_s[h][:, :HD] for h in range(H)], 1)
            for b, e_o in enumerate((e0, e1, e2, e3)):
                at = slice(b * R, (b + 1) * R)
                e_o[...] = jnp.concatenate(
                    [dk_s[h, at, :HD] for h in range(H)] + [dv_s[h, at, :HD] for h in range(H)], 1
                )

        return run(
            kernel,
            [qa] + list(kvs) + [da],
            [((R, A), bf16)] + [((R, 2 * A), bf16)] * 4,
            [pltpu.VMEM((H, K, WIDE), bf16)] * 4 + [pltpu.VMEM((H, R, WIDE), bf16)],
            flops=10 * H * R * K * 128,
            name="attend_back",
        )

    def pair_sum(parts, count):
        flat = [a for group in parts for a in group]

        def kernel(*refs):
            ins, outs = refs[: len(flat)], refs[len(flat) :]
            at = 0
            for o, group in zip(outs, parts):
                total = ins[at][...].astype(f32)
                for k in range(1, len(group)):
                    total = total + ins[at + k][...].astype(f32)
                at += len(group)
                o[...] = total.astype(bf16)

        return run(kernel, flat, [(g[0].shape, bf16) for g in parts], name="pair_sum")

    def proj_back(scal, dqs, kv_parts, pieces):
        n = len(pieces)

        def kernel(scal_r, q0, q1, *refs):
            kvp = (refs[:3], refs[3:6])
            piece_r = refs[6 : 6 + n]
            own_o, snd_o, part_o, w_s, sems = refs[6 + n :]
            copies = weight_copies(scal_r, piece_r, pl.ds(0, z.a_cols), w_s, sems, True)
            start_all(copies)
            both = []
            for e, q_r in enumerate((q0, q1)):
                a, b, c = (r[...].astype(f32) for r in kvp[e])
                both.append(jnp.concatenate([q_r[...], (a + b + c).astype(bf16)], 1))
            odd = scal_r[8] == 1
            own_o[...] = jnp.where(odd, both[1], both[0])
            snd_o[...] = jnp.where(odd, both[0], both[1])
            wait_all(copies)
            part = mm(both[0], w_s[0, :, : 3 * A], NT) + mm(both[1], w_s[1, :, : 3 * A], NT)
            part_o[...] = part.astype(bf16)

        ins = list(dqs) + list(kv_parts[0]) + list(kv_parts[1])
        outs = [((R, 3 * A), bf16)] * 2 + [((R, D), bf16)]
        return run(
            kernel,
            ins,
            outs,
            [pltpu.VMEM((2, D, z.a_cols), bf16), dma((n,))],
            pieces,
            scal,
            4 * R * D * 3 * A,
            "project_back",
        )

    def proj_grads(n1, n1_r, dp, dp_r, g1, g1_r, o, o_r):
        def kernel(n_r, nr_r, p_r, pr_r, g_r, gr_r, o_i, or_i, g_o, b_o):
            first = mm(n_r[...], p_r[...], TN) + mm(nr_r[...], pr_r[...], TN)
            second = mm(g_r[...], o_i[...], TN) + mm(gr_r[...], or_i[...], TN)
            g_o[...] = jnp.concatenate([first.astype(bf16), second.astype(bf16)], 1)
            b_o[...] = jnp.sum(p_r[...].astype(f32), 0, keepdims=True) + jnp.sum(
                pr_r[...].astype(f32), 0, keepdims=True
            )

        return run(
            kernel,
            [n1, n1_r, dp, dp_r, g1, g1_r, o, o_r],
            [((D, z.a_cols), bf16), ((1, 3 * A), f32)],
            flops=4 * R * D * 4 * A,
            name="project_grads",
        )

    def input_back(x, dy, pa, pb, vec):
        def kernel(x_r, dy_r, pa_r, pb_r, vec_r, o, sums_o):
            dn = pa_r[...].astype(f32) + pb_r[...].astype(f32)
            dx, dgain, dshift = ln_back(x_r[...].astype(f32), vec_r[0:1, :], dn)
            o[...] = (dy_r[...] + dx).astype(bf16)
            sums_o[0:1, :] = dgain
            sums_o[1:2, :] = dshift

        return run(kernel, [x, dy, pa, pb, vec], [((R, D), bf16), ((2, D), f32)], name="input_back")

    return dict(locals())


def local(mesh):
    def fn(frames, cotangent, w_qkv, qv_bias, w_out, w_up, up_bias, w_down, norm_gains, shifts):
        z = Sizes(mesh, frames, w_qkv, w_up)
        assert mesh.shape["tp"] == 4 and mesh.shape["ctx"] == 2 and frames.shape[0] == 1
        k = make(z)
        L, m, R, D, A, F, H, HD, S = z.layers, z.m, z.rows, z.width, z.att, z.hidden, z.heads, z.hd, z.shards
        parity = lax.axis_index("tp") % 2
        odd = parity == 1

        qkv = w_qkv.reshape(L, m, H, 3, HD).transpose(0, 1, 3, 2, 4).reshape(L, m, 3 * A)
        own_a = jnp.concatenate([qkv, w_out.reshape(L, A, m).transpose(0, 2, 1)], -1)
        own_b = jnp.concatenate([w_up, w_down.transpose(0, 2, 1)], -1)
        offsets = piece_offsets(m, S)
        scal = jnp.stack(offsets + [jnp.int32(0)] * (8 - len(offsets)) + [parity.astype(jnp.int32)])

        def both_cores(x):
            mine = gather_rows(x, S)
            return mine + [core_swap(p) for p in mine]

        pieces_a, pieces_b, cols_b = [None] * L, [None] * L, [None] * L
        pieces_a[0] = both_cores(own_a[0])
        small = jnp.concatenate(
            [qv_bias.reshape(-1), up_bias.reshape(-1), norm_gains.reshape(-1), shifts.reshape(-1)]
        )
        small = lax.all_gather(small, "shard").astype(f32)
        cuts = [qv_bias.size, up_bias.size, norm_gains.size, shifts.size]
        cuts = [sum(cuts[: i + 1]) for i in range(4)]
        qvb = small[:, : cuts[0]].reshape(S, L, H, 2 * HD // S).transpose(1, 2, 0, 3).reshape(L, H, 2, HD)
        qvb = qvb.transpose(0, 2, 1, 3).reshape(L, 2, A)
        qb = jnp.concatenate([qvb[:, 0], jnp.zeros((L, A), f32), qvb[:, 1]], -1)
        upb = small[:, cuts[0] : cuts[1]].reshape(S, L, F // 64, 64 // S).transpose(1, 2, 0, 3).reshape(L, F)
        biases = jnp.concatenate([qb, upb], -1)
        other = core_swap(biases)
        qb_pair = jnp.stack([biases[:, : 3 * A], other[:, : 3 * A]], 1)
        qb_pair = jnp.where(odd, qb_pair[:, ::-1], qb_pair)
        upb_pair = jnp.stack([biases[:, 3 * A :], other[:, 3 * A :]], 1)
        gains = small[:, cuts[1] : cuts[2]].reshape(S, L, 2, m).transpose(1, 2, 0, 3).reshape(L, 2, D)
        offs = small[:, cuts[2] :].reshape(S, L, 4, m).transpose(1, 2, 0, 3).reshape(L, 4, D)
        vecs = jnp.concatenate([gains, offs, jnp.zeros((L, 2, D), f32)], 1)

        pieces_b[0] = both_cores(own_b[0])
        cols_b[0] = pl.ds(0, 2 * F)
        for layer in range(1, L):
            pieces_a[layer] = both_cores(jnp.concatenate([own_a[layer], own_b[layer]], -1))
            pieces_b[layer] = pieces_a[layer]
            cols_b[layer] = pl.ds(z.a_cols, 2 * F)

        def my_rows(x):
            return lax.dynamic_slice_in_dim(x.reshape(2 * R, D), parity * R, R, 0)

        stream = my_rows(frames)
        kept = []
        part = None
        for layer in range(L):
            vec = vecs[layer]
            if layer == 0:
                x = stream
                n1, q0, q1, kv0, kv1 = k["proj"](scal, x, vec, qb_pair[0], pieces_a[0], True)
            else:
                x, n1, q0, q1, kv0, kv1 = k["proj"](
                    scal, y, vec, qb_pair[layer], pieces_a[layer], False, (part, x_swap(part), vecs[layer - 1])
                )
            kvs = []
            for kv in (kv0, kv1):
                far = y_swap(kv)
                kvs.append((kv, core_swap(kv), far, core_swap(far)))
            o0, qa0 = k["attend"](q0, kvs[0])
            o1, qa1, o_own, o_snd, att_part = k["attend"](q1, kvs[1], True, scal, o0, pieces_a[layer])
            y, swap_f, hid, gp, part = k["feed"](
                scal, x, att_part, x_swap(att_part), vec, upb_pair[layer], pieces_b[layer], cols_b[layer]
            )
            kept.append((x, n1, kvs, (qa0, qa1), (o0, o1), o_own, o_snd, y, swap_f, hid, gp))
        out_rows = k["finish"](y, part, x_swap(part), vecs[L - 1])

        def whole_rows(mine):
            theirs = core_swap(mine)
            return jnp.where(
                odd, jnp.concatenate([theirs, mine], 0), jnp.concatenate([mine, theirs], 0)
            )[None]

        out_frames = whole_rows(out_rows)

        grads_a, grads_b, rows_small, cols_small = [None] * L, [None] * L, [None] * L, [None] * L
        before = None
        g = my_rows(cotangent)
        pre = None
        for layer in reversed(range(L)):
            vec = vecs[layer]
            x, n1, kvs, qas, os, o_own, o_snd, y, swap_f, hid, gp = kept[layer]
            if before is None:
                swap_b, du, part, sum_g2 = k["feed_back"](scal, g, gp, pieces_b[layer], cols_b[layer])
            else:
                swap_b, du, part, sum_g2, g, pre = k["feed_back"](
                    scal, None, gp, pieces_b[layer], cols_b[layer], before
                )
                rows_small[layer + 1] = (pre,) + rows_small[layer + 1]
            far = x_swap(part)
            grad_b, d_upb = k["feed_grads"](swap_f, core_swap(swap_f), hid, swap_b, core_swap(swap_b), du)
            grads_b[layer] = grad_b
            dy, g1, d0, d1, mid = k["middle_back"](
                scal, y, g, part, far, vec, os[0], os[1], pieces_a[layer]
            )
            dqs, kv_parts = [], []
            for e in range(2):
                dq, own, near, y_own, y_near = k["attend_back"](qas[e], kvs[e], (d0, d1)[e])
                pair = core_swap(jnp.stack([near, y_near]))
                cross = k["pair_sum"]([[y_own, pair[1]]], 1)[0]
                dqs.append(dq)
                kv_parts.append((own, pair[0], y_swap(cross)))
            dp, dp_snd, part = k["proj_back"](scal, dqs, kv_parts, pieces_a[layer])
            far = x_swap(part)
            grad_a, d_qvb = k["proj_grads"](
                n1, core_swap(n1), dp, core_swap(dp_snd), g1, core_swap(g1), o_own, core_swap(o_snd)
            )
            grads_a[layer] = grad_a
            before = (x, dy, part, far, vec)
            rows_small[layer] = (mid, sum_g2)
            cols_small[layer] = (d_qvb, d_upb)
        grad_rows, pre = k["input_back"](*before)
        rows_small[0] = (pre,) + rows_small[0]
        frames_grad = whole_rows(grad_rows)

        def reduce(grad):
            mine = lax.psum_scatter(grad, "shard", scatter_dimension=0, tiled=True)
            return mine.astype(f32) + y_swap(mine).astype(f32)

        outs_qkv, outs_out, outs_up, outs_down = [], [], [], []
        for layer in range(L):
            ga, gb = reduce(grads_a[layer]), reduce(grads_b[layer])
            outs_qkv.append(ga[:, : 3 * A].reshape(m, 3, H, HD).transpose(0, 2, 1, 3).reshape(m, H, 3 * HD))
            outs_out.append(ga[:, 3 * A :].T.reshape(H, HD, m))
            outs_up.append(gb[:, :F])
            outs_down.append(gb[:, F:].T)

        wide = []
        for layer in range(L):
            pre, mid, sum_g2 = rows_small[layer]
            wide.append(jnp.concatenate([pre[0:1], mid[0:1], pre[1:2], mid[1:3], sum_g2], 0))
        wide = jnp.stack(wide)
        wide = wide + core_swap(wide)
        qvs = jnp.stack([jnp.concatenate([c[0][0, :A], c[0][0, 2 * A :]]) for c in cols_small])
        ups = jnp.stack([c[1][0] for c in cols_small])
        wide = wide.reshape(L, 6, S, m).transpose(2, 0, 1, 3).reshape(S, -1)
        qvs = qvs.reshape(L, 2, H, HD).transpose(0, 2, 1, 3).reshape(L, H, S, 2 * HD // S)
        qvs = qvs.transpose(2, 0, 1, 3).reshape(S, -1)
        ups = ups.reshape(L, F // 64, S, 64 // S).transpose(2, 0, 1, 3).reshape(S, -1)
        tiny = jnp.concatenate([wide, qvs, ups], 1)
        tiny = lax.psum(tiny, ("shard", "ctx"))
        tiny = lax.dynamic_index_in_dim(tiny, lax.axis_index("shard"), 0, keepdims=False)
        n_wide, n_qv = L * 6 * m, L * H * 2 * HD // S
        wide = tiny[:n_wide].reshape(L, 6, m)
        g_qvb = tiny[n_wide : n_wide + n_qv].reshape(L, H, 2 * HD // S)
        g_upb = tiny[n_wide + n_qv :].reshape(L, F // 64, 64 // S)
        return (
            out_frames,
            frames_grad,
            jnp.stack(outs_qkv),
            g_qvb,
            jnp.stack(outs_out),
            jnp.stack(outs_up),
            g_upb,
            jnp.stack(outs_down),
            wide[:, :2],
            wide[:, 2:],
        )

    return fn


def solution(mesh):
    specs = (
        P("shard", "ctx", None),
        P("shard", "ctx", None),
        P(None, "shard", "tp", None),
        P(None, "tp", "shard"),
        P(None, "tp", None, "shard"),
        P(None, "shard", "tp"),
        P(None, "tp", "shard"),
        P(None, "tp", "shard"),
        P(None, None, "shard"),
        P(None, None, "shard"),
    )
    return jax.shard_map(local(mesh), mesh=mesh, in_specs=specs, out_specs=specs, check_vma=False)
```

time: 1330 us -> 555 us (0.42)
  waiting for transfers between devices: 716 us -> 215 us
  matrix products: 157 us -> 0 us
  blocking collectives: 205 us -> 58.3 us
  Pallas kernels: 0 us -> 103 us
  other arithmetic: 99.9 us -> 15.1 us
  starting transfers between devices: 2.31 us -> 54.2 us
  local copies, waits for them, and re-layouts: 125 us -> 81.2 us
    reduce_scatter x8 -> x4, waiting for transfers between devices: 295 us -> 0.05 us  [reduce(): mine = lax.psum_scatter(grad, 'shard', scatter_dimension=0, tiled=True)]
    psum x8 -> x0, waiting for transfers between devices: 262 us -> none  [the longest x3 167 us: input_reduce(): return lax.psum(partial_sum, 'tp')]
    ppermute x0 -> x75, waiting for transfers between devices: none -> 215 us  [the longest x8 95.8 us: x_swap(): return lax.ppermute(x, 'tp', [(i, i ^ 2) for i in range(4)])]
    all_gather x12 -> x0, blocking collectives: 197 us -> none  [the longest x2 49.6 us: fetch_layer(): lax.all_gather(w_qkv[layer_idx], 'shard', axis=0, tiled=True)]
    dot_general x36 -> x0, matrix products: 157 us -> none  [the longest x2 18.1 us: forward_layer(): jnp.dot(normed_mid, w_up, preferred_element_type=jnp.float32)]
    unnamed x42 -> x4, waiting for transfers between devices: 150 us -> 0.07 us
    pallas_call x0 -> x28, Pallas kernels: none -> 103 us  [run(): pl.pallas_call(kernel, out_shape=[jax.ShapeDtypeStruct(s, d) for s, d in...]
    ppermute x0 -> x75, starting transfers between devices: none -> 54 us  [the longest x12 14.1 us: y_swap(): return lax.ppermute(x, 'ctx', [(0, 1), (1, 0)])]
  transfers between devices with their start and end apart: 32 -> 79, of which waited for: 23 -> 36; matrix products, arithmetic and copies ran while one was open for 13% -> 6% of each run, Pallas kernels for 0% -> 13%
where the time goes in v1:
time: 555 us; the launch traced here: 544 us
  waiting for transfers between devices  215 us (39%)
  Pallas kernels  103 us (19%)
  local copies, waits for them, and re-layouts  81.2 us (15%)
  blocking collectives  58.3 us (11%)
  starting transfers between devices  54.2 us (10%)
  between operations  16.7 us (3%)
  other arithmetic  15.1 us (3%)
    pallas_call x28, Pallas kernels, run(): pl.pallas_call(kernel, out_shape=[jax.ShapeDtypeStruct(s, d) for s, d in...  103 us
    ppermute x8, waiting for transfers between devices, x_swap(): return lax.ppermute(x, 'tp', [(i, i ^ 2) for i in range(4)])  95.8 us
    unnamed x337, local copies, waits for them, and re-layouts  62.3 us
    ppermute x12, waiting for transfers between devices, y_swap(): return lax.ppermute(x, 'ctx', [(0, 1), (1, 0)])  56.8 us
    psum x1, blocking collectives, fn(): tiny = lax.psum(tiny, ('shard', 'ctx'))  37.5 us
    ppermute x3, waiting for transfers between devices, gather_rows(): far_low = lax.ppermute(below[:half], 'shard', up)  35.4 us
    unnamed x1, blocking collectives  20.8 us
    ppermute x43, waiting for transfers between devices, core_swap(): return lax.ppermute(x, 'tp', [(i, i ^ 1) for i in range(4)])  14.8 us
  transfers between devices with their start and end apart: 79, of which 36 were waited for; matrix products, arithmetic and copies ran while one was open for 6% of the time, Pallas kernels for 13%

profile of v1, /device:TPU:0, one launch (start us, length us, event | category | flops | bytes accessed | tf_op | source)
XLA Modules:
  0.0 543.8 jit_solution(6774597631717518927)
XLA Ops:
  10.6 3.0 collective-permute-start.1
  19.0 20.8 %all-reduce = bf16[11520]{0:T(1024)(128)(2,1)S(1)} all-reduce(bf16[11520]{0:T(1024)(128)(2,1)S(1)} %dynamic-update-slice), channel_id=2, replica_groups=mesh['shard'=4,'ctx'=2,'tp'=4] {'shard'}, use_global_device_ids=true, to_apply=%add | all-reduce | flops 11520 | bytes 46080
  49.6 2.8 collective-permute-start.4
  52.9 11.6 %collective-permute-done.3.refs_7_.refs_10_.refs_3_.refs_9_ = bf16[96,768]{1,0:T(8,128)(2,1)S(1)} collective-permute-done((bf16[96,768]{1,0:T(8,128)(2,1)S(1)}, bf16[96,768]{1,0:T(8,128)(2,1)S(1)}, u32[]{:S(2)}, u32[]{:S(2)}) %collective-permute-start.3) | collective-permute-done | bytes 147488 | tf_op jit(solution)/shard_map/ppermute | solution.py:44
  69.0 3.5 project.2
  75.7 6.8 %collective-permute-done.18.refs_2_.refs_9_ = bf16[192,1536]{1,0:T(8,128)(2,1)S(1)} collective-permute-done((bf16[192,1536]{1,0:T(8,128)(2,1)S(1)}, bf16[192,1536]{1,0:T(8,128)(2,1)S(1)}, u32[]{:S(2)}, u32[]{:S(2)}) %collective-permute-start.18) | collective-permute-done | bytes 589856 | tf_op jit(solution)/shard_map/ppermute | solution.py:43
  83.2 3.1 collective-permute-start.28
  94.2 5.3 attend.4
  99.7 6.7 %attend.5 = (bf16[384,192]{1,0:T(8,128)(2,1)S(1)}, bf16[3,384,128]{2,1,0:T(8,128)(2,1)S(1)}, bf16[384,192]{1,0:T(8,128)(2,1)S(1)}, bf16[384,192]{1,0:T(8,128)(2,1)S(1)}, bf16[384,768]{1,0:T(8,128)(2,1)S(1)}) custom-call(s32[9]{0:T(128)S(1)} %stack.123.refs_0_.scal_r, bf16[384,192]{1,0:T(8,128)(2,1)S(1)} %get-tuple-element.101.refs_1_, ...), custom_call_target="tpu_custom_call" | custom-call | flops 905969664 | bytes 5160996 | tf_op jit(solution)/shard_map/attend/pallas_call | solution.py:69
  108.5 23.7 %collective-permute-done.19.refs_3_.refs_10_ = bf16[96,1536]{1,0:T(8,128)(2,1)S(1)} collective-permute-done((bf16[96,1536]{1,0:T(8,128)(2,1)S(1)}, bf16[96,1536]{1,0:T(8,128)(2,1)S(1)}, u32[]{:S(2)}, u32[]{:S(2)}) %collective-permute-start.19) | collective-permute-done | bytes 294944 | tf_op jit(solution)/shard_map/ppermute | solution.py:44
  132.3 2.9 collective-permute-done.20.refs_4_.refs_11_
  146.2 4.8 collective-permute-done.16.pb_r
  166.7 4.6 feed.2
  178.4 11.6 %collective-permute-done.26.refs_5_ = bf16[384,768]{1,0:T(8,128)(2,1)S(1)} collective-permute-done((bf16[384,768]{1,0:T(8,128)(2,1)S(1)}, bf16[384,768]{1,0:T(8,128)(2,1)S(1)}, u32[]{:S(2)}, u32[]{:S(2)}) %collective-permute-start.26) | collective-permute-done | bytes 589856 | tf_op jit(solution)/shard_map/ppermute | solution.py:29
  190.0 3.1 project.3
  195.2 7.9 %collective-permute-done.40.refs_3_.k2 = bf16[384,384]{1,0:T(8,128)(2,1)S(1)} collective-permute-done((bf16[384,384]{1,0:T(8,128)(2,1)S(1)}, bf16[384,384]{1,0:T(8,128)(2,1)S(1)}, u32[]{:S(2)}, u32[]{:S(2)}) %collective-permute-start.40) | collective-permute-done | bytes 294944 | tf_op jit(solution)/shard_map/ppermute | solution.py:33
  203.6 4.5 collective-permute-done.37.refs_4_.k2
  208.1 5.3 attend.6
  213.5 6.7 %attend.7 = (bf16[384,192]{1,0:T(8,128)(2,1)S(1)}, bf16[3,384,128]{2,1,0:T(8,128)(2,1)S(1)}, bf16[384,192]{1,0:T(8,128)(2,1)S(1)}, bf16[384,192]{1,0:T(8,128)(2,1)S(1)}, bf16[384,768]{1,0:T(8,128)(2,1)S(1)}) custom-call(s32[9]{0:T(128)S(1)} %stack.123.refs_0_.scal_r, bf16[384,192]{1,0:T(8,128)(2,1)S(1)} %get-tuple-element.110.refs_1_, ...), custom_call_target="tpu_custom_call" | custom-call | flops 905969664 | bytes 9879588 | tf_op jit(solution)/shard_map/attend/pallas_call | solution.py:69
  221.7 14.2 %collective-permute-done.42.pb_r = bf16[384,768]{1,0:T(8,128)(2,1)S(1)} collective-permute-done((bf16[384,768]{1,0:T(8,128)(2,1)S(1)}, bf16[384,768]{1,0:T(8,128)(2,1)S(1)}, u32[]{:S(2)}, u32[]{:S(2)}) %collective-permute-start.42) | collective-permute-done | bytes 589856 | tf_op jit(solution)/shard_map/ppermute | solution.py:29
  235.9 4.7 feed.3
  241.5 5.0 feed_back.2
  248.1 13.5 %collective-permute-done.45.pb_r = bf16[384,768]{1,0:T(8,128)(2,1)S(1)} collective-permute-done((bf16[384,768]{1,0:T(8,128)(2,1)S(1)}, bf16[384,768]{1,0:T(8,128)(2,1)S(1)}, u32[]{:S(2)}, u32[]{:S(2)}) %collective-permute-start.45) | collective-permute-done | bytes 589856 | tf_op jit(solution)/shard_map/ppermute | solution.py:29
  261.6 3.7 middle_back.2
  265.3 6.2 %attend_back.5 = (bf16[384,192]{1,0:T(8,128)(2,1)S(1)}, bf16[384,384]{1,0:T(8,128)(2,1)S(1)}, bf16[384,384]{1,0:T(8,128)(2,1)S(1)}, bf16[384,384]{1,0:T(8,128)(2,1)S(1)}, bf16[384,384]{1,0:T(8,128)(2,1)S(1)}) custom-call(bf16[3,384,128]{2,1,0:T(8,128)(2,1)S(1)} %get-tuple-element.125.qa_r, bf16[384,384]{1,0:T(8,128)(2,1)S(1)} %get-tuple-element.111.refs_2_.k0, ...), custom_call_target="tpu_custom_call" | custom-call | flops 2264924160 | bytes 3096576 | tf_op jit(solution)/shard_map/attend_back/pallas_call | solution.py:69
  271.6 6.4 %attend_back.4 = (bf16[384,192]{1,0:T(8,128)(2,1)S(1)}, bf16[384,384]{1,0:T(8,128)(2,1)S(1)}, bf16[384,384]{1,0:T(8,128)(2,1)S(1)}, bf16[384,384]{1,0:T(8,128)(2,1)S(1)}, bf16[384,384]{1,0:T(8,128)(2,1)S(1)}) custom-call(bf16[3,384,128]{2,1,0:T(8,128)(2,1)S(1)} %get-tuple-element.122.qa_r, bf16[384,384]{1,0:T(8,128)(2,1)S(1)} %get-tuple-element.113.refs_1_.k0, ...), custom_call_target="tpu_custom_call" | custom-call | flops 2264924160 | bytes 3096576 | tf_op jit(solution)/shard_map/attend_back/pallas_call | solution.py:69
  282.5 6.2 %collective-permute-done.49.refs_5_ = bf16[384,384]{1,0:T(8,128)(2,1)S(1)} collective-permute-done((bf16[384,384]{1,0:T(8,128)(2,1)S(1)}, bf16[384,384]{1,0:T(8,128)(2,1)S(1)}, u32[]{:S(2)}, u32[]{:S(2)}) %collective-permute-start.49) | collective-permute-done | bytes 294944 | tf_op jit(solution)/shard_map/ppermute | solution.py:33
  288.7 5.4 collective-permute-done.47.refs_2_
  294.1 3.0 project_back.2
  300.1 2.9 project_grads.3
  310.4 2.8 feed_grads.3
  316.8 14.1 %collective-permute-done.50.refs_4_ = bf16[384,768]{1,0:T(8,128)(2,1)S(1)} collective-permute-done((bf16[384,768]{1,0:T(8,128)(2,1)}, bf16[384,768]{1,0:T(8,128)(2,1)S(1)}, u32[]{:S(2)}, u32[]{:S(2)}) %collective-permute-start.50) | collective-permute-done | bytes 589856 | tf_op jit(solution)/shard_map/ppermute | solution.py:29
  341.2 5.2 feed_back.3
  350.4 13.2 %collective-permute-done.51.pb_r = bf16[384,768]{1,0:T(8,128)(2,1)S(1)} collective-permute-done((bf16[384,768]{1,0:T(8,128)(2,1)S(1)}, bf16[384,768]{1,0:T(8,128)(2,1)S(1)}, u32[]{:S(2)}, u32[]{:S(2)}) %collective-permute-start.51) | collective-permute-done | bytes 589856 | tf_op jit(solution)/shard_map/ppermute | solution.py:29
  363.7 3.7 middle_back.3
  368.0 6.2 %attend_back.7 = (bf16[384,192]{1,0:T(8,128)(2,1)S(1)}, bf16[384,384]{1,0:T(8,128)(2,1)S(1)}, bf16[384,384]{1,0:T(8,128)(2,1)S(1)}, bf16[384,384]{1,0:T(8,128)(2,1)S(1)}, bf16[384,384]{1,0:T(8,128)(2,1)S(1)}) custom-call(bf16[3,384,128]{2,1,0:T(8,128)(2,1)S(1)} %copy-done.136, bf16[384,384]{1,0:T(8,128)(2,1)S(1)} %copy-done.74, ...), custom_call_target="tpu_custom_call" | custom-call | flops 2264924160 | bytes 3096576 | tf_op jit(solution)/shard_map/attend_back/pallas_call | solution.py:69
  375.5 6.2 %attend_back.6 = (bf16[384,192]{1,0:T(8,128)(2,1)S(1)}, bf16[384,384]{1,0:T(8,128)(2,1)S(1)}, bf16[384,384]{1,0:T(8,128)(2,1)S(1)}, bf16[384,384]{1,0:T(8,128)(2,1)S(1)}, bf16[384,384]{1,0:T(8,128)(2,1)S(1)}) custom-call(bf16[3,384,128]{2,1,0:T(8,128)(2,1)S(1)} %copy-done.142, bf16[384,384]{1,0:T(8,128)(2,1)S(1)} %copy-done.128, ...), custom_call_target="tpu_custom_call" | custom-call | flops 2264924160 | bytes 3096576 | tf_op jit(solution)/shard_map/attend_back/pallas_call | solution.py:69
  386.1 5.8 %collective-permute-done.55.refs_5_ = bf16[384,384]{1,0:T(8,128)(2,1)S(1)} collective-permute-done((bf16[384,384]{1,0:T(8,128)(2,1)S(1)}, bf16[384,384]{1,0:T(8,128)(2,1)S(1)}, u32[]{:S(2)}, u32[]{:S(2)}) %collective-permute-start.55) | collective-permute-done | bytes 294944 | tf_op jit(solution)/shard_map/ppermute | solution.py:33
  391.8 5.9 %collective-permute-done.53.refs_2_ = bf16[384,384]{1,0:T(8,128)(2,1)S(1)} collective-permute-done((bf16[384,384]{1,0:T(8,128)(2,1)S(1)}, bf16[384,384]{1,0:T(8,128)(2,1)S(1)}, u32[]{:S(2)}, u32[]{:S(2)}) %collective-permute-start.53) | collective-permute-done | bytes 294944 | tf_op jit(solution)/shard_map/ppermute | solution.py:33
  397.8 3.6 project_back.3
  404.3 2.9 project_grads.2
  415.1 4.1 feed_grads.2
  422.4 13.9 %collective-permute-done.43.pb_r = bf16[384,768]{1,0:T(8,128)(2,1)S(1)} collective-permute-done((bf16[384,768]{1,0:T(8,128)(2,1)S(1)}, bf16[384,768]{1,0:T(8,128)(2,1)S(1)}, u32[]{:S(2)}, u32[]{:S(2)}) %collective-permute-start.43) | collective-permute-done | bytes 589856 | tf_op jit(solution)/shard_map/ppermute | solution.py:29
  448.2 10.5 %collective-permute-done.56.pb_r = bf16[384,768]{1,0:T(8,128)(2,1)S(1)} collective-permute-done((bf16[384,768]{1,0:T(8,128)(2,1)S(1)}, bf16[384,768]{1,0:T(8,128)(2,1)S(1)}, u32[]{:S(2)}, u32[]{:S(2)}) %collective-permute-start.56) | collective-permute-done | bytes 589856 | tf_op jit(solution)/shard_map/ppermute | solution.py:29
  464.1 37.5 %psum.7 = f32[4,2880]{1,0:T(4,128)S(1)} all-reduce(f32[4,2880]{1,0:T(4,128)S(1)} %concatenate.105), channel_id=1, replica_groups=mesh['shard'=4,'ctx'=2,'tp'=4] {'shard','ctx'}, use_global_device_ids=true, to_apply=%region_2.3 | all-reduce | flops 11520 | bytes 92160 | tf_op jit(solution)/shard_map/psum | solution.py:707
  509.5 11.5 %collective-permute-done.74 = bf16[192,1536]{1,0:T(8,128)(2,1)} collective-permute-done((bf16[192,1536]{1,0:T(8,128)(2,1)}, bf16[192,1536]{1,0:T(8,128)(2,1)}, u32[]{:S(2)}, u32[]{:S(2)}) %collective-permute-start.74) | collective-permute-done | bytes 589856 | tf_op jit(solution)/shard_map/ppermute | solution.py:33
  522.5 3.6 collective-permute-done.62
  529.0 3.6 collective-permute-done.73
  (605 shorter events, 163.0 us)
Async XLA Ops:
  7.2 454.6 %reduce-scatter.7.cloned.1.call-start = ((), (), s32[]{:S(2)}) async-start(), calls=%async_computation.5 | async-start | bytes 1474560 | tf_op jit(solution)/shard_map/reduce_scatter | solution.py:683
  10.6 37.1 %collective-permute-start.1 = (bf16[192,768]{1,0:T(8,128)(2,1)S(1)}, bf16[192,768]{1,0:T(8,128)(2,1)S(1)}, u32[]{:S(2)}, u32[]{:S(2)}) collective-permute-start(bf16[192,768]{1,0:T(8,128)(2,1)S(1)} %get-tuple-element.219.refs_4_.refs_7_.refs_0_.refs_6_), channel_id=1, source_target_pairs={{0,8},{8,16},{16,24},{24,0},{1,9},{9,17},{17,25},{25,1},{2,10},{10... | collective-permute-start | bytes 884744 | tf_op jit(solution)/shard_map/ppermute | solution.py:42
  13.6 36.0 %collective-permute-start.2 = (bf16[192,768]{1,0:T(8,128)(2,1)S(1)}, bf16[192,768]{1,0:T(8,128)(2,1)S(1)}, u32[]{:S(2)}, u32[]{:S(2)}) collective-permute-start(bf16[192,768]{1,0:T(8,128)(2,1)S(1)} %get-tuple-element.219.refs_4_.refs_7_.refs_0_.refs_6_), channel_id=1, source_target_pairs={{0,24},{8,0},{16,8},{24,16},{1,25},{9,1},{17,9},{25,17},{2,26},{10... | collective-permute-start | bytes 884744 | tf_op jit(solution)/shard_map/ppermute | solution.py:43
  15.6 36.8 %collective-permute-start.5 = (bf16[192,768]{1,0:T(8,128)(2,1)S(1)}, bf16[192,768]{1,0:T(8,128)(2,1)S(1)}, u32[]{:S(2)}, u32[]{:S(2)}) collective-permute-start(bf16[192,768]{1,0:T(8,128)(2,1)S(1)} %get-tuple-element.219.refs_4_.refs_7_.refs_0_.refs_6_), channel_id=1, source_target_pairs={{0,1},{1,0},{2,3},{3,2},{4,5},{5,4},{6,7},{7,6},{8,9},{9,8},{10,11... | collective-permute-start | bytes 884744 | tf_op jit(solution)/shard_map/ppermute | solution.py:25
  43.4 32.0 %collective-permute-start.17 = (bf16[192,1536]{1,0:T(8,128)(2,1)S(1)}, bf16[192,1536]{1,0:T(8,128)(2,1)}, u32[]{:S(2)}, u32[]{:S(2)}) collective-permute-start(bf16[192,1536]{1,0:T(8,128)(2,1)S(1)} %get-tuple-element.217.refs_0_.refs_7_), channel_id=1, source_target_pairs={{0,8},{8,16},{16,24},{24,0},{1,9},{9,17},{17,25},{25,1},{2,10},{10... | collective-permute-start | bytes 1769480 | tf_op jit(solution)/shard_map/ppermute | solution.py:42
  47.7 16.8 %collective-permute-start.3 = (bf16[96,768]{1,0:T(8,128)(2,1)S(1)}, bf16[96,768]{1,0:T(8,128)(2,1)S(1)}, u32[]{:S(2)}, u32[]{:S(2)}) collective-permute-start(bf16[96,768]{1,0:T(8,128)(2,1)S(1)} %slice.246), channel_id=1, source_target_pairs={{0,8},{8,16},{16,24},{24,0},{1,9},{9,17},{17,25},{25,1},{2,10},{10... | collective-permute-start | bytes 442376 | tf_op jit(solution)/shard_map/ppermute | solution.py:44
  49.6 17.6 %collective-permute-start.4 = (bf16[96,768]{1,0:T(8,128)(2,1)S(1)}, bf16[96,768]{1,0:T(8,128)(2,1)S(1)}, u32[]{:S(2)}, u32[]{:S(2)}) collective-permute-start(bf16[96,768]{1,0:T(8,128)(2,1)S(1)} %slice.247), channel_id=1, source_target_pairs={{0,24},{8,0},{16,8},{24,16},{1,25},{9,1},{17,9},{25,17},{2,26},{10... | collective-permute-start | bytes 442376 | tf_op jit(solution)/shard_map/ppermute | solution.py:45
  52.4 16.6 %collective-permute-start.6 = (bf16[192,768]{1,0:T(8,128)(2,1)S(1)}, bf16[192,768]{1,0:T(8,128)(2,1)S(1)}, u32[]{:S(2)}, u32[]{:S(2)}) collective-permute-start(bf16[192,768]{1,0:T(8,128)(2,1)S(1)} %collective-permute-done.1.refs_5_.refs_8_.refs_1_.refs_7_), channel_id=1, source_target_pairs={{0,1},{1,0},{2,3},{3,2},{4,5},{5,4},{6,7},{7,6},{8,9},{9,8},{10,11... | collective-permute-start | bytes 884744 | tf_op jit(solution)/shard_map/ppermute | solution.py:25
  52.4 16.6 %collective-permute-start.7 = (bf16[192,768]{1,0:T(8,128)(2,1)S(1)}, bf16[192,768]{1,0:T(8,128)(2,1)S(1)}, u32[]{:S(2)}, u32[]{:S(2)}) collective-permute-start(bf16[192,768]{1,0:T(8,128)(2,1)S(1)} %collective-permute-done.2.refs_6_.refs_9_.refs_2_.refs_8_), channel_id=1, source_target_pairs={{0,1},{1,0},{2,3},{3,2},{4,5},{5,4},{6,7},{7,6},{8,9},{9,8},{10,11... | collective-permute-start | bytes 884744 | tf_op jit(solution)/shard_map/ppermute | solution.py:25
  67.3 15.2 %collective-permute-start.18 = (bf16[192,1536]{1,0:T(8,128)(2,1)S(1)}, bf16[192,1536]{1,0:T(8,128)(2,1)S(1)}, u32[]{:S(2)}, u32[]{:S(2)}) collective-permute-start(bf16[192,1536]{1,0:T(8,128)(2,1)S(1)} %get-tuple-element.217.refs_0_.refs_7_), channel_id=1, source_target_pairs={{0,24},{8,0},{16,8},{24,16},{1,25},{9,1},{17,9},{25,17},{2,26},{10... | collective-permute-start | bytes 1769480 | tf_op jit(solution)/shard_map/ppermute | solution.py:43
  74.9 11.5 %collective-permute-start.13 = (bf16[384,384]{1,0:T(8,128)(2,1)S(1)}, bf16[384,384]{1,0:T(8,128)(2,1)S(1)}, u32[]{:S(2)}, u32[]{:S(2)}) collective-permute-start(bf16[384,384]{1,0:T(8,128)(2,1)S(1)} %get-tuple-element.104.refs_1_.k0), channel_id=1, source_target_pairs={{0,1},{1,0},{2,3},{3,2},{4,5},{5,4},{6,7},{7,6},{8,9},{9,8},{10,11... | collective-permute-start | bytes 884744 | tf_op jit(solution)/shard_map/ppermute | solution.py:25
  74.9 13.9 %collective-permute-start.11 = (bf16[384,384]{1,0:T(8,128)(2,1)S(1)}, bf16[384,384]{1,0:T(8,128)(2,1)S(1)}, u32[]{:S(2)}, u32[]{:S(2)}) collective-permute-start(bf16[384,384]{1,0:T(8,128)(2,1)S(1)} %get-tuple-element.102.refs_2_.k0), channel_id=1, source_target_pairs={{0,4},{4,0},{1,5},{5,1},{2,6},{6,2},{3,7},{7,3},{8,12},{12,8},{9,1... | collective-permute-start | bytes 884744 | tf_op jit(solution)/shard_map/ppermute | solution.py:33
  75.4 13.4 %collective-permute-start.10 = (bf16[384,384]{1,0:T(8,128)(2,1)S(1)}, bf16[384,384]{1,0:T(8,128)(2,1)S(1)}, u32[]{:S(2)}, u32[]{:S(2)}) collective-permute-start(bf16[384,384]{1,0:T(8,128)(2,1)S(1)} %get-tuple-element.102.refs_2_.k0), channel_id=1, source_target_pairs={{0,1},{1,0},{2,3},{3,2},{4,5},{5,4},{6,7},{7,6},{8,9},{9,8},{10,11... | collective-permute-start | bytes 884744 | tf_op jit(solution)/shard_map/ppermute | solution.py:25
  82.5 52.7 %collective-permute-start.27 = (bf16[192,2304]{1,0:T(8,128)(2,1)S(1)}, bf16[192,2304]{1,0:T(8,128)(2,1)S(1)}, u32[]{:S(2)}, u32[]{:S(2)}) collective-permute-start(bf16[192,2304]{1,0:T(8,128)(2,1)S(1)} %pad_maximum_fusion.3.refs_7_.refs_0_.refs_3_.refs_6_), channel_id=1, source_target_pairs={{0,8},{8,16},{16,24},{24,0},{1,9},{9,17},{17,25},{25,1},{2,10},{10... | collective-permute-start | bytes 2654216 | tf_op jit(solution)/shard_map/ppermute | solution.py:42
  83.2 52.5 %collective-permute-start.28 = (bf16[192,2304]{1,0:T(8,128)(2,1)S(1)}, bf16[192,2304]{1,0:T(8,128)(2,1)S(1)}, u32[]{:S(2)}, u32[]{:S(2)}) collective-permute-start(bf16[192,2304]{1,0:T(8,128)(2,1)S(1)} %pad_maximum_fusion.3.refs_7_.refs_0_.refs_3_.refs_6_), channel_id=1, source_target_pairs={{0,24},{8,0},{16,8},{24,16},{1,25},{9,1},{17,9},{25,17},{2,26},{10... | collective-permute-start | bytes 2654216 | tf_op jit(solution)/shard_map/ppermute | solution.py:43
  86.4 22.1 %collective-permute-start.21 = (bf16[192,1536]{1,0:T(8,128)(2,1)S(1)}, bf16[192,1536]{1,0:T(8,128)(2,1)S(1)}, u32[]{:S(2)}, u32[]{:S(2)}) collective-permute-start(bf16[192,1536]{1,0:T(8,128)(2,1)S(1)} %copy-done.33), channel_id=1, source_target_pairs={{0,1},{1,0},{2,3},{3,2},{4,5},{5,4},{6,7},{7,6},{8,9},{9,8},{10,11... | collective-permute-start | bytes 1769480 | tf_op jit(solution)/shard_map/ppermute | solution.py:25
  90.3 41.9 %collective-permute-start.19 = (bf16[96,1536]{1,0:T(8,128)(2,1)S(1)}, bf16[96,1536]{1,0:T(8,128)(2,1)S(1)}, u32[]{:S(2)}, u32[]{:S(2)}) collective-permute-start(bf16[96,1536]{1,0:T(8,128)(2,1)S(1)} %slice.253), channel_id=1, source_target_pairs={{0,8},{8,16},{16,24},{24,0},{1,9},{9,17},{17,25},{25,1},{2,10},{10... | collective-permute-start | bytes 884744 | tf_op jit(solution)/shard_map/ppermute | solution.py:44
  92.1 43.1 %collective-permute-start.20 = (bf16[96,1536]{1,0:T(8,128)(2,1)S(1)}, bf16[96,1536]{1,0:T(8,128)(2,1)S(1)}, u32[]{:S(2)}, u32[]{:S(2)}) collective-permute-start(bf16[96,1536]{1,0:T(8,128)(2,1)S(1)} %slice.254), channel_id=1, source_target_pairs={{0,24},{8,0},{16,8},{24,16},{1,25},{9,1},{17,9},{25,17},{2,26},{10... | collective-permute-start | bytes 884744 | tf_op jit(solution)/shard_map/ppermute | solution.py:45
  108.5 65.7 %collective-permute-start.31 = (bf16[192,2304]{1,0:T(8,128)(2,1)S(1)}, bf16[192,2304]{1,0:T(8,128)(2,1)S(1)}, u32[]{:S(2)}, u32[]{:S(2)}) collective-permute-start(bf16[192,2304]{1,0:T(8,128)(2,1)S(1)} %pad_maximum_fusion.3.refs_7_.refs_0_.refs_3_.refs_6_), channel_id=1, source_target_pairs={{0,1},{1,0},{2,3},{3,2},{4,5},{5,4},{6,7},{7,6},{8,9},{9,8},{10,11... | collective-permute-start | bytes 2654216 | tf_op jit(solution)/shard_map/ppermute | solution.py:25
  135.7 15.3 %collective-permute-start.16 = (bf16[384,768]{1,0:T(8,128)(2,1)S(1)}, bf16[384,768]{1,0:T(8,128)(2,1)S(1)}, u32[]{:S(2)}, u32[]{:S(2)}) collective-permute-start(bf16[384,768]{1,0:T(8,128)(2,1)S(1)} %get-tuple-element.106.pa_r), channel_id=1, source_target_pairs={{0,2},{1,3},{2,0},{3,1},{4,6},{5,7},{6,4},{7,5},{8,10},{9,11},{10,... | collective-permute-start | bytes 1769480 | tf_op jit(solution)/shard_map/ppermute | solution.py:29
  140.4 35.3 %collective-permute-start.29 = (bf16[96,2304]{1,0:T(8,128)(2,1)}, bf16[96,2304]{1,0:T(8,128)(2,1)}, u32[]{:S(2)}, u32[]{:S(2)}) collective-permute-start(bf16[96,2304]{1,0:T(8,128)(2,1)} %slice.257), channel_id=1, source_target_pairs={{0,8},{8,16},{16,24},{24,0},{1,9},{9,17},{17,25},{25,1},{2,10},{10... | collective-permute-start | bytes 1327112 | tf_op jit(solution)/shard_map/ppermute | solution.py:44
  142.7 33.2 %collective-permute-start.30 = (bf16[96,2304]{1,0:T(8,128)(2,1)}, bf16[96,2304]{1,0:T(8,128)(2,1)}, u32[]{:S(2)}, u32[]{:S(2)}) collective-permute-start(bf16[96,2304]{1,0:T(8,128)(2,1)} %slice.258), channel_id=1, source_target_pairs={{0,24},{8,0},{16,8},{24,16},{1,25},{9,1},{17,9},{25,17},{2,26},{10... | collective-permute-start | bytes 1327112 | tf_op jit(solution)/shard_map/ppermute | solution.py:45
  146.2 32.2 %collective-permute-start.32 = (bf16[192,2304]{1,0:T(8,128)(2,1)S(1)}, bf16[192,2304]{1,0:T(8,128)(2,1)}, u32[]{:S(2)}, u32[]{:S(2)}) collective-permute-start(bf16[192,2304]{1,0:T(8,128)(2,1)S(1)} %collective-permute-done.27.refs_8_.refs_1_.refs_4_.refs_7_), channel_id=1, source_target_pairs={{0,1},{1,0},{2,3},{3,2},{4,5},{5,4},{6,7},{7,6},{8,9},{9,8},{10,11... | collective-permute-start | bytes 2654216 | tf_op jit(solution)/shard_map/ppermute | solution.py:25
  151.9 26.5 %collective-permute-start.33 = (bf16[192,2304]{1,0:T(8,128)(2,1)S(1)}, bf16[192,2304]{1,0:T(8,128)(2,1)}, u32[]{:S(2)}, u32[]{:S(2)}) collective-permute-start(bf16[192,2304]{1,0:T(8,128)(2,1)S(1)} %collective-permute-done.28.refs_9_.refs_2_.refs_5_.refs_8_), channel_id=1, source_target_pairs={{0,1},{1,0},{2,3},{3,2},{4,5},{5,4},{6,7},{7,6},{8,9},{9,8},{10,11... | collective-permute-start | bytes 2654216 | tf_op jit(solution)/shard_map/ppermute | solution.py:25
  174.2 15.7 %collective-permute-start.26 = (bf16[384,768]{1,0:T(8,128)(2,1)S(1)}, bf16[384,768]{1,0:T(8,128)(2,1)S(1)}, u32[]{:S(2)}, u32[]{:S(2)}) collective-permute-start(bf16[384,768]{1,0:T(8,128)(2,1)S(1)} %get-tuple-element.108.refs_4_), channel_id=1, source_target_pairs={{0,2},{1,3},{2,0},{3,1},{4,6},{5,7},{6,4},{7,5},{8,10},{9,11},{10,... | collective-permute-start | bytes 1769480 | tf_op jit(solution)/shard_map/ppermute | solution.py:29
  194.7 13.4 %collective-permute-start.37 = (bf16[384,384]{1,0:T(8,128)(2,1)S(1)}, bf16[384,384]{1,0:T(8,128)(2,1)S(1)}, u32[]{:S(2)}, u32[]{:S(2)}) collective-permute-start(bf16[384,384]{1,0:T(8,128)(2,1)S(1)} %get-tuple-element.111.refs_2_.k0), channel_id=1, source_target_pairs={{0,4},{4,0},{1,5},{5,1},{2,6},{6,2},{3,7},{7,3},{8,12},{12,8},{9,1... | collective-permute-start | bytes 884744 | tf_op jit(solution)/shard_map/ppermute | solution.py:33
  195.2 12.9 %collective-permute-start.39 = (bf16[384,384]{1,0:T(8,128)(2,1)S(1)}, bf16[384,384]{1,0:T(8,128)(2,1)S(1)}, u32[]{:S(2)}, u32[]{:S(2)}) collective-permute-start(bf16[384,384]{1,0:T(8,128)(2,1)S(1)} %get-tuple-element.113.refs_1_.k0), channel_id=1, source_target_pairs={{0,1},{1,0},{2,3},{3,2},{4,5},{5,4},{6,7},{7,6},{8,9},{9,8},{10,11... | collective-permute-start | bytes 884744 | tf_op jit(solution)/shard_map/ppermute | solution.py:25
  203.1 10.4 %collective-permute-start.36 = (bf16[384,384]{1,0:T(8,128)(2,1)S(1)}, bf16[384,384]{1,0:T(8,128)(2,1)S(1)}, u32[]{:S(2)}, u32[]{:S(2)}) collective-permute-start(bf16[384,384]{1,0:T(8,128)(2,1)S(1)} %get-tuple-element.111.refs_2_.k0), channel_id=1, source_target_pairs={{0,1},{1,0},{2,3},{3,2},{4,5},{5,4},{6,7},{7,6},{8,9},{9,8},{10,11... | collective-permute-start | bytes 884744 | tf_op jit(solution)/shard_map/ppermute | solution.py:25
  220.1 15.8 %collective-permute-start.42 = (bf16[384,768]{1,0:T(8,128)(2,1)S(1)}, bf16[384,768]{1,0:T(8,128)(2,1)S(1)}, u32[]{:S(2)}, u32[]{:S(2)}) collective-permute-start(bf16[384,768]{1,0:T(8,128)(2,1)S(1)} %get-tuple-element.115.pa_r), channel_id=1, source_target_pairs={{0,2},{1,3},{2,0},{3,1},{4,6},{5,7},{6,4},{7,5},{8,10},{9,11},{10,... | collective-permute-start | bytes 1769480 | tf_op jit(solution)/shard_map/ppermute | solution.py:29
  246.6 15.0 %collective-permute-start.45 = (bf16[384,768]{1,0:T(8,128)(2,1)S(1)}, bf16[384,768]{1,0:T(8,128)(2,1)S(1)}, u32[]{:S(2)}, u32[]{:S(2)}) collective-permute-start(bf16[384,768]{1,0:T(8,128)(2,1)S(1)} %get-tuple-element.119.pa_r), channel_id=1, source_target_pairs={{0,2},{1,3},{2,0},{3,1},{4,6},{5,7},{6,4},{7,5},{8,10},{9,11},{10,... | collective-permute-start | bytes 1769480 | tf_op jit(solution)/shard_map/ppermute | solution.py:29
  280.5 13.6 %collective-permute-start.47 = (bf16[384,384]{1,0:T(8,128)(2,1)S(1)}, bf16[384,384]{1,0:T(8,128)(2,1)S(1)}, u32[]{:S(2)}, u32[]{:S(2)}) collective-permute-start(bf16[384,384]{1,0:T(8,128)(2,1)S(1)} %pair_sum.4), channel_id=1, source_target_pairs={{0,4},{4,0},{1,5},{5,1},{2,6},{6,2},{3,7},{7,3},{8,12},{12,8},{9,1... | collective-permute-start | bytes 884744 | tf_op jit(solution)/shard_map/ppermute | solution.py:33
  282.0 16.5 %collective-permute-start.63 = (bf16[384,768]{1,0:T(8,128)(2,1)S(1)}, bf16[384,768]{1,0:T(8,128)(2,1)S(1)}, u32[]{:S(2)}, u32[]{:S(2)}) collective-permute-start(bf16[384,768]{1,0:T(8,128)(2,1)S(1)} %get-tuple-element.165.n_r), channel_id=1, source_target_pairs={{0,1},{1,0},{2,3},{3,2},{4,5},{5,4},{6,7},{7,6},{8,9},{9,8},{10,11... | collective-permute-start | bytes 1769480 | tf_op jit(solution)/shard_map/ppermute | solution.py:25
  282.1 18.0 %collective-permute-start.65 = (bf16[384,768]{1,0:T(8,128)(2,1)S(1)}, bf16[384,768]{1,0:T(8,128)(2,1)S(1)}, u32[]{:S(2)}, u32[]{:S(2)}) collective-permute-start(bf16[384,768]{1,0:T(8,128)(2,1)S(1)} %get-tuple-element.168.g_r), channel_id=1, source_target_pairs={{0,1},{1,0},{2,3},{3,2},{4,5},{5,4},{6,7},{7,6},{8,9},{9,8},{10,11... | collective-permute-start | bytes 1769480 | tf_op jit(solution)/shard_map/ppermute | solution.py:25
  303.6 200.8 %reduce-scatter.11.cloned.1.call-start = ((), (), s32[]{:S(2)}) async-start(), calls=%async_computation.7 | async-start | bytes 2949120 | tf_op jit(solution)/shard_map/reduce_scatter | solution.py:683
  315.2 192.3 %reduce-scatter.5.cloned.1.call-start = ((), (), s32[]{:S(2)}) async-start(), calls=%async_computation.4 | async-start | bytes 1474560 | tf_op jit(solution)/shard_map/reduce_scatter | solution.py:683
  315.2 15.7 %collective-permute-start.50 = (bf16[384,768]{1,0:T(8,128)(2,1)}, bf16[384,768]{1,0:T(8,128)(2,1)S(1)}, u32[]{:S(2)}, u32[]{:S(2)}) collective-permute-start(bf16[384,768]{1,0:T(8,128)(2,1)} %copy-done.62), channel_id=1, source_target_pairs={{0,2},{1,3},{2,0},{3,1},{4,6},{5,7},{6,4},{7,5},{8,10},{9,11},{10,... | collective-permute-start | bytes 1769480 | tf_op jit(solution)/shard_map/ppermute | solution.py:29
  348.9 14.7 %collective-permute-start.51 = (bf16[384,768]{1,0:T(8,128)(2,1)S(1)}, bf16[384,768]{1,0:T(8,128)(2,1)S(1)}, u32[]{:S(2)}, u32[]{:S(2)}) collective-permute-start(bf16[384,768]{1,0:T(8,128)(2,1)S(1)} %get-tuple-element.139.pa_r), channel_id=1, source_target_pairs={{0,2},{1,3},{2,0},{3,1},{4,6},{5,7},{6,4},{7,5},{8,10},{9,11},{10,... | collective-permute-start | bytes 1769480 | tf_op jit(solution)/shard_map/ppermute | solution.py:29
  383.9 13.8 %collective-permute-start.53 = (bf16[384,384]{1,0:T(8,128)(2,1)S(1)}, bf16[384,384]{1,0:T(8,128)(2,1)S(1)}, u32[]{:S(2)}, u32[]{:S(2)}) collective-permute-start(bf16[384,384]{1,0:T(8,128)(2,1)S(1)} %pair_sum.6), channel_id=1, source_target_pairs={{0,4},{4,0},{1,5},{5,1},{2,6},{6,2},{3,7},{7,3},{8,12},{12,8},{9,1... | collective-permute-start | bytes 884744 | tf_op jit(solution)/shard_map/ppermute | solution.py:33
  385.5 17.1 %collective-permute-start.58 = (bf16[384,768]{1,0:T(8,128)(2,1)S(1)}, bf16[384,768]{1,0:T(8,128)(2,1)S(1)}, u32[]{:S(2)}, u32[]{:S(2)}) collective-permute-start(bf16[384,768]{1,0:T(8,128)(2,1)S(1)} %copy-done.65), channel_id=1, source_target_pairs={{0,1},{1,0},{2,3},{3,2},{4,5},{5,4},{6,7},{7,6},{8,9},{9,8},{10,11... | collective-permute-start | bytes 1769480 | tf_op jit(solution)/shard_map/ppermute | solution.py:25
  385.6 18.7 %collective-permute-start.60 = (bf16[384,768]{1,0:T(8,128)(2,1)S(1)}, bf16[384,768]{1,0:T(8,128)(2,1)S(1)}, u32[]{:S(2)}, u32[]{:S(2)}) collective-permute-start(bf16[384,768]{1,0:T(8,128)(2,1)S(1)} %get-tuple-element.161.g_r), channel_id=1, source_target_pairs={{0,1},{1,0},{2,3},{3,2},{4,5},{5,4},{6,7},{7,6},{8,9},{9,8},{10,11... | collective-permute-start | bytes 1769480 | tf_op jit(solution)/shard_map/ppermute | solution.py:25
  407.8 114.6 %reduce-scatter.9.cloned.1.call-start = ((), (), s32[]{:S(2)}) async-start(), calls=%async_computation.6 | async-start | bytes 2949120 | tf_op jit(solution)/shard_map/reduce_scatter | solution.py:683
  420.9 15.4 %collective-permute-start.43 = (bf16[384,768]{1,0:T(8,128)(2,1)S(1)}, bf16[384,768]{1,0:T(8,128)(2,1)S(1)}, u32[]{:S(2)}, u32[]{:S(2)}) collective-permute-start(bf16[384,768]{1,0:T(8,128)(2,1)S(1)} %copy-done.67), channel_id=1, source_target_pairs={{0,2},{1,3},{2,0},{3,1},{4,6},{5,7},{6,4},{7,5},{8,10},{9,11},{10,... | collective-permute-start | bytes 1769480 | tf_op jit(solution)/shard_map/ppermute | solution.py:29
  443.3 15.4 %collective-permute-start.56 = (bf16[384,768]{1,0:T(8,128)(2,1)S(1)}, bf16[384,768]{1,0:T(8,128)(2,1)S(1)}, u32[]{:S(2)}, u32[]{:S(2)}) collective-permute-start(bf16[384,768]{1,0:T(8,128)(2,1)S(1)} %copy-done.70), channel_id=1, source_target_pairs={{0,2},{1,3},{2,0},{3,1},{4,6},{5,7},{6,4},{7,5},{8,10},{9,11},{10,... | collective-permute-start | bytes 1769480 | tf_op jit(solution)/shard_map/ppermute | solution.py:29
  461.8 42.7 %collective-permute-start.67 = (bf16[192,768]{1,0:T(8,128)(2,1)}, bf16[192,768]{1,0:T(8,128)(2,1)S(1)}, u32[]{:S(2)}, u32[]{:S(2)}) collective-permute-start(bf16[192,768]{1,0:T(8,128)(2,1)} %reduce-scatter.7.cloned.1.call-done), channel_id=1, source_target_pairs={{0,4},{4,0},{1,5},{5,1},{2,6},{6,2},{3,7},{7,3},{8,12},{12,8},{9,1... | collective-permute-start | bytes 884744 | tf_op jit(solution)/shard_map/ppermute | solution.py:33
  463.6 42.5 %collective-permute-start.57 = (bf16[384,768]{1,0:T(8,128)(2,1)S(1)}, bf16[384,768]{1,0:T(8,128)(2,1)S(1)}, u32[]{:S(2)}, u32[]{:S(2)}) collective-permute-start(bf16[384,768]{1,0:T(8,128)(2,1)S(1)} %get-tuple-element.157), channel_id=1, source_target_pairs={{0,1},{1,0},{2,3},{3,2},{4,5},{5,4},{6,7},{7,6},{8,9},{9,8},{10,11... | collective-permute-start | bytes 1769480 | tf_op jit(solution)/shard_map/ppermute | solution.py:25
  504.4 16.6 %collective-permute-start.74 = (bf16[192,1536]{1,0:T(8,128)(2,1)}, bf16[192,1536]{1,0:T(8,128)(2,1)}, u32[]{:S(2)}, u32[]{:S(2)}) collective-permute-start(bf16[192,1536]{1,0:T(8,128)(2,1)} %reduce-scatter.11.cloned.1.call-done), channel_id=1, source_target_pairs={{0,4},{4,0},{1,5},{5,1},{2,6},{6,2},{3,7},{7,3},{8,12},{12,8},{9,1... | collective-permute-start | bytes 1769480 | tf_op jit(solution)/shard_map/ppermute | solution.py:33
  507.5 18.5 %collective-permute-start.62 = (bf16[192,768]{1,0:T(8,128)(2,1)}, bf16[192,768]{1,0:T(8,128)(2,1)S(1)}, u32[]{:S(2)}, u32[]{:S(2)}) collective-permute-start(bf16[192,768]{1,0:T(8,128)(2,1)} %reduce-scatter.5.cloned.1.call-done), channel_id=1, source_target_pairs={{0,4},{4,0},{1,5},{5,1},{2,6},{6,2},{3,7},{7,3},{8,12},{12,8},{9,1... | collective-permute-start | bytes 884744 | tf_op jit(solution)/shard_map/ppermute | solution.py:33
  522.4 10.3 %collective-permute-start.73 = (bf16[192,1536]{1,0:T(8,128)(2,1)}, bf16[192,1536]{1,0:T(8,128)(2,1)}, u32[]{:S(2)}, u32[]{:S(2)}) collective-permute-start(bf16[192,1536]{1,0:T(8,128)(2,1)} %reduce-scatter.9.cloned.1.call-done), channel_id=1, source_target_pairs={{0,4},{4,0},{1,5},{5,1},{2,6},{6,2},{3,7},{7,3},{8,12},{12,8},{9,1... | collective-permute-start | bytes 1769480 | tf_op jit(solution)/shard_map/ppermute | solution.py:33
  (194 other events, 1902.4 us)
Sparse Core Ops, SparseCore 0:
  303.7 28.9 reduce-scatter.6
  335.0 46.7 reduce-scatter.10
  407.9 28.8 reduce-scatter.4
  439.0 47.1 reduce-scatter.8

commit v2 on v1

v2 whole, which is shorter than its diff:
```python
import math

import jax
import jax.numpy as jnp
from jax import lax
from jax.experimental import pallas as pl
from jax.experimental.pallas import tpu as pltpu
from jax.sharding import Mesh
from jax.sharding import PartitionSpec as P

f32 = jnp.float32
bf16 = jnp.bfloat16
EPSILON = 1e-05
NN = (((1,), (0,)), ((), ()))
NT = (((1,), (1,)), ((), ()))
TN = (((0,), (0,)), ((), ()))
VMEM_MIB = {
    "attend": 10,
    "attend_back": 8.5,
    "feed": 13,
    "feed_back": 12,
    "feed_grads": 9,
    "feed_out": 5,
    "input_back": 7,
    "middle_back": 7,
    "pair_grads": 5,
    "project": 6,
    "project_back": 8.5,
    "project_grads": 5,
    "project_out": 4.5,
}
WIDE = 128
TAIL = 16
COST = 500_000_000


def mm(a, b, dims=NN):
    return lax.dot_general(a, b, dims, preferred_element_type=f32)


def core_swap(x):
    return lax.ppermute(x, "tc", [(0, 1), (1, 0)])


def x_swap(x):
    return lax.ppermute(x, "tx", [(0, 1), (1, 0)])


def y_swap(x):
    return lax.ppermute(x, "ctx", [(0, 1), (1, 0)])


def after(x, *others):
    return lax.optimization_barrier((x,) + others)[0]


def ring(shift):
    return [(i, (i + shift) % 4) for i in range(4)]


def ring_scalars(shards):
    me = lax.axis_index("shard").astype(jnp.int32)
    zero = jnp.int32(0)
    order = [me, (me + shards - 1) % shards, (me + 1) % shards, (me + 2) % shards]
    return jnp.stack([zero] * 8 + [lax.axis_index("tc").astype(jnp.int32)] + order + [zero] * 3)


class Pieces:
    def __init__(self, x, tail=0):
        self.rows = x.shape[0] - tail
        self.mine = [x] + [lax.ppermute(x, "shard", ring(s)) for s in (1, 3, 2)]
        self.arrays = self.mine + [core_swap(p) for p in self.mine]

    def copies(self, scal, refs, columns, dest, sems):
        out = []
        for k, ref in enumerate(refs):
            slot = scal[8] if k < 4 else 1 - scal[8]
            to = dest.at[slot, scal[9 + k % 4]]
            out.append(pltpu.make_async_copy(ref.at[pl.ds(0, self.rows), columns], to, sems.at[k]))
        return out

    def tails(self, scal, refs, dest, sems):
        out = []
        for k, ref in enumerate(refs):
            slot = scal[8] if k < 4 else 1 - scal[8]
            to = dest.at[slot, scal[9 + k % 4]]
            out.append(pltpu.make_async_copy(ref.at[pl.ds(self.rows, TAIL), :], to, sems.at[k]))
        return out


class Gathered:
    def __init__(self, x, shards, tail=0):
        self.rows = x.shape[0] - tail
        whole = lax.all_gather(x, ("shard", "tc"), axis=0, tiled=False)
        self.arrays = [whole.reshape((shards, 2) + x.shape)]

    def copies(self, scal, refs, columns, dest, sems):
        ref = refs[0]
        return [
            pltpu.make_async_copy(ref.at[:, c, pl.ds(0, self.rows), columns], dest.at[c], sems.at[c])
            for c in range(2)
        ]

    def tails(self, scal, refs, dest, sems):
        ref = refs[0]
        return [
            pltpu.make_async_copy(ref.at[:, c, pl.ds(self.rows, TAIL), :], dest.at[c], sems.at[c])
            for c in range(2)
        ]


def vmem():
    return pl.BlockSpec(memory_space=pltpu.VMEM)


class Far:
    def __init__(self, array):
        self.array = array


class Reading:
    def __init__(self, buffer, copy):
        self.buffer, self.copy, self.waited = buffer, copy, False

    def need(self):
        if not self.waited:
            self.copy.wait()
            self.waited = True
        return self.buffer

    def __getitem__(self, index):
        return self.need()[index]

    @property
    def shape(self):
        return self.buffer.shape


class Writing:
    def __init__(self, buffer, copy):
        self.buffer, self.copy, self.sent = buffer, copy, False

    def __setitem__(self, index, value):
        self.buffer[index] = value

    @property
    def at(self):
        return self.buffer.at

    def send(self):
        if not self.sent:
            self.copy.start()
            self.sent = True


def send(*refs):
    for r in refs:
        if isinstance(r, Writing):
            r.send()


def need(*refs):
    for r in refs:
        if isinstance(r, Reading):
            r.need()


FAR = "far"


def run(kernel, ins, outs, scratch=(), w=None, scalars=None, name=None, us=1.0):
    pieces = [] if w is None else w.arrays
    n_in, n_out, n_pieces = len(ins), len(outs), len(pieces)
    far_in = [i for i, a in enumerate(ins) if isinstance(a, Far)]
    far_out = [i for i, o in enumerate(outs) if len(o) == 3]
    any_space = pl.BlockSpec(memory_space=pl.ANY)
    specs, args = [], []
    if scalars is not None:
        specs.append(pl.BlockSpec(memory_space=pltpu.SMEM))
        args.append(scalars)
    for a in ins:
        if isinstance(a, Far):
            specs.append(any_space)
            args.append(pltpu.with_memory_space_constraint(a.array, pltpu.HBM))
        else:
            specs.append(vmem())
            args.append(a)
    for p in pieces:
        specs.append(any_space)
        args.append(pltpu.with_memory_space_constraint(p, pltpu.HBM))
    first = len(args) - n_in - n_pieces
    shapes = [
        pltpu.HBM(o[0], o[1]) if len(o) == 3 else jax.ShapeDtypeStruct(o[0], o[1]) for o in outs
    ]
    buffers = [pltpu.VMEM(ins[i].array.shape, ins[i].array.dtype) for i in far_in]
    buffers += [pltpu.VMEM(outs[i][0], outs[i][1]) for i in far_out]
    sems = [pltpu.SemaphoreType.DMA((len(buffers),))] if buffers else []

    def wrapped(*refs):
        refs = list(refs)
        n_all = len(args) + n_out + len(scratch)
        own, extra = refs[:n_all], refs[n_all:]
        reads, writes = [], []
        for k, i in enumerate(far_in):
            copy = pltpu.make_async_copy(own[first + i], extra[k], extra[-1].at[k])
            copy.start()
            own[first + i] = Reading(extra[k], copy)
            reads.append(own[first + i])
        for k, i in enumerate(far_out):
            k += len(far_in)
            at = len(args) + i
            own[at] = Writing(extra[k], pltpu.make_async_copy(extra[k], own[at], extra[-1].at[k]))
            writes.append(own[at])
        kernel(*own)
        for w in writes:
            w.send()
        for r in reads:
            r.need()
        for w in writes:
            w.copy.wait()

    return pl.pallas_call(
        wrapped,
        out_shape=shapes,
        in_specs=specs,
        out_specs=[any_space if len(o) == 3 else vmem() for o in outs],
        scratch_shapes=list(scratch) + buffers + sems,
        compiler_params=pltpu.CompilerParams(vmem_limit_bytes=int(VMEM_MIB.get(name, 4) * 1024 * 1024)),
        cost_estimate=pl.CostEstimate(flops=int(us * COST), bytes_accessed=1000, transcendentals=0),
        name=name,
    )(*args)


def spread(shard, shards, units):
    part = 64 // shards
    bits, low = part.bit_length() - 1, part - 1
    i = lax.broadcasted_iota(jnp.int32, (units // shards, units), 0)
    j = lax.broadcasted_iota(jnp.int32, (units // shards, units), 1)
    same = ((j >> 6) == (i >> bits)) & ((j & 63) == shard * part + (i & low))
    return jnp.where(same, 1.0, 0.0).astype(bf16)


def start_all(copies):
    for c in copies:
        c.start()


def wait_all(copies):
    for c in copies:
        c.wait()


def ln_parts(x):
    centred = x - jnp.mean(x, -1, keepdims=True)
    inv = lax.rsqrt(jnp.mean(centred * centred, -1, keepdims=True) + EPSILON)
    return centred * inv, inv


def ln_back(x, gain, dn):
    hat, inv = ln_parts(x)
    dhat = dn * gain
    dx = inv * (
        dhat
        - jnp.mean(dhat, -1, keepdims=True)
        - hat * jnp.mean(dhat * hat, -1, keepdims=True)
    )
    return dx, jnp.sum(dn * hat, 0, keepdims=True), jnp.sum(dn, 0, keepdims=True)


def split3(v):
    a = v.astype(bf16)
    r = v - a.astype(f32)
    b = r.astype(bf16)
    c = (r - b.astype(f32)).astype(bf16)
    return a, b, c


def beside(wide, column):
    a, b, c = split3(column)
    rows, size = wide.shape[0], wide.shape[1]
    return jnp.concatenate([wide, a, b, c, jnp.zeros((rows, WIDE - size - 3), bf16)], 1)


class Sizes:
    def __init__(self, mesh, frames, w_qkv, w_up):
        self.shards = mesh.shape["shard"]
        self.layers = w_qkv.shape[0]
        self.width = frames.shape[-1]
        self.rows = frames.shape[1] // 2
        self.heads = w_qkv.shape[2]
        self.hd = w_qkv.shape[3] // 3
        self.att = self.heads * self.hd
        self.hidden = w_up.shape[2]
        self.m = w_qkv.shape[1]
        self.a_cols = 4 * self.att
        self.b_cols = 2 * self.hidden


def make(z):
    R, D, A, H, HD, F = z.rows, z.width, z.att, z.heads, z.hd, z.hidden
    L, S, M = z.layers, z.shards, z.m
    coef = HD ** (-0.5) / math.log(2.0)
    scale = HD ** (-0.5)
    dma = pltpu.SemaphoreType.DMA
    q_at, u_at = M, M + 2 * A // S

    def weight_scratch(columns):
        return [pltpu.VMEM((2, S, M, columns), bf16), dma((8,))]

    def weight(w_s, c, start, stop):
        return w_s[c, :, :, start:stop].reshape(D, stop - start)

    def proj(scal, x, layer, w, biases=None, prev=None):
        first = biases is None
        n = len(w.arrays)
        part = 2 * HD // S

        def kernel(*refs):
            it = iter(refs)
            scal_r, x_r = next(it), next(it)
            if not first:
                vec_r, qb_r, pa_r, pb_r = (next(it) for _ in range(4))
            piece_r = [next(it) for _ in range(n)]
            n_o, q0, q1, kv0, kv1 = (next(it) for _ in range(5))
            if first:
                vec_r, qb_r, tail_o = (next(it) for _ in range(3))
            else:
                x_o = next(it)
            w_s, sems = next(it), next(it)
            if first:
                tail_sems = next(it)
                tails = w.tails(scal_r, piece_r, tail_o, tail_sems)
                start_all(tails)
            copies = w.copies(scal_r, piece_r, pl.ds(0, z.a_cols), w_s, sems)
            start_all(copies)
            xv = x_r[...].astype(f32)
            if not first:
                at = 6 * (layer - 1) + 5
                xv = xv + (pa_r[...].astype(f32) + pb_r[...].astype(f32) + vec_r[at : at + 1, :])
                x_o[...] = xv
            hat, _ = ln_parts(xv)
            if first:
                wait_all(tails)
                vec_r[...] = jnp.concatenate([tail_o[0, t][:, :M] for t in range(S)], 1).astype(f32)
                for l in range(L):
                    for p in range(2):
                        rows = [tail_o[p, t].astype(f32)[l : l + 1, q_at:u_at] for t in range(S)]
                        seq = []
                        for side in range(2):
                            for h in range(H):
                                seq += [
                                    rows[t][:, h * part : (h + 1) * part]
                                    for t in range(side * S // 2, (side + 1) * S // 2)
                                ]
                            if side == 0:
                                seq.append(jnp.zeros((1, A), f32))
                        qb_r[2 * l + p : 2 * l + p + 1, :] = jnp.concatenate(seq, 1)
            g = 6 * layer
            nv = (hat * vec_r[g : g + 1, :] + vec_r[g + 2 : g + 3, :]).astype(bf16)
            n_o[...] = nv
            send(n_o)
            wait_all(copies)
            for e, (q_o, kv_o) in enumerate(((q0, kv0), (q1, kv1))):
                b = 2 * layer + e
                p = (mm(nv, weight(w_s, e, 0, 3 * A)) + qb_r[b : b + 1, :]).astype(bf16)
                q_o[...] = p[:, :A]
                kv_o[...] = p[:, A:]
                send(kv_o)

        ins = [x] + ([] if first else list(biases) + list(prev))
        outs = [((R, D), bf16)] + [((R, A), bf16)] * 2 + [((R, 2 * A), bf16, FAR)] * 2
        scratch = weight_scratch(z.a_cols)
        if first:
            outs += [((TAIL, D), f32), ((2 * L, 3 * A), f32), ((2, S, TAIL, z.a_cols), bf16)]
            scratch += [dma((8,))]
        else:
            outs += [((R, D), f32)]
        return run(kernel, ins, outs, scratch, w, scal, "project", 3.5)

    def aug(block, offset, fill):
        return jnp.concatenate([block[:, offset : offset + HD], fill], 1)

    def attend(q, kvs, scal=None, o_prev=None, w=None):
        K = 4 * R
        last = w is not None
        n = len(w.arrays) if last else 0

        def kernel(*refs):
            it = iter(refs)
            if last:
                scal_r = next(it)
            q_r = next(it)
            kv_r = [next(it) for _ in range(4)]
            if last:
                op_r = next(it)
                piece_r = [next(it) for _ in range(n)]
            o_o, qa_o = next(it), next(it)
            if last:
                own_o, snd_o, part_o = (next(it) for _ in range(3))
            q_s, k_s, v_s, o_s = (next(it) for _ in range(4))
            if last:
                w_s, sems = next(it), next(it)
                copies = w.copies(scal_r, piece_r, pl.ds(z.a_cols - 256, 256), w_s, sems)
                start_all(copies)
            ones = jnp.ones((R, HD), bf16)
            zeros = jnp.zeros((R, HD), bf16)
            for h in range(H):
                q_s[h] = aug(q_r[...], h * HD, zeros)
                for b in range(4):
                    blk = kv_r[b][...]
                    k_s[h, b * R : (b + 1) * R, :] = aug(blk, h * HD, ones)
                    v_s[h, b * R : (b + 1) * R, :] = aug(blk, A + h * HD, ones)

            def head(h, carry):
                s = mm(q_s[h], k_s[h], NT)
                top = jnp.max(s, -1, keepdims=True)
                p = jnp.exp2((s - top) * coef).astype(bf16)
                oe = mm(p, v_s[h])
                total = oe[:, HD : HD + 1]
                o_s[h] = (oe[:, :HD] / total).astype(bf16)
                lse = top + jnp.log2(total) * (1.0 / coef)
                qa_o[h] = beside(q_s[h][:, :HD], -lse)
                return carry

            lax.fori_loop(0, H, head, 0)
            o_new = jnp.concatenate([o_s[h] for h in range(H)], 1)
            o_o[...] = o_new
            if last:
                o_old = op_r[...]
                odd = scal_r[8] == 1
                own_o[...] = jnp.where(odd, o_new, o_old)
                snd_o[...] = jnp.where(odd, o_old, o_new)
                send(snd_o)
                wait_all(copies)
                part = mm(o_old, weight(w_s, 0, 256 - A, 256), NT) + mm(o_new, weight(w_s, 1, 256 - A, 256), NT)
                part_o[...] = part.astype(bf16)

        ins = [q] + list(kvs) + ([o_prev] if last else [])
        outs = [((R, A), bf16), ((H, R, WIDE), bf16)]
        scratch = [
            pltpu.VMEM((H, R, WIDE), bf16),
            pltpu.VMEM((H, K, WIDE), bf16),
            pltpu.VMEM((H, K, WIDE), bf16),
            pltpu.VMEM((H, R, HD), bf16),
        ]
        if last:
            outs += [((R, A), bf16), ((R, A), bf16), ((R, D), bf16, FAR)]
            scratch += weight_scratch(256)
        return run(kernel, ins, outs, scratch, w, scal, "attend", 6)

    def feed(scal, x, pa, pb, vec, tails, layer, w):
        n = len(w.arrays)
        g = 6 * layer

        def kernel(scal_r, x_r, pa_r, pb_r, vec_r, tail_r, *refs):
            piece_r = refs[:n]
            y_o, n_o, *hid_gp, part_o, w_s, sems = refs[n:]
            copies = w.copies(scal_r, piece_r, pl.ds(0, 2 * F), w_s, sems)
            start_all(copies)
            y = x_r[...].astype(f32) + (
                pa_r[...].astype(f32) + pb_r[...].astype(f32) + vec_r[g + 3 : g + 4, :]
            )
            y_o[...] = y
            hat, _ = ln_parts(y)
            nv = (hat * vec_r[g + 1 : g + 2, :] + vec_r[g + 4 : g + 5, :]).astype(bf16)
            n_o[...] = nv
            send(n_o)
            bias = [None, None]
            for t in range(S):
                e = spread(t, S, F)
                for s in range(2):
                    add = mm(tail_r[s, t][:, u_at : u_at + F // S], e)
                    bias[s] = add if t == 0 else bias[s] + add
            part = None
            for s in range(2):
                copies[s].wait()
                u = mm(nv, weight(w_s, s, 0, F)) + bias[s][layer : layer + 1, :]
                cdf = 0.5 * (1.0 + lax.erf(u * (0.5**0.5)))
                pdf = jnp.exp(-0.5 * u * u) * (1.0 / math.sqrt(2.0 * math.pi))
                hidden = (u * cdf).astype(bf16)
                hid_gp[s][...] = hidden
                hid_gp[2 + s][...] = (cdf + u * pdf).astype(bf16)
                send(hid_gp[s], hid_gp[2 + s])
                t = mm(hidden, weight(w_s, s, F, 2 * F), NT)
                part = t if part is None else part + t
            part_o[...] = part.astype(bf16)

        outs = [
            ((R, D), f32),
            ((R, D), bf16, FAR),
            ((R, F), bf16, FAR),
            ((R, F), bf16, FAR),
            ((R, F), bf16, FAR),
            ((R, F), bf16, FAR),
            ((R, D), bf16, FAR),
        ]
        return run(
            kernel, [x, pa, pb, vec, tails], outs, weight_scratch(2 * F), w, scal, "feed", 6
        )

    def finish(y, pa, pb, vec):
        at = 6 * (L - 1) + 5

        def kernel(y_r, pa_r, pb_r, vec_r, o):
            v = y_r[...] + (pa_r[...].astype(f32) + pb_r[...].astype(f32) + vec_r[at : at + 1, :])
            o[...] = v.astype(bf16)

        return run(kernel, [y, pa, pb, vec], [((R, D), bf16, FAR)], name="finish")

    def feed_back(scal, grad, gp, layer, w, before=None):
        n = len(w.arrays)
        up = 6 * (layer + 1)

        def kernel(*refs):
            it = iter(refs)
            scal_r = next(it)
            if before is None:
                g_r = next(it)
            else:
                x_r, dy_r, pa_r, pb_r, vec_r = (next(it) for _ in range(5))
            gp_r = (next(it), next(it))
            piece_r = [next(it) for _ in range(n)]
            g2_o, du_o, part_o, sums_o = (next(it) for _ in range(4))
            if before is not None:
                g_o, pre_o = next(it), next(it)
            w_s, sems = next(it), next(it)
            copies = w.copies(scal_r, piece_r, pl.ds(0, 2 * F), w_s, sems)
            start_all(copies)
            if before is None:
                g = g_r[...].astype(f32)
            else:
                dn = pa_r[...].astype(f32) + pb_r[...].astype(f32)
                dx, dgain, dshift = ln_back(x_r[...], vec_r[up : up + 1, :], dn)
                g = dy_r[...] + dx
                g_o[...] = g
                pre_o[0:1, :] = dgain
                pre_o[1:2, :] = dshift
            g2 = g.astype(bf16)
            g2_o[...] = g2
            sums_o[...] = jnp.sum(g2.astype(f32), 0, keepdims=True)
            part = None
            for s in range(2):
                copies[s].wait()
                dh = mm(g2, weight(w_s, s, F, 2 * F))
                du = (gp_r[s][...].astype(f32) * dh).astype(bf16)
                du_o[:, s * F : (s + 1) * F] = du
                t = mm(du, weight(w_s, s, 0, F), NT)
                part = t if part is None else part + t
            part_o[...] = part.astype(bf16)

        ins = ([grad] if before is None else list(before)) + [Far(gp[0]), Far(gp[1])]
        outs = [((R, D), bf16), ((R, 2 * F), bf16), ((R, D), bf16, FAR), ((1, D), f32)]
        if before is not None:
            outs += [((R, D), f32), ((2, D), f32)]
        return run(kernel, ins, outs, weight_scratch(2 * F), w, scal, "feed_back", 6)

    def blocks_out(scal_r, full, outs):
        if S == 4:
            for o, at in zip(outs, (9, 11, 10, 12)):
                o[...] = full[scal_r[at]]
        else:
            outs[0][...] = full[...]

    def block_shapes(rows, columns):
        return [((rows, columns), bf16, FAR)] * 4 if S == 4 else [((S, rows, columns), bf16, FAR)]

    def feed_grads(n2, hid, g2, du):
        def kernel(n_r, h0, h1, g_r, du_r, g_o, b_o):
            for s, h_r in enumerate((h0, h1)):
                at = slice(s * F, (s + 1) * F)
                d = du_r[:, at]
                g_o[:, s, :, :F] = mm(n_r[...], d, TN).astype(bf16).reshape(S, M, F)
                g_o[:, s, :, F:] = mm(g_r[...], h_r[...], TN).astype(bf16).reshape(S, M, F)
                b_o[s : s + 1, :] = jnp.sum(d.astype(f32), 0, keepdims=True)

        return run(
            kernel,
            [Far(n2), Far(hid[0]), Far(hid[1]), g2, du],
            [((S, 2, M, 2 * F), bf16, FAR), ((2, F), f32)],
            name="feed_grads",
            us=3,
        )

    def middle_back(scal, y, g, pa, pb, vec, o0, o1, layer, w):
        n = len(w.arrays)
        gain = 6 * layer + 1

        def kernel(scal_r, y_r, g_r, pa_r, pb_r, vec_r, o0_r, o1_r, *refs):
            piece_r = refs[:n]
            dy_o, g1_o, d0_o, d1_o, sums_o, w_s, sems = refs[n:]
            copies = w.copies(scal_r, piece_r, pl.ds(z.a_cols - 256, 256), w_s, sems)
            start_all(copies)
            dn = pa_r[...].astype(f32) + pb_r[...].astype(f32)
            dx, dgain, dshift = ln_back(y_r[...], vec_r[gain : gain + 1, :], dn)
            dy = g_r[...].astype(f32) + dx
            dy_o[...] = dy
            g1 = dy.astype(bf16)
            g1_o[...] = g1
            send(g1_o)
            sums_o[0:1, :] = dgain
            sums_o[1:2, :] = jnp.sum(g1.astype(f32), 0, keepdims=True)
            sums_o[2:3, :] = dshift
            wait_all(copies)
            for e, (o_r, d_o) in enumerate(((o0_r, d0_o), (o1_r, d1_o))):
                do = mm(g1, weight(w_s, e, 256 - A, 256)).astype(bf16)
                prod = do.astype(f32) * o_r[...].astype(f32)
                for h in range(H):
                    lanes = slice(h * HD, (h + 1) * HD)
                    d_o[h] = beside(do[:, lanes], -jnp.sum(prod[:, lanes], -1, keepdims=True))

        outs = [((R, D), f32), ((R, D), bf16, FAR)] + [((H, R, WIDE), bf16)] * 2 + [((3, D), f32)]
        return run(
            kernel,
            [y, g, pa, pb, vec, o0, o1],
            outs,
            weight_scratch(256),
            w,
            scal,
            "middle_back",
            4,
        )

    def attend_back(qa, kvs, da):
        K = 4 * R

        def kernel(qa_r, k0, k1, k2, k3, da_r, dq_o, e0, e2, snd, k_s, v_s, dk_s, dv_s, dq_s):
            ones = jnp.ones((R, HD), bf16)
            for h in range(H):
                for b, kv_r in enumerate((k0, k1, k2, k3)):
                    blk = kv_r[...]
                    k_s[h, b * R : (b + 1) * R, :] = aug(blk, h * HD, ones)
                    v_s[h, b * R : (b + 1) * R, :] = aug(blk, A + h * HD, ones)

            def head(h, carry):
                qv = qa_r[h]
                dv_in = da_r[h]
                dqt = jnp.zeros((WIDE, R), f32)
                for b in range(4):
                    at = slice(b * R, (b + 1) * R)
                    kb = k_s[h, at, :]
                    p = jnp.exp2(mm(kb, qv, NT) * coef)
                    ds = (p * mm(v_s[h, at, :], dv_in, NT)).astype(bf16)
                    dv_s[h, at, :] = mm(p.astype(bf16), dv_in).astype(bf16)
                    dk_s[h, at, :] = (mm(ds, qv) * scale).astype(bf16)
                    dqt = dqt + mm(kb, ds, TN)
                dq_s[h] = (dqt.T * scale).astype(bf16)
                return carry

            lax.fori_loop(0, H, head, 0)
            dq_o[...] = jnp.concatenate([dq_s[h][:, :HD] for h in range(H)], 1)
            for b in range(4):
                at = slice(b * R, (b + 1) * R)
                e_o = (e0, snd.at[0], e2, snd.at[1])[b]
                e_o[...] = jnp.concatenate(
                    [dk_s[h, at, :HD] for h in range(H)] + [dv_s[h, at, :HD] for h in range(H)], 1
                )

        return run(
            kernel,
            [qa] + list(kvs) + [da],
            [((R, A), bf16)] + [((R, 2 * A), bf16)] * 2 + [((2, R, 2 * A), bf16, FAR)],
            [pltpu.VMEM((H, K, WIDE), bf16)] * 4 + [pltpu.VMEM((H, R, WIDE), bf16)],
            name="attend_back",
            us=6,
        )

    def cross_sum(own, pair):
        def kernel(a, b, o):
            o[...] = (a[...].astype(f32) + b[1].astype(f32)).astype(bf16)

        return run(kernel, [own, pair], [(own.shape, bf16, FAR)], name="cross_sum")[0]

    def proj_back(scal, dqs, kv_parts, layer, w, x=None):
        n = len(w.arrays)

        def kernel(scal_r, q0, q1, a0, p0, c0, a1, p1, c1, *refs):
            refs = list(refs)
            if x is not None:
                x_r = refs.pop(0)
            piece_r, refs = refs[:n], refs[n:]
            own_o, snd_o, part_o, b_o = refs[:4]
            w_s, sems = refs[-2:]
            copies = w.copies(scal_r, piece_r, pl.ds(0, z.a_cols), w_s, sems)
            start_all(copies)
            both = []
            for e, (q_r, a, p, c) in enumerate(((q0, a0, p0, c0), (q1, a1, p1, c1))):
                total = a[...].astype(f32) + p[0].astype(f32) + c[...].astype(f32)
                both.append(jnp.concatenate([q_r[...], total.astype(bf16)], 1))
                b_o[e : e + 1, :] = jnp.sum(both[e].astype(f32), 0, keepdims=True)
            if x is None:
                own_o[...], snd_o[...] = both
            else:
                odd = scal_r[8] == 1
                own_o[...] = jnp.where(odd, both[1], both[0])
                snd_o[...] = jnp.where(odd, both[0], both[1])
                send(snd_o)
                hat, _ = ln_parts(x_r[...].astype(f32))
            wait_all(copies)
            part = mm(both[0], weight(w_s, 0, 0, 3 * A), NT) + mm(both[1], weight(w_s, 1, 0, 3 * A), NT)
            part_o[...] = part.astype(bf16)
            if x is not None:
                send(part_o)
                refs[4][0:1, :] = jnp.sum(part * hat, 0, keepdims=True)
                refs[4][1:2, :] = jnp.sum(part, 0, keepdims=True)

        ins = list(dqs)
        for own, pair, cross in kv_parts:
            ins += [own, pair, cross]
        snd = ((R, 3 * A), bf16) if x is None else ((R, 3 * A), bf16, FAR)
        outs = [((R, 3 * A), bf16), snd, ((R, D), bf16, FAR), ((2, 3 * A), f32)]
        if x is not None:
            ins.append(x)
            outs.append(((2, D), f32))
        return run(kernel, ins, outs, weight_scratch(z.a_cols), w, scal, "project_back", 4)

    def proj_grads(scal, n1, n1_r, dp, dp_r, g1, g1_r, o, o_r):
        def kernel(scal_r, n_r, nr_r, p_r, pr_r, g_r, gr_r, o_i, or_i, *refs):
            first = mm(n_r[...], p_r[...], TN) + mm(nr_r[...], pr_r[...], TN)
            second = mm(g_r[...], o_i[...], TN) + mm(gr_r[...], or_i[...], TN)
            both = jnp.concatenate([first.astype(bf16), second.astype(bf16)], 1)
            refs[-1][...] = both.reshape(S, M, z.a_cols)
            if S == 4:
                refs[3][...] = refs[-1][scal_r[12], : M // 2, :]
                refs[4][...] = refs[-1][scal_r[12], M // 2 :, :]
                send(refs[3], refs[4])
                for o_, at in zip(refs[:3], (9, 11, 10)):
                    o_[...] = refs[-1][scal_r[at]]
            else:
                refs[0][...] = refs[-1][...]

        far = [((M // 2, z.a_cols), bf16, FAR)] * 2 if S == 4 else []
        return run(
            kernel,
            [n1, n1_r, dp, dp_r, g1, g1_r, o, o_r],
            (block_shapes(M, z.a_cols)[:3] if S == 4 else block_shapes(M, z.a_cols)) + far,
            [pltpu.VMEM((S, M, z.a_cols), bf16)],
            scalars=scal,
            name="project_grads",
            us=3,
        )

    def pair_grads(n1, dp0, dp1, g1, o0, o1):
        def kernel(n_r, p0, p1, g_r, o0_r, o1_r, out):
            for c, (p_r, o_r) in enumerate(((p0, o0_r), (p1, o1_r))):
                first = mm(n_r[...], p_r[...], TN).astype(bf16)
                second = mm(g_r[...], o_r[...], TN).astype(bf16)
                out[:, c] = jnp.concatenate([first, second], 1).reshape(S, M, z.a_cols)

        return run(
            kernel,
            [n1, dp0, dp1, g1, o0, o1],
            [((S, 2, M, z.a_cols), bf16, FAR)],
            name="pair_grads",
            us=3,
        )[0]

    def pass_on(up, down, low, high):
        def kernel(up_r, down_r, low_r, high_r, up_o, down_o):
            half = M // 2
            up_o[:half, :] = (up_r[:half, :].astype(f32) + low_r[...].astype(f32)).astype(bf16)
            up_o[half:, :] = up_r[half:, :]
            send(up_o)
            down_o[:half, :] = down_r[:half, :]
            down_o[half:, :] = (down_r[half:, :].astype(f32) + high_r[...].astype(f32)).astype(bf16)

        return run(
            kernel, [up, down, low, high], [((M, z.a_cols), bf16, FAR)] * 2, name="pass_on"
        )

    def small_grads(scal, mine, theirs):
        tall = 6 * L

        def kernel(scal_r, a_r, b_r, *refs):
            outs, all_s = refs[:-1], refs[-1]
            total = a_r[...] + b_r[...]
            odd = scal_r[8] == 1
            part = 2 * HD // S

            def pick(at):
                return jnp.where(odd, total[at + 1 : at + 2, :], total[at : at + 1, :])

            units = [pick(tall + 2 * l) for l in range(L)]
            units = jnp.concatenate(units + [jnp.zeros((TAIL - L, D), f32)], 0)[:, :F].astype(bf16)
            heads = [pick(tall + 2 * L + 2 * l) for l in range(L)]
            for t in range(S):
                side, place = divmod(t, S // 2)
                rows = []
                for row in heads:
                    cut = row[:, side * 2 * A : side * 2 * A + A]
                    at = place * part
                    rows.append(
                        jnp.concatenate([cut[:, h * HD + at : h * HD + at + part] for h in range(H)], 1)
                    )
                qv = jnp.concatenate(rows + [jnp.zeros((TAIL - L, 2 * A // S), f32)], 0)
                up = mm(units, spread(t, S, F), NT)
                rest = jnp.zeros((TAIL, z.a_cols - u_at - F // S), f32)
                all_s[t] = jnp.concatenate([total[:TAIL, t * M : (t + 1) * M], qv, up, rest], 1).astype(bf16)
            blocks_out(scal_r, all_s, outs)

        return run(
            kernel,
            [mine, theirs],
            block_shapes(TAIL, z.a_cols),
            [pltpu.VMEM((S, TAIL, z.a_cols), bf16)],
            scalars=scal,
            name="small_grads",
        )

    def pack_small(wide, ups, heads, pre_r):
        def kernel(*refs):
            o = refs[-1]
            o[...] = jnp.zeros((-(-10 * L // 8) * 8, D), f32)
            for l in range(L):
                pre_i, mid_i, last_i = refs[3 * l : 3 * l + 3]
                first = pre_i[...]
                if l == 0:
                    first = first + refs[5 * L][...]
                at = 6 * l
                o[at : at + 1, :] = first[0:1]
                o[at + 1 : at + 2, :] = mid_i[0:1, :]
                o[at + 2 : at + 3, :] = first[1:2]
                o[at + 3 : at + 5, :] = mid_i[1:3, :]
                o[at + 5 : at + 6, :] = last_i[...]
                o[6 * L + 2 * l : 6 * L + 2 * l + 2, :F] = refs[3 * L + l][...]
                o[8 * L + 2 * l : 8 * L + 2 * l + 2, : 3 * A] = refs[4 * L + l][...]

        flat = [a for row in wide for a in row] + list(ups) + list(heads) + [pre_r]
        flat = [Far(a) for a in flat]
        return run(kernel, flat, [((-(-10 * L // 8) * 8, D), f32, FAR)], name="pack_small")[0]

    def join_rows(scal, mine, theirs):
        def kernel(scal_r, a, b, o):
            start = pl.multiple_of(scal_r[8] * R, 16)
            o[pl.ds(start, R), :] = a[...]
            o[pl.ds(pl.multiple_of(R - start, 16), R), :] = b[...]

        return run(kernel, [mine, theirs], [((2 * R, D), bf16, FAR)], scalars=scal, name="join_rows")[0]

    def sum_blocks(blocks):
        def kernel(*refs):
            total = refs[0][...].astype(f32)
            for r in refs[1:-1]:
                total = total + r[...].astype(f32)
            refs[-1][...] = total.astype(bf16)

        return run(kernel, list(blocks), [(blocks[0].shape, bf16, FAR)], name="sum_blocks")[0]

    def feed_out(pairs):
        def kernel(*refs):
            up_o, down_o = refs[-2:]
            for l in range(L):
                total = refs[2 * l][...].astype(f32) + refs[2 * l + 1][...].astype(f32)
                up_o[l] = total[:, :F]
                down_o[l] = total[:, F:]

        return run(
            kernel,
            [a for p in pairs for a in p],
            [((L, M, F), f32, FAR), ((L, M, F), f32, FAR)],
            name="feed_out",
        )

    def proj_out(pairs, small):
        def kernel(*refs):
            qkv_o, out_o, qvb_o, upb_o, gain_o, shift_o = refs[-6:]
            for l in range(L):
                total = refs[2 * l][...].astype(f32) + refs[2 * l + 1][...].astype(f32)
                for h in range(H):
                    cuts = [total[:, i * A + h * HD : i * A + (h + 1) * HD] for i in range(3)]
                    qkv_o[l, h] = jnp.concatenate(cuts, 1)
                out_o[l] = total[:, 3 * A :].T
            tiny = refs[2 * L][...].astype(f32) + refs[2 * L + 1][...].astype(f32)
            part, unit = 2 * HD // S, 64 // S
            for l in range(L):
                gain_o[l] = tiny[6 * l : 6 * l + 2, :M]
                shift_o[l] = tiny[6 * l + 2 : 6 * l + 6, :M]
                for h in range(H):
                    qvb_o[h, l : l + 1, :] = tiny[l : l + 1, q_at + h * part : q_at + (h + 1) * part]
                for r in range(F // 64):
                    upb_o[r, l : l + 1, :] = tiny[l : l + 1, u_at + r * unit : u_at + (r + 1) * unit]

        return run(
            kernel,
            [a for p in list(pairs) + [small] for a in p],
            [
                ((L, H, M, 3 * HD), f32, FAR),
                ((L, A, M), f32, FAR),
                ((H, L, 2 * HD // S), f32),
                ((F // 64, L, 64 // S), f32),
                ((L, 2, M), f32),
                ((L, 4, M), f32),
            ],
            name="project_out",
        )

    def input_back(x, dy, pa, pb, vec):
        def kernel(x_r, dy_r, pa_r, pb_r, vec_r, o, sums_o):
            dn = pa_r[...].astype(f32) + pb_r[...].astype(f32)
            dx, dgain, dshift = ln_back(x_r[...].astype(f32), vec_r[0:1, :], dn)
            o[...] = (dy_r[...] + dx).astype(bf16)
            sums_o[0:1, :] = dgain
            sums_o[1:2, :] = dshift

        return run(kernel, [x, dy, pa, pb, vec], [((R, D), bf16, FAR), ((2, D), f32)], name="input_back")

    return dict(locals())


def local(mesh):
    def fn(frames, cotangent, w_qkv, qv_bias, w_out, w_up, up_bias, w_down, norm_gains, shifts):
        z = Sizes(mesh, frames, w_qkv, w_up)
        assert frames.shape[0] == 1
        k = make(z)
        L, m, R, D, A, F, H, HD, S = z.layers, z.m, z.rows, z.width, z.att, z.hidden, z.heads, z.hd, z.shards
        core = lax.axis_index("tc")
        scal = ring_scalars(S)

        def part_a(l, *then):
            qkv = after(w_qkv[l], *then).reshape(m, H, 3, HD).transpose(0, 2, 1, 3).reshape(m, 3 * A)
            return jnp.concatenate([qkv, after(w_out[l], *then).reshape(A, m).T], -1)

        def part_b(l, *then):
            return jnp.concatenate([after(w_up[l], *then), after(w_down[l], *then).T], -1)

        vec_rows = jnp.concatenate([norm_gains, shifts], 1).reshape(6 * L, m)
        bias_rows = jnp.concatenate([qv_bias.reshape(L, -1), up_bias.reshape(L, -1)], 1)
        bias_rows = jnp.pad(bias_rows, ((0, TAIL - L), (0, z.a_cols - m - bias_rows.shape[1])))
        tail = jnp.concatenate([jnp.pad(vec_rows, ((0, TAIL - 6 * L), (0, 0))), bias_rows], 1)
        message = jnp.concatenate([part_a(0), tail], 0)
        w_a = [Pieces(message, TAIL) if S == 4 else Gathered(message, S, TAIL)]
        w_b = [Gathered(after(part_b(0, message), *w_a[0].arrays[1:4]), S)]

        def my_rows(x):
            return lax.dynamic_slice_in_dim(x.reshape(2 * R, D), core * R, R, 0)

        kept = []
        x = my_rows(frames)
        for layer in range(L):
            if layer == 0:
                n1, q0, q1, kv0, kv1, vec, qb, tails = k["proj"](scal, x, 0, w_a[0])
            else:
                n1, q0, q1, kv0, kv1, x = k["proj"](scal, y, layer, w_a[layer], (vec, qb), (part, x_swap(part)))
            kvs = []
            for kv in (kv0, kv1):
                far = y_swap(kv)
                kvs.append((kv, core_swap(kv), far, core_swap(far)))
            if layer + 1 < L:
                next_a, next_b = part_a(layer + 1, n1), part_b(layer + 1, n1)
                q0 = after(q0, next_a)
            q0 = after(q0, kvs[1][2])
            o0, qa0 = k["attend"](q0, kvs[0])
            o1, qa1, o_own, o_snd, att_part = k["attend"](q1, kvs[1], scal, o0, w_a[layer])
            far = x_swap(att_part)
            n1_r = o_rcv = None
            if layer == 0:
                n1_r, o_rcv = core_swap(n1), core_swap(o_snd)
                x = after(x, n1_r, o_rcv)
            if layer + 1 < L:
                w_a.append(Gathered(after(next_a, kvs[0][2]), S))
                w_b.append(Gathered(after(next_b, o0), S))
            y, n2, *hid_gp, part = k["feed"](
                scal, x, att_part, far, vec, tails, layer, w_b[layer]
            )
            hid, gp = hid_gp[:2], hid_gp[2:]
            kept.append((x, n1, n1_r, kvs, (qa0, qa1), (o0, o1), o_own, o_rcv, y, n2, hid, gp))

        def whole_rows(mine):
            return k["join_rows"](scal, mine, core_swap(mine))[None]

        def send_blocks(blocks):
            if S == 4:
                return [blocks[0]] + [lax.ppermute(b, "shard", ring(s)) for b, s in zip(blocks[1:], (1, 3, 2))]
            return [lax.psum_scatter(blocks[0], "shard", scatter_dimension=0, tiled=True)[0]]

        def scatter(grad):
            flat = grad.reshape(2 * S * m, grad.shape[-1])
            return lax.psum_scatter(flat, ("shard", "tc"), scatter_dimension=0, tiled=True)

        def first_hops(blocks):
            if S != 4:
                return []
            return [lax.ppermute(blocks[3], "shard", ring(1)), lax.ppermute(blocks[4], "shard", ring(3))]

        def last_hops(blocks, hops):
            if S != 4:
                return [lax.psum_scatter(blocks[0], "shard", scatter_dimension=0, tiled=True)[0]]
            up, down = k["pass_on"](blocks[1], blocks[2], *hops)
            return [blocks[0], lax.ppermute(up, "shard", ring(1)), lax.ppermute(down, "shard", ring(3))]

        y_last, part_last = y, part
        g = my_rows(cotangent)
        wide, d_qv, d_up = [None] * L, [None] * L, [None] * L
        sum_a, sum_b = [None] * L, [None] * L
        before = None
        for layer in reversed(range(L)):
            x, n1, n1_r, kvs, qas, os, o_own, o_rcv, y, n2, hid, gp = kept[layer]
            if before is None:
                g2, du, part, sum_g2 = k["feed_back"](scal, g, gp, layer, w_b[layer])
            else:
                gp = [after(gp[0], grad_a), gp[1]]
                g2, du, part, sum_g2, g, pre = k["feed_back"](scal, None, gp, layer, w_b[layer], before)
                wide[layer + 1] = [pre] + wide[layer + 1]
            far = x_swap(part)
            grad_b, d_up[layer] = k["feed_grads"](n2, hid, g2, du)
            y = after(y, grad_b)
            if before is not None:
                sum_b[layer + 1] = (part_b_sum, y_swap(after(part_b_sum, part)))
                y = after(y, sum_b[layer + 1][1])
            dy, g1, d0, d1, mid = k["middle_back"](
                scal, y, g, part, far, vec, os[0], os[1], layer, w_a[layer]
            )
            part_b_sum = scatter(after(grad_b, d0))
            if layer == 0:
                g1_r = core_swap(g1)
                qas = (qas[0], after(qas[1], g1_r, part_a_sum))
            dqs, kv_parts, hold, far_kv = [], [], None, None
            for e in range(2):
                qa = qas[e]
                if e == 1:
                    qa = after(qa, hold)
                dq, own, y_own, snd = k["attend_back"](qa, kvs[e], (d0, d1)[e])
                if far_kv is not None:
                    snd = after(snd, far_kv)
                pair = core_swap(snd)
                hold = k["cross_sum"](y_own, pair)
                far_kv = y_swap(hold)
                dqs.append(dq)
                kv_parts.append((own, pair, far_kv))
            if before is None:
                part_last = after(part_last, dy)
                far_last = x_swap(part_last)
                dqs[0] = after(dqs[0], far_last)
            dp, dp_snd, part, d_qv[layer], *pre = k["proj_back"](
                scal, dqs, kv_parts, layer, w_a[layer], *([x] if layer == 0 else [])
            )
            far = x_swap(part)
            if layer > 0:
                grad_a = k["pair_grads"](n1, dp, dp_snd, g1, *os)
                part_a_sum = scatter(after(grad_a, part_b_sum, far))
            else:
                sum_a[1] = (part_a_sum, y_swap(after(part_a_sum, part)))
                blocks = k["proj_grads"](scal, n1, n1_r, dp, core_swap(dp_snd), g1, g1_r, o_own, o_rcv)
            wide[layer] = pre + [mid, sum_g2]
            before = (x, dy, part, far, vec)
        before = (x, after(dy, blocks[0]), part, far, vec)
        hops = first_hops(blocks)
        got_a = last_hops(blocks, hops)
        grad_rows, _ = k["input_back"](*before)
        frames_grad = whole_rows(grad_rows)
        pre = after(wide[0][0], blocks[0])
        sums = k["pack_small"](wide, d_up, d_qv, x_swap(pre))
        got_small = send_blocks(k["small_grads"](scal, sums, core_swap(sums)))
        mine = k["sum_blocks"](got_a)
        sum_a[0] = (mine, y_swap(mine))
        small = k["sum_blocks"](got_small)
        part_b_sum = after(part_b_sum, part)
        sum_b[0] = (part_b_sum, y_swap(part_b_sum))
        out_frames = whole_rows(k["finish"](y_last, part_last, far_last, vec)[0])
        outs_up, outs_down = k["feed_out"](sum_b)
        outs_qkv, outs_out, g_qvb, g_upb, g_gains, g_shifts = k["proj_out"](sum_a, (small, y_swap(small)))
        return (
            out_frames,
            frames_grad,
            outs_qkv.transpose(0, 2, 1, 3),
            g_qvb.transpose(1, 0, 2),
            outs_out.reshape(L, H, HD, m),
            outs_up,
            g_upb.transpose(1, 0, 2),
            outs_down.transpose(0, 2, 1),
            g_gains,
            g_shifts,
        )

    return fn


def solution(mesh):
    assert mesh.axis_names == ("shard", "ctx", "tp") and mesh.shape["tp"] == 4 and mesh.shape["ctx"] == 2
    split = Mesh(mesh.devices.reshape(mesh.shape["shard"], 2, 2, 2), ("shard", "ctx", "tx", "tc"))
    tp = ("tx", "tc")
    specs = (
        P("shard", "ctx", None),
        P("shard", "ctx", None),
        P(None, "shard", tp, None),
        P(None, tp, "shard"),
        P(None, tp, None, "shard"),
        P(None, "shard", tp),
        P(None, tp, "shard"),
        P(None, tp, "shard"),
        P(None, None, "shard"),
        P(None, None, "shard"),
    )
    return jax.shard_map(local(split), mesh=split, in_specs=specs, out_specs=specs, check_vma=False)
```

time: 555 us -> 447 us (0.81)
  blocking collectives: 58.3 us -> 0 us
  Pallas kernels: 103 us -> 152 us
  waiting for transfers between devices: 215 us -> 167 us
  local copies, waits for them, and re-layouts: 81.2 us -> 50 us
  other arithmetic: 15.1 us -> 4.44 us
    ppermute x63 -> x42, waiting for transfers between devices: 158 us -> 102 us  [the longest x9 46 us: x_swap(): return lax.ppermute(x, 'tx', [(0, 1), (1, 0)])]
    pallas_call x28 -> x37, Pallas kernels: 103 us -> 152 us  [run(): pl.pallas_call(wrapped, out_shape=shapes, in_specs=specs, out_specs=[any_...]
    psum x1 -> x0, blocking collectives: 37.5 us -> none  [fn(): tiny = lax.psum(tiny, ('shard', 'ctx'))]
    all_gather x0 -> x3, waiting for transfers between devices: none -> 26.3 us  [__init__(): whole = lax.all_gather(x, ('shard', 'tc'), axis=0, tiled=False)]
    unnamed x1 -> x0, blocking collectives: 20.8 us -> none
    unnamed x337 -> x280, local copies, waits for them, and re-layouts: 62.3 us -> 43.6 us
    ppermute x12 -> x13, waiting for transfers between devices: 56.8 us -> 39.1 us  [y_swap(): return lax.ppermute(x, 'ctx', [(0, 1), (1, 0)])]
    slice x29 -> x1, local copies, waits for them, and re-layouts: 10.4 us -> 1.09 us  [part_a(): w_qkv[l]]
  transfers between devices with their start and end apart: 79 -> 61, of which waited for: 36 -> 36; matrix products, arithmetic and copies ran while one was open for 6% -> 1% of each run, Pallas kernels for 13% -> 30%
where the time goes in v2:
time: 447 us; the launch traced here: 440 us
  waiting for transfers between devices  167 us (37%)
  Pallas kernels  152 us (34%)
  local copies, waits for them, and re-layouts  50 us (11%)
  starting transfers between devices  50 us (11%)
  between operations  16 us (4%)
    pallas_call x37, Pallas kernels, run(): pl.pallas_call(wrapped, out_shape=shapes, in_specs=specs, out_specs=[any_...  152 us
    ppermute x9, waiting for transfers between devices, x_swap(): return lax.ppermute(x, 'tx', [(0, 1), (1, 0)])  46 us
    unnamed x280, local copies, waits for them, and re-layouts  43.6 us
    ppermute x13, waiting for transfers between devices, y_swap(): return lax.ppermute(x, 'ctx', [(0, 1), (1, 0)])  39.1 us
    all_gather x3, waiting for transfers between devices, __init__(): whole = lax.all_gather(x, ('shard', 'tc'), axis=0, tiled=False)  26.3 us
    ppermute x3, waiting for transfers between devices, __init__(): self.mine = [x] + [lax.ppermute(x, 'shard', ring(s)) for s in (1, 3, 2)]  18.4 us
    ppermute x13, starting transfers between devices, y_swap(): return lax.ppermute(x, 'ctx', [(0, 1), (1, 0)])  17 us
    ppermute x9, starting transfers between devices, x_swap(): return lax.ppermute(x, 'tx', [(0, 1), (1, 0)])  13.6 us
  transfers between devices with their start and end apart: 61, of which 36 were waited for; matrix products, arithmetic and copies ran while one was open for 1% of the time, Pallas kernels for 30%

profile of v2, /device:TPU:0, one launch (start us, length us, event | category | flops | bytes accessed | tf_op | source)
XLA Modules:
  0.0 440.1 jit_solution(1192491994782688513)
XLA Ops:
  15.0 4.0 collective-permute-start.2
  23.4 12.0 %collective-permute-done.2.refs_5_.refs_10_.refs_11_.refs_13_ = bf16[208,768]{1,0:T(8,128)(2,1)} collective-permute-done((bf16[208,768]{1,0:T(8,128)(2,1)}, bf16[208,768]{1,0:T(8,128)(2,1)}, u32[]{:S(2)}, u32[]{:S(2)}) %collective-permute-start.2) | collective-permute-done | bytes 319520 | tf_op jit(solution)/shard_map/ppermute | solution.py:71
  35.4 6.3 %collective-permute-done.refs_3_.refs_8_.refs_9_.refs_11_ = bf16[208,768]{1,0:T(8,128)(2,1)} collective-permute-done((bf16[208,768]{1,0:T(8,128)(2,1)}, bf16[208,768]{1,0:T(8,128)(2,1)}, u32[]{:S(2)}, u32[]{:S(2)}) %collective-permute-start) | collective-permute-done | bytes 319520 | tf_op jit(solution)/shard_map/ppermute | solution.py:71
  45.8 4.6 %project.2 = (bf16[384,768]{1,0:T(8,128)(2,1)S(1)}, bf16[384,192]{1,0:T(8,128)(2,1)S(1)}, bf16[384,192]{1,0:T(8,128)(2,1)S(1)}, bf16[384,384]{1,0:T(8,128)(2,1)}...) custom-call(s32[16]{0:T(128)S(1)} %stack.23.refs_0_, ...), custom_call_target="tpu_custom_call" | custom-call | flops 1750000000 | bytes 1000 | tf_op jit(solution)/shard_map/project/pallas_call | solution.py:222
  52.9 7.4 %collective-permute-done.12.refs_3_ = bf16[384,384]{1,0:T(8,128)(2,1)S(1)} collective-permute-done((bf16[384,384]{1,0:T(8,128)(2,1)}, bf16[384,384]{1,0:T(8,128)(2,1)S(1)}, u32[]{:S(2)}, u32[]{:S(2)}) %collective-permute-start.12) | collective-permute-done | bytes 294944 | tf_op jit(solution)/shard_map/ppermute | solution.py:50
  65.4 4.5 %collective-permute-done.9.refs_4_.refs_3_ = bf16[384,384]{1,0:T(8,128)(2,1)} collective-permute-done((bf16[384,384]{1,0:T(8,128)(2,1)S(1)}, bf16[384,384]{1,0:T(8,128)(2,1)}, u32[]{:S(2)}, u32[]{:S(2)}) %collective-permute-start.9) | collective-permute-done | bytes 294944 | tf_op jit(solution)/shard_map/ppermute | solution.py:50
  69.9 5.4 %attend.4 = (bf16[384,192]{1,0:T(8,128)(2,1)S(1)}, bf16[3,384,128]{2,1,0:T(8,128)(2,1)S(1)}) custom-call(bf16[384,192]{1,0:T(8,128)(2,1)S(1)} %get-tuple-element.158.refs_0_, bf16[384,384]{1,0:T(8,128)(2,1)S(1)} %copy-done.43, bf16[384,384]{1,0:T(8,128)(2,1)S(1)} %collective-permute-done.11.refs_2_, bf16[384,384]{1,0:T(8,128)(2,1)S(1)} %collective-permute-done.12.refs_3_, ...), custom_call_target="tpu_custom_call" | custom-call | flops 3000000000 | bytes 1000 | tf_op jit(solution)/shard_map/attend/pallas_call | solution.py:222
  78.3 8.2 %attend.5 = (bf16[384,192]{1,0:T(8,128)(2,1)S(1)}, bf16[3,384,128]{2,1,0:T(8,128)(2,1)S(1)}, bf16[384,192]{1,0:T(8,128)(2,1)S(1)}, bf16[384,192]{1,0:T(8,128)(2,1)S(1)}, bf16[384,768]{1,0:T(8,128)(2,1)}) custom-call(s32[16]{0:T(128)S(1)} %stack.23.refs_0_, bf16[384,192]{1,0:T(8,128)(2,1)S(1)} %get-tuple-element.152.refs_1_, bf16[384,384]{1,0:T(8,128)(2,1)S(1)} %copy-done.41, ...), custom_call_target="tpu_custom_call" | custom-call | flops 3000000000 | bytes 1000 | tf_op jit(solution)/shard_map/attend/pallas_call | solution.py:222
  92.2 12.0 %collective-permute-done.15.refs_3_ = bf16[384,768]{1,0:T(8,128)(2,1)S(1)} collective-permute-done((bf16[384,768]{1,0:T(8,128)(2,1)}, bf16[384,768]{1,0:T(8,128)(2,1)S(1)}, u32[]{:S(2)}, u32[]{:S(2)}) %collective-permute-start.15) | collective-permute-done | bytes 589856 | tf_op jit(solution)/shard_map/ppermute | solution.py:46
  108.1 7.2 %feed.2 = (f32[384,768]{1,0:T(8,128)S(1)}, bf16[384,768]{1,0:T(8,128)(2,1)}, bf16[384,768]{1,0:T(8,128)(2,1)}, bf16[384,768]{1,0:T(8,128)(2,1)}, bf16[384,768]{1...) custom-call(s32[16]{0:T(128)S(1)} %stack.23.refs_0_, ...), custom_call_target="tpu_custom_call" | custom-call | flops 3000000000 | bytes 1000 | tf_op jit(solution)/shard_map/feed/pallas_call | solution.py:222
  116.9 14.8 %all-gather.9.cloned.1.call-done = bf16[1536,768]{1,0:T(8,128)(2,1)} async-done(((bf16[192,768]{1,0:T(8,128)(2,1)}), bf16[1536,768]{1,0:T(8,128)(2,1)}) %all-gather.9.cloned.1.call-update) | async-done | bytes 2359312 | tf_op jit(solution)/shard_map/all_gather | solution.py:94
  132.8 4.2 project.3
  140.8 8.0 %collective-permute-done.21.refs_3_ = bf16[384,384]{1,0:T(8,128)(2,1)S(1)} collective-permute-done((bf16[384,384]{1,0:T(8,128)(2,1)}, bf16[384,384]{1,0:T(8,128)(2,1)S(1)}, u32[]{:S(2)}, u32[]{:S(2)}) %collective-permute-start.21) | collective-permute-done | bytes 294944 | tf_op jit(solution)/shard_map/ppermute | solution.py:50
  149.4 5.1 %collective-permute-done.18.refs_4_.refs_3_ = bf16[384,384]{1,0:T(8,128)(2,1)S(1)} collective-permute-done((bf16[384,384]{1,0:T(8,128)(2,1)}, bf16[384,384]{1,0:T(8,128)(2,1)S(1)}, u32[]{:S(2)}, u32[]{:S(2)}) %collective-permute-start.18) | collective-permute-done | bytes 294944 | tf_op jit(solution)/shard_map/ppermute | solution.py:50
  155.7 5.4 %attend.6 = (bf16[384,192]{1,0:T(8,128)(2,1)S(1)}, bf16[3,384,128]{2,1,0:T(8,128)(2,1)S(1)}) custom-call(bf16[384,192]{1,0:T(8,128)(2,1)S(1)} %get-tuple-element.177.refs_0_, bf16[384,384]{1,0:T(8,128)(2,1)S(1)} %copy-done.59, bf16[384,384]{1,0:T(8,128)(2,1)S(1)} %collective-permute-done.20.refs_2_, bf16[384,384]{1,0:T(8,128)(2,1)S(1)} %collective-permute-done.21.refs_3_, ...), custom_call_target="tpu_custom_call" | custom-call | flops 3000000000 | bytes 1000 | tf_op jit(solution)/shard_map/attend/pallas_call | solution.py:222
  161.9 8.6 %attend.7 = (bf16[384,192]{1,0:T(8,128)(2,1)S(1)}, bf16[3,384,128]{2,1,0:T(8,128)(2,1)S(1)}, bf16[384,192]{1,0:T(8,128)(2,1)}, bf16[384,192]{1,0:T(8,128)(2,1)}, bf16[384,768]{1,0:T(8,128)(2,1)}) custom-call(s32[16]{0:T(128)S(1)} %stack.23.refs_0_, bf16[384,192]{1,0:T(8,128)(2,1)S(1)} %get-tuple-element.174.refs_1_, bf16[384,384]{1,0:T(8,128)(2,1)S(1)} %copy-done.55, ...), custom_call_target="tpu_custom_call" | custom-call | flops 3000000000 | bytes 1000 | tf_op jit(solution)/shard_map/attend/pallas_call | solution.py:222
  172.8 11.4 %all-gather.11.cloned.1.call-done = bf16[1536,1536]{1,0:T(8,128)(2,1)} async-done(((bf16[192,1536]{1,0:T(8,128)(2,1)}), bf16[1536,1536]{1,0:T(8,128)(2,1)}) %all-gather.11.cloned.1.call-update) | async-done | bytes 4718608 | tf_op jit(solution)/shard_map/all_gather | solution.py:94
  184.2 2.9 collective-permute-done.23.refs_3_
  192.1 7.1 %feed.3 = (f32[384,768]{1,0:T(8,128)S(1)}, bf16[384,768]{1,0:T(8,128)(2,1)}, bf16[384,768]{1,0:T(8,128)(2,1)}, bf16[384,768]{1,0:T(8,128)(2,1)}, bf16[384,768]{1...) custom-call(s32[16]{0:T(128)S(1)} %stack.23.refs_0_, f32[384,768]{1,0:T(8,128)S(1)} %copy-done.84, ...), custom_call_target="tpu_custom_call" | custom-call | flops 3000000000 | bytes 1000 | tf_op jit(solution)/shard_map/feed/pallas_call | solution.py:222
  199.2 6.6 %feed_back.2 = (bf16[384,768]{1,0:T(8,128)(2,1)S(1)}, bf16[384,1536]{1,0:T(8,128)(2,1)S(1)}, bf16[384,768]{1,0:T(8,128)(2,1)}, f32[1,768]{1,0:T(1,128)S(1)}) custom-call(s32[16]{0:T(128)S(1)} %stack.23.refs_0_, bf16[384,768]{1,0:T(8,128)(2,1)S(1)} %dynamic-slice_bitcast_fusion.refs_1_.refs_2_, bf16[384,768]{1,0:T(8,128)(2,1)} %get-tuple-element.189.refs_2_, ...), custom_call_target="tpu_custom_call" | custom-call | flops 3000000000 | bytes 1000 | tf_op jit(solution)/shard_map/feed_back/pallas_call | solution.py:222
  207.4 6.9 %feed_grads.2 = (bf16[4,2,192,1536]{3,2,1,0:T(8,128)(2,1)}, f32[2,768]{1,0:T(2,128)S(1)}) custom-call(bf16[384,768]{1,0:T(8,128)(2,1)} %get-tuple-element.186.refs_0_, bf16[384,768]{1,0:T(8,128)(2,1)} %get-tuple-element.187.refs_1_, bf16[384,768]{1,0:T(8,128)(2,1)} %get-tuple-element.188.refs_2_, bf16[384,768]{1,0:T(8,128)(2,1)S(1)} %get-tuple-element.191.refs_3_, ...), custom_call_target="tpu_custom_call" | custom-call | flops 1500000000 | bytes 1000 | tf_op jit(solution)/shard_map/feed_grads/pallas_call | solution.py:222
  214.3 6.6 %collective-permute-done.24.refs_4_ = bf16[384,768]{1,0:T(8,128)(2,1)S(1)} collective-permute-done((bf16[384,768]{1,0:T(8,128)(2,1)}, bf16[384,768]{1,0:T(8,128)(2,1)S(1)}, u32[]{:S(2)}, u32[]{:S(2)}) %collective-permute-start.24) | collective-permute-done | bytes 589856 | tf_op jit(solution)/shard_map/ppermute | solution.py:46
  220.9 3.6 middle_back.2
  230.8 7.0 %attend_back.4 = (bf16[384,192]{1,0:T(8,128)(2,1)S(1)}, bf16[384,384]{1,0:T(8,128)(2,1)S(1)}, bf16[384,384]{1,0:T(8,128)(2,1)S(1)}, bf16[2,384,384]{2,1,0:T(8,128)(2,1)}) custom-call(bf16[3,384,128]{2,1,0:T(8,128)(2,1)S(1)} %copy-done.121, bf16[384,384]{1,0:T(8,128)(2,1)S(1)} %copy-done.60, bf16[384,384]{1,0:T(8,128)(2,1)S(1)} %copy-done.68, ...), custom_call_target="tpu_custom_call" | custom-call | flops 3000000000 | bytes 1000 | tf_op jit(solution)/shard_map/attend_back/pallas_call | solution.py:222
  237.9 2.2 collective-permute-done.27.refs_1_.refs_4_
  242.5 7.0 %attend_back.5 = (bf16[384,192]{1,0:T(8,128)(2,1)S(1)}, bf16[384,384]{1,0:T(8,128)(2,1)S(1)}, bf16[384,384]{1,0:T(8,128)(2,1)S(1)}, bf16[2,384,384]{2,1,0:T(8,128)(2,1)}) custom-call(bf16[3,384,128]{2,1,0:T(8,128)(2,1)S(1)} %copy-done.116, bf16[384,384]{1,0:T(8,128)(2,1)S(1)} %copy-done.56, bf16[384,384]{1,0:T(8,128)(2,1)S(1)} %copy-done.62, ...), custom_call_target="tpu_custom_call" | custom-call | flops 3000000000 | bytes 1000 | tf_op jit(solution)/shard_map/attend_back/pallas_call | solution.py:222
  254.8 11.2 %collective-permute-done.25.refs_2_ = bf16[384,768]{1,0:T(8,128)(2,1)S(1)} collective-permute-done((bf16[384,768]{1,0:T(8,128)(2,1)S(1)}, bf16[384,768]{1,0:T(8,128)(2,1)S(1)}, u32[]{:S(2)}, u32[]{:S(2)}) %collective-permute-start.25) | collective-permute-done | bytes 589856 | tf_op jit(solution)/shard_map/ppermute | solution.py:46
  266.8 4.5 %project_back.2 = (bf16[384,576]{1,0:T(8,128)(2,1)S(1)}, bf16[384,576]{1,0:T(8,128)(2,1)S(1)}, bf16[384,768]{1,0:T(8,128)(2,1)}, f32[2,576]{1,0:T(2,128)S(1)}) custom-call(s32[16]{0:T(128)S(1)} %stack.23.refs_0_, bf16[384,192]{1,0:T(8,128)(2,1)S(1)} %get-tuple-element.205.refs_1_, bf16[384,192]{1,0:T(8,128)(2,1)S(1)} %get-tuple-element.211.refs_2_, ...), custom_call_target="tpu_custom_call" | custom-call | flops 2000000000 | bytes 1000 | tf_op jit(solution)/shard_map/project_back/pallas_call | solution.py:222
  272.9 3.2 pair_grads.1
  276.1 10.6 %collective-permute-done.31.refs_4_ = bf16[384,768]{1,0:T(8,128)(2,1)S(1)} collective-permute-done((bf16[384,768]{1,0:T(8,128)(2,1)}, bf16[384,768]{1,0:T(8,128)(2,1)S(1)}, u32[]{:S(2)}, u32[]{:S(2)}) %collective-permute-start.31) | collective-permute-done | bytes 589856 | tf_op jit(solution)/shard_map/ppermute | solution.py:46
  292.4 7.1 %feed_back.3 = (bf16[384,768]{1,0:T(8,128)(2,1)S(1)}, bf16[384,1536]{1,0:T(8,128)(2,1)S(1)}, bf16[384,768]{1,0:T(8,128)(2,1)}, f32[1,768]{1,0:T(1,128)S(1)}, f32...) custom-call(s32[16]{0:T(128)S(1)} %stack.23.refs_0_, f32[384,768]{1,0:T(8,128)S(1)} %copy-done.85, f32[384,768]{1,0:T(8,128)S(1)} %copy-done.87, ...), custom_call_target="tpu_custom_call" | custom-call | flops 3000000000 | bytes 1000 | tf_op jit(solution)/shard_map/feed_back/pallas_call | solution.py:222
  302.5 7.0 %feed_grads.3 = (bf16[4,2,192,1536]{3,2,1,0:T(8,128)(2,1)}, f32[2,768]{1,0:T(2,128)S(1)}) custom-call(bf16[384,768]{1,0:T(8,128)(2,1)} %get-tuple-element.199.refs_0_, bf16[384,768]{1,0:T(8,128)(2,1)} %get-tuple-element.200.refs_1_, bf16[384,768]{1,0:T(8,128)(2,1)} %get-tuple-element.201.refs_2_, bf16[384,768]{1,0:T(8,128)(2,1)S(1)} %get-tuple-element.225.refs_3_, ...), custom_call_target="tpu_custom_call" | custom-call | flops 1500000000 | bytes 1000 | tf_op jit(solution)/shard_map/feed_grads/pallas_call | solution.py:222
  310.1 3.5 collective-permute-done.32.refs_3_
  315.1 4.4 middle_back.3
  325.7 7.2 %attend_back.6 = (bf16[384,192]{1,0:T(8,128)(2,1)S(1)}, bf16[384,384]{1,0:T(8,128)(2,1)S(1)}, bf16[384,384]{1,0:T(8,128)(2,1)S(1)}, bf16[2,384,384]{2,1,0:T(8,128)(2,1)}) custom-call(bf16[3,384,128]{2,1,0:T(8,128)(2,1)S(1)} %copy-done.119, bf16[384,384]{1,0:T(8,128)(2,1)S(1)} %copy-done.44, bf16[384,384]{1,0:T(8,128)(2,1)S(1)} %copy-done.48, ...), custom_call_target="tpu_custom_call" | custom-call | flops 3000000000 | bytes 1000 | tf_op jit(solution)/shard_map/attend_back/pallas_call | solution.py:222
  339.9 8.0 %attend_back.7 = (bf16[384,192]{1,0:T(8,128)(2,1)S(1)}, bf16[384,384]{1,0:T(8,128)(2,1)S(1)}, bf16[384,384]{1,0:T(8,128)(2,1)S(1)}, bf16[2,384,384]{2,1,0:T(8,128)(2,1)}) custom-call(bf16[3,384,128]{2,1,0:T(8,128)(2,1)S(1)} %copy-done.114, bf16[384,384]{1,0:T(8,128)(2,1)S(1)} %copy-done.42, bf16[384,384]{1,0:T(8,128)(2,1)S(1)} %copy-done.50, ...), custom_call_target="tpu_custom_call" | custom-call | flops 3000000000 | bytes 1000 | tf_op jit(solution)/shard_map/attend_back/pallas_call | solution.py:222
  351.4 9.0 %collective-permute-done.38.refs_8_ = bf16[384,384]{1,0:T(8,128)(2,1)S(1)} collective-permute-done((bf16[384,384]{1,0:T(8,128)(2,1)}, bf16[384,384]{1,0:T(8,128)(2,1)S(1)}, u32[]{:S(2)}, u32[]{:S(2)}) %collective-permute-start.38) | collective-permute-done | bytes 294944 | tf_op jit(solution)/shard_map/ppermute | solution.py:50
  360.5 5.5 %project_back.3 = (bf16[384,576]{1,0:T(8,128)(2,1)S(1)}, bf16[384,576]{1,0:T(8,128)(2,1)}, bf16[384,768]{1,0:T(8,128)(2,1)}, f32[2,576]{1,0:T(2,128)S(1)}, f32[2,768]{1,0:T(2,128)S(1)}) custom-call(s32[16]{0:T(128)S(1)} %stack.23.refs_0_, bf16[384,192]{1,0:T(8,128)(2,1)S(1)} %copy-done.105, bf16[384,192]{1,0:T(8,128)(2,1)S(1)} %get-tuple-element.247.refs_2_, ...), custom_call_target="tpu_custom_call" | custom-call | flops 2000000000 | bytes 1000 | tf_op jit(solution)/shard_map/project_back/pallas_call | solution.py:222
  368.2 3.4 project_grads.1
  376.7 6.9 %collective-permute-done.42.refs_2_ = bf16[96,768]{1,0:T(8,128)(2,1)S(1)} collective-permute-done((bf16[96,768]{1,0:T(8,128)(2,1)}, bf16[96,768]{1,0:T(8,128)(2,1)S(1)}, u32[]{:S(2)}, u32[]{:S(2)}) %collective-permute-start.42) | collective-permute-done | bytes 147488 | tf_op jit(solution)/shard_map/ppermute | solution.py:982
  383.6 2.4 collective-permute-done.43.refs_3_
  388.4 2.3 collective-permute-start.45
  390.8 2.4 input_back.1
  400.2 3.4 collective-permute-done.45.refs_2_
  409.3 5.0 %collective-permute-done.50.refs_1_ = bf16[16,768]{1,0:T(8,128)(2,1)S(1)} collective-permute-done((bf16[16,768]{1,0:T(8,128)(2,1)}, bf16[16,768]{1,0:T(8,128)(2,1)S(1)}, u32[]{:S(2)}, u32[]{:S(2)}) %collective-permute-start.50) | collective-permute-done | bytes 24608 | tf_op jit(solution)/shard_map/ppermute | solution.py:972
  414.5 3.9 collective-permute-done.51.refs_2_
  420.0 3.3 collective-permute-done.52.refs_3_
  428.1 3.1 project_out.1
  (420 shorter events, 127.7 us)
Async XLA Ops:
  7.2 97.8 %all-gather.7.cloned.1.call-start = ((), (), s32[]{:S(2)}) async-start(), calls=%async_computation.6 | async-start | bytes 5308416 | tf_op jit(solution)/shard_map/all_gather | solution.py:94
  15.0 20.5 %collective-permute-start.2 = (bf16[208,768]{1,0:T(8,128)(2,1)}, bf16[208,768]{1,0:T(8,128)(2,1)}, u32[]{:S(2)}, u32[]{:S(2)}) collective-permute-start(bf16[208,768]{1,0:T(8,128)(2,1)} %fusion.4.refs_2_.refs_7_.refs_8_.refs_10_), channel_id=1, source_target_pairs={{0,16},{8,24},{16,0},{24,8},{1,17},{9,25},{17,1},{25,9},{2,18},{10... | collective-permute-start | bytes 958472 | tf_op jit(solution)/shard_map/ppermute | solution.py:71
  19.0 16.4 %collective-permute-start.1 = (bf16[208,768]{1,0:T(8,128)(2,1)}, bf16[208,768]{1,0:T(8,128)(2,1)}, u32[]{:S(2)}, u32[]{:S(2)}) collective-permute-start(bf16[208,768]{1,0:T(8,128)(2,1)} %fusion.4.refs_2_.refs_7_.refs_8_.refs_10_), channel_id=1, source_target_pairs={{0,24},{8,0},{16,8},{24,16},{1,25},{9,1},{17,9},{25,17},{2,26},{10... | collective-permute-start | bytes 958472 | tf_op jit(solution)/shard_map/ppermute | solution.py:71
  20.3 21.4 %collective-permute-start = (bf16[208,768]{1,0:T(8,128)(2,1)}, bf16[208,768]{1,0:T(8,128)(2,1)}, u32[]{:S(2)}, u32[]{:S(2)}) collective-permute-start(bf16[208,768]{1,0:T(8,128)(2,1)} %fusion.4.refs_2_.refs_7_.refs_8_.refs_10_), channel_id=1, source_target_pairs={{0,8},{8,16},{16,24},{24,0},{1,9},{9,17},{17,25},{25,1},{2,10},{10... | collective-permute-start | bytes 958472 | tf_op jit(solution)/shard_map/ppermute | solution.py:71
  41.8 89.9 %all-gather.9.cloned.1.call-start = ((), (), s32[]{:S(2)}) async-start(), calls=%async_computation.7 | async-start | bytes 2654208 | tf_op jit(solution)/shard_map/all_gather | solution.py:94
  51.1 9.3 %collective-permute-start.12 = (bf16[384,384]{1,0:T(8,128)(2,1)}, bf16[384,384]{1,0:T(8,128)(2,1)S(1)}, u32[]{:S(2)}, u32[]{:S(2)}) collective-permute-start(bf16[384,384]{1,0:T(8,128)(2,1)} %get-tuple-element.159.refs_1_), channel_id=1, source_target_pairs={{0,4},{4,0},{1,5},{5,1},{2,6},{6,2},{3,7},{7,3},{8,12},{12,8},{9,1... | collective-permute-start | bytes 884744 | tf_op jit(solution)/shard_map/ppermute | solution.py:50
  61.3 122.9 %all-gather.11.cloned.1.call-start = ((), (), s32[]{:S(2)}) async-start(), calls=%async_computation.8 | async-start | bytes 5308416 | tf_op jit(solution)/shard_map/all_gather | solution.py:94
  61.3 8.5 %collective-permute-start.9 = (bf16[384,384]{1,0:T(8,128)(2,1)S(1)}, bf16[384,384]{1,0:T(8,128)(2,1)}, u32[]{:S(2)}, u32[]{:S(2)}) collective-permute-start(bf16[384,384]{1,0:T(8,128)(2,1)S(1)} %copy-done.41), channel_id=1, source_target_pairs={{0,4},{4,0},{1,5},{5,1},{2,6},{6,2},{3,7},{7,3},{8,12},{12,8},{9,1... | collective-permute-start | bytes 884744 | tf_op jit(solution)/shard_map/ppermute | solution.py:50
  62.9 6.9 %collective-permute-start.11 = (bf16[384,384]{1,0:T(8,128)(2,1)S(1)}, bf16[384,384]{1,0:T(8,128)(2,1)S(1)}, u32[]{:S(2)}, u32[]{:S(2)}) collective-permute-start(bf16[384,384]{1,0:T(8,128)(2,1)S(1)} %copy-done.43), channel_id=1, source_target_pairs={{0,1},{1,0},{2,3},{3,2},{4,5},{5,4},{6,7},{7,6},{8,9},{9,8},{10,11... | collective-permute-start | bytes 884744 | tf_op jit(solution)/shard_map/ppermute | solution.py:42
  62.9 6.9 %collective-permute-start.13 = (bf16[384,384]{1,0:T(8,128)(2,1)S(1)}, bf16[384,384]{1,0:T(8,128)(2,1)S(1)}, u32[]{:S(2)}, u32[]{:S(2)}) collective-permute-start(bf16[384,384]{1,0:T(8,128)(2,1)S(1)} %collective-permute-done.12.refs_3_), channel_id=1, source_target_pairs={{0,1},{1,0},{2,3},{3,2},{4,5},{5,4},{6,7},{7,6},{8,9},{9,8},{10,11... | collective-permute-start | bytes 884744 | tf_op jit(solution)/shard_map/ppermute | solution.py:42
  76.0 210.7 %reduce-scatter.4.cloned.1.call-start = ((), (), s32[]{:S(2)}) async-start(), calls=%async_computation.3 | async-start | bytes 5308416 | tf_op jit(solution)/shard_map/reduce_scatter | solution.py:977
  76.6 13.5 %collective-permute-start.7 = (bf16[384,768]{1,0:T(8,128)(2,1)S(1)}, bf16[384,768]{1,0:T(8,128)(2,1)S(1)}, u32[]{:S(2)}, u32[]{:S(2)}) collective-permute-start(bf16[384,768]{1,0:T(8,128)(2,1)S(1)} %get-tuple-element.151.refs_1_), channel_id=1, source_target_pairs={{0,1},{1,0},{2,3},{3,2},{4,5},{5,4},{6,7},{7,6},{8,9},{9,8},{10,11... | collective-permute-start | bytes 1769480 | tf_op jit(solution)/shard_map/ppermute | solution.py:42
  88.6 15.6 %collective-permute-start.15 = (bf16[384,768]{1,0:T(8,128)(2,1)}, bf16[384,768]{1,0:T(8,128)(2,1)S(1)}, u32[]{:S(2)}, u32[]{:S(2)}) collective-permute-start(bf16[384,768]{1,0:T(8,128)(2,1)} %get-tuple-element.163.refs_2_), channel_id=1, source_target_pairs={{0,2},{2,0},{1,3},{3,1},{4,6},{6,4},{5,7},{7,5},{8,10},{10,8},{9,1... | collective-permute-start | bytes 1769480 | tf_op jit(solution)/shard_map/ppermute | solution.py:46
  115.3 16.4 %collective-permute-start.16 = (bf16[384,768]{1,0:T(8,128)(2,1)}, bf16[384,768]{1,0:T(8,128)(2,1)S(1)}, u32[]{:S(2)}, u32[]{:S(2)}) collective-permute-start(bf16[384,768]{1,0:T(8,128)(2,1)} %get-tuple-element.171.refs_4_), channel_id=1, source_target_pairs={{0,2},{2,0},{1,3},{3,1},{4,6},{6,4},{5,7},{7,5},{8,10},{10,8},{9,1... | collective-permute-start | bytes 1769480 | tf_op jit(solution)/shard_map/ppermute | solution.py:46
  138.8 10.1 %collective-permute-start.21 = (bf16[384,384]{1,0:T(8,128)(2,1)}, bf16[384,384]{1,0:T(8,128)(2,1)S(1)}, u32[]{:S(2)}, u32[]{:S(2)}) collective-permute-start(bf16[384,384]{1,0:T(8,128)(2,1)} %get-tuple-element.178.refs_1_), channel_id=1, source_target_pairs={{0,4},{4,0},{1,5},{5,1},{2,6},{6,2},{3,7},{7,3},{8,12},{12,8},{9,1... | collective-permute-start | bytes 884744 | tf_op jit(solution)/shard_map/ppermute | solution.py:50
  140.3 14.2 %collective-permute-start.18 = (bf16[384,384]{1,0:T(8,128)(2,1)}, bf16[384,384]{1,0:T(8,128)(2,1)S(1)}, u32[]{:S(2)}, u32[]{:S(2)}) collective-permute-start(bf16[384,384]{1,0:T(8,128)(2,1)} %get-tuple-element.175.refs_2_.refs_1_), channel_id=1, source_target_pairs={{0,4},{4,0},{1,5},{5,1},{2,6},{6,2},{3,7},{7,3},{8,12},{12,8},{9,1... | collective-permute-start | bytes 884744 | tf_op jit(solution)/shard_map/ppermute | solution.py:50
  140.8 13.7 %collective-permute-start.20 = (bf16[384,384]{1,0:T(8,128)(2,1)}, bf16[384,384]{1,0:T(8,128)(2,1)S(1)}, u32[]{:S(2)}, u32[]{:S(2)}) collective-permute-start(bf16[384,384]{1,0:T(8,128)(2,1)} %get-tuple-element.178.refs_1_), channel_id=1, source_target_pairs={{0,1},{1,0},{2,3},{3,2},{4,5},{5,4},{6,7},{7,6},{8,9},{9,8},{10,11... | collective-permute-start | bytes 884744 | tf_op jit(solution)/shard_map/ppermute | solution.py:42
  148.9 5.6 %collective-permute-start.22 = (bf16[384,384]{1,0:T(8,128)(2,1)S(1)}, bf16[384,384]{1,0:T(8,128)(2,1)S(1)}, u32[]{:S(2)}, u32[]{:S(2)}) collective-permute-start(bf16[384,384]{1,0:T(8,128)(2,1)S(1)} %collective-permute-done.21.refs_3_), channel_id=1, source_target_pairs={{0,1},{1,0},{2,3},{3,2},{4,5},{5,4},{6,7},{7,6},{8,9},{9,8},{10,11... | collective-permute-start | bytes 884744 | tf_op jit(solution)/shard_map/ppermute | solution.py:42
  148.9 13.0 %collective-permute-start.17 = (bf16[384,384]{1,0:T(8,128)(2,1)}, bf16[384,384]{1,0:T(8,128)(2,1)S(1)}, u32[]{:S(2)}, u32[]{:S(2)}) collective-permute-start(bf16[384,384]{1,0:T(8,128)(2,1)} %get-tuple-element.175.refs_2_.refs_1_), channel_id=1, source_target_pairs={{0,1},{1,0},{2,3},{3,2},{4,5},{5,4},{6,7},{7,6},{8,9},{9,8},{10,11... | collective-permute-start | bytes 884744 | tf_op jit(solution)/shard_map/ppermute | solution.py:42
  154.5 7.4 %collective-permute-start.19 = (bf16[384,384]{1,0:T(8,128)(2,1)S(1)}, bf16[384,384]{1,0:T(8,128)(2,1)S(1)}, u32[]{:S(2)}, u32[]{:S(2)}) collective-permute-start(bf16[384,384]{1,0:T(8,128)(2,1)S(1)} %collective-permute-done.18.refs_4_.refs_3_), channel_id=1, source_target_pairs={{0,1},{1,0},{2,3},{3,2},{4,5},{5,4},{6,7},{7,6},{8,9},{9,8},{10,11... | collective-permute-start | bytes 884744 | tf_op jit(solution)/shard_map/ppermute | solution.py:42
  171.3 15.8 %collective-permute-start.23 = (bf16[384,768]{1,0:T(8,128)(2,1)}, bf16[384,768]{1,0:T(8,128)(2,1)S(1)}, u32[]{:S(2)}, u32[]{:S(2)}) collective-permute-start(bf16[384,768]{1,0:T(8,128)(2,1)} %get-tuple-element.180.refs_2_), channel_id=1, source_target_pairs={{0,2},{2,0},{1,3},{3,1},{4,6},{6,4},{5,7},{7,5},{8,10},{10,8},{9,1... | collective-permute-start | bytes 1769480 | tf_op jit(solution)/shard_map/ppermute | solution.py:46
  205.9 15.1 %collective-permute-start.24 = (bf16[384,768]{1,0:T(8,128)(2,1)}, bf16[384,768]{1,0:T(8,128)(2,1)S(1)}, u32[]{:S(2)}, u32[]{:S(2)}) collective-permute-start(bf16[384,768]{1,0:T(8,128)(2,1)} %get-tuple-element.195.refs_3_), channel_id=1, source_target_pairs={{0,2},{2,0},{1,3},{3,1},{4,6},{6,4},{5,7},{7,5},{8,10},{10,8},{9,1... | collective-permute-start | bytes 1769480 | tf_op jit(solution)/shard_map/ppermute | solution.py:46
  227.6 111.3 %reduce-scatter.6.cloned.1.call-start = ((), (), s32[]{:S(2)}) async-start(), calls=%async_computation.4 | async-start | bytes 2654208 | tf_op jit(solution)/shard_map/reduce_scatter | solution.py:977
  240.9 9.3 %collective-permute-start.28 = (bf16[384,384]{1,0:T(8,128)(2,1)}, bf16[384,384]{1,0:T(8,128)(2,1)S(1)}, u32[]{:S(2)}, u32[]{:S(2)}) collective-permute-start(bf16[384,384]{1,0:T(8,128)(2,1)} %cross_sum.4), channel_id=1, source_target_pairs={{0,4},{4,0},{1,5},{5,1},{2,6},{6,2},{3,7},{7,3},{8,12},{12,8},{9,1... | collective-permute-start | bytes 884744 | tf_op jit(solution)/shard_map/ppermute | solution.py:50
  250.2 15.7 %collective-permute-start.25 = (bf16[384,768]{1,0:T(8,128)(2,1)S(1)}, bf16[384,768]{1,0:T(8,128)(2,1)S(1)}, u32[]{:S(2)}, u32[]{:S(2)}) collective-permute-start(bf16[384,768]{1,0:T(8,128)(2,1)S(1)} %copy-done.9), channel_id=1, source_target_pairs={{0,2},{2,0},{1,3},{3,1},{4,6},{6,4},{5,7},{7,5},{8,10},{10,8},{9,1... | collective-permute-start | bytes 1769480 | tf_op jit(solution)/shard_map/ppermute | solution.py:46
  253.2 13.6 %collective-permute-start.30 = (bf16[384,384]{1,0:T(8,128)(2,1)}, bf16[384,384]{1,0:T(8,128)(2,1)S(1)}, u32[]{:S(2)}, u32[]{:S(2)}) collective-permute-start(bf16[384,384]{1,0:T(8,128)(2,1)} %cross_sum.5), channel_id=1, source_target_pairs={{0,4},{4,0},{1,5},{5,1},{2,6},{6,2},{3,7},{7,3},{8,12},{12,8},{9,1... | collective-permute-start | bytes 884744 | tf_op jit(solution)/shard_map/ppermute | solution.py:50
  271.3 15.3 %collective-permute-start.31 = (bf16[384,768]{1,0:T(8,128)(2,1)}, bf16[384,768]{1,0:T(8,128)(2,1)S(1)}, u32[]{:S(2)}, u32[]{:S(2)}) collective-permute-start(bf16[384,768]{1,0:T(8,128)(2,1)} %get-tuple-element.217.refs_3_), channel_id=1, source_target_pairs={{0,2},{2,0},{1,3},{3,1},{4,6},{6,4},{5,7},{7,5},{8,10},{10,8},{9,1... | collective-permute-start | bytes 1769480 | tf_op jit(solution)/shard_map/ppermute | solution.py:46
  287.5 107.4 %reduce-scatter.8.cloned.1.call-start = ((), (), s32[]{:S(2)}) async-start(), calls=%async_computation.5 | async-start | bytes 5308416 | tf_op jit(solution)/shard_map/reduce_scatter | solution.py:977
  299.5 14.1 %collective-permute-start.32 = (bf16[192,1536]{1,0:T(8,128)(2,1)S(1)}, bf16[192,1536]{1,0:T(8,128)(2,1)S(1)}, u32[]{:S(2)}, u32[]{:S(2)}) collective-permute-start(bf16[192,1536]{1,0:T(8,128)(2,1)S(1)} %copy-done.6), channel_id=1, source_target_pairs={{0,4},{4,0},{1,5},{5,1},{2,6},{6,2},{3,7},{7,3},{8,12},{12,8},{9,1... | collective-permute-start | bytes 1769480 | tf_op jit(solution)/shard_map/ppermute | solution.py:50
  301.0 14.0 %collective-permute-start.33 = (bf16[384,768]{1,0:T(8,128)(2,1)}, bf16[384,768]{1,0:T(8,128)(2,1)S(1)}, u32[]{:S(2)}, u32[]{:S(2)}) collective-permute-start(bf16[384,768]{1,0:T(8,128)(2,1)} %get-tuple-element.230.refs_3_), channel_id=1, source_target_pairs={{0,2},{2,0},{1,3},{3,1},{4,6},{6,4},{5,7},{7,5},{8,10},{10,8},{9,1... | collective-permute-start | bytes 1769480 | tf_op jit(solution)/shard_map/ppermute | solution.py:46
  333.1 5.0 %collective-permute-start.34 = (bf16[384,768]{1,0:T(8,128)(2,1)S(1)}, bf16[384,768]{1,0:T(8,128)(2,1)S(1)}, u32[]{:S(2)}, u32[]{:S(2)}) collective-permute-start(bf16[384,768]{1,0:T(8,128)(2,1)S(1)} %copy-done.23), channel_id=1, source_target_pairs={{0,1},{1,0},{2,3},{3,2},{4,5},{5,4},{6,7},{7,6},{8,9},{9,8},{10,11... | collective-permute-start | bytes 1769480 | tf_op jit(solution)/shard_map/ppermute | solution.py:42
  336.3 11.7 %collective-permute-start.36 = (bf16[384,384]{1,0:T(8,128)(2,1)}, bf16[384,384]{1,0:T(8,128)(2,1)}, u32[]{:S(2)}, u32[]{:S(2)}) collective-permute-start(bf16[384,384]{1,0:T(8,128)(2,1)} %cross_sum.6), channel_id=1, source_target_pairs={{0,4},{4,0},{1,5},{5,1},{2,6},{6,2},{3,7},{7,3},{8,12},{12,8},{9,1... | collective-permute-start | bytes 884744 | tf_op jit(solution)/shard_map/ppermute | solution.py:50
  351.1 9.3 %collective-permute-start.38 = (bf16[384,384]{1,0:T(8,128)(2,1)}, bf16[384,384]{1,0:T(8,128)(2,1)S(1)}, u32[]{:S(2)}, u32[]{:S(2)}) collective-permute-start(bf16[384,384]{1,0:T(8,128)(2,1)} %cross_sum.7), channel_id=1, source_target_pairs={{0,4},{4,0},{1,5},{5,1},{2,6},{6,2},{3,7},{7,3},{8,12},{12,8},{9,1... | collective-permute-start | bytes 884744 | tf_op jit(solution)/shard_map/ppermute | solution.py:50
  366.1 24.7 %collective-permute-start.40 = (bf16[384,768]{1,0:T(8,128)(2,1)}, bf16[384,768]{1,0:T(8,128)(2,1)S(1)}, u32[]{:S(2)}, u32[]{:S(2)}) collective-permute-start(bf16[384,768]{1,0:T(8,128)(2,1)} %get-tuple-element.258.refs_2_), channel_id=1, source_target_pairs={{0,2},{2,0},{1,3},{3,1},{4,6},{6,4},{5,7},{7,5},{8,10},{10,8},{9,1... | collective-permute-start | bytes 1769480 | tf_op jit(solution)/shard_map/ppermute | solution.py:46
  371.7 11.9 %collective-permute-start.42 = (bf16[96,768]{1,0:T(8,128)(2,1)}, bf16[96,768]{1,0:T(8,128)(2,1)S(1)}, u32[]{:S(2)}, u32[]{:S(2)}) collective-permute-start(bf16[96,768]{1,0:T(8,128)(2,1)} %get-tuple-element.262), channel_id=1, source_target_pairs={{0,8},{8,16},{16,24},{24,0},{1,9},{9,17},{17,25},{25,1},{2,10},{10... | collective-permute-start | bytes 442376 | tf_op jit(solution)/shard_map/ppermute | solution.py:982
  373.9 12.1 %collective-permute-start.43 = (bf16[96,768]{1,0:T(8,128)(2,1)}, bf16[96,768]{1,0:T(8,128)(2,1)S(1)}, u32[]{:S(2)}, u32[]{:S(2)}) collective-permute-start(bf16[96,768]{1,0:T(8,128)(2,1)} %get-tuple-element.263), channel_id=1, source_target_pairs={{0,24},{8,0},{16,8},{24,16},{1,25},{9,1},{17,9},{25,17},{2,26},{10... | collective-permute-start | bytes 442376 | tf_op jit(solution)/shard_map/ppermute | solution.py:982
  376.6 31.7 %collective-permute-start.26 = (bf16[384,768]{1,0:T(8,128)(2,1)}, bf16[384,768]{1,0:T(8,128)(2,1)S(1)}, u32[]{:S(2)}, u32[]{:S(2)}) collective-permute-start(bf16[384,768]{1,0:T(8,128)(2,1)} %finish.1.refs_1_), channel_id=1, source_target_pairs={{0,1},{1,0},{2,3},{3,2},{4,5},{5,4},{6,7},{7,6},{8,9},{9,8},{10,11... | collective-permute-start | bytes 1769480 | tf_op jit(solution)/shard_map/ppermute | solution.py:42
  386.9 13.2 %collective-permute-start.44 = (bf16[192,768]{1,0:T(8,128)(2,1)}, bf16[192,768]{1,0:T(8,128)(2,1)S(1)}, u32[]{:S(2)}, u32[]{:S(2)}) collective-permute-start(bf16[192,768]{1,0:T(8,128)(2,1)} %get-tuple-element.264), channel_id=1, source_target_pairs={{0,8},{8,16},{16,24},{24,0},{1,9},{9,17},{17,25},{25,1},{2,10},{10... | collective-permute-start | bytes 884744 | tf_op jit(solution)/shard_map/ppermute | solution.py:988
  388.4 15.2 %collective-permute-start.45 = (bf16[192,768]{1,0:T(8,128)(2,1)}, bf16[192,768]{1,0:T(8,128)(2,1)S(1)}, u32[]{:S(2)}, u32[]{:S(2)}) collective-permute-start(bf16[192,768]{1,0:T(8,128)(2,1)} %get-tuple-element.265), channel_id=1, source_target_pairs={{0,24},{8,0},{16,8},{24,16},{1,25},{9,1},{17,9},{25,17},{2,26},{10... | collective-permute-start | bytes 884744 | tf_op jit(solution)/shard_map/ppermute | solution.py:988
  393.2 32.3 %collective-permute-start.41 = (bf16[384,768]{1,0:T(8,128)(2,1)}, bf16[384,768]{1,0:T(8,128)(2,1)S(1)}, u32[]{:S(2)}, u32[]{:S(2)}) collective-permute-start(bf16[384,768]{1,0:T(8,128)(2,1)} %get-tuple-element.259.refs_1_), channel_id=1, source_target_pairs={{0,1},{1,0},{2,3},{3,2},{4,5},{5,4},{6,7},{7,6},{8,9},{9,8},{10,11... | collective-permute-start | bytes 1769480 | tf_op jit(solution)/shard_map/ppermute | solution.py:42
  397.0 34.2 %collective-permute-start.54 = (bf16[192,1536]{1,0:T(8,128)(2,1)}, bf16[192,1536]{1,0:T(8,128)(2,1)S(1)}, u32[]{:S(2)}, u32[]{:S(2)}) collective-permute-start(bf16[192,1536]{1,0:T(8,128)(2,1)} %reduce-scatter.8.cloned.1.call-done.refs_0_), channel_id=1, source_target_pairs={{0,4},{4,0},{1,5},{5,1},{2,6},{6,2},{3,7},{7,3},{8,12},{12,8},{9,1... | collective-permute-start | bytes 1769480 | tf_op jit(solution)/shard_map/ppermute | solution.py:50
  400.1 5.8 %collective-permute-start.49 = (f32[24,768]{1,0:T(8,128)}, f32[24,768]{1,0:T(8,128)S(1)}, u32[]{:S(2)}, u32[]{:S(2)}) collective-permute-start(f32[24,768]{1,0:T(8,128)} %pack_small.1.refs_1_), channel_id=1, source_target_pairs={{0,1},{1,0},{2,3},{3,2},{4,5},{5,4},{6,7},{7,6},{8,9},{9,8},{10,11... | collective-permute-start | bytes 221192 | tf_op jit(solution)/shard_map/ppermute | solution.py:42
  403.6 23.6 %collective-permute-start.47 = (bf16[192,768]{1,0:T(8,128)(2,1)}, bf16[192,768]{1,0:T(8,128)(2,1)S(1)}, u32[]{:S(2)}, u32[]{:S(2)}) collective-permute-start(bf16[192,768]{1,0:T(8,128)(2,1)} %reduce-scatter.6.cloned.1.call-done.refs_2_), channel_id=1, source_target_pairs={{0,4},{4,0},{1,5},{5,1},{2,6},{6,2},{3,7},{7,3},{8,12},{12,8},{9,1... | collective-permute-start | bytes 884744 | tf_op jit(solution)/shard_map/ppermute | solution.py:50
  405.9 22.2 %collective-permute-start.46 = (bf16[192,768]{1,0:T(8,128)(2,1)}, bf16[192,768]{1,0:T(8,128)(2,1)S(1)}, u32[]{:S(2)}, u32[]{:S(2)}) collective-permute-start(bf16[192,768]{1,0:T(8,128)(2,1)} %sum_blocks.2.refs_0_), channel_id=1, source_target_pairs={{0,4},{4,0},{1,5},{5,1},{2,6},{6,2},{3,7},{7,3},{8,12},{12,8},{9,1... | collective-permute-start | bytes 884744 | tf_op jit(solution)/shard_map/ppermute | solution.py:50
  408.3 6.0 %collective-permute-start.50 = (bf16[16,768]{1,0:T(8,128)(2,1)}, bf16[16,768]{1,0:T(8,128)(2,1)S(1)}, u32[]{:S(2)}, u32[]{:S(2)}) collective-permute-start(bf16[16,768]{1,0:T(8,128)(2,1)} %get-tuple-element.279), channel_id=1, source_target_pairs={{0,8},{8,16},{16,24},{24,0},{1,9},{9,17},{17,25},{25,1},{2,10},{10... | collective-permute-start | bytes 73736 | tf_op jit(solution)/shard_map/ppermute | solution.py:972
  414.3 4.0 collective-permute-start.51
  418.4 4.9 %collective-permute-start.52 = (bf16[16,768]{1,0:T(8,128)(2,1)}, bf16[16,768]{1,0:T(8,128)(2,1)S(1)}, u32[]{:S(2)}, u32[]{:S(2)}) collective-permute-start(bf16[16,768]{1,0:T(8,128)(2,1)} %get-tuple-element.281), channel_id=1, source_target_pairs={{0,16},{8,24},{16,0},{24,8},{1,17},{9,25},{17,1},{25,9},{2,18},{10... | collective-permute-start | bytes 73736 | tf_op jit(solution)/shard_map/ppermute | solution.py:972
  424.0 4.1 collective-permute-start.53
  (151 other events, 892.0 us)
Sparse Core Ops, SparseCore 0:
  41.9 57.6 all-gather.6
  101.3 30.4 all-gather.8
  133.4 50.8 all-gather.10
  227.8 57.5 reduce-scatter.3
  287.5 38.1 reduce-scatter.5
  327.8 58.1 reduce-scatter.7

commit v3 on v2

v3 whole, which is shorter than its diff:
```python
import math

import jax
import jax.numpy as jnp
from jax import lax
from jax.experimental import pallas as pl
from jax.experimental.pallas import tpu as pltpu
from jax.sharding import Mesh
from jax.sharding import PartitionSpec as P

f32 = jnp.float32
bf16 = jnp.bfloat16
EPSILON = 1e-05
NN = (((1,), (0,)), ((), ()))
NT = (((1,), (1,)), ((), ()))
TN = (((0,), (0,)), ((), ()))
VMEM_MIB = {
    "attend_far": 13,
    "attend_near": 10,
    "attend_back": 14,
    "feed": 16,
    "feed_back": 16,
    "feed_grads": 12,
    "own_grads": 9,
    "feed_out": 7.6,
    "finish": 6,
    "input_back": 10,
    "middle_back": 11,
    "pack_first": 6,
    "pair_grads": 9,
    "project": 9.5,
    "project_back": 9.5,
    "project_grads": 13,
    "project_out": 5,
}
WIDE = 128
TAIL = 16
COST = 500_000_000


def mm(a, b, dims=NN):
    return lax.dot_general(a, b, dims, preferred_element_type=f32)


def core_swap(x):
    return lax.ppermute(x, "tc", [(0, 1), (1, 0)])


def x_swap(x):
    return lax.ppermute(x, "tx", [(0, 1), (1, 0)])


def y_swap(x):
    return lax.ppermute(x, "ctx", [(0, 1), (1, 0)])


def after(x, *others):
    return lax.optimization_barrier((x,) + others)[0]


def ring(shift):
    return [(i, (i + shift) % 4) for i in range(4)]


def ring_scalars(shards):
    me = lax.axis_index("shard").astype(jnp.int32)
    zero = jnp.int32(0)
    order = [me, (me + shards - 1) % shards, (me + 1) % shards, (me + 2) % shards]
    return jnp.stack([zero] * 8 + [lax.axis_index("tc").astype(jnp.int32)] + order + [zero] * 3)


class Pieces:
    def __init__(self, x, tail=0):
        self.rows = x.shape[0] - tail
        self.mine = [x] + [lax.ppermute(x, "shard", ring(s)) for s in (1, 3, 2)]
        self.arrays = self.mine + [core_swap(p) for p in self.mine]

    def copies(self, scal, refs, columns, dest, sems):
        out = []
        for k, ref in enumerate(refs):
            slot = scal[8] if k < 4 else 1 - scal[8]
            to = dest.at[slot, scal[9 + k % 4]]
            out.append(pltpu.make_async_copy(ref.at[pl.ds(0, self.rows), columns], to, sems.at[k]))
        return out

    def tails(self, scal, refs, dest, sems):
        out = []
        for k, ref in enumerate(refs):
            slot = scal[8] if k < 4 else 1 - scal[8]
            to = dest.at[slot, scal[9 + k % 4]]
            out.append(pltpu.make_async_copy(ref.at[pl.ds(self.rows, TAIL), :], to, sems.at[k]))
        return out


class Gathered:
    def __init__(self, x, shards, tail=0):
        self.rows = x.shape[0] - tail
        whole = lax.all_gather(x, ("shard", "tc"), axis=0, tiled=False)
        self.arrays = [whole.reshape((shards, 2) + x.shape)]

    def copies(self, scal, refs, columns, dest, sems):
        ref = refs[0]
        return [
            pltpu.make_async_copy(ref.at[:, c, pl.ds(0, self.rows), columns], dest.at[c], sems.at[c])
            for c in range(2)
        ]

    def tails(self, scal, refs, dest, sems):
        ref = refs[0]
        return [
            pltpu.make_async_copy(ref.at[:, c, pl.ds(self.rows, TAIL), :], dest.at[c], sems.at[c])
            for c in range(2)
        ]


def vmem():
    return pl.BlockSpec(memory_space=pltpu.VMEM)


class Far:
    def __init__(self, array):
        self.array = array


class Reading:
    def __init__(self, buffer, copy):
        self.buffer, self.copy, self.waited = buffer, copy, False

    def need(self):
        if not self.waited:
            self.copy.wait()
            self.waited = True
        return self.buffer

    def __getitem__(self, index):
        return self.need()[index]

    @property
    def shape(self):
        return self.buffer.shape


class Writing:
    def __init__(self, buffer, copy):
        self.buffer, self.copy, self.sent = buffer, copy, False

    def __setitem__(self, index, value):
        self.buffer[index] = value

    @property
    def at(self):
        return self.buffer.at

    def send(self):
        if not self.sent:
            self.copy.start()
            self.sent = True


def send(*refs):
    for r in refs:
        if isinstance(r, Writing):
            r.send()


def need(*refs):
    for r in refs:
        if isinstance(r, Reading):
            r.need()


FAR = "far"


def run(kernel, ins, outs, scratch=(), w=None, scalars=None, name=None, us=1.0):
    pieces = [] if w is None else w.arrays
    n_in, n_out, n_pieces = len(ins), len(outs), len(pieces)
    far_in = [i for i, a in enumerate(ins) if isinstance(a, Far)]
    far_out = [i for i, o in enumerate(outs) if len(o) == 3]
    any_space = pl.BlockSpec(memory_space=pl.ANY)
    specs, args = [], []
    if scalars is not None:
        specs.append(pl.BlockSpec(memory_space=pltpu.SMEM))
        args.append(scalars)
    for a in ins:
        if isinstance(a, Far):
            specs.append(any_space)
            args.append(pltpu.with_memory_space_constraint(a.array, pltpu.HBM))
        else:
            specs.append(vmem())
            args.append(a)
    for p in pieces:
        specs.append(any_space)
        args.append(pltpu.with_memory_space_constraint(p, pltpu.HBM))
    first = len(args) - n_in - n_pieces
    shapes = [
        pltpu.HBM(o[0], o[1]) if len(o) == 3 else jax.ShapeDtypeStruct(o[0], o[1]) for o in outs
    ]
    buffers = [pltpu.VMEM(ins[i].array.shape, ins[i].array.dtype) for i in far_in]
    buffers += [pltpu.VMEM(outs[i][0], outs[i][1]) for i in far_out]
    sems = [pltpu.SemaphoreType.DMA((len(buffers),))] if buffers else []

    def wrapped(*refs):
        refs = list(refs)
        n_all = len(args) + n_out + len(scratch)
        own, extra = refs[:n_all], refs[n_all:]
        reads, writes = [], []
        for k, i in enumerate(far_in):
            copy = pltpu.make_async_copy(own[first + i], extra[k], extra[-1].at[k])
            copy.start()
            own[first + i] = Reading(extra[k], copy)
            reads.append(own[first + i])
        for k, i in enumerate(far_out):
            k += len(far_in)
            at = len(args) + i
            own[at] = Writing(extra[k], pltpu.make_async_copy(extra[k], own[at], extra[-1].at[k]))
            writes.append(own[at])
        kernel(*own)
        for w in writes:
            w.send()
        for r in reads:
            r.need()
        for w in writes:
            w.copy.wait()

    return pl.pallas_call(
        wrapped,
        out_shape=shapes,
        in_specs=specs,
        out_specs=[any_space if len(o) == 3 else vmem() for o in outs],
        scratch_shapes=list(scratch) + buffers + sems,
        compiler_params=pltpu.CompilerParams(vmem_limit_bytes=int(VMEM_MIB.get(name, 4) * 1024 * 1024)),
        cost_estimate=pl.CostEstimate(flops=int(us * COST), bytes_accessed=1000, transcendentals=0),
        name=name,
    )(*args)


def spread(shard, shards, units):
    part = 64 // shards
    bits, low = part.bit_length() - 1, part - 1
    i = lax.broadcasted_iota(jnp.int32, (units // shards, units), 0)
    j = lax.broadcasted_iota(jnp.int32, (units // shards, units), 1)
    same = ((j >> 6) == (i >> bits)) & ((j & 63) == shard * part + (i & low))
    return jnp.where(same, 1.0, 0.0).astype(bf16)


def start_all(copies):
    for c in copies:
        c.start()


def wait_all(copies):
    for c in copies:
        c.wait()


def ln_parts(x):
    centred = x - jnp.mean(x, -1, keepdims=True)
    inv = lax.rsqrt(jnp.mean(centred * centred, -1, keepdims=True) + EPSILON)
    return centred * inv, inv


def ln_back(x, gain, dn):
    hat, inv = ln_parts(x)
    dhat = dn * gain
    dx = inv * (
        dhat
        - jnp.mean(dhat, -1, keepdims=True)
        - hat * jnp.mean(dhat * hat, -1, keepdims=True)
    )
    return dx, jnp.sum(dn * hat, 0, keepdims=True), jnp.sum(dn, 0, keepdims=True)


def split3(v):
    a = v.astype(bf16)
    r = v - a.astype(f32)
    b = r.astype(bf16)
    c = (r - b.astype(f32)).astype(bf16)
    return a, b, c


def beside(wide, column):
    a, b, c = split3(column)
    rows, size = wide.shape[0], wide.shape[1]
    return jnp.concatenate([wide, a, b, c, jnp.zeros((rows, WIDE - size - 3), bf16)], 1)


class Sizes:
    def __init__(self, mesh, frames, w_qkv, w_up):
        self.shards = mesh.shape["shard"]
        self.layers = w_qkv.shape[0]
        self.width = frames.shape[-1]
        self.rows = frames.shape[1] // 2
        self.heads = w_qkv.shape[2]
        self.hd = w_qkv.shape[3] // 3
        self.att = self.heads * self.hd
        self.hidden = w_up.shape[2]
        self.m = w_qkv.shape[1]
        self.a_cols = 4 * self.att
        self.b_cols = 2 * self.hidden


def make(z):
    R, D, A, H, HD, F = z.rows, z.width, z.att, z.heads, z.hd, z.hidden
    L, S, M = z.layers, z.shards, z.m
    coef = HD ** (-0.5) / math.log(2.0)
    scale = HD ** (-0.5)
    dma = pltpu.SemaphoreType.DMA
    q_at, u_at = M, M + 2 * A // S

    def weight_scratch(columns):
        return [pltpu.VMEM((2, S, M, columns), bf16), dma((8,))]

    def weight(w_s, c, start, stop):
        return w_s[c, :, :, start:stop].reshape(D, stop - start)

    def pack_first(w_qkv, w_out, qv_bias, up_bias, norm_gains, shifts):
        nq, nu = 2 * HD // S, 64 // S

        def kernel(w_r, o_r, qv_r, up_r, g_r, s_r, out):
            for side in range(3):
                cuts = [w_r[h][:, side * HD : (side + 1) * HD] for h in range(H)]
                out[:M, side * A : (side + 1) * A] = jnp.concatenate(cuts, 1)
            out[:M, 3 * A :] = o_r[...].astype(f32).T.astype(bf16)
            vecs = []
            for l in range(L):
                vecs += [g_r[l].astype(f32), s_r[l].astype(f32)]
            vecs = jnp.concatenate(vecs + [jnp.zeros((TAIL - 6 * L, M), f32)], 0)
            rows = []
            for l in range(L):
                q, u = qv_r[l].astype(f32), up_r[l].astype(f32)
                cuts = [q[h : h + 1, :] for h in range(H)] + [u[r : r + 1, :] for r in range(F // 64)]
                rows.append(jnp.concatenate(cuts, 1))
            rows = jnp.concatenate(rows + [jnp.zeros((TAIL - L, H * nq + F // 64 * nu), f32)], 0)
            rest = jnp.zeros((TAIL, z.a_cols - M - rows.shape[1]), f32)
            out[M:, :] = jnp.concatenate([vecs, rows, rest], 1).astype(bf16)

        return run(
            kernel,
            [w_qkv.transpose(1, 0, 2), w_out, qv_bias, up_bias, norm_gains, shifts],
            [((M + TAIL, z.a_cols), bf16, FAR)],
            name="pack_first",
        )[0]

    def proj(scal, x, layer, w, biases=None, prev=None):
        first = biases is None
        n = len(w.arrays)
        part = 2 * HD // S

        def kernel(*refs):
            it = iter(refs)
            scal_r, x_r = next(it), next(it)
            if not first:
                vec_r, qb_r, pa_r, pb_r = (next(it) for _ in range(4))
            piece_r = [next(it) for _ in range(n)]
            n_o, q_o, kv_o = (next(it) for _ in range(3))
            if first:
                vec_r, qb_r, tail_o = (next(it) for _ in range(3))
            else:
                x_o = next(it)
            w_s, sems = next(it), next(it)
            if first:
                tail_sems = next(it)
                tails = w.tails(scal_r, piece_r, tail_o, tail_sems)
                start_all(tails)
            copies = w.copies(scal_r, piece_r, pl.ds(0, z.a_cols), w_s, sems)
            start_all(copies)
            xv = x_r[...].astype(f32)
            if not first:
                at = 6 * (layer - 1) + 5
                xv = xv + (pa_r[...].astype(f32) + pb_r[...].astype(f32) + vec_r[at : at + 1, :])
                x_o[...] = xv
                send(x_o)
            hat, _ = ln_parts(xv)
            if first:
                wait_all(tails)
                vec_r[...] = jnp.concatenate([tail_o[0, t][:, :M] for t in range(S)], 1).astype(f32)
                for l in range(L):
                    for p in range(2):
                        rows = [tail_o[p, t].astype(f32)[l : l + 1, q_at:u_at] for t in range(S)]
                        seq = []
                        for side in range(2):
                            for h in range(H):
                                seq += [
                                    rows[t][:, h * part : (h + 1) * part]
                                    for t in range(side * S // 2, (side + 1) * S // 2)
                                ]
                            if side == 0:
                                seq.append(jnp.zeros((1, A), f32))
                        qb_r[2 * l + p : 2 * l + p + 1, :] = jnp.concatenate(seq, 1)
            g = 6 * layer
            nv = (hat * vec_r[g : g + 1, :] + vec_r[g + 2 : g + 3, :]).astype(bf16)
            n_o[...] = nv
            send(n_o)
            wait_all(copies)
            both = []
            for e in range(2):
                b = 2 * layer + e
                p = (mm(nv, weight(w_s, e, 0, 3 * A)) + qb_r[b : b + 1, :]).astype(bf16)
                kv_o[:, e * 2 * A : (e + 1) * 2 * A] = p[:, A:]
                both.append(p[:, :A])
            send(kv_o)
            q_o[...] = jnp.concatenate(both, 1)

        ins = [Far(x)] + ([] if first else list(biases) + [Far(p) for p in prev])
        outs = [((R, D), bf16, FAR), ((R, 2 * A), bf16), ((R, 4 * A), bf16, FAR)]
        scratch = weight_scratch(z.a_cols)
        if first:
            outs += [((TAIL, D), f32), ((2 * L, 3 * A), f32), ((2, S, TAIL, z.a_cols), bf16)]
            scratch += [dma((8,))]
        else:
            outs += [((R, D), f32, FAR)]
        return run(kernel, ins, outs, scratch, w, scal, "project", 3.5)

    def aug(block, offset, fill):
        return jnp.concatenate([block[:, offset : offset + HD], fill], 1)

    def head_lanes(j):
        e, h = divmod(j, H)
        return j * HD, e * 2 * A + h * HD, e * 2 * A + A + h * HD

    def load_heads(kv_refs, k_s, v_s):
        ones = jnp.ones((R, HD), bf16)
        for b, ref in enumerate(kv_refs):
            blk = ref[...]
            for j in range(2 * H):
                _, k_at, v_at = head_lanes(j)
                k_s[j, b * R : (b + 1) * R, :] = aug(blk, k_at, ones)
                v_s[j, b * R : (b + 1) * R, :] = aug(blk, v_at, ones)

    def attend_near(q, kvs):
        K = 2 * R

        def kernel(q_r, kv0, kv1, acc_o, q_s, k_s, v_s):
            zeros = jnp.zeros((R, HD), bf16)
            for j in range(2 * H):
                q_s[j] = aug(q_r[...], j * HD, zeros)
            load_heads((kv0, kv1), k_s, v_s)

            def head(j, carry):
                s = mm(q_s[j], k_s[j], NT)
                top = jnp.max(s, -1, keepdims=True)
                oe = mm(jnp.exp2((s - top) * coef).astype(bf16), v_s[j])
                acc_o[j] = jnp.concatenate(
                    [oe[:, : HD + 1], top, jnp.zeros((R, WIDE - HD - 2), f32)], 1
                )
                return carry

            lax.fori_loop(0, 2 * H, head, 0)

        return run(
            kernel,
            [q] + list(kvs),
            [((2 * H, R, WIDE), f32)],
            [pltpu.VMEM((2 * H, R, WIDE), bf16)] + [pltpu.VMEM((2 * H, K, WIDE), bf16)] * 2,
            name="attend_near",
            us=6,
        )[0]

    def attend_far(scal, q, kvs, acc, w):
        K = 2 * R
        n = len(w.arrays)

        def kernel(scal_r, q_r, kv2, kv3, acc_r, *refs):
            piece_r = refs[:n]
            o0_o, o1_o, qa_o, own_o, snd_o, part_o, q_s, k_s, v_s, o_s, w_s, sems = refs[n:]
            copies = w.copies(scal_r, piece_r, pl.ds(z.a_cols - 256, 256), w_s, sems)
            start_all(copies)
            zeros = jnp.zeros((R, HD), bf16)
            for j in range(2 * H):
                q_s[j] = aug(q_r[...], j * HD, zeros)
            load_heads((kv2, kv3), k_s, v_s)

            def head(j, carry):
                s = mm(q_s[j], k_s[j], NT)
                old = acc_r[j]
                old_top = old[:, HD + 1 : HD + 2]
                top = jnp.maximum(jnp.max(s, -1, keepdims=True), old_top)
                oe = mm(jnp.exp2((s - top) * coef).astype(bf16), v_s[j])
                oe = oe + old * jnp.exp2((old_top - top) * coef)
                total = oe[:, HD : HD + 1]
                o_s[j] = (oe[:, :HD] / total).astype(bf16)
                lse = top + jnp.log2(total) * (1.0 / coef)
                qa_o.buffer[j] = beside(q_s[j][:, :HD], -lse)
                return carry

            lax.fori_loop(0, 2 * H, head, 0)
            send(qa_o)
            o0 = jnp.concatenate([o_s[j] for j in range(H)], 1)
            o1 = jnp.concatenate([o_s[H + j] for j in range(H)], 1)
            wait_all(copies)
            part = mm(o0, weight(w_s, 0, 256 - A, 256), NT) + mm(o1, weight(w_s, 1, 256 - A, 256), NT)
            part_o[...] = part.astype(bf16)
            send(part_o)
            odd = scal_r[8] == 1
            o0_o[...] = o0
            o1_o[...] = o1
            own_o[...] = jnp.where(odd, o1, o0)
            snd_o[...] = jnp.where(odd, o0, o1)

        return run(
            kernel,
            [q] + list(kvs) + [acc],
            [((R, A), bf16, FAR)] * 2
            + [((2 * H, R, WIDE), bf16, FAR)]
            + [((R, A), bf16, FAR)] * 2
            + [((R, D), bf16, FAR)],
            [pltpu.VMEM((2 * H, R, WIDE), bf16)]
            + [pltpu.VMEM((2 * H, K, WIDE), bf16)] * 2
            + [pltpu.VMEM((2 * H, R, HD), bf16)]
            + weight_scratch(256),
            w,
            scal,
            "attend_far",
            8,
        )

    def feed(scal, x, pa, pb, vec, tails, layer, w):
        n = len(w.arrays)
        g = 6 * layer

        def kernel(scal_r, x_r, pa_r, pb_r, vec_r, tail_r, *refs):
            piece_r = refs[:n]
            y_o, n_o, *hid_gp, part_o, w_s, sems = refs[n:]
            copies = w.copies(scal_r, piece_r, pl.ds(0, 2 * F), w_s, sems)
            start_all(copies)
            y = x_r[...].astype(f32) + (
                pa_r[...].astype(f32) + pb_r[...].astype(f32) + vec_r[g + 3 : g + 4, :]
            )
            y_o[...] = y
            send(y_o)
            hat, _ = ln_parts(y)
            nv = (hat * vec_r[g + 1 : g + 2, :] + vec_r[g + 4 : g + 5, :]).astype(bf16)
            n_o[...] = nv
            send(n_o)
            bias = [None, None]
            for t in range(S):
                e = spread(t, S, F)
                for s in range(2):
                    add = mm(tail_r[s, t][:, u_at : u_at + F // S], e)
                    bias[s] = add if t == 0 else bias[s] + add
            part, hiddens = None, []
            for s in range(2):
                copies[s].wait()
                u = mm(nv, weight(w_s, s, 0, F)) + bias[s][layer : layer + 1, :]
                cdf = 0.5 * (1.0 + lax.erf(u * (0.5**0.5)))
                pdf = jnp.exp(-0.5 * u * u) * (1.0 / math.sqrt(2.0 * math.pi))
                hidden = (u * cdf).astype(bf16)
                hid_gp[2 + s][...] = (cdf + u * pdf).astype(bf16)
                send(hid_gp[2 + s])
                hiddens.append(hidden)
                t = mm(hidden, weight(w_s, s, F, 2 * F), NT)
                part = t if part is None else part + t
            part_o[...] = part.astype(bf16)
            send(part_o)
            odd = scal_r[8] == 1
            hid_gp[0][...] = jnp.where(odd, hiddens[1], hiddens[0])
            hid_gp[1][...] = jnp.where(odd, hiddens[0], hiddens[1])

        outs = [
            ((R, D), f32, FAR),
            ((R, D), bf16, FAR),
            ((R, F), bf16, FAR),
            ((R, F), bf16, FAR),
            ((R, F), bf16, FAR),
            ((R, F), bf16, FAR),
            ((R, D), bf16, FAR),
        ]
        return run(
            kernel, [Far(x), Far(pa), Far(pb), vec, tails], outs, weight_scratch(2 * F), w, scal, "feed", 6
        )

    def finish(y, pa, pb, vec):
        at = 6 * (L - 1) + 5

        def kernel(y_r, pa_r, pb_r, vec_r, o):
            v = y_r[...] + (pa_r[...].astype(f32) + pb_r[...].astype(f32) + vec_r[at : at + 1, :])
            o[...] = v.astype(bf16)

        return run(kernel, [Far(y), Far(pa), Far(pb), vec], [((R, D), bf16, FAR)], name="finish")

    def feed_back(scal, grad, gp, layer, w, before=None):
        n = len(w.arrays)
        up = 6 * (layer + 1)

        def kernel(*refs):
            it = iter(refs)
            scal_r = next(it)
            if before is None:
                g_r = next(it)
            else:
                x_r, dy_r, pa_r, pb_r, vec_r = (next(it) for _ in range(5))
            gp_r = (next(it), next(it))
            piece_r = [next(it) for _ in range(n)]
            swap_o, du_o, part_o, sums_o = (next(it) for _ in range(4))
            if before is not None:
                g_o, pre_o = next(it), next(it)
            w_s, sems = next(it), next(it)
            copies = w.copies(scal_r, piece_r, pl.ds(0, 2 * F), w_s, sems)
            start_all(copies)
            if before is None:
                g = g_r[...].astype(f32)
            else:
                dn = pa_r[...].astype(f32) + pb_r[...].astype(f32)
                dx, dgain, dshift = ln_back(x_r[...], vec_r[up : up + 1, :], dn)
                g = dy_r[...] + dx
                g_o[...] = g
                pre_o[0:1, :] = dgain
                pre_o[1:2, :] = dshift
            g2 = g.astype(bf16)
            swap_o[:, :D] = g2
            sums_o[...] = jnp.sum(g2.astype(f32), 0, keepdims=True)
            part, dus = None, []
            for s in range(2):
                copies[s].wait()
                dh = mm(g2, weight(w_s, s, F, 2 * F))
                du = (gp_r[s][...].astype(f32) * dh).astype(bf16)
                dus.append(du)
                t = mm(du, weight(w_s, s, 0, F), NT)
                part = t if part is None else part + t
            part_o[...] = part.astype(bf16)
            send(part_o)
            odd = scal_r[8] == 1
            du_o[...] = jnp.where(odd, dus[1], dus[0])
            swap_o[:, D:] = jnp.where(odd, dus[0], dus[1])

        ins = [grad] if before is None else [Far(b) for b in before[:4]] + [before[4]]
        ins += [Far(gp[0]), Far(gp[1])]
        outs = [((R, D + F), bf16, FAR), ((R, F), bf16), ((R, D), bf16, FAR), ((1, D), f32)]
        if before is not None:
            outs += [((R, D), f32), ((2, D), f32)]
        return run(kernel, ins, outs, weight_scratch(2 * F), w, scal, "feed_back", 6)

    def blocks_out(scal_r, full, outs):
        if S == 4:
            for o, at in zip(outs, (9, 11, 10, 12)):
                o[...] = full[scal_r[at]]
        else:
            outs[0][...] = full[...]

    def block_shapes(rows, columns):
        return [((rows, columns), bf16, FAR)] * 4 if S == 4 else [((S, rows, columns), bf16, FAR)]

    def feed_grads(scal, n2, n2_r, hid, hid_r, swap, swap_r, du):
        def kernel(scal_r, n_r, nr_r, h_r, hr_r, s_r, sr_r, du_r, g_o, b_o):
            other = sr_r[:, D:]
            g_o[:, :F] = (mm(n_r[...], du_r[...], TN) + mm(nr_r[...], other, TN)).astype(bf16)
            g_o[:, F:] = (mm(s_r[:, :D], h_r[...], TN) + mm(sr_r[:, :D], hr_r[...], TN)).astype(bf16)
            total = jnp.sum(du_r[...].astype(f32), 0, keepdims=True) + jnp.sum(
                other.astype(f32), 0, keepdims=True
            )
            odd = scal_r[8] == 1
            b_o[0:1, :] = jnp.where(odd, 0.0, total)
            b_o[1:2, :] = jnp.where(odd, total, 0.0)

        return run(
            kernel,
            [Far(n2), Far(n2_r), Far(hid), Far(hid_r), Far(swap), Far(swap_r), du],
            [((D, 2 * F), bf16, FAR), ((2, F), f32)],
            scalars=scal,
            name="feed_grads",
            us=3,
        )

    def middle_back(scal, y, g, pa, pb, vec, o0, o1, layer, w):
        n = len(w.arrays)
        gain = 6 * layer + 1

        def kernel(scal_r, y_r, g_r, pa_r, pb_r, vec_r, o0_r, o1_r, *refs):
            piece_r = refs[:n]
            dy_o, g1_o, d_o, sums_o, w_s, sems = refs[n:]
            copies = w.copies(scal_r, piece_r, pl.ds(z.a_cols - 256, 256), w_s, sems)
            start_all(copies)
            dn = pa_r[...].astype(f32) + pb_r[...].astype(f32)
            dx, dgain, dshift = ln_back(y_r[...], vec_r[gain : gain + 1, :], dn)
            dy = g_r[...].astype(f32) + dx
            dy_o[...] = dy
            send(dy_o)
            g1 = dy.astype(bf16)
            g1_o[...] = g1
            send(g1_o)
            sums_o[0:1, :] = dgain
            sums_o[1:2, :] = jnp.sum(g1.astype(f32), 0, keepdims=True)
            sums_o[2:3, :] = dshift
            wait_all(copies)
            for e, o_r in enumerate((o0_r, o1_r)):
                do = mm(g1, weight(w_s, e, 256 - A, 256)).astype(bf16)
                prod = do.astype(f32) * o_r[...].astype(f32)
                for h in range(H):
                    lanes = slice(h * HD, (h + 1) * HD)
                    d_o[e * H + h] = beside(do[:, lanes], -jnp.sum(prod[:, lanes], -1, keepdims=True))

        outs = [((R, D), f32, FAR), ((R, D), bf16, FAR), ((2 * H, R, WIDE), bf16), ((3, D), f32)]
        return run(
            kernel,
            [Far(y), g, Far(pa), Far(pb), vec, Far(o0), Far(o1)],
            outs,
            weight_scratch(256),
            w,
            scal,
            "middle_back",
            4,
        )

    def attend_back(qa, kvs, da, before=None):
        K = 2 * R

        def kernel(qa_r, kv0, kv1, da_r, *refs):
            refs = list(refs)
            if before is not None:
                old_r = refs.pop(0)
            dq_o, e0, e1, k_s, v_s, dk_s, dv_s, *dq_s = refs
            need(qa_r)
            load_heads((kv0, kv1), k_s, v_s)

            def head(j, carry):
                qv = qa_r[j]
                dv_in = da_r[j]
                dqt = None
                for b in range(2):
                    at = slice(b * R, (b + 1) * R)
                    kb = k_s[j, at, :]
                    p = jnp.exp2(mm(kb, qv, NT) * coef)
                    ds = (p * mm(v_s[j, at, :], dv_in, NT)).astype(bf16)
                    dv_s[j, at, :] = mm(p.astype(bf16), dv_in).astype(bf16)
                    dk_s[j, at, :] = (mm(ds, qv) * scale).astype(bf16)
                    t = mm(kb, ds, TN)
                    dqt = t if dqt is None else dqt + t
                if before is None:
                    dq_o[j] = dqt
                else:
                    dq_s[0][j] = ((dqt + old_r[j]).T * scale).astype(bf16)
                return carry

            lax.fori_loop(0, 2 * H, head, 0)
            for b, e_o in ((1, e1), (0, e0)):
                at = slice(b * R, (b + 1) * R)
                cols = []
                for e in range(2):
                    cols += [dk_s[e * H + h, at, :HD] for h in range(H)]
                    cols += [dv_s[e * H + h, at, :HD] for h in range(H)]
                e_o[...] = jnp.concatenate(cols, 1)
                send(e_o)
            if before is not None:
                dq_o[...] = jnp.concatenate([dq_s[0][j][:, :HD] for j in range(2 * H)], 1)

        ins = [Far(qa)] + [Far(a) for a in kvs] + [da]
        outs = [((R, 4 * A), bf16), ((R, 4 * A), bf16, FAR)]
        scratch = [pltpu.VMEM((2 * H, K, WIDE), bf16)] * 4
        if before is None:
            outs = [((2 * H, WIDE, R), f32)] + outs
        else:
            ins.append(before)
            outs = [((R, 2 * A), bf16)] + outs
            scratch.append(pltpu.VMEM((2 * H, R, WIDE), bf16))
        return run(kernel, ins, outs, scratch, name="attend_back", us=8)

    def cross_sum(own, theirs):
        def kernel(a, b, o):
            o[...] = (a[...].astype(f32) + b[...].astype(f32)).astype(bf16)

        return run(kernel, [own, theirs], [(own.shape, bf16, FAR)], name="cross_sum")[0]

    def proj_back(scal, dq, kv_parts, layer, w, x=None):
        n = len(w.arrays)

        def kernel(scal_r, q_r, a, p, c, *refs):
            refs = list(refs)
            if x is not None:
                x_r = refs.pop(0)
            piece_r, refs = refs[:n], refs[n:]
            own_o, snd_o, part_o, b_o = refs[:4]
            w_s, sems = refs[-2:]
            copies = w.copies(scal_r, piece_r, pl.ds(0, z.a_cols), w_s, sems)
            start_all(copies)
            both = []
            for e in range(2):
                at = slice(e * 2 * A, (e + 1) * 2 * A)
                total = a[:, at].astype(f32) + p[:, at].astype(f32) + c[:, at].astype(f32)
                both.append(jnp.concatenate([q_r[:, e * A : (e + 1) * A], total.astype(bf16)], 1))
                b_o[e : e + 1, :] = jnp.sum(both[e].astype(f32), 0, keepdims=True)
            odd = scal_r[8] == 1
            own_o[...] = jnp.where(odd, both[1], both[0])
            snd_o[...] = jnp.where(odd, both[0], both[1])
            send(snd_o)
            if x is not None:
                hat, _ = ln_parts(x_r[...].astype(f32))
            wait_all(copies)
            part = mm(both[0], weight(w_s, 0, 0, 3 * A), NT) + mm(both[1], weight(w_s, 1, 0, 3 * A), NT)
            part_o[...] = part.astype(bf16)
            if x is not None:
                send(part_o)
                refs[4][0:1, :] = jnp.sum(part * hat, 0, keepdims=True)
                refs[4][1:2, :] = jnp.sum(part, 0, keepdims=True)

        ins = [dq] + list(kv_parts)
        outs = [((R, 3 * A), bf16), ((R, 3 * A), bf16, FAR), ((R, D), bf16, FAR), ((2, 3 * A), f32)]
        if x is not None:
            ins.append(Far(x))
            outs.append(((2, D), f32))
        return run(kernel, ins, outs, weight_scratch(z.a_cols), w, scal, "project_back", 4)

    def proj_grads(scal, n1, n1_r, dp, dp_r, g1, g1_r, o, o_r, small):
        flat = [a for row in small for a in row]
        half = M // 2

        def kernel(scal_r, n_r, nr_r, p_r, pr_r, g_r, gr_r, o_i, or_i, *refs):
            parts, outs, all_s = refs[: len(flat)], refs[len(flat) : -1], refs[-1]
            first = mm(n_r[...], p_r[...], TN) + mm(nr_r[...], pr_r[...], TN)
            second = mm(g_r[...], o_i[...], TN) + mm(gr_r[...], or_i[...], TN)
            both = jnp.concatenate([first.astype(bf16), second.astype(bf16)], 1)
            all_s[:, :M, :] = both.reshape(S, M, z.a_cols)
            wide, units, heads = [], [], []
            for l in range(L):
                pre, mid, last, up, qv = (r[...] for r in parts[5 * l : 5 * l + 5])
                wide += [pre[0:1], mid[0:1], pre[1:2], mid[1:3], last]
                units.append(up)
                heads.append(qv)
            wide = jnp.concatenate(wide + [jnp.zeros((TAIL - 6 * L, D), f32)], 0)
            pad = TAIL - 2 * L
            units = jnp.concatenate(units + [jnp.zeros((pad, F), f32)], 0).astype(bf16)
            heads = jnp.concatenate(heads + [jnp.zeros((pad, 3 * A), f32)], 0)
            part = 2 * HD // S
            for t in range(S):
                side, place = divmod(t, S // 2)
                cuts = []
                for h in range(H):
                    at = side * 2 * A + h * HD + place * part
                    cuts.append(heads[:, at : at + part])
                up = mm(units, spread(t, S, F), NT)
                rest = jnp.zeros((TAIL, z.a_cols - u_at - F // S), f32)
                all_s[t, M:, :] = jnp.concatenate(
                    [wide[:, t * M : (t + 1) * M]] + cuts + [up, rest], 1
                ).astype(bf16)
            if S == 4:
                outs[3][...] = all_s[scal_r[12], :half, :]
                outs[4][...] = all_s[scal_r[12], half:, :]
                send(outs[3], outs[4])
                for o_, at in zip(outs[:3], (9, 11, 10)):
                    o_[...] = all_s[scal_r[at]]
            else:
                outs[0][...] = all_s[...]

        block = (M + TAIL, z.a_cols)
        outs = [((S,) + block, bf16, FAR)]
        if S == 4:
            outs = [(block, bf16, FAR)] * 3
            outs += [((half, z.a_cols), bf16, FAR), ((M + TAIL - half, z.a_cols), bf16, FAR)]
        return run(
            kernel,
            [Far(n1), Far(n1_r), dp, Far(dp_r), Far(g1), Far(g1_r), Far(o), Far(o_r)] + [Far(a) for a in flat],
            outs,
            [pltpu.VMEM((S,) + block, bf16)],
            scalars=scal,
            name="project_grads",
            us=3,
        )

    def own_grads(n1, n1_r, dp, dp_r, g1, g1_r, o, o_r):
        def kernel(n_r, nr_r, p_r, pr_r, g_r, gr_r, o_i, or_i, out):
            first = mm(n_r[...], p_r[...], TN) + mm(nr_r[...], pr_r[...], TN)
            second = mm(g_r[...], o_i[...], TN) + mm(gr_r[...], or_i[...], TN)
            both = jnp.concatenate([first.astype(bf16), second.astype(bf16)], 1)
            out[...] = both.reshape(S, M, z.a_cols)

        return run(
            kernel,
            [Far(n1), Far(n1_r), dp, Far(dp_r), Far(g1), Far(g1_r), Far(o), Far(o_r)],
            [((S, M, z.a_cols), bf16, FAR)],
            name="own_grads",
            us=3,
        )[0]

    def pass_on(up, down, low, high):
        half = M // 2

        def kernel(up_r, down_r, low_r, high_r, up_o, down_o):
            up_o[:half, :] = (up_r[:half, :].astype(f32) + low_r[...].astype(f32)).astype(bf16)
            up_o[half:, :] = up_r[half:, :]
            send(up_o)
            down_o[:half, :] = down_r[:half, :]
            down_o[half:, :] = (down_r[half:, :].astype(f32) + high_r[...].astype(f32)).astype(bf16)

        return run(
            kernel,
            [Far(up), Far(down), Far(low), Far(high)],
            [((M + TAIL, z.a_cols), bf16, FAR)] * 2,
            name="pass_on",
        )

    def join_rows(scal, mine, theirs):
        def kernel(scal_r, a, b, o):
            start = pl.multiple_of(scal_r[8] * R, 16)
            o[pl.ds(start, R), :] = a[...]
            o[pl.ds(pl.multiple_of(R - start, 16), R), :] = b[...]

        return run(kernel, [Far(mine), Far(theirs)], [((2 * R, D), bf16, FAR)], scalars=scal, name="join_rows")[0]

    def sum_blocks(own, others):
        def kernel(own_r, a_r, b_r, o):
            o[...] = (own_r[...].astype(f32) + a_r[...].astype(f32) + b_r[...].astype(f32)).astype(bf16)

        return run(
            kernel,
            [Far(a) for a in [own] + others],
            [((M + TAIL, z.a_cols), bf16, FAR)],
            name="sum_blocks",
        )[0]

    def feed_out(pairs):
        def kernel(*refs):
            up_o, down_o = refs[-2:]
            for l in range(L):
                total = refs[2 * l][...].astype(f32) + refs[2 * l + 1][...].astype(f32)
                up_o[l] = total[:, :F]
                down_o[l] = total[:, F:]

        return run(
            kernel,
            [Far(a) for p in pairs for a in p],
            [((L, M, F), f32, FAR), ((L, M, F), f32, FAR)],
            name="feed_out",
        )

    def proj_out(pairs):
        def kernel(*refs):
            qkv_o, out_o = refs[-2:]
            for l in range(L):
                total = refs[2 * l][...].astype(f32) + refs[2 * l + 1][...].astype(f32)
                if l == 0:
                    total = total[:M]
                for h in range(H):
                    cuts = [total[:, i * A + h * HD : i * A + (h + 1) * HD] for i in range(3)]
                    qkv_o[l, h] = jnp.concatenate(cuts, 1)
                out_o[l] = total[:, 3 * A :].T
        return run(
            kernel,
            [Far(a) for p in pairs for a in p],
            [((L, H, M, 3 * HD), f32, FAR), ((L, A, M), f32, FAR)],
            name="project_out",
        )

    def small_sum(mine, theirs):
        def kernel(a_r, b_r, o):
            o[...] = a_r[M:, :].astype(f32) + b_r[M:, :].astype(f32)

        return run(kernel, [Far(mine), Far(theirs)], [((TAIL, z.a_cols), f32, FAR)], name="small_sum")[0]

    def small_out(scal, mine, x_side, core_side, far_side):
        def kernel(scal_r, a_r, x_r, c_r, f_r, qvb_o, upb_o, gain_o, shift_o):
            both = a_r[...] + c_r[...]
            other = x_r[...] + f_r[...]
            odd = scal_r[8] == 1
            part, unit = 2 * HD // S, 64 // S
            for l in range(L):
                rows = both[6 * l : 6 * l + 6, :M]
                first, third = rows[0:1], rows[2:3]
                if l == 0:
                    first, third = first + other[0:1, :M], third + other[2:3, :M]
                gain_o[l] = jnp.concatenate([first, rows[1:2]], 0)
                shift_o[l] = jnp.concatenate([third, rows[3:6]], 0)
                bias = jnp.where(odd, both[2 * l + 1 : 2 * l + 2], both[2 * l : 2 * l + 1])
                for h in range(H):
                    qvb_o[h, l : l + 1, :] = bias[:, q_at + h * part : q_at + (h + 1) * part]
                for r in range(F // 64):
                    upb_o[r, l : l + 1, :] = bias[:, u_at + r * unit : u_at + (r + 1) * unit]

        return run(
            kernel,
            [Far(mine), Far(x_side), Far(core_side), Far(far_side)],
            [
                ((H, L, 2 * HD // S), f32),
                ((F // 64, L, 64 // S), f32),
                ((L, 2, M), f32),
                ((L, 4, M), f32),
            ],
            scalars=scal,
            name="small_out",
        )

    def input_back(x, dy, pa, pb, vec):
        def kernel(x_r, dy_r, pa_r, pb_r, vec_r, o, sums_o):
            dn = pa_r[...].astype(f32) + pb_r[...].astype(f32)
            dx, dgain, dshift = ln_back(x_r[...].astype(f32), vec_r[0:1, :], dn)
            o[...] = (dy_r[...] + dx).astype(bf16)
            sums_o[0:1, :] = dgain
            sums_o[1:2, :] = dshift

        return run(kernel, [Far(x), Far(dy), Far(pa), Far(pb), vec], [((R, D), bf16, FAR), ((2, D), f32)], name="input_back")

    return dict(locals())


def local(mesh):
    def fn(frames, cotangent, w_qkv, qv_bias, w_out, w_up, up_bias, w_down, norm_gains, shifts):
        z = Sizes(mesh, frames, w_qkv, w_up)
        assert frames.shape[0] == 1
        k = make(z)
        L, m, R, D, A, F, H, HD, S = z.layers, z.m, z.rows, z.width, z.att, z.hidden, z.heads, z.hd, z.shards
        core = lax.axis_index("tc")
        scal = ring_scalars(S)

        def part_a(l, *then):
            qkv = after(w_qkv[l], *then).reshape(m, H, 3, HD).transpose(0, 2, 1, 3).reshape(m, 3 * A)
            return jnp.concatenate([qkv, after(w_out[l], *then).reshape(A, m).T], -1)

        def part_b(l, *then):
            return jnp.concatenate([after(w_up[l], *then), after(w_down[l], *then).T], -1)

        message = k["pack_first"](
            w_qkv[0], w_out[0].reshape(A, m), qv_bias, up_bias, norm_gains, shifts
        )
        w_a = [Pieces(message, TAIL) if S == 4 else Gathered(message, S, TAIL)]
        w_b = [Gathered(after(part_b(0, message), *w_a[0].arrays[1:4]), S)]

        def my_rows(x):
            return lax.dynamic_slice_in_dim(x.reshape(2 * R, D), core * R, R, 0)

        kept = []
        x = my_rows(frames)
        for layer in range(L):
            if layer == 0:
                n1, q, kv, vec, qb, tails = k["proj"](scal, x, 0, w_a[0])
            else:
                n1, q, kv, x = k["proj"](scal, after(y, *hid[1:]), layer, w_a[layer], (vec, qb), (part, x_swap(part)))
            far = y_swap(kv)
            near = core_swap(kv)
            if layer + 1 < L:
                next_a, next_b = part_a(layer + 1, n1), part_b(layer + 1, n1)
            acc = k["attend_near"](q, (kv, near))
            kvs = (kv, near, far, core_swap(after(far, acc)))
            o0, o1, qa, o_own, o_snd, att_part = k["attend_far"](scal, q, kvs[2:], acc, w_a[layer])
            far = x_swap(att_part)
            n1_r, o_rcv = core_swap(n1), core_swap(o_snd)
            x = after(x, n1_r, o_rcv)
            if layer + 1 < L:
                w_a.append(Gathered(after(next_a, kvs[1]), S))
                w_b.append(Gathered(after(next_b, att_part), S))
            y, n2, *hid_gp, part = k["feed"](
                scal, x, att_part, far, vec, tails, layer, w_b[layer]
            )
            n2_r, hid_r, gp = core_swap(n2), core_swap(hid_gp[1]), hid_gp[2:]
            hid = (hid_gp[0], hid_r, n2_r)
            kept.append((x, n1, n1_r, kvs, qa, (o0, o1), o_own, o_rcv, y, n2, hid, gp))

        def whole_rows(mine):
            return k["join_rows"](scal, mine, core_swap(mine))[None]

        def scatter(grad):
            return lax.psum_scatter(grad.reshape(D, -1), "shard", scatter_dimension=0, tiled=True)

        y_last, part_last = y, part
        g = my_rows(cotangent)
        wide, d_qv, d_up = [None] * L, [None] * L, [None] * L
        sum_a, sum_b = [None] * L, [None] * L
        before = None
        for layer in reversed(range(L)):
            x, n1, n1_r, kvs, qa, os, o_own, o_rcv, y, n2, hid, gp = kept[layer]
            if before is None:
                swap_b, du, part, sum_g2 = k["feed_back"](scal, g, gp, layer, w_b[layer])
            else:
                gp = [after(gp[0], grad_a), gp[1]]
                swap_b, du, part, sum_g2, g, pre = k["feed_back"](scal, None, gp, layer, w_b[layer], before)
                wide[layer + 1] = [pre] + wide[layer + 1]
            far = x_swap(part)
            grad_b, d_up[layer] = k["feed_grads"](
                scal, n2, hid[2], hid[0], hid[1], swap_b, core_swap(swap_b), du
            )
            y = after(y, grad_b)
            if before is not None:
                sum_b[layer + 1] = (part_b_sum, y_swap(after(part_b_sum, part)))
                y = after(y, sum_b[layer + 1][1])
            if layer > 0:
                part_b_sum = scatter(after(grad_b, far))
            dy, g1, da, mid = k["middle_back"](
                scal, y, g, part, far, vec, os[0], os[1], layer, w_a[layer]
            )
            if layer == 0:
                part_b_sum = scatter(after(grad_b, da))
            g1_r = core_swap(g1)
            dqt, own, snd = k["attend_back"](qa, kvs[2:], da)
            cross = k["cross_sum"](own, core_swap(snd))
            dqt = after(dqt, cross, g1_r, *([part_a_sum] if layer == 0 else []))
            cross = y_swap(cross)
            dq, own, snd = k["attend_back"](qa, kvs[:2], da, dqt)
            snd = after(snd, cross)
            kv_parts = (own, core_swap(snd), cross)
            dp, dp_snd, part, d_qv[layer], *pre = k["proj_back"](
                scal, dq, kv_parts, layer, w_a[layer], *([x] if layer == 0 else [])
            )
            far = x_swap(part)
            swaps = (n1, n1_r, dp, core_swap(dp_snd), g1, g1_r, o_own, o_rcv)
            if layer > 0:
                grad_a = k["own_grads"](*swaps)
                part_a_sum = scatter(after(grad_a, far))
            else:
                sum_a[1] = (part_a_sum, y_swap(after(part_a_sum, part)))
                wide[0] = pre + [mid, sum_g2]
                small = [wide[l] + [d_up[l], d_qv[l]] for l in range(L)]
                blocks = k["proj_grads"](scal, *swaps, small)
            wide[layer] = pre + [mid, sum_g2]
            before = (x, dy, part, far, vec)
        grad_rows, _ = k["input_back"](x, after(dy, blocks[0]), part, far, vec)
        if S == 4:
            hops = [lax.ppermute(b, "shard", ring(s)) for b, s in zip(blocks[3:], (1, 3))]
            up, down = k["pass_on"](after(blocks[1], grad_rows, sum_a[1][1]), blocks[2], *hops)
            ready = up
            others = [lax.ppermute(up, "shard", ring(1)), lax.ppermute(down, "shard", ring(3))]
        else:
            ready = blocks[0]
        part_b_sum = after(part_b_sum, ready)
        sum_b[0] = (part_b_sum, y_swap(part_b_sum))
        far_last = x_swap(after(part_last, ready))
        frames_grad = whole_rows(grad_rows)
        block = after(blocks[0], sum_b[0][1], frames_grad)
        if S == 4:
            mine = k["sum_blocks"](block, others)
        else:
            mine = lax.psum_scatter(block, "shard", scatter_dimension=0, tiled=True)[0]
        theirs = y_swap(mine)
        sum_a[0] = (mine, theirs)
        out_frames = whole_rows(k["finish"](y_last, part_last, after(far_last, mine), vec)[0])
        outs_up, outs_down = k["feed_out"]([sum_b[0], (after(sum_b[1][0], mine), sum_b[1][1])])
        tiny = k["small_sum"](after(mine, outs_up, out_frames), theirs)
        tiny_x = x_swap(tiny)
        tiny_c, tiny_f = core_swap(tiny), core_swap(tiny_x)
        outs_qkv, outs_out = k["proj_out"]([(after(mine, tiny), theirs), sum_a[1]])
        g_qvb, g_upb, g_gains, g_shifts = k["small_out"](
            scal, after(tiny, outs_qkv), tiny_x, tiny_c, tiny_f
        )
        return (
            out_frames,
            frames_grad,
            outs_qkv.transpose(0, 2, 1, 3),
            g_qvb.transpose(1, 0, 2),
            outs_out.reshape(L, H, HD, m),
            outs_up,
            g_upb.transpose(1, 0, 2),
            outs_down.transpose(0, 2, 1),
            g_gains,
            g_shifts,
        )

    return fn


def solution(mesh):
    assert mesh.axis_names == ("shard", "ctx", "tp") and mesh.shape["tp"] == 4 and mesh.shape["ctx"] == 2
    split = Mesh(mesh.devices.reshape(mesh.shape["shard"], 2, 2, 2), ("shard", "ctx", "tx", "tc"))
    tp = ("tx", "tc")
    specs = (
        P("shard", "ctx", None),
        P("shard", "ctx", None),
        P(None, "shard", tp, None),
        P(None, tp, "shard"),
        P(None, tp, None, "shard"),
        P(None, "shard", tp),
        P(None, tp, "shard"),
        P(None, tp, "shard"),
        P(None, None, "shard"),
        P(None, None, "shard"),
    )
    return jax.shard_map(local(split), mesh=split, in_specs=specs, out_specs=specs, check_vma=False)
```

time: 447 us -> 424 us (0.949)
  Pallas kernels: 152 us -> 187 us
  local copies, waits for them, and re-layouts: 50 us -> 26.5 us
  waiting for transfers between devices: 167 us -> 148 us
  starting transfers between devices: 50 us -> 38.2 us
    pallas_call x37 -> x35, Pallas kernels: 152 us -> 187 us  [run(): pl.pallas_call(wrapped, out_shape=shapes, in_specs=specs, out_specs=[any_...]
    ppermute x7 -> x4, waiting for transfers between devices: 24.8 us -> 3.46 us  [the longest x1 3.45 us: fn(): lax.ppermute(up, 'shard', ring(1))]
    unnamed x280 -> x151, local copies, waits for them, and re-layouts: 43.6 us -> 22.5 us
    ppermute x9, waiting for transfers between devices: 46 us -> 30.5 us  [x_swap(): return lax.ppermute(x, 'tx', [(0, 1), (1, 0)])]
    ppermute x23 -> x30, waiting for transfers between devices: 12.5 us -> 22.3 us  [core_swap(): return lax.ppermute(x, 'tc', [(0, 1), (1, 0)])]
    all_gather x3, waiting for transfers between devices: 26.3 us -> 34.3 us  [__init__(): whole = lax.all_gather(x, ('shard', 'tc'), axis=0, tiled=False)]
    ppermute x13 -> x8, starting transfers between devices: 17 us -> 9.39 us  [y_swap(): return lax.ppermute(x, 'ctx', [(0, 1), (1, 0)])]
    ppermute x7 -> x4, starting transfers between devices: 8.92 us -> 4.1 us  [the longest x2 2.08 us: fn(): lax.ppermute(b, 'shard', ring(s))]
  transfers between devices with their start and end apart: 61 -> 60, of which waited for: 36 -> 39; matrix products, arithmetic and copies ran while one was open for 1% -> 1% of each run, Pallas kernels for 30% -> 39%
where the time goes in v3:
time: 424 us; the launch traced here: 418 us
  Pallas kernels  187 us (44%)
  waiting for transfers between devices  148 us (35%)
  starting transfers between devices  38.2 us (9%)
  local copies, waits for them, and re-layouts  26.5 us (6%)
  between operations  15.6 us (4%)
    pallas_call x35, Pallas kernels, run(): pl.pallas_call(wrapped, out_shape=shapes, in_specs=specs, out_specs=[any_...  187 us
    ppermute x8, waiting for transfers between devices, y_swap(): return lax.ppermute(x, 'ctx', [(0, 1), (1, 0)])  37.7 us
    all_gather x3, waiting for transfers between devices, __init__(): whole = lax.all_gather(x, ('shard', 'tc'), axis=0, tiled=False)  34.3 us
    ppermute x9, waiting for transfers between devices, x_swap(): return lax.ppermute(x, 'tx', [(0, 1), (1, 0)])  30.5 us
    unnamed x151, local copies, waits for them, and re-layouts  22.5 us
    ppermute x30, waiting for transfers between devices, core_swap(): return lax.ppermute(x, 'tc', [(0, 1), (1, 0)])  22.3 us
    ppermute x3, waiting for transfers between devices, __init__(): self.mine = [x] + [lax.ppermute(x, 'shard', ring(s)) for s in (1, 3, 2)]  19.8 us
    ppermute x9, starting transfers between devices, x_swap(): return lax.ppermute(x, 'tx', [(0, 1), (1, 0)])  12.5 us
  transfers between devices with their start and end apart: 60, of which 39 were waited for; matrix products, arithmetic and copies ran while one was open for 1% of the time, Pallas kernels for 39%

profile of v3, /device:TPU:0, one launch (start us, length us, event | category | flops | bytes accessed | tf_op | source)
XLA Modules:
  0.0 417.5 jit_solution(4107225635637060574)
XLA Ops:
  12.0 4.1 collective-permute-start.2
  19.1 13.4 %collective-permute-done.2.refs_5_.refs_8_.refs_11_.refs_9_ = bf16[208,768]{1,0:T(8,128)(2,1)} collective-permute-done((bf16[208,768]{1,0:T(8,128)(2,1)}, bf16[208,768]{1,0:T(8,128)(2,1)}, u32[]{:S(2)}, u32[]{:S(2)}) %collective-permute-start.2) | collective-permute-done | bytes 319520 | tf_op jit(solution)/shard_map/ppermute | solution.py:75
  32.5 6.3 %collective-permute-done.refs_3_.refs_6_.refs_9_.refs_7_ = bf16[208,768]{1,0:T(8,128)(2,1)} collective-permute-done((bf16[208,768]{1,0:T(8,128)(2,1)}, bf16[208,768]{1,0:T(8,128)(2,1)}, u32[]{:S(2)}, u32[]{:S(2)}) %collective-permute-start) | collective-permute-done | bytes 319520 | tf_op jit(solution)/shard_map/ppermute | solution.py:75
  42.3 5.2 %project.2 = (bf16[384,768]{1,0:T(8,128)(2,1)}, bf16[384,384]{1,0:T(8,128)(2,1)S(1)}, bf16[384,768]{1,0:T(8,128)(2,1)}, f32[16,768]{1,0:T(8,128)S(1)}, f32[4,576...) custom-call(s32[16]{0:T(128)S(1)} %stack.23.refs_0_, ...), custom_call_target="tpu_custom_call" | custom-call | flops 1750000000 | bytes 1000 | tf_op jit(solution)/shard_map/project/pallas_call | solution.py:226
  52.4 5.7 %attend_near.2.refs_4_ = f32[6,384,128]{2,1,0:T(8,128)S(1)} custom-call(bf16[384,384]{1,0:T(8,128)(2,1)S(1)} %get-tuple-element.143.refs_0_.refs_1_, bf16[384,768]{1,0:T(8,128)(2,1)S(1)} %copy-done.2, bf16[384,768]{1,0:T(8,128)(2,1)S(1)} %collective-permute-done.9.refs_2_), custom_call_target="tpu_custom_call" | custom-call | flops 3000000000 | bytes 1000 | tf_op jit(solution)/shard_map/attend_near/pallas_call | solution.py:226
  59.1 7.1 %collective-permute-done.8.refs_2_.refs_1_ = bf16[384,768]{1,0:T(8,128)(2,1)S(1)} collective-permute-done((bf16[384,768]{1,0:T(8,128)(2,1)S(1)}, bf16[384,768]{1,0:T(8,128)(2,1)S(1)}, u32[]{:S(2)}, u32[]{:S(2)}) %collective-permute-start.8) | collective-permute-done | bytes 589856 | tf_op jit(solution)/shard_map/ppermute | solution.py:54
  69.6 10.7 %attend_far.2 = (bf16[384,192]{1,0:T(8,128)(2,1)}, bf16[384,192]{1,0:T(8,128)(2,1)}, bf16[6,384,128]{2,1,0:T(8,128)(2,1)}, bf16[384,192]{1,0:T(8,128)(2,1)}, bf1...) custom-call(s32[16]{0:T(128)S(1)} %stack.23.refs_0_, bf16[384,384]{1,0:T(8,128)(2,1)S(1)} %get-tuple-element.143.refs_0_.refs_1_, ...), custom_call_target="tpu_custom_call" | custom-call | flops 4000000000 | bytes 1000 | tf_op jit(solution)/shard_map/attend_far/pallas_call | solution.py:226
  83.9 12.7 %collective-permute-done.12.refs_3_ = bf16[384,768]{1,0:T(8,128)(2,1)S(1)} collective-permute-done((bf16[384,768]{1,0:T(8,128)(2,1)}, bf16[384,768]{1,0:T(8,128)(2,1)S(1)}, u32[]{:S(2)}, u32[]{:S(2)}) %collective-permute-start.12) | collective-permute-done | bytes 589856 | tf_op jit(solution)/shard_map/ppermute | solution.py:50
  97.4 8.0 %feed.2 = (f32[384,768]{1,0:T(8,128)}, bf16[384,768]{1,0:T(8,128)(2,1)}, bf16[384,768]{1,0:T(8,128)(2,1)}, bf16[384,768]{1,0:T(8,128)(2,1)}, bf16[384,768]{1,0:T...) custom-call(s32[16]{0:T(128)S(1)} %stack.23.refs_0_, ...), custom_call_target="tpu_custom_call" | custom-call | flops 3000000000 | bytes 1000 | tf_op jit(solution)/shard_map/feed/pallas_call | solution.py:226
  108.6 20.2 %all-gather.9.cloned.1.call-done = bf16[1536,768]{1,0:T(8,128)(2,1)} async-done(((bf16[192,768]{1,0:T(8,128)(2,1)}), bf16[1536,768]{1,0:T(8,128)(2,1)}) %all-gather.9.cloned.1.call-update) | async-done | bytes 2359312 | tf_op jit(solution)/shard_map/all_gather | solution.py:98
  129.6 5.1 %project.3 = (bf16[384,768]{1,0:T(8,128)(2,1)}, bf16[384,384]{1,0:T(8,128)(2,1)S(1)}, bf16[384,768]{1,0:T(8,128)(2,1)}, f32[384,768]{1,0:T(8,128)}) custom-call(s32[16]{0:T(128)S(1)} %stack.23.refs_0_, f32[384,768]{1,0:T(8,128)} %get-tuple-element.216.refs_1_, f32[16,768]{1,0:T(8,128)S(1)} %get-tuple-element.149.refs_4_.refs_2_.refs_5_.refs_3_, ...), custom_call_target="tpu_custom_call" | custom-call | flops 1750000000 | bytes 1000 | tf_op jit(solution)/shard_map/project/pallas_call | solution.py:226
  138.3 5.7 %attend_near.3.refs_4_ = f32[6,384,128]{2,1,0:T(8,128)S(1)} custom-call(bf16[384,384]{1,0:T(8,128)(2,1)S(1)} %get-tuple-element.165.refs_0_.refs_1_, bf16[384,768]{1,0:T(8,128)(2,1)S(1)} %copy-done.6, bf16[384,768]{1,0:T(8,128)(2,1)S(1)} %collective-permute-done.18.refs_2_), custom_call_target="tpu_custom_call" | custom-call | flops 3000000000 | bytes 1000 | tf_op jit(solution)/shard_map/attend_near/pallas_call | solution.py:226
  144.1 6.7 %collective-permute-done.17.refs_2_.refs_1_ = bf16[384,768]{1,0:T(8,128)(2,1)S(1)} collective-permute-done((bf16[384,768]{1,0:T(8,128)(2,1)}, bf16[384,768]{1,0:T(8,128)(2,1)S(1)}, u32[]{:S(2)}, u32[]{:S(2)}) %collective-permute-start.17) | collective-permute-done | bytes 589856 | tf_op jit(solution)/shard_map/ppermute | solution.py:54
  152.9 11.1 %attend_far.3 = (bf16[384,192]{1,0:T(8,128)(2,1)}, bf16[384,192]{1,0:T(8,128)(2,1)}, bf16[6,384,128]{2,1,0:T(8,128)(2,1)}, bf16[384,192]{1,0:T(8,128)(2,1)}, bf1...) custom-call(s32[16]{0:T(128)S(1)} %stack.23.refs_0_, bf16[384,384]{1,0:T(8,128)(2,1)S(1)} %get-tuple-element.165.refs_0_.refs_1_, ...), custom_call_target="tpu_custom_call" | custom-call | flops 4000000000 | bytes 1000 | tf_op jit(solution)/shard_map/attend_far/pallas_call | solution.py:226
  167.2 14.1 %all-gather.11.cloned.1.call-done = bf16[1536,1536]{1,0:T(8,128)(2,1)} async-done(((bf16[192,1536]{1,0:T(8,128)(2,1)}), bf16[1536,1536]{1,0:T(8,128)(2,1)}) %all-gather.11.cloned.1.call-update) | async-done | bytes 4718608 | tf_op jit(solution)/shard_map/all_gather | solution.py:98
  182.1 8.3 %feed.3 = (f32[384,768]{1,0:T(8,128)}, bf16[384,768]{1,0:T(8,128)(2,1)}, bf16[384,768]{1,0:T(8,128)(2,1)}, bf16[384,768]{1,0:T(8,128)(2,1)}, bf16[384,768]{1,0:T...) custom-call(s32[16]{0:T(128)S(1)} %stack.23.refs_0_, f32[384,768]{1,0:T(8,128)} %get-tuple-element.169.refs_1_, ...), custom_call_target="tpu_custom_call" | custom-call | flops 3000000000 | bytes 1000 | tf_op jit(solution)/shard_map/feed/pallas_call | solution.py:226
  190.4 7.1 %feed_back.2 = (bf16[384,1536]{1,0:T(8,128)(2,1)}, bf16[384,768]{1,0:T(8,128)(2,1)S(1)}, bf16[384,768]{1,0:T(8,128)(2,1)}, f32[1,768]{1,0:T(1,128)S(1)}) custom-call(s32[16]{0:T(128)S(1)} %stack.23.refs_0_, bf16[384,768]{1,0:T(8,128)(2,1)S(1)} %dynamic-slice_bitcast_fusion.refs_1_.refs_2_, bf16[384,768]{1,0:T(8,128)(2,1)} %get-tuple-element.181.refs_2_, ...), custom_call_target="tpu_custom_call" | custom-call | flops 3000000000 | bytes 1000 | tf_op jit(solution)/shard_map/feed_back/pallas_call | solution.py:226
  203.4 8.4 %feed_grads.2 = (bf16[768,1536]{1,0:T(8,128)(2,1)}, f32[2,768]{1,0:T(2,128)S(1)}) custom-call(s32[16]{0:T(128)S(1)} %stack.23.refs_0_, bf16[384,768]{1,0:T(8,128)(2,1)} %get-tuple-element.178.refs_1_, bf16[384,768]{1,0:T(8,128)(2,1)} %copy-done.54, bf16[384,768]{1,0:T(8,128)(2,1)} %get-tuple-element.179.refs_3_, bf16[384,768]{1,0:T(8,128)(2,1)} %copy-done.53, ...), custom_call_target="tpu_custom_call" | custom-call | flops 1500000000 | bytes 1000 | tf_op jit(solution)/shard_map/feed_grads/pallas_call | solution.py:226
  211.9 2.3 collective-permute-done.25.refs_4_
  215.1 4.9 %middle_back.2 = (f32[384,768]{1,0:T(8,128)}, bf16[384,768]{1,0:T(8,128)(2,1)}, bf16[6,384,128]{2,1,0:T(8,128)(2,1)S(1)}, f32[3,768]{1,0:T(4,128)S(1)}) custom-call(s32[16]{0:T(128)S(1)} %stack.23.refs_0_, f32[384,768]{1,0:T(8,128)} %get-tuple-element.186.refs_1_.refs_0_, bf16[384,768]{1,0:T(8,128)(2,1)S(1)} %dynamic-slice_bitcast_fusion.refs_1_.refs_2_, ...), custom_call_target="tpu_custom_call" | custom-call | flops 2000000000 | bytes 1000 | tf_op jit(solution)/shard_map/middle_back/pallas_call | solution.py:226
  220.0 8.3 %attend_back.4 = (f32[6,128,384]{2,1,0:T(8,128)S(1)}, bf16[384,768]{1,0:T(8,128)(2,1)S(1)}, bf16[384,768]{1,0:T(8,128)(2,1)}) custom-call(bf16[6,384,128]{2,1,0:T(8,128)(2,1)} %get-tuple-element.191.refs_0_, bf16[384,768]{1,0:T(8,128)(2,1)} %copy-done.8, bf16[384,768]{1,0:T(8,128)(2,1)} %copy-done.9, bf16[6,384,128]{2,1,0:T(8,128)(2,1)S(1)} %get-tuple-element.192.refs_3_), custom_call_target="tpu_custom_call" | custom-call | flops 4000000000 | bytes 1000 | tf_op jit(solution)/shard_map/attend_back/pallas_call | solution.py:226
  233.1 9.1 %attend_back.5 = (bf16[384,384]{1,0:T(8,128)(2,1)S(1)}, bf16[384,768]{1,0:T(8,128)(2,1)S(1)}, bf16[384,768]{1,0:T(8,128)(2,1)}) custom-call(bf16[6,384,128]{2,1,0:T(8,128)(2,1)} %get-tuple-element.191.refs_0_, bf16[384,768]{1,0:T(8,128)(2,1)} %get-tuple-element.166.refs_1_, bf16[384,768]{1,0:T(8,128)(2,1)} %copy-done.7, ...), custom_call_target="tpu_custom_call" | custom-call | flops 4000000000 | bytes 1000 | tf_op jit(solution)/shard_map/attend_back/pallas_call | solution.py:226
  242.3 4.9 %collective-permute-done.28.refs_4_ = bf16[384,768]{1,0:T(8,128)(2,1)S(1)} collective-permute-done((bf16[384,768]{1,0:T(8,128)(2,1)}, bf16[384,768]{1,0:T(8,128)(2,1)S(1)}, u32[]{:S(2)}, u32[]{:S(2)}) %collective-permute-start.28) | collective-permute-done | bytes 589856 | tf_op jit(solution)/shard_map/ppermute | solution.py:54
  247.2 2.2 collective-permute-done.29.refs_3_
  249.4 4.4 %project_back.2 = (bf16[384,576]{1,0:T(8,128)(2,1)S(1)}, bf16[384,576]{1,0:T(8,128)(2,1)}, bf16[384,768]{1,0:T(8,128)(2,1)}, f32[2,576]{1,0:T(2,128)S(1)}) custom-call(s32[16]{0:T(128)S(1)} %stack.23.refs_0_, bf16[384,384]{1,0:T(8,128)(2,1)S(1)} %get-tuple-element.198.refs_1_, bf16[384,768]{1,0:T(8,128)(2,1)S(1)} %get-tuple-element.199.refs_2_, ...), custom_call_target="tpu_custom_call" | custom-call | flops 2000000000 | bytes 1000 | tf_op jit(solution)/shard_map/project_back/pallas_call | solution.py:226
  258.2 5.0 %own_grads.1 = bf16[4,192,768]{2,1,0:T(8,128)(2,1)} custom-call(bf16[384,768]{1,0:T(8,128)(2,1)} %get-tuple-element.164.refs_0_, bf16[384,768]{1,0:T(8,128)(2,1)} %copy-done.42, bf16[384,576]{1,0:T(8,128)(2,1)S(1)} %get-tuple-element.204.refs_2_, bf16[384,576]{1,0:T(8,128)(2,1)} %copy-done.57, bf16[384,768]{1,0:T(8,128)(2,1)} %get-tuple-element.196.refs_4_, ...), custom_call_target="tpu_custom_call" | custom-call | flops 1500000000 | bytes 1000 | tf_op jit(solution)/shard_map/own_grads/pallas_call | solution.py:226
  263.2 6.3 %collective-permute-done.30.refs_4_ = bf16[384,768]{1,0:T(8,128)(2,1)S(1)} collective-permute-done((bf16[384,768]{1,0:T(8,128)(2,1)}, bf16[384,768]{1,0:T(8,128)(2,1)S(1)}, u32[]{:S(2)}, u32[]{:S(2)}) %collective-permute-start.30) | collective-permute-done | bytes 589856 | tf_op jit(solution)/shard_map/ppermute | solution.py:50
  270.3 8.3 %feed_back.3 = (bf16[384,1536]{1,0:T(8,128)(2,1)}, bf16[384,768]{1,0:T(8,128)(2,1)S(1)}, bf16[384,768]{1,0:T(8,128)(2,1)}, f32[1,768]{1,0:T(1,128)S(1)}, f32[384,768]{1,0:T(8,128)S(1)}, /*index=5*/f32[2,768]{1,0:T(2,128)S(1)}) custom-call(s32[16]{0:T(128)S(1)} %stack.23.refs_0_, f32[384,768]{1,0:T(8,128)} %get-tuple-element.169.refs_1_, ...), custom_call_target="tpu_custom_call" | custom-call | flops 3000000000 | bytes 1000 | tf_op jit(solution)/shard_map/feed_back/pallas_call | solution.py:226
  282.4 8.4 %feed_grads.3 = (bf16[768,1536]{1,0:T(8,128)(2,1)}, f32[2,768]{1,0:T(2,128)S(1)}) custom-call(s32[16]{0:T(128)S(1)} %stack.23.refs_0_, bf16[384,768]{1,0:T(8,128)(2,1)} %get-tuple-element.156.refs_1_, bf16[384,768]{1,0:T(8,128)(2,1)} %copy-done.40, bf16[384,768]{1,0:T(8,128)(2,1)} %get-tuple-element.177.refs_3_, bf16[384,768]{1,0:T(8,128)(2,1)} %copy-done.39, ...), custom_call_target="tpu_custom_call" | custom-call | flops 1500000000 | bytes 1000 | tf_op jit(solution)/shard_map/feed_grads/pallas_call | solution.py:226
  290.8 4.3 %collective-permute-done.33.refs_3_ = bf16[192,1536]{1,0:T(8,128)(2,1)S(1)} collective-permute-done((bf16[192,1536]{1,0:T(8,128)(2,1)}, bf16[192,1536]{1,0:T(8,128)(2,1)S(1)}, u32[]{:S(2)}, u32[]{:S(2)}) %collective-permute-start.33) | collective-permute-done | bytes 589856 | tf_op jit(solution)/shard_map/ppermute | solution.py:54
  297.1 5.1 %middle_back.3 = (f32[384,768]{1,0:T(8,128)}, bf16[384,768]{1,0:T(8,128)(2,1)}, bf16[6,384,128]{2,1,0:T(8,128)(2,1)S(1)}, f32[3,768]{1,0:T(4,128)S(1)}) custom-call(s32[16]{0:T(128)S(1)} %stack.23.refs_0_, f32[384,768]{1,0:T(8,128)} %get-tuple-element.216.refs_1_, f32[384,768]{1,0:T(8,128)S(1)} %get-tuple-element.217.refs_2_, ...), custom_call_target="tpu_custom_call" | custom-call | flops 2000000000 | bytes 1000 | tf_op jit(solution)/shard_map/middle_back/pallas_call | solution.py:226
  302.8 8.6 %attend_back.6 = (f32[6,128,384]{2,1,0:T(8,128)S(1)}, bf16[384,768]{1,0:T(8,128)(2,1)S(1)}, bf16[384,768]{1,0:T(8,128)(2,1)}) custom-call(bf16[6,384,128]{2,1,0:T(8,128)(2,1)} %get-tuple-element.176.refs_0_, bf16[384,768]{1,0:T(8,128)(2,1)} %copy-done.4, bf16[384,768]{1,0:T(8,128)(2,1)} %copy-done.5, bf16[6,384,128]{2,1,0:T(8,128)(2,1)S(1)} %get-tuple-element.220.refs_3_), custom_call_target="tpu_custom_call" | custom-call | flops 4000000000 | bytes 1000 | tf_op jit(solution)/shard_map/attend_back/pallas_call | solution.py:226
  316.6 9.0 %attend_back.7 = (bf16[384,384]{1,0:T(8,128)(2,1)S(1)}, bf16[384,768]{1,0:T(8,128)(2,1)S(1)}, bf16[384,768]{1,0:T(8,128)(2,1)}) custom-call(bf16[6,384,128]{2,1,0:T(8,128)(2,1)} %get-tuple-element.176.refs_0_, bf16[384,768]{1,0:T(8,128)(2,1)} %get-tuple-element.144.refs_1_, bf16[384,768]{1,0:T(8,128)(2,1)} %copy-done.3, ...), custom_call_target="tpu_custom_call" | custom-call | flops 4000000000 | bytes 1000 | tf_op jit(solution)/shard_map/attend_back/pallas_call | solution.py:226
  325.6 4.7 %collective-permute-done.37.refs_4_ = bf16[384,768]{1,0:T(8,128)(2,1)S(1)} collective-permute-done((bf16[384,768]{1,0:T(8,128)(2,1)}, bf16[384,768]{1,0:T(8,128)(2,1)S(1)}, u32[]{:S(2)}, u32[]{:S(2)}) %collective-permute-start.37) | collective-permute-done | bytes 589856 | tf_op jit(solution)/shard_map/ppermute | solution.py:54
  330.3 2.2 collective-permute-done.38.refs_3_
  332.5 4.8 %project_back.3 = (bf16[384,576]{1,0:T(8,128)(2,1)S(1)}, bf16[384,576]{1,0:T(8,128)(2,1)}, bf16[384,768]{1,0:T(8,128)(2,1)}, f32[2,576]{1,0:T(2,128)S(1)}, f32[2,768]{1,0:T(2,128)S(1)}) custom-call(s32[16]{0:T(128)S(1)} %stack.23.refs_0_, bf16[384,384]{1,0:T(8,128)(2,1)S(1)} %get-tuple-element.227.refs_1_, bf16[384,768]{1,0:T(8,128)(2,1)S(1)} %get-tuple-element.228.refs_2_, ...), custom_call_target="tpu_custom_call" | custom-call | flops 2000000000 | bytes 1000 | tf_op jit(solution)/shard_map/project_back/pallas_call | solution.py:226
  340.4 6.6 %project_grads.1 = (bf16[208,768]{1,0:T(8,128)(2,1)}, bf16[208,768]{1,0:T(8,128)(2,1)}, bf16[208,768]{1,0:T(8,128)(2,1)}, bf16[96,768]{1,0:T(8,128)(2,1)}, bf16[112,768]{1,0:T(8,128)(2,1)}) custom-call(s32[16]{0:T(128)S(1)} %stack.23.refs_0_, bf16[384,768]{1,0:T(8,128)(2,1)} %get-tuple-element.142.refs_1_, bf16[384,768]{1,0:T(8,128)(2,1)} %copy-done.38, ...), custom_call_target="tpu_custom_call" | custom-call | flops 1500000000 | bytes 1000 | tf_op jit(solution)/shard_map/project_grads/pallas_call | solution.py:226
  349.1 4.3 %collective-permute-done.40.refs_3_ = bf16[384,768]{1,0:T(8,128)(2,1)S(1)} collective-permute-done((bf16[384,768]{1,0:T(8,128)(2,1)}, bf16[384,768]{1,0:T(8,128)(2,1)S(1)}, u32[]{:S(2)}, u32[]{:S(2)}) %collective-permute-start.40) | collective-permute-done | bytes 589856 | tf_op jit(solution)/shard_map/ppermute | solution.py:50
  354.2 4.3 %input_back.1 = (bf16[384,768]{1,0:T(8,128)(2,1)}, f32[2,768]{1,0:T(2,128)}) custom-call(bf16[384,768]{1,0:T(8,128)(2,1)} %dynamic-slice_bitcast_fusion.1.refs_1_.refs_5_.refs_0_, f32[384,768]{1,0:T(8,128)} %get-tuple-element.247.refs_1_, bf16[384,768]{1,0:T(8,128)(2,1)} %get-tuple-element.248.refs_2_, bf16[384,768]{1,0:T(8,128)(2,1)} %copy-done.32, ...), custom_call_target="tpu_custom_call" | custom-call | flops 500000000 | bytes 1000 | tf_op jit(solution)/shard_map/input_back/pallas_call | solution.py:226
  366.4 2.9 join_rows.2
  369.3 8.2 %collective-permute-done.45.refs_1_ = bf16[192,1536]{1,0:T(8,128)(2,1)S(1)} collective-permute-done((bf16[192,1536]{1,0:T(8,128)(2,1)}, bf16[192,1536]{1,0:T(8,128)(2,1)S(1)}, u32[]{:S(2)}, u32[]{:S(2)}) %collective-permute-start.45) | collective-permute-done | bytes 589856 | tf_op jit(solution)/shard_map/ppermute | solution.py:54
  377.5 3.5 collective-permute-done.47.refs_1_
  384.5 2.6 finish.1.refs_1_
  388.7 3.1 feed_out.1
  392.6 2.9 join_rows.3
  400.3 3.7 collective-permute-done.51.refs_2_
  404.0 2.8 project_out.1
  408.1 2.1 small_out.1
  (278 shorter events, 92.1 us)
Async XLA Ops:
  7.2 89.5 %all-gather.7.cloned.1.call-start = ((), (), s32[]{:S(2)}) async-start(), calls=%async_computation.6 | async-start | bytes 5308416 | tf_op jit(solution)/shard_map/all_gather | solution.py:98
  12.0 20.5 %collective-permute-start.2 = (bf16[208,768]{1,0:T(8,128)(2,1)}, bf16[208,768]{1,0:T(8,128)(2,1)}, u32[]{:S(2)}, u32[]{:S(2)}) collective-permute-start(bf16[208,768]{1,0:T(8,128)(2,1)} %pack_first.1.refs_2_.refs_5_.refs_8_.refs_6_), channel_id=1, source_target_pairs={{0,16},{8,24},{16,0},{24,8},{1,17},{9,25},{17,1},{25,9},{2,18},{10... | collective-permute-start | bytes 958472 | tf_op jit(solution)/shard_map/ppermute | solution.py:75
  16.1 16.4 %collective-permute-start.1 = (bf16[208,768]{1,0:T(8,128)(2,1)}, bf16[208,768]{1,0:T(8,128)(2,1)}, u32[]{:S(2)}, u32[]{:S(2)}) collective-permute-start(bf16[208,768]{1,0:T(8,128)(2,1)} %pack_first.1.refs_2_.refs_5_.refs_8_.refs_6_), channel_id=1, source_target_pairs={{0,24},{8,0},{16,8},{24,16},{1,25},{9,1},{17,9},{25,17},{2,26},{10... | collective-permute-start | bytes 958472 | tf_op jit(solution)/shard_map/ppermute | solution.py:75
  17.4 21.4 %collective-permute-start = (bf16[208,768]{1,0:T(8,128)(2,1)}, bf16[208,768]{1,0:T(8,128)(2,1)}, u32[]{:S(2)}, u32[]{:S(2)}) collective-permute-start(bf16[208,768]{1,0:T(8,128)(2,1)} %pack_first.1.refs_2_.refs_5_.refs_8_.refs_6_), channel_id=1, source_target_pairs={{0,8},{8,16},{16,24},{24,0},{1,9},{9,17},{17,25},{25,1},{2,10},{10... | collective-permute-start | bytes 958472 | tf_op jit(solution)/shard_map/ppermute | solution.py:75
  38.9 89.9 %all-gather.9.cloned.1.call-start = ((), (), s32[]{:S(2)}) async-start(), calls=%async_computation.7 | async-start | bytes 2654208 | tf_op jit(solution)/shard_map/all_gather | solution.py:98
  39.5 2.4 collective-permute-start.5
  39.6 2.7 collective-permute-start.4
  47.5 2.3 collective-permute-start.9
  50.7 130.6 %all-gather.11.cloned.1.call-start = ((), (), s32[]{:S(2)}) async-start(), calls=%async_computation.8 | async-start | bytes 5308416 | tf_op jit(solution)/shard_map/all_gather | solution.py:98
  50.8 15.4 %collective-permute-start.8 = (bf16[384,768]{1,0:T(8,128)(2,1)S(1)}, bf16[384,768]{1,0:T(8,128)(2,1)S(1)}, u32[]{:S(2)}, u32[]{:S(2)}) collective-permute-start(bf16[384,768]{1,0:T(8,128)(2,1)S(1)} %copy-done.2), channel_id=1, source_target_pairs={{0,4},{4,0},{1,5},{5,1},{2,6},{6,2},{3,7},{7,3},{8,12},{12,8},{9,1... | collective-permute-start | bytes 1769480 | tf_op jit(solution)/shard_map/ppermute | solution.py:54
  80.3 198.8 %reduce-scatter.4.cloned.1.call-start = ((), (), s32[]{:S(2)}) async-start(), calls=%async_computation.3 | async-start | bytes 2949120 | tf_op jit(solution)/shard_map/reduce_scatter | solution.py:1050
  80.8 15.8 %collective-permute-start.12 = (bf16[384,768]{1,0:T(8,128)(2,1)}, bf16[384,768]{1,0:T(8,128)(2,1)S(1)}, u32[]{:S(2)}, u32[]{:S(2)}) collective-permute-start(bf16[384,768]{1,0:T(8,128)(2,1)} %get-tuple-element.148.refs_2_), channel_id=1, source_target_pairs={{0,2},{2,0},{1,3},{3,1},{4,6},{6,4},{5,7},{7,5},{8,10},{10,8},{9,1... | collective-permute-start | bytes 1769480 | tf_op jit(solution)/shard_map/ppermute | solution.py:50
  105.5 2.3 collective-permute-start.13
  105.6 3.0 collective-permute-start.14
  106.1 22.7 %collective-permute-start.15 = (bf16[384,768]{1,0:T(8,128)(2,1)}, bf16[384,768]{1,0:T(8,128)(2,1)S(1)}, u32[]{:S(2)}, u32[]{:S(2)}) collective-permute-start(bf16[384,768]{1,0:T(8,128)(2,1)} %get-tuple-element.159.refs_4_), channel_id=1, source_target_pairs={{0,2},{2,0},{1,3},{3,1},{4,6},{6,4},{5,7},{7,5},{8,10},{10,8},{9,1... | collective-permute-start | bytes 1769480 | tf_op jit(solution)/shard_map/ppermute | solution.py:50
  134.7 2.3 collective-permute-start.18
  135.0 15.7 %collective-permute-start.17 = (bf16[384,768]{1,0:T(8,128)(2,1)}, bf16[384,768]{1,0:T(8,128)(2,1)S(1)}, u32[]{:S(2)}, u32[]{:S(2)}) collective-permute-start(bf16[384,768]{1,0:T(8,128)(2,1)} %get-tuple-element.166.refs_1_), channel_id=1, source_target_pairs={{0,4},{4,0},{1,5},{5,1},{2,6},{6,2},{3,7},{7,3},{8,12},{12,8},{9,1... | collective-permute-start | bytes 1769480 | tf_op jit(solution)/shard_map/ppermute | solution.py:54
  150.8 14.8 %collective-permute-start.16 = (bf16[384,768]{1,0:T(8,128)(2,1)S(1)}, bf16[384,768]{1,0:T(8,128)(2,1)S(1)}, u32[]{:S(2)}, u32[]{:S(2)}) collective-permute-start(bf16[384,768]{1,0:T(8,128)(2,1)S(1)} %copy-done.41), channel_id=1, source_target_pairs={{0,1},{1,0},{2,3},{3,2},{4,5},{5,4},{6,7},{7,6},{8,9},{9,8},{10,11... | collective-permute-start | bytes 1769480 | tf_op jit(solution)/shard_map/ppermute | solution.py:46
  164.0 17.3 %collective-permute-start.21 = (bf16[384,768]{1,0:T(8,128)(2,1)}, bf16[384,768]{1,0:T(8,128)(2,1)S(1)}, u32[]{:S(2)}, u32[]{:S(2)}) collective-permute-start(bf16[384,768]{1,0:T(8,128)(2,1)} %get-tuple-element.170.refs_2_), channel_id=1, source_target_pairs={{0,2},{2,0},{1,3},{3,1},{4,6},{6,4},{5,7},{7,5},{8,10},{10,8},{9,1... | collective-permute-start | bytes 1769480 | tf_op jit(solution)/shard_map/ppermute | solution.py:50
  197.6 4.6 %collective-permute-start.24 = (bf16[384,1536]{1,0:T(8,128)(2,1)}, bf16[384,1536]{1,0:T(8,128)(2,1)S(1)}, u32[]{:S(2)}, u32[]{:S(2)}) collective-permute-start(bf16[384,1536]{1,0:T(8,128)(2,1)} %get-tuple-element.183.refs_5_), channel_id=1, source_target_pairs={{0,1},{1,0},{2,3},{3,2},{4,5},{5,4},{6,7},{7,6},{8,9},{9,8},{10,11... | collective-permute-start | bytes 3538952 | tf_op jit(solution)/shard_map/ppermute | solution.py:46
  197.9 3.5 collective-permute-start.23
  198.2 4.0 collective-permute-start.22
  198.4 15.7 %collective-permute-start.25 = (bf16[384,768]{1,0:T(8,128)(2,1)}, bf16[384,768]{1,0:T(8,128)(2,1)S(1)}, u32[]{:S(2)}, u32[]{:S(2)}) collective-permute-start(bf16[384,768]{1,0:T(8,128)(2,1)} %get-tuple-element.187.refs_3_), channel_id=1, source_target_pairs={{0,2},{2,0},{1,3},{3,1},{4,6},{6,4},{5,7},{7,5},{8,10},{10,8},{9,1... | collective-permute-start | bytes 1769480 | tf_op jit(solution)/shard_map/ppermute | solution.py:50
  215.0 100.3 %reduce-scatter.6.cloned.1.call-start = ((), (), s32[]{:S(2)}) async-start(), calls=%async_computation.4 | async-start | bytes 1474560 | tf_op jit(solution)/shard_map/reduce_scatter | solution.py:1050
  228.3 2.3 collective-permute-start.26
  228.4 4.7 %collective-permute-start.27 = (bf16[384,768]{1,0:T(8,128)(2,1)S(1)}, bf16[384,768]{1,0:T(8,128)(2,1)S(1)}, u32[]{:S(2)}, u32[]{:S(2)}) collective-permute-start(bf16[384,768]{1,0:T(8,128)(2,1)S(1)} %copy-done.44), channel_id=1, source_target_pairs={{0,1},{1,0},{2,3},{3,2},{4,5},{5,4},{6,7},{7,6},{8,9},{9,8},{10,11... | collective-permute-start | bytes 1769480 | tf_op jit(solution)/shard_map/ppermute | solution.py:46
  231.6 15.6 %collective-permute-start.28 = (bf16[384,768]{1,0:T(8,128)(2,1)}, bf16[384,768]{1,0:T(8,128)(2,1)S(1)}, u32[]{:S(2)}, u32[]{:S(2)}) collective-permute-start(bf16[384,768]{1,0:T(8,128)(2,1)} %cross_sum.2), channel_id=1, source_target_pairs={{0,4},{4,0},{1,5},{5,1},{2,6},{6,2},{3,7},{7,3},{8,12},{12,8},{9,1... | collective-permute-start | bytes 1769480 | tf_op jit(solution)/shard_map/ppermute | solution.py:54
  253.8 15.7 %collective-permute-start.30 = (bf16[384,768]{1,0:T(8,128)(2,1)}, bf16[384,768]{1,0:T(8,128)(2,1)S(1)}, u32[]{:S(2)}, u32[]{:S(2)}) collective-permute-start(bf16[384,768]{1,0:T(8,128)(2,1)} %get-tuple-element.202.refs_3_), channel_id=1, source_target_pairs={{0,2},{2,0},{1,3},{3,1},{4,6},{6,4},{5,7},{7,5},{8,10},{10,8},{9,1... | collective-permute-start | bytes 1769480 | tf_op jit(solution)/shard_map/ppermute | solution.py:50
  269.5 91.9 %reduce-scatter.8.cloned.1.call-start = ((), (), s32[]{:S(2)}) async-start(), calls=%async_computation.5 | async-start | bytes 2949120 | tf_op jit(solution)/shard_map/reduce_scatter | solution.py:1050
  279.2 3.2 collective-permute-start.32
  279.2 16.0 %collective-permute-start.33 = (bf16[192,1536]{1,0:T(8,128)(2,1)}, bf16[192,1536]{1,0:T(8,128)(2,1)S(1)}, u32[]{:S(2)}, u32[]{:S(2)}) collective-permute-start(bf16[192,1536]{1,0:T(8,128)(2,1)} %reduce-scatter.4.cloned.1.call-done.refs_2_), channel_id=1, source_target_pairs={{0,4},{4,0},{1,5},{5,1},{2,6},{6,2},{3,7},{7,3},{8,12},{12,8},{9,1... | collective-permute-start | bytes 1769480 | tf_op jit(solution)/shard_map/ppermute | solution.py:54
  280.7 15.7 %collective-permute-start.34 = (bf16[384,768]{1,0:T(8,128)(2,1)}, bf16[384,768]{1,0:T(8,128)(2,1)S(1)}, u32[]{:S(2)}, u32[]{:S(2)}) collective-permute-start(bf16[384,768]{1,0:T(8,128)(2,1)} %get-tuple-element.214.refs_3_), channel_id=1, source_target_pairs={{0,2},{2,0},{1,3},{3,1},{4,6},{6,4},{5,7},{7,5},{8,10},{10,8},{9,1... | collective-permute-start | bytes 1769480 | tf_op jit(solution)/shard_map/ppermute | solution.py:50
  311.5 3.8 collective-permute-start.36
  314.7 15.6 %collective-permute-start.37 = (bf16[384,768]{1,0:T(8,128)(2,1)}, bf16[384,768]{1,0:T(8,128)(2,1)S(1)}, u32[]{:S(2)}, u32[]{:S(2)}) collective-permute-start(bf16[384,768]{1,0:T(8,128)(2,1)} %cross_sum.3), channel_id=1, source_target_pairs={{0,4},{4,0},{1,5},{5,1},{2,6},{6,2},{3,7},{7,3},{8,12},{12,8},{9,1... | collective-permute-start | bytes 1769480 | tf_op jit(solution)/shard_map/ppermute | solution.py:54
  337.6 15.8 %collective-permute-start.40 = (bf16[384,768]{1,0:T(8,128)(2,1)}, bf16[384,768]{1,0:T(8,128)(2,1)S(1)}, u32[]{:S(2)}, u32[]{:S(2)}) collective-permute-start(bf16[384,768]{1,0:T(8,128)(2,1)} %get-tuple-element.248.refs_2_), channel_id=1, source_target_pairs={{0,2},{2,0},{1,3},{3,1},{4,6},{6,4},{5,7},{7,5},{8,10},{10,8},{9,1... | collective-permute-start | bytes 1769480 | tf_op jit(solution)/shard_map/ppermute | solution.py:50
  339.1 19.5 %collective-permute-start.41 = (bf16[192,768]{1,0:T(8,128)(2,1)S(1)}, bf16[192,768]{1,0:T(8,128)(2,1)S(1)}, u32[]{:S(2)}, u32[]{:S(2)}) collective-permute-start(bf16[192,768]{1,0:T(8,128)(2,1)S(1)} %copy-done.65), channel_id=1, source_target_pairs={{0,4},{4,0},{1,5},{5,1},{2,6},{6,2},{3,7},{7,3},{8,12},{12,8},{9,1... | collective-permute-start | bytes 884744 | tf_op jit(solution)/shard_map/ppermute | solution.py:54
  347.0 11.6 %collective-permute-start.43 = (bf16[112,768]{1,0:T(8,128)(2,1)}, bf16[112,768]{1,0:T(8,128)(2,1)S(1)}, u32[]{:S(2)}, u32[]{:S(2)}) collective-permute-start(bf16[112,768]{1,0:T(8,128)(2,1)} %get-tuple-element.254), channel_id=1, source_target_pairs={{0,24},{8,0},{16,8},{24,16},{1,25},{9,1},{17,9},{25,17},{2,26},{10... | collective-permute-start | bytes 516104 | tf_op jit(solution)/shard_map/ppermute | solution.py:1105
  348.2 10.5 %collective-permute-start.42 = (bf16[96,768]{1,0:T(8,128)(2,1)}, bf16[96,768]{1,0:T(8,128)(2,1)S(1)}, u32[]{:S(2)}, u32[]{:S(2)}) collective-permute-start(bf16[96,768]{1,0:T(8,128)(2,1)} %get-tuple-element.253), channel_id=1, source_target_pairs={{0,8},{8,16},{16,24},{24,0},{1,9},{9,17},{17,25},{25,1},{2,10},{10... | collective-permute-start | bytes 442376 | tf_op jit(solution)/shard_map/ppermute | solution.py:1105
  358.6 7.0 %collective-permute-start.46 = (bf16[384,768]{1,0:T(8,128)(2,1)}, bf16[384,768]{1,0:T(8,128)(2,1)S(1)}, u32[]{:S(2)}, u32[]{:S(2)}) collective-permute-start(bf16[384,768]{1,0:T(8,128)(2,1)} %get-tuple-element.249.refs_1_), channel_id=1, source_target_pairs={{0,1},{1,0},{2,3},{3,2},{4,5},{5,4},{6,7},{7,6},{8,9},{9,8},{10,11... | collective-permute-start | bytes 1769480 | tf_op jit(solution)/shard_map/ppermute | solution.py:46
  361.4 16.0 %collective-permute-start.45 = (bf16[192,1536]{1,0:T(8,128)(2,1)}, bf16[192,1536]{1,0:T(8,128)(2,1)S(1)}, u32[]{:S(2)}, u32[]{:S(2)}) collective-permute-start(bf16[192,1536]{1,0:T(8,128)(2,1)} %reduce-scatter.8.cloned.1.call-done.refs_0_), channel_id=1, source_target_pairs={{0,4},{4,0},{1,5},{5,1},{2,6},{6,2},{3,7},{7,3},{8,12},{12,8},{9,1... | collective-permute-start | bytes 1769480 | tf_op jit(solution)/shard_map/ppermute | solution.py:54
  362.1 21.5 %collective-permute-start.44 = (bf16[384,768]{1,0:T(8,128)(2,1)S(1)}, bf16[384,768]{1,0:T(8,128)(2,1)S(1)}, u32[]{:S(2)}, u32[]{:S(2)}) collective-permute-start(bf16[384,768]{1,0:T(8,128)(2,1)S(1)} %copy-done.30), channel_id=1, source_target_pairs={{0,2},{2,0},{1,3},{3,1},{4,6},{6,4},{5,7},{7,5},{8,10},{10,8},{9,1... | collective-permute-start | bytes 1769480 | tf_op jit(solution)/shard_map/ppermute | solution.py:50
  363.6 13.9 %collective-permute-start.48 = (bf16[208,768]{1,0:T(8,128)(2,1)}, bf16[208,768]{1,0:T(8,128)(2,1)S(1)}, u32[]{:S(2)}, u32[]{:S(2)}) collective-permute-start(bf16[208,768]{1,0:T(8,128)(2,1)} %get-tuple-element.260), channel_id=1, source_target_pairs={{0,24},{8,0},{16,8},{24,16},{1,25},{9,1},{17,9},{25,17},{2,26},{10... | collective-permute-start | bytes 958472 | tf_op jit(solution)/shard_map/ppermute | solution.py:1108
  364.6 16.3 %collective-permute-start.47 = (bf16[208,768]{1,0:T(8,128)(2,1)}, bf16[208,768]{1,0:T(8,128)(2,1)S(1)}, u32[]{:S(2)}, u32[]{:S(2)}) collective-permute-start(bf16[208,768]{1,0:T(8,128)(2,1)} %get-tuple-element.255), channel_id=1, source_target_pairs={{0,8},{8,16},{16,24},{24,0},{1,9},{9,17},{17,25},{25,1},{2,10},{10... | collective-permute-start | bytes 958472 | tf_op jit(solution)/shard_map/ppermute | solution.py:1108
  387.1 4.6 %collective-permute-start.49 = (bf16[384,768]{1,0:T(8,128)(2,1)}, bf16[384,768]{1,0:T(8,128)(2,1)S(1)}, u32[]{:S(2)}, u32[]{:S(2)}) collective-permute-start(bf16[384,768]{1,0:T(8,128)(2,1)} %finish.1.refs_1_), channel_id=1, source_target_pairs={{0,1},{1,0},{2,3},{3,2},{4,5},{5,4},{6,7},{7,6},{8,9},{9,8},{10,11... | collective-permute-start | bytes 1769480 | tf_op jit(solution)/shard_map/ppermute | solution.py:46
  387.2 9.9 %collective-permute-start.50 = (bf16[208,768]{1,0:T(8,128)(2,1)S(1)}, bf16[208,768]{1,0:T(8,128)(2,1)S(1)}, u32[]{:S(2)}, u32[]{:S(2)}) collective-permute-start(bf16[208,768]{1,0:T(8,128)(2,1)S(1)} %copy-done.61), channel_id=1, source_target_pairs={{0,4},{4,0},{1,5},{5,1},{2,6},{6,2},{3,7},{7,3},{8,12},{12,8},{9,1... | collective-permute-start | bytes 958472 | tf_op jit(solution)/shard_map/ppermute | solution.py:54
  399.6 4.4 %collective-permute-start.51 = (f32[16,768]{1,0:T(8,128)}, f32[16,768]{1,0:T(8,128)S(1)}, u32[]{:S(2)}, u32[]{:S(2)}) collective-permute-start(f32[16,768]{1,0:T(8,128)} %small_sum.1.refs_1_), channel_id=1, source_target_pairs={{0,2},{2,0},{1,3},{3,1},{4,6},{6,4},{5,7},{7,5},{8,10},{10,8},{9,1... | collective-permute-start | bytes 147464 | tf_op jit(solution)/shard_map/ppermute | solution.py:50
  400.3 6.6 %collective-permute-start.52 = (f32[16,768]{1,0:T(8,128)}, f32[16,768]{1,0:T(8,128)S(1)}, u32[]{:S(2)}, u32[]{:S(2)}) collective-permute-start(f32[16,768]{1,0:T(8,128)} %small_sum.1.refs_1_), channel_id=1, source_target_pairs={{0,1},{1,0},{2,3},{3,2},{4,5},{5,4},{6,7},{7,6},{8,9},{9,8},{10,11... | collective-permute-start | bytes 147464 | tf_op jit(solution)/shard_map/ppermute | solution.py:46
  404.0 2.9 collective-permute-start.53
  (86 other events, 499.8 us)
Sparse Core Ops, SparseCore 0:
  39.0 57.6 all-gather.6
  98.3 30.4 all-gather.8
  130.4 50.8 all-gather.10
  214.3 46.8 reduce-scatter.3
  269.6 28.1 reduce-scatter.5
  302.4 46.1 reduce-scatter.7

commit v4 on v3

--- a/solution.py
+++ b/solution.py
@@ -319,17 +319,17 @@
 
         def kernel(w_r, o_r, qv_r, up_r, g_r, s_r, out):
             for side in range(3):
-                cuts = [w_r[h][:, side * HD : (side + 1) * HD] for h in range(H)]
+                cuts = [w_r[0, h][:, side * HD : (side + 1) * HD] for h in range(H)]
                 out[:M, side * A : (side + 1) * A] = jnp.concatenate(cuts, 1)
-            out[:M, 3 * A :] = o_r[...].astype(f32).T.astype(bf16)
+            out[:M, 3 * A :] = o_r[0].astype(f32).T.astype(bf16)
             vecs = []
             for l in range(L):
                 vecs += [g_r[l].astype(f32), s_r[l].astype(f32)]
             vecs = jnp.concatenate(vecs + [jnp.zeros((TAIL - 6 * L, M), f32)], 0)
             rows = []
             for l in range(L):
-                q, u = qv_r[l].astype(f32), up_r[l].astype(f32)
-                cuts = [q[h : h + 1, :] for h in range(H)] + [u[r : r + 1, :] for r in range(F // 64)]
+                cuts = [qv_r[h].astype(f32)[l : l + 1, :] for h in range(H)]
+                cuts += [up_r[r].astype(f32)[l : l + 1, :] for r in range(F // 64)]
                 rows.append(jnp.concatenate(cuts, 1))
             rows = jnp.concatenate(rows + [jnp.zeros((TAIL - L, H * nq + F // 64 * nu), f32)], 0)
             rest = jnp.zeros((TAIL, z.a_cols - M - rows.shape[1]), f32)
@@ -337,7 +337,17 @@
 
         return run(
             kernel,
-            [w_qkv.transpose(1, 0, 2), w_out, qv_bias, up_bias, norm_gains, shifts],
+            [
+                Far(a)
+                for a in (
+                    w_qkv.transpose(0, 2, 1, 3),
+                    w_out.reshape(L, A, M),
+                    qv_bias.transpose(1, 0, 2),
+                    up_bias.transpose(1, 0, 2),
+                    norm_gains,
+                    shifts,
+                )
+            ],
             [((M + TAIL, z.a_cols), bf16, FAR)],
             name="pack_first",
         )[0]
@@ -402,7 +412,7 @@
             send(kv_o)
             q_o[...] = jnp.concatenate(both, 1)
 
-        ins = [Far(x)] + ([] if first else list(biases) + [Far(p) for p in prev])
+        ins = [Far(x)] + ([] if first else list(biases) + [Far(prev[0]), prev[1]])
         outs = [((R, D), bf16, FAR), ((R, 2 * A), bf16), ((R, 4 * A), bf16, FAR)]
         scratch = weight_scratch(z.a_cols)
         if first:
@@ -567,7 +577,7 @@
             ((R, D), bf16, FAR),
         ]
         return run(
-            kernel, [Far(x), Far(pa), Far(pb), vec, tails], outs, weight_scratch(2 * F), w, scal, "feed", 6
+            kernel, [Far(x), Far(pa), pb, vec, tails], outs, weight_scratch(2 * F), w, scal, "feed", 6
         )
 
     def finish(y, pa, pb, vec):
@@ -624,7 +634,7 @@
             du_o[...] = jnp.where(odd, dus[1], dus[0])
             swap_o[:, D:] = jnp.where(odd, dus[0], dus[1])
 
-        ins = [grad] if before is None else [Far(b) for b in before[:4]] + [before[4]]
+        ins = [grad] if before is None else [Far(b) for b in before[:3]] + list(before[3:])
         ins += [Far(gp[0]), Far(gp[1])]
         outs = [((R, D + F), bf16, FAR), ((R, F), bf16), ((R, D), bf16, FAR), ((1, D), f32)]
         if before is not None:
@@ -693,7 +703,7 @@
         outs = [((R, D), f32, FAR), ((R, D), bf16, FAR), ((2 * H, R, WIDE), bf16), ((3, D), f32)]
         return run(
             kernel,
-            [Far(y), g, Far(pa), Far(pb), vec, Far(o0), Far(o1)],
+            [Far(y), g, Far(pa), pb, vec, Far(o0), Far(o1)],
             outs,
             weight_scratch(256),
             w,
@@ -744,7 +754,7 @@
             if before is not None:
                 dq_o[...] = jnp.concatenate([dq_s[0][j][:, :HD] for j in range(2 * H)], 1)
 
-        ins = [Far(qa)] + [Far(a) for a in kvs] + [da]
+        ins = [Far(qa)] + [Far(a) for a in kvs] + [da] if before is None else [qa] + list(kvs) + [da]
         outs = [((R, 4 * A), bf16), ((R, 4 * A), bf16, FAR)]
         scratch = [pltpu.VMEM((2 * H, K, WIDE), bf16)] * 4
         if before is None:
@@ -986,7 +996,7 @@
             sums_o[0:1, :] = dgain
             sums_o[1:2, :] = dshift
 
-        return run(kernel, [Far(x), Far(dy), Far(pa), Far(pb), vec], [((R, D), bf16, FAR), ((2, D), f32)], name="input_back")
+        return run(kernel, [x, dy, pa, pb, vec], [((R, D), bf16, FAR), ((2, D), f32)], name="input_back")
 
     return dict(locals())
 
@@ -1008,7 +1018,7 @@
             return jnp.concatenate([after(w_up[l], *then), after(w_down[l], *then).T], -1)
 
         message = k["pack_first"](
-            w_qkv[0], w_out[0].reshape(A, m), qv_bias, up_bias, norm_gains, shifts
+            w_qkv, w_out, qv_bias, up_bias, norm_gains, shifts
         )
         w_a = [Pieces(message, TAIL) if S == 4 else Gathered(message, S, TAIL)]
         w_b = [Gathered(after(part_b(0, message), *w_a[0].arrays[1:4]), S)]
@@ -1111,22 +1121,24 @@
         part_b_sum = after(part_b_sum, ready)
         sum_b[0] = (part_b_sum, y_swap(part_b_sum))
         far_last = x_swap(after(part_last, ready))
+        last_rows = k["finish"](y_last, part_last, far_last, vec)[0]
         frames_grad = whole_rows(grad_rows)
-        block = after(blocks[0], sum_b[0][1], frames_grad)
+        block = after(blocks[0], sum_b[0][1], frames_grad, last_rows)
         if S == 4:
             mine = k["sum_blocks"](block, others)
         else:
             mine = lax.psum_scatter(block, "shard", scatter_dimension=0, tiled=True)[0]
         theirs = y_swap(mine)
         sum_a[0] = (mine, theirs)
-        out_frames = whole_rows(k["finish"](y_last, part_last, after(far_last, mine), vec)[0])
+        out_frames = whole_rows(after(last_rows, mine))
         outs_up, outs_down = k["feed_out"]([sum_b[0], (after(sum_b[1][0], mine), sum_b[1][1])])
         tiny = k["small_sum"](after(mine, outs_up, out_frames), theirs)
         tiny_x = x_swap(tiny)
-        tiny_c, tiny_f = core_swap(tiny), core_swap(tiny_x)
+        tiny_c = core_swap(tiny)
         outs_qkv, outs_out = k["proj_out"]([(after(mine, tiny), theirs), sum_a[1]])
+        tiny_f = core_swap(after(tiny_x, outs_qkv))
         g_qvb, g_upb, g_gains, g_shifts = k["small_out"](
-            scal, after(tiny, outs_qkv), tiny_x, tiny_c, tiny_f
+            scal, tiny, tiny_x, tiny_c, tiny_f
         )
         return (
             out_frames,

time: 424 us -> 414 us (0.976)
    ppermute x8, waiting for transfers between devices: 37.7 us -> 33.2 us  [y_swap(): return lax.ppermute(x, 'ctx', [(0, 1), (1, 0)])]
    unnamed x151 -> x147, local copies, waits for them, and re-layouts: 22.5 us -> 19.3 us
where the time goes in v4:
time: 414 us; the launch traced here: 408 us
  Pallas kernels  183 us (44%)
  waiting for transfers between devices  145 us (35%)
  starting transfers between devices  39.7 us (10%)
  local copies, waits for them, and re-layouts  22.8 us (6%)
  between operations  15.5 us (4%)
    pallas_call x35, Pallas kernels, run(): pl.pallas_call(wrapped, out_shape=shapes, in_specs=specs, out_specs=[any_...  183 us
    all_gather x3, waiting for transfers between devices, __init__(): whole = lax.all_gather(x, ('shard', 'tc'), axis=0, tiled=False)  36.9 us
    ppermute x8, waiting for transfers between devices, y_swap(): return lax.ppermute(x, 'ctx', [(0, 1), (1, 0)])  33.2 us
    ppermute x9, waiting for transfers between devices, x_swap(): return lax.ppermute(x, 'tx', [(0, 1), (1, 0)])  33 us
    ppermute x30, waiting for transfers between devices, core_swap(): return lax.ppermute(x, 'tc', [(0, 1), (1, 0)])  21.7 us
    unnamed x147, local copies, waits for them, and re-layouts  19.3 us
    ppermute x3, waiting for transfers between devices, __init__(): self.mine = [x] + [lax.ppermute(x, 'shard', ring(s)) for s in (1, 3, 2)]  18.3 us
    ppermute x9, starting transfers between devices, x_swap(): return lax.ppermute(x, 'tx', [(0, 1), (1, 0)])  13.9 us
  transfers between devices with their start and end apart: 60, of which 39 were waited for; matrix products, arithmetic and copies ran while one was open for 1% of the time, Pallas kernels for 39%

profile of v4, /device:TPU:0, one launch (start us, length us, event | category | flops | bytes accessed | tf_op | source)
XLA Modules:
  0.0 407.6 jit_solution(13471176348236991916)
XLA Ops:
  7.3 2.6 pack_first.1.refs_2_.refs_5_.refs_8_.refs_6_
  9.8 4.1 %collective-permute-start.2 = (bf16[208,768]{1,0:T(8,128)(2,1)}, bf16[208,768]{1,0:T(8,128)(2,1)S(1)}, u32[]{:S(2)}, u32[]{:S(2)}) collective-permute-start(bf16[208,768]{1,0:T(8,128)(2,1)} %pack_first.1.refs_2_.refs_5_.refs_8_.refs_6_), channel_id=1, source_target_pairs={{0,16},{8,24},{16,0},{24,8},{1,17},{9,25},{17,1},{25,9},{2,18},{10... | collective-permute-start | bytes 958472 | tf_op jit(solution)/shard_map/ppermute | solution.py:75
  18.3 11.9 %collective-permute-done.2.refs_5_.refs_8_.refs_11_.refs_9_ = bf16[208,768]{1,0:T(8,128)(2,1)S(1)} collective-permute-done((bf16[208,768]{1,0:T(8,128)(2,1)}, bf16[208,768]{1,0:T(8,128)(2,1)S(1)}, u32[]{:S(2)}, u32[]{:S(2)}) %collective-permute-start.2) | collective-permute-done | bytes 319520 | tf_op jit(solution)/shard_map/ppermute | solution.py:75
  30.3 6.3 %collective-permute-done.refs_3_.refs_6_.refs_9_.refs_7_ = bf16[208,768]{1,0:T(8,128)(2,1)S(1)} collective-permute-done((bf16[208,768]{1,0:T(8,128)(2,1)}, bf16[208,768]{1,0:T(8,128)(2,1)S(1)}, u32[]{:S(2)}, u32[]{:S(2)}) %collective-permute-start) | collective-permute-done | bytes 319520 | tf_op jit(solution)/shard_map/ppermute | solution.py:75
  39.9 5.2 %project.2 = (bf16[384,768]{1,0:T(8,128)(2,1)}, bf16[384,384]{1,0:T(8,128)(2,1)S(1)}, bf16[384,768]{1,0:T(8,128)(2,1)}, f32[16,768]{1,0:T(8,128)S(1)}, f32[4,576...) custom-call(s32[16]{0:T(128)S(1)} %stack.23.refs_0_, ...), custom_call_target="tpu_custom_call" | custom-call | flops 1750000000 | bytes 1000 | tf_op jit(solution)/shard_map/project/pallas_call | solution.py:226
  49.9 5.7 %attend_near.2.refs_4_ = f32[6,384,128]{2,1,0:T(8,128)S(1)} custom-call(bf16[384,384]{1,0:T(8,128)(2,1)S(1)} %get-tuple-element.143.refs_0_.refs_1_, bf16[384,768]{1,0:T(8,128)(2,1)S(1)} %copy-done.5, bf16[384,768]{1,0:T(8,128)(2,1)S(1)} %collective-permute-done.9.refs_2_), custom_call_target="tpu_custom_call" | custom-call | flops 3000000000 | bytes 1000 | tf_op jit(solution)/shard_map/attend_near/pallas_call | solution.py:226
  56.7 7.1 %collective-permute-done.8.refs_2_.refs_1_ = bf16[384,768]{1,0:T(8,128)(2,1)S(1)} collective-permute-done((bf16[384,768]{1,0:T(8,128)(2,1)S(1)}, bf16[384,768]{1,0:T(8,128)(2,1)S(1)}, u32[]{:S(2)}, u32[]{:S(2)}) %collective-permute-start.8) | collective-permute-done | bytes 589856 | tf_op jit(solution)/shard_map/ppermute | solution.py:54
  67.0 10.7 %attend_far.2 = (bf16[384,192]{1,0:T(8,128)(2,1)}, bf16[384,192]{1,0:T(8,128)(2,1)}, bf16[6,384,128]{2,1,0:T(8,128)(2,1)}, bf16[384,192]{1,0:T(8,128)(2,1)}, bf1...) custom-call(s32[16]{0:T(128)S(1)} %stack.23.refs_0_, bf16[384,384]{1,0:T(8,128)(2,1)S(1)} %get-tuple-element.143.refs_0_.refs_1_, ...), custom_call_target="tpu_custom_call" | custom-call | flops 4000000000 | bytes 1000 | tf_op jit(solution)/shard_map/attend_far/pallas_call | solution.py:226
  81.4 12.6 %collective-permute-done.12.refs_3_ = bf16[384,768]{1,0:T(8,128)(2,1)S(1)} collective-permute-done((bf16[384,768]{1,0:T(8,128)(2,1)}, bf16[384,768]{1,0:T(8,128)(2,1)S(1)}, u32[]{:S(2)}, u32[]{:S(2)}) %collective-permute-start.12) | collective-permute-done | bytes 589856 | tf_op jit(solution)/shard_map/ppermute | solution.py:50
  94.5 7.9 %feed.2 = (f32[384,768]{1,0:T(8,128)}, bf16[384,768]{1,0:T(8,128)(2,1)}, bf16[384,768]{1,0:T(8,128)(2,1)}, bf16[384,768]{1,0:T(8,128)(2,1)}, bf16[384,768]{1,0:T...) custom-call(s32[16]{0:T(128)S(1)} %stack.23.refs_0_, ...), custom_call_target="tpu_custom_call" | custom-call | flops 3000000000 | bytes 1000 | tf_op jit(solution)/shard_map/feed/pallas_call | solution.py:226
  105.8 20.7 %all-gather.9.cloned.1.call-done = bf16[1536,768]{1,0:T(8,128)(2,1)} async-done(((bf16[192,768]{1,0:T(8,128)(2,1)}), bf16[1536,768]{1,0:T(8,128)(2,1)}) %all-gather.9.cloned.1.call-update) | async-done | bytes 2359312 | tf_op jit(solution)/shard_map/all_gather | solution.py:98
  126.5 5.0 %project.3 = (bf16[384,768]{1,0:T(8,128)(2,1)}, bf16[384,384]{1,0:T(8,128)(2,1)S(1)}, bf16[384,768]{1,0:T(8,128)(2,1)}, f32[384,768]{1,0:T(8,128)}) custom-call(s32[16]{0:T(128)S(1)} %stack.23.refs_0_, f32[384,768]{1,0:T(8,128)} %get-tuple-element.216.refs_1_, f32[16,768]{1,0:T(8,128)S(1)} %get-tuple-element.149.refs_4_.refs_2_.refs_5_.refs_3_, ...), custom_call_target="tpu_custom_call" | custom-call | flops 1750000000 | bytes 1000 | tf_op jit(solution)/shard_map/project/pallas_call | solution.py:226
  134.9 5.7 %attend_near.3.refs_4_ = f32[6,384,128]{2,1,0:T(8,128)S(1)} custom-call(bf16[384,384]{1,0:T(8,128)(2,1)S(1)} %get-tuple-element.165.refs_0_.refs_1_, bf16[384,768]{1,0:T(8,128)(2,1)S(1)} %copy-done.8, bf16[384,768]{1,0:T(8,128)(2,1)S(1)} %collective-permute-done.18.refs_2_), custom_call_target="tpu_custom_call" | custom-call | flops 3000000000 | bytes 1000 | tf_op jit(solution)/shard_map/attend_near/pallas_call | solution.py:226
  140.6 6.9 %collective-permute-done.17.refs_2_.refs_1_ = bf16[384,768]{1,0:T(8,128)(2,1)S(1)} collective-permute-done((bf16[384,768]{1,0:T(8,128)(2,1)}, bf16[384,768]{1,0:T(8,128)(2,1)S(1)}, u32[]{:S(2)}, u32[]{:S(2)}) %collective-permute-start.17) | collective-permute-done | bytes 589856 | tf_op jit(solution)/shard_map/ppermute | solution.py:54
  149.5 11.1 %attend_far.3 = (bf16[384,192]{1,0:T(8,128)(2,1)}, bf16[384,192]{1,0:T(8,128)(2,1)}, bf16[6,384,128]{2,1,0:T(8,128)(2,1)}, bf16[384,192]{1,0:T(8,128)(2,1)}, bf1...) custom-call(s32[16]{0:T(128)S(1)} %stack.23.refs_0_, bf16[384,384]{1,0:T(8,128)(2,1)S(1)} %get-tuple-element.165.refs_0_.refs_1_, ...), custom_call_target="tpu_custom_call" | custom-call | flops 4000000000 | bytes 1000 | tf_op jit(solution)/shard_map/attend_far/pallas_call | solution.py:226
  163.9 15.8 %all-gather.11.cloned.1.call-done = bf16[1536,1536]{1,0:T(8,128)(2,1)} async-done(((bf16[192,1536]{1,0:T(8,128)(2,1)}), bf16[1536,1536]{1,0:T(8,128)(2,1)}) %all-gather.11.cloned.1.call-update) | async-done | bytes 4718608 | tf_op jit(solution)/shard_map/all_gather | solution.py:98
  179.6 8.1 %feed.3 = (f32[384,768]{1,0:T(8,128)}, bf16[384,768]{1,0:T(8,128)(2,1)}, bf16[384,768]{1,0:T(8,128)(2,1)}, bf16[384,768]{1,0:T(8,128)(2,1)}, bf16[384,768]{1,0:T...) custom-call(s32[16]{0:T(128)S(1)} %stack.23.refs_0_, f32[384,768]{1,0:T(8,128)} %get-tuple-element.169.refs_1_, ...), custom_call_target="tpu_custom_call" | custom-call | flops 3000000000 | bytes 1000 | tf_op jit(solution)/shard_map/feed/pallas_call | solution.py:226
  187.8 7.1 %feed_back.2 = (bf16[384,1536]{1,0:T(8,128)(2,1)}, bf16[384,768]{1,0:T(8,128)(2,1)S(1)}, bf16[384,768]{1,0:T(8,128)(2,1)}, f32[1,768]{1,0:T(1,128)S(1)}) custom-call(s32[16]{0:T(128)S(1)} %stack.23.refs_0_, bf16[384,768]{1,0:T(8,128)(2,1)S(1)} %dynamic-slice_bitcast_fusion.refs_1_.refs_2_, bf16[384,768]{1,0:T(8,128)(2,1)} %get-tuple-element.181.refs_2_, ...), custom_call_target="tpu_custom_call" | custom-call | flops 3000000000 | bytes 1000 | tf_op jit(solution)/shard_map/feed_back/pallas_call | solution.py:226
  200.7 8.4 %feed_grads.2 = (bf16[768,1536]{1,0:T(8,128)(2,1)}, f32[2,768]{1,0:T(2,128)S(1)}) custom-call(s32[16]{0:T(128)S(1)} %stack.23.refs_0_, bf16[384,768]{1,0:T(8,128)(2,1)} %get-tuple-element.178.refs_1_, bf16[384,768]{1,0:T(8,128)(2,1)} %copy-done.53, bf16[384,768]{1,0:T(8,128)(2,1)} %get-tuple-element.179.refs_3_, bf16[384,768]{1,0:T(8,128)(2,1)} %copy-done.52, ...), custom_call_target="tpu_custom_call" | custom-call | flops 1500000000 | bytes 1000 | tf_op jit(solution)/shard_map/feed_grads/pallas_call | solution.py:226
  209.2 2.3 collective-permute-done.25.refs_4_
  211.7 4.7 %middle_back.2 = (f32[384,768]{1,0:T(8,128)}, bf16[384,768]{1,0:T(8,128)(2,1)}, bf16[6,384,128]{2,1,0:T(8,128)(2,1)S(1)}, f32[3,768]{1,0:T(4,128)S(1)}) custom-call(s32[16]{0:T(128)S(1)} %stack.23.refs_0_, f32[384,768]{1,0:T(8,128)} %get-tuple-element.186.refs_1_.refs_0_, bf16[384,768]{1,0:T(8,128)(2,1)S(1)} %dynamic-slice_bitcast_fusion.refs_1_.refs_2_, ...), custom_call_target="tpu_custom_call" | custom-call | flops 2000000000 | bytes 1000 | tf_op jit(solution)/shard_map/middle_back/pallas_call | solution.py:226
  216.5 8.3 %attend_back.4 = (f32[6,128,384]{2,1,0:T(8,128)S(1)}, bf16[384,768]{1,0:T(8,128)(2,1)S(1)}, bf16[384,768]{1,0:T(8,128)(2,1)}) custom-call(bf16[6,384,128]{2,1,0:T(8,128)(2,1)} %get-tuple-element.191.refs_0_, bf16[384,768]{1,0:T(8,128)(2,1)} %copy-done.10, bf16[384,768]{1,0:T(8,128)(2,1)} %copy-done.11, bf16[6,384,128]{2,1,0:T(8,128)(2,1)S(1)} %get-tuple-element.192.refs_3_), custom_call_target="tpu_custom_call" | custom-call | flops 4000000000 | bytes 1000 | tf_op jit(solution)/shard_map/attend_back/pallas_call | solution.py:226
  229.7 7.6 %attend_back.5 = (bf16[384,384]{1,0:T(8,128)(2,1)S(1)}, bf16[384,768]{1,0:T(8,128)(2,1)S(1)}, bf16[384,768]{1,0:T(8,128)(2,1)}) custom-call(bf16[6,384,128]{2,1,0:T(8,128)(2,1)S(1)} %copy-done.22, bf16[384,768]{1,0:T(8,128)(2,1)S(1)} %copy-done.9, bf16[384,768]{1,0:T(8,128)(2,1)S(1)} %collective-permute-done.18.refs_2_, ...), custom_call_target="tpu_custom_call" | custom-call | flops 4000000000 | bytes 1000 | tf_op jit(solution)/shard_map/attend_back/pallas_call | solution.py:226
  237.3 6.4 %collective-permute-done.28.refs_4_ = bf16[384,768]{1,0:T(8,128)(2,1)S(1)} collective-permute-done((bf16[384,768]{1,0:T(8,128)(2,1)}, bf16[384,768]{1,0:T(8,128)(2,1)S(1)}, u32[]{:S(2)}, u32[]{:S(2)}) %collective-permute-start.28) | collective-permute-done | bytes 589856 | tf_op jit(solution)/shard_map/ppermute | solution.py:54
  243.7 2.2 collective-permute-done.29.refs_3_
  245.9 4.3 %project_back.2 = (bf16[384,576]{1,0:T(8,128)(2,1)S(1)}, bf16[384,576]{1,0:T(8,128)(2,1)}, bf16[384,768]{1,0:T(8,128)(2,1)}, f32[2,576]{1,0:T(2,128)S(1)}) custom-call(s32[16]{0:T(128)S(1)} %stack.23.refs_0_, bf16[384,384]{1,0:T(8,128)(2,1)S(1)} %get-tuple-element.198.refs_1_, bf16[384,768]{1,0:T(8,128)(2,1)S(1)} %get-tuple-element.199.refs_2_, ...), custom_call_target="tpu_custom_call" | custom-call | flops 2000000000 | bytes 1000 | tf_op jit(solution)/shard_map/project_back/pallas_call | solution.py:226
  254.7 5.0 %own_grads.1 = bf16[4,192,768]{2,1,0:T(8,128)(2,1)} custom-call(bf16[384,768]{1,0:T(8,128)(2,1)} %get-tuple-element.164.refs_0_, bf16[384,768]{1,0:T(8,128)(2,1)} %copy-done.47, bf16[384,576]{1,0:T(8,128)(2,1)S(1)} %get-tuple-element.204.refs_2_, bf16[384,576]{1,0:T(8,128)(2,1)} %copy-done.55, bf16[384,768]{1,0:T(8,128)(2,1)} %get-tuple-element.196.refs_4_, ...), custom_call_target="tpu_custom_call" | custom-call | flops 1500000000 | bytes 1000 | tf_op jit(solution)/shard_map/own_grads/pallas_call | solution.py:226
  259.8 6.2 %collective-permute-done.30.refs_4_ = bf16[384,768]{1,0:T(8,128)(2,1)S(1)} collective-permute-done((bf16[384,768]{1,0:T(8,128)(2,1)}, bf16[384,768]{1,0:T(8,128)(2,1)S(1)}, u32[]{:S(2)}, u32[]{:S(2)}) %collective-permute-start.30) | collective-permute-done | bytes 589856 | tf_op jit(solution)/shard_map/ppermute | solution.py:50
  266.2 8.1 %feed_back.3 = (bf16[384,1536]{1,0:T(8,128)(2,1)}, bf16[384,768]{1,0:T(8,128)(2,1)S(1)}, bf16[384,768]{1,0:T(8,128)(2,1)}, f32[1,768]{1,0:T(1,128)S(1)}, f32[384,768]{1,0:T(8,128)S(1)}, /*index=5*/f32[2,768]{1,0:T(2,128)S(1)}) custom-call(s32[16]{0:T(128)S(1)} %stack.23.refs_0_, f32[384,768]{1,0:T(8,128)} %get-tuple-element.169.refs_1_, ...), custom_call_target="tpu_custom_call" | custom-call | flops 3000000000 | bytes 1000 | tf_op jit(solution)/shard_map/feed_back/pallas_call | solution.py:226
  279.2 8.4 %feed_grads.3 = (bf16[768,1536]{1,0:T(8,128)(2,1)}, f32[2,768]{1,0:T(2,128)S(1)}) custom-call(s32[16]{0:T(128)S(1)} %stack.23.refs_0_, bf16[384,768]{1,0:T(8,128)(2,1)} %get-tuple-element.156.refs_1_, bf16[384,768]{1,0:T(8,128)(2,1)} %collective-permute-done.14.refs_2_, bf16[384,768]{1,0:T(8,128)(2,1)} %get-tuple-element.177.refs_3_, ...), custom_call_target="tpu_custom_call" | custom-call | flops 1500000000 | bytes 1000 | tf_op jit(solution)/shard_map/feed_grads/pallas_call | solution.py:226
  287.6 4.4 %collective-permute-done.33.refs_3_ = bf16[192,1536]{1,0:T(8,128)(2,1)S(1)} collective-permute-done((bf16[192,1536]{1,0:T(8,128)(2,1)}, bf16[192,1536]{1,0:T(8,128)(2,1)S(1)}, u32[]{:S(2)}, u32[]{:S(2)}) %collective-permute-start.33) | collective-permute-done | bytes 589856 | tf_op jit(solution)/shard_map/ppermute | solution.py:54
  294.5 5.0 %middle_back.3 = (f32[384,768]{1,0:T(8,128)}, bf16[384,768]{1,0:T(8,128)(2,1)}, bf16[6,384,128]{2,1,0:T(8,128)(2,1)S(1)}, f32[3,768]{1,0:T(4,128)S(1)}) custom-call(s32[16]{0:T(128)S(1)} %stack.23.refs_0_, f32[384,768]{1,0:T(8,128)} %get-tuple-element.216.refs_1_, f32[384,768]{1,0:T(8,128)S(1)} %copy-done.13, bf16[384,768]{1,0:T(8,128)(2,1)} %get-tuple-element.214.refs_3_, ...), custom_call_target="tpu_custom_call" | custom-call | flops 2000000000 | bytes 1000 | tf_op jit(solution)/shard_map/middle_back/pallas_call | solution.py:226
  300.1 8.4 %attend_back.6 = (f32[6,128,384]{2,1,0:T(8,128)S(1)}, bf16[384,768]{1,0:T(8,128)(2,1)S(1)}, bf16[384,768]{1,0:T(8,128)(2,1)}) custom-call(bf16[6,384,128]{2,1,0:T(8,128)(2,1)} %get-tuple-element.176.refs_0_, bf16[384,768]{1,0:T(8,128)(2,1)} %copy-done.6, bf16[384,768]{1,0:T(8,128)(2,1)} %copy-done.7, bf16[6,384,128]{2,1,0:T(8,128)(2,1)S(1)} %get-tuple-element.220.refs_3_), custom_call_target="tpu_custom_call" | custom-call | flops 4000000000 | bytes 1000 | tf_op jit(solution)/shard_map/attend_back/pallas_call | solution.py:226
  313.7 7.7 %attend_back.7 = (bf16[384,384]{1,0:T(8,128)(2,1)S(1)}, bf16[384,768]{1,0:T(8,128)(2,1)S(1)}, bf16[384,768]{1,0:T(8,128)(2,1)}) custom-call(bf16[6,384,128]{2,1,0:T(8,128)(2,1)S(1)} %copy-done.21, bf16[384,768]{1,0:T(8,128)(2,1)S(1)} %copy-done.5, bf16[384,768]{1,0:T(8,128)(2,1)S(1)} %collective-permute-done.9.refs_2_, ...), custom_call_target="tpu_custom_call" | custom-call | flops 4000000000 | bytes 1000 | tf_op jit(solution)/shard_map/attend_back/pallas_call | solution.py:226
  321.4 6.1 %collective-permute-done.37.refs_4_ = bf16[384,768]{1,0:T(8,128)(2,1)S(1)} collective-permute-done((bf16[384,768]{1,0:T(8,128)(2,1)}, bf16[384,768]{1,0:T(8,128)(2,1)S(1)}, u32[]{:S(2)}, u32[]{:S(2)}) %collective-permute-start.37) | collective-permute-done | bytes 589856 | tf_op jit(solution)/shard_map/ppermute | solution.py:54
  327.5 2.2 collective-permute-done.38.refs_3_
  329.7 4.8 %project_back.3 = (bf16[384,576]{1,0:T(8,128)(2,1)S(1)}, bf16[384,576]{1,0:T(8,128)(2,1)}, bf16[384,768]{1,0:T(8,128)(2,1)}, f32[2,576]{1,0:T(2,128)S(1)}, f32[2,768]{1,0:T(2,128)S(1)}) custom-call(s32[16]{0:T(128)S(1)} %stack.23.refs_0_, bf16[384,384]{1,0:T(8,128)(2,1)S(1)} %get-tuple-element.227.refs_1_, bf16[384,768]{1,0:T(8,128)(2,1)S(1)} %get-tuple-element.228.refs_2_, ...), custom_call_target="tpu_custom_call" | custom-call | flops 2000000000 | bytes 1000 | tf_op jit(solution)/shard_map/project_back/pallas_call | solution.py:226
  337.7 6.8 %project_grads.1 = (bf16[208,768]{1,0:T(8,128)(2,1)}, bf16[208,768]{1,0:T(8,128)(2,1)}, bf16[208,768]{1,0:T(8,128)(2,1)}, bf16[96,768]{1,0:T(8,128)(2,1)}, bf16[112,768]{1,0:T(8,128)(2,1)}) custom-call(s32[16]{0:T(128)S(1)} %stack.23.refs_0_, bf16[384,768]{1,0:T(8,128)(2,1)} %get-tuple-element.142.refs_1_, bf16[384,768]{1,0:T(8,128)(2,1)} %copy-done.45, ...), custom_call_target="tpu_custom_call" | custom-call | flops 1500000000 | bytes 1000 | tf_op jit(solution)/shard_map/project_grads/pallas_call | solution.py:226
  346.6 4.0 collective-permute-done.40.refs_3_
  350.6 2.5 input_back.1
  362.5 2.9 join_rows.2
  365.3 6.6 %collective-permute-done.44.refs_2_ = bf16[384,768]{1,0:T(8,128)(2,1)S(1)} collective-permute-done((bf16[384,768]{1,0:T(8,128)(2,1)S(1)}, bf16[384,768]{1,0:T(8,128)(2,1)S(1)}, u32[]{:S(2)}, u32[]{:S(2)}) %collective-permute-start.44) | collective-permute-done | bytes 589856 | tf_op jit(solution)/shard_map/ppermute | solution.py:50
  372.8 2.6 finish.1.refs_1_
  380.1 3.1 feed_out.1
  384.0 2.9 join_rows.3
  386.9 2.3 collective-permute-done.50.refs_1_
  393.3 2.8 project_out.1
  398.2 2.1 small_out.1
  (274 shorter events, 88.4 us)
Async XLA Ops:
  7.2 87.3 %all-gather.7.cloned.1.call-start = ((), (), s32[]{:S(2)}) async-start(), calls=%async_computation.6 | async-start | bytes 5308416 | tf_op jit(solution)/shard_map/all_gather | solution.py:98
  9.8 20.4 %collective-permute-start.2 = (bf16[208,768]{1,0:T(8,128)(2,1)}, bf16[208,768]{1,0:T(8,128)(2,1)S(1)}, u32[]{:S(2)}, u32[]{:S(2)}) collective-permute-start(bf16[208,768]{1,0:T(8,128)(2,1)} %pack_first.1.refs_2_.refs_5_.refs_8_.refs_6_), channel_id=1, source_target_pairs={{0,16},{8,24},{16,0},{24,8},{1,17},{9,25},{17,1},{25,9},{2,18},{10... | collective-permute-start | bytes 958472 | tf_op jit(solution)/shard_map/ppermute | solution.py:75
  13.9 16.3 %collective-permute-start.1 = (bf16[208,768]{1,0:T(8,128)(2,1)}, bf16[208,768]{1,0:T(8,128)(2,1)S(1)}, u32[]{:S(2)}, u32[]{:S(2)}) collective-permute-start(bf16[208,768]{1,0:T(8,128)(2,1)} %pack_first.1.refs_2_.refs_5_.refs_8_.refs_6_), channel_id=1, source_target_pairs={{0,24},{8,0},{16,8},{24,16},{1,25},{9,1},{17,9},{25,17},{2,26},{10... | collective-permute-start | bytes 958472 | tf_op jit(solution)/shard_map/ppermute | solution.py:75
  15.3 21.3 %collective-permute-start = (bf16[208,768]{1,0:T(8,128)(2,1)}, bf16[208,768]{1,0:T(8,128)(2,1)S(1)}, u32[]{:S(2)}, u32[]{:S(2)}) collective-permute-start(bf16[208,768]{1,0:T(8,128)(2,1)} %pack_first.1.refs_2_.refs_5_.refs_8_.refs_6_), channel_id=1, source_target_pairs={{0,8},{8,16},{16,24},{24,0},{1,9},{9,17},{17,25},{25,1},{2,10},{10... | collective-permute-start | bytes 958472 | tf_op jit(solution)/shard_map/ppermute | solution.py:75
  36.6 89.9 %all-gather.9.cloned.1.call-start = ((), (), s32[]{:S(2)}) async-start(), calls=%async_computation.7 | async-start | bytes 2654208 | tf_op jit(solution)/shard_map/all_gather | solution.py:98
  37.3 2.5 collective-permute-start.4
  45.1 2.3 collective-permute-start.9
  48.2 131.4 %all-gather.11.cloned.1.call-start = ((), (), s32[]{:S(2)}) async-start(), calls=%async_computation.8 | async-start | bytes 5308416 | tf_op jit(solution)/shard_map/all_gather | solution.py:98
  48.3 15.4 %collective-permute-start.8 = (bf16[384,768]{1,0:T(8,128)(2,1)S(1)}, bf16[384,768]{1,0:T(8,128)(2,1)S(1)}, u32[]{:S(2)}, u32[]{:S(2)}) collective-permute-start(bf16[384,768]{1,0:T(8,128)(2,1)S(1)} %copy-done.5), channel_id=1, source_target_pairs={{0,4},{4,0},{1,5},{5,1},{2,6},{6,2},{3,7},{7,3},{8,12},{12,8},{9,1... | collective-permute-start | bytes 1769480 | tf_op jit(solution)/shard_map/ppermute | solution.py:54
  77.7 198.2 %reduce-scatter.4.cloned.1.call-start = ((), (), s32[]{:S(2)}) async-start(), calls=%async_computation.3 | async-start | bytes 2949120 | tf_op jit(solution)/shard_map/reduce_scatter | solution.py:1060
  78.0 2.3 collective-permute-start.7
  78.2 15.8 %collective-permute-start.12 = (bf16[384,768]{1,0:T(8,128)(2,1)}, bf16[384,768]{1,0:T(8,128)(2,1)S(1)}, u32[]{:S(2)}, u32[]{:S(2)}) collective-permute-start(bf16[384,768]{1,0:T(8,128)(2,1)} %get-tuple-element.148.refs_2_), channel_id=1, source_target_pairs={{0,2},{2,0},{1,3},{3,1},{4,6},{6,4},{5,7},{7,5},{8,10},{10,8},{9,1... | collective-permute-start | bytes 1769480 | tf_op jit(solution)/shard_map/ppermute | solution.py:50
  102.4 2.6 collective-permute-start.13
  102.7 3.2 collective-permute-start.14
  102.9 23.6 %collective-permute-start.15 = (bf16[384,768]{1,0:T(8,128)(2,1)}, bf16[384,768]{1,0:T(8,128)(2,1)S(1)}, u32[]{:S(2)}, u32[]{:S(2)}) collective-permute-start(bf16[384,768]{1,0:T(8,128)(2,1)} %get-tuple-element.159.refs_4_), channel_id=1, source_target_pairs={{0,2},{2,0},{1,3},{3,1},{4,6},{6,4},{5,7},{7,5},{8,10},{10,8},{9,1... | collective-permute-start | bytes 1769480 | tf_op jit(solution)/shard_map/ppermute | solution.py:50
  131.5 2.3 collective-permute-start.18
  131.8 15.7 %collective-permute-start.17 = (bf16[384,768]{1,0:T(8,128)(2,1)}, bf16[384,768]{1,0:T(8,128)(2,1)S(1)}, u32[]{:S(2)}, u32[]{:S(2)}) collective-permute-start(bf16[384,768]{1,0:T(8,128)(2,1)} %get-tuple-element.166.refs_1_), channel_id=1, source_target_pairs={{0,4},{4,0},{1,5},{5,1},{2,6},{6,2},{3,7},{7,3},{8,12},{12,8},{9,1... | collective-permute-start | bytes 1769480 | tf_op jit(solution)/shard_map/ppermute | solution.py:54
  147.6 14.7 %collective-permute-start.16 = (bf16[384,768]{1,0:T(8,128)(2,1)S(1)}, bf16[384,768]{1,0:T(8,128)(2,1)S(1)}, u32[]{:S(2)}, u32[]{:S(2)}) collective-permute-start(bf16[384,768]{1,0:T(8,128)(2,1)S(1)} %copy-done.46), channel_id=1, source_target_pairs={{0,1},{1,0},{2,3},{3,2},{4,5},{5,4},{6,7},{7,6},{8,9},{9,8},{10,11... | collective-permute-start | bytes 1769480 | tf_op jit(solution)/shard_map/ppermute | solution.py:46
  160.7 19.0 %collective-permute-start.21 = (bf16[384,768]{1,0:T(8,128)(2,1)}, bf16[384,768]{1,0:T(8,128)(2,1)S(1)}, u32[]{:S(2)}, u32[]{:S(2)}) collective-permute-start(bf16[384,768]{1,0:T(8,128)(2,1)} %get-tuple-element.170.refs_2_), channel_id=1, source_target_pairs={{0,2},{2,0},{1,3},{3,1},{4,6},{6,4},{5,7},{7,5},{8,10},{10,8},{9,1... | collective-permute-start | bytes 1769480 | tf_op jit(solution)/shard_map/ppermute | solution.py:50
  194.9 4.6 %collective-permute-start.24 = (bf16[384,1536]{1,0:T(8,128)(2,1)}, bf16[384,1536]{1,0:T(8,128)(2,1)S(1)}, u32[]{:S(2)}, u32[]{:S(2)}) collective-permute-start(bf16[384,1536]{1,0:T(8,128)(2,1)} %get-tuple-element.183.refs_5_), channel_id=1, source_target_pairs={{0,1},{1,0},{2,3},{3,2},{4,5},{5,4},{6,7},{7,6},{8,9},{9,8},{10,11... | collective-permute-start | bytes 3538952 | tf_op jit(solution)/shard_map/ppermute | solution.py:46
  195.2 3.4 collective-permute-start.23
  195.5 4.0 collective-permute-start.22
  195.8 15.7 %collective-permute-start.25 = (bf16[384,768]{1,0:T(8,128)(2,1)}, bf16[384,768]{1,0:T(8,128)(2,1)S(1)}, u32[]{:S(2)}, u32[]{:S(2)}) collective-permute-start(bf16[384,768]{1,0:T(8,128)(2,1)} %get-tuple-element.187.refs_3_), channel_id=1, source_target_pairs={{0,2},{2,0},{1,3},{3,1},{4,6},{6,4},{5,7},{7,5},{8,10},{10,8},{9,1... | collective-permute-start | bytes 1769480 | tf_op jit(solution)/shard_map/ppermute | solution.py:50
  211.5 100.9 %reduce-scatter.6.cloned.1.call-start = ((), (), s32[]{:S(2)}) async-start(), calls=%async_computation.4 | async-start | bytes 1474560 | tf_op jit(solution)/shard_map/reduce_scatter | solution.py:1060
  224.8 2.3 collective-permute-start.26
  224.9 4.8 %collective-permute-start.27 = (bf16[384,768]{1,0:T(8,128)(2,1)S(1)}, bf16[384,768]{1,0:T(8,128)(2,1)S(1)}, u32[]{:S(2)}, u32[]{:S(2)}) collective-permute-start(bf16[384,768]{1,0:T(8,128)(2,1)S(1)} %copy-done.48), channel_id=1, source_target_pairs={{0,1},{1,0},{2,3},{3,2},{4,5},{5,4},{6,7},{7,6},{8,9},{9,8},{10,11... | collective-permute-start | bytes 1769480 | tf_op jit(solution)/shard_map/ppermute | solution.py:46
  228.1 15.6 %collective-permute-start.28 = (bf16[384,768]{1,0:T(8,128)(2,1)}, bf16[384,768]{1,0:T(8,128)(2,1)S(1)}, u32[]{:S(2)}, u32[]{:S(2)}) collective-permute-start(bf16[384,768]{1,0:T(8,128)(2,1)} %cross_sum.2), channel_id=1, source_target_pairs={{0,4},{4,0},{1,5},{5,1},{2,6},{6,2},{3,7},{7,3},{8,12},{12,8},{9,1... | collective-permute-start | bytes 1769480 | tf_op jit(solution)/shard_map/ppermute | solution.py:54
  250.3 15.6 %collective-permute-start.30 = (bf16[384,768]{1,0:T(8,128)(2,1)}, bf16[384,768]{1,0:T(8,128)(2,1)S(1)}, u32[]{:S(2)}, u32[]{:S(2)}) collective-permute-start(bf16[384,768]{1,0:T(8,128)(2,1)} %get-tuple-element.202.refs_3_), channel_id=1, source_target_pairs={{0,2},{2,0},{1,3},{3,1},{4,6},{6,4},{5,7},{7,5},{8,10},{10,8},{9,1... | collective-permute-start | bytes 1769480 | tf_op jit(solution)/shard_map/ppermute | solution.py:50
  265.9 93.1 %reduce-scatter.8.cloned.1.call-start = ((), (), s32[]{:S(2)}) async-start(), calls=%async_computation.5 | async-start | bytes 2949120 | tf_op jit(solution)/shard_map/reduce_scatter | solution.py:1060
  276.0 3.2 collective-permute-start.32
  276.0 16.0 %collective-permute-start.33 = (bf16[192,1536]{1,0:T(8,128)(2,1)}, bf16[192,1536]{1,0:T(8,128)(2,1)S(1)}, u32[]{:S(2)}, u32[]{:S(2)}) collective-permute-start(bf16[192,1536]{1,0:T(8,128)(2,1)} %reduce-scatter.4.cloned.1.call-done.refs_2_), channel_id=1, source_target_pairs={{0,4},{4,0},{1,5},{5,1},{2,6},{6,2},{3,7},{7,3},{8,12},{12,8},{9,1... | collective-permute-start | bytes 1769480 | tf_op jit(solution)/shard_map/ppermute | solution.py:54
  277.5 15.7 %collective-permute-start.34 = (bf16[384,768]{1,0:T(8,128)(2,1)}, bf16[384,768]{1,0:T(8,128)(2,1)S(1)}, u32[]{:S(2)}, u32[]{:S(2)}) collective-permute-start(bf16[384,768]{1,0:T(8,128)(2,1)} %get-tuple-element.214.refs_3_), channel_id=1, source_target_pairs={{0,2},{2,0},{1,3},{3,1},{4,6},{6,4},{5,7},{7,5},{8,10},{10,8},{9,1... | collective-permute-start | bytes 1769480 | tf_op jit(solution)/shard_map/ppermute | solution.py:50
  308.6 2.3 collective-permute-start.35
  308.6 3.8 collective-permute-start.36
  311.9 15.6 %collective-permute-start.37 = (bf16[384,768]{1,0:T(8,128)(2,1)}, bf16[384,768]{1,0:T(8,128)(2,1)S(1)}, u32[]{:S(2)}, u32[]{:S(2)}) collective-permute-start(bf16[384,768]{1,0:T(8,128)(2,1)} %cross_sum.3), channel_id=1, source_target_pairs={{0,4},{4,0},{1,5},{5,1},{2,6},{6,2},{3,7},{7,3},{8,12},{12,8},{9,1... | collective-permute-start | bytes 1769480 | tf_op jit(solution)/shard_map/ppermute | solution.py:54
  334.8 15.8 %collective-permute-start.40 = (bf16[384,768]{1,0:T(8,128)(2,1)}, bf16[384,768]{1,0:T(8,128)(2,1)S(1)}, u32[]{:S(2)}, u32[]{:S(2)}) collective-permute-start(bf16[384,768]{1,0:T(8,128)(2,1)} %get-tuple-element.248.refs_2_), channel_id=1, source_target_pairs={{0,2},{2,0},{1,3},{3,1},{4,6},{6,4},{5,7},{7,5},{8,10},{10,8},{9,1... | collective-permute-start | bytes 1769480 | tf_op jit(solution)/shard_map/ppermute | solution.py:50
  336.3 16.9 %collective-permute-start.41 = (bf16[192,768]{1,0:T(8,128)(2,1)S(1)}, bf16[192,768]{1,0:T(8,128)(2,1)S(1)}, u32[]{:S(2)}, u32[]{:S(2)}) collective-permute-start(bf16[192,768]{1,0:T(8,128)(2,1)S(1)} %copy-done.64), channel_id=1, source_target_pairs={{0,4},{4,0},{1,5},{5,1},{2,6},{6,2},{3,7},{7,3},{8,12},{12,8},{9,1... | collective-permute-start | bytes 884744 | tf_op jit(solution)/shard_map/ppermute | solution.py:54
  344.5 10.2 %collective-permute-start.43 = (bf16[112,768]{1,0:T(8,128)(2,1)}, bf16[112,768]{1,0:T(8,128)(2,1)S(1)}, u32[]{:S(2)}, u32[]{:S(2)}) collective-permute-start(bf16[112,768]{1,0:T(8,128)(2,1)} %get-tuple-element.254), channel_id=1, source_target_pairs={{0,24},{8,0},{16,8},{24,16},{1,25},{9,1},{17,9},{25,17},{2,26},{10... | collective-permute-start | bytes 516104 | tf_op jit(solution)/shard_map/ppermute | solution.py:1115
  345.5 9.2 %collective-permute-start.42 = (bf16[96,768]{1,0:T(8,128)(2,1)}, bf16[96,768]{1,0:T(8,128)(2,1)S(1)}, u32[]{:S(2)}, u32[]{:S(2)}) collective-permute-start(bf16[96,768]{1,0:T(8,128)(2,1)} %get-tuple-element.253), channel_id=1, source_target_pairs={{0,8},{8,16},{16,24},{24,0},{1,9},{9,17},{17,25},{25,1},{2,10},{10... | collective-permute-start | bytes 442376 | tf_op jit(solution)/shard_map/ppermute | solution.py:1115
  353.1 8.5 %collective-permute-start.46 = (bf16[384,768]{1,0:T(8,128)(2,1)}, bf16[384,768]{1,0:T(8,128)(2,1)S(1)}, u32[]{:S(2)}, u32[]{:S(2)}) collective-permute-start(bf16[384,768]{1,0:T(8,128)(2,1)} %get-tuple-element.249.refs_1_), channel_id=1, source_target_pairs={{0,1},{1,0},{2,3},{3,2},{4,5},{5,4},{6,7},{7,6},{8,9},{9,8},{10,11... | collective-permute-start | bytes 1769480 | tf_op jit(solution)/shard_map/ppermute | solution.py:46
  357.5 14.5 %collective-permute-start.44 = (bf16[384,768]{1,0:T(8,128)(2,1)S(1)}, bf16[384,768]{1,0:T(8,128)(2,1)S(1)}, u32[]{:S(2)}, u32[]{:S(2)}) collective-permute-start(bf16[384,768]{1,0:T(8,128)(2,1)S(1)} %copy-done.37), channel_id=1, source_target_pairs={{0,2},{2,0},{1,3},{3,1},{4,6},{6,4},{5,7},{7,5},{8,10},{10,8},{9,1... | collective-permute-start | bytes 1769480 | tf_op jit(solution)/shard_map/ppermute | solution.py:50
  359.0 16.4 %collective-permute-start.45 = (bf16[192,1536]{1,0:T(8,128)(2,1)}, bf16[192,1536]{1,0:T(8,128)(2,1)S(1)}, u32[]{:S(2)}, u32[]{:S(2)}) collective-permute-start(bf16[192,1536]{1,0:T(8,128)(2,1)} %reduce-scatter.8.cloned.1.call-done.refs_0_), channel_id=1, source_target_pairs={{0,4},{4,0},{1,5},{5,1},{2,6},{6,2},{3,7},{7,3},{8,12},{12,8},{9,1... | collective-permute-start | bytes 1769480 | tf_op jit(solution)/shard_map/ppermute | solution.py:54
  359.6 15.9 %collective-permute-start.48 = (bf16[208,768]{1,0:T(8,128)(2,1)}, bf16[208,768]{1,0:T(8,128)(2,1)S(1)}, u32[]{:S(2)}, u32[]{:S(2)}) collective-permute-start(bf16[208,768]{1,0:T(8,128)(2,1)} %get-tuple-element.260), channel_id=1, source_target_pairs={{0,24},{8,0},{16,8},{24,16},{1,25},{9,1},{17,9},{25,17},{2,26},{10... | collective-permute-start | bytes 958472 | tf_op jit(solution)/shard_map/ppermute | solution.py:1118
  361.4 14.1 %collective-permute-start.47 = (bf16[208,768]{1,0:T(8,128)(2,1)}, bf16[208,768]{1,0:T(8,128)(2,1)S(1)}, u32[]{:S(2)}, u32[]{:S(2)}) collective-permute-start(bf16[208,768]{1,0:T(8,128)(2,1)} %get-tuple-element.255), channel_id=1, source_target_pairs={{0,8},{8,16},{16,24},{24,0},{1,9},{9,17},{17,25},{25,1},{2,10},{10... | collective-permute-start | bytes 958472 | tf_op jit(solution)/shard_map/ppermute | solution.py:1118
  378.9 4.2 %collective-permute-start.49 = (bf16[384,768]{1,0:T(8,128)(2,1)S(1)}, bf16[384,768]{1,0:T(8,128)(2,1)S(1)}, u32[]{:S(2)}, u32[]{:S(2)}) collective-permute-start(bf16[384,768]{1,0:T(8,128)(2,1)S(1)} %copy-done.30), channel_id=1, source_target_pairs={{0,1},{1,0},{2,3},{3,2},{4,5},{5,4},{6,7},{7,6},{8,9},{9,8},{10,11... | collective-permute-start | bytes 1769480 | tf_op jit(solution)/shard_map/ppermute | solution.py:46
  379.0 10.2 %collective-permute-start.50 = (bf16[208,768]{1,0:T(8,128)(2,1)}, bf16[208,768]{1,0:T(8,128)(2,1)S(1)}, u32[]{:S(2)}, u32[]{:S(2)}) collective-permute-start(bf16[208,768]{1,0:T(8,128)(2,1)} %sum_blocks.1.refs_0_), channel_id=1, source_target_pairs={{0,4},{4,0},{1,5},{5,1},{2,6},{6,2},{3,7},{7,3},{8,12},{12,8},{9,1... | collective-permute-start | bytes 958472 | tf_op jit(solution)/shard_map/ppermute | solution.py:54
  391.6 4.5 %collective-permute-start.51 = (f32[16,768]{1,0:T(8,128)}, f32[16,768]{1,0:T(8,128)S(1)}, u32[]{:S(2)}, u32[]{:S(2)}) collective-permute-start(f32[16,768]{1,0:T(8,128)} %small_sum.1.refs_1_), channel_id=1, source_target_pairs={{0,2},{2,0},{1,3},{3,1},{4,6},{6,4},{5,7},{7,5},{8,10},{10,8},{9,1... | collective-permute-start | bytes 147464 | tf_op jit(solution)/shard_map/ppermute | solution.py:50
  393.3 3.4 collective-permute-start.52
  (85 other events, 483.1 us)
Sparse Core Ops, SparseCore 0:
  36.7 57.6 all-gather.6
  96.1 30.3 all-gather.8
  128.8 50.8 all-gather.10
  211.6 46.8 reduce-scatter.3
  266.1 27.9 reduce-scatter.5
  299.6 45.8 reduce-scatter.7

commit v5 on v4

--- a/solution.py
+++ b/solution.py
@@ -35,7 +35,7 @@
 }
 WIDE = 128
 TAIL = 16
-COST = 500_000_000
+COST = 200_000_000
 
 
 def mm(a, b, dims=NN):
@@ -620,19 +620,22 @@
             g2 = g.astype(bf16)
             swap_o[:, :D] = g2
             sums_o[...] = jnp.sum(g2.astype(f32), 0, keepdims=True)
-            part, dus = None, []
-            for s in range(2):
-                copies[s].wait()
-                dh = mm(g2, weight(w_s, s, F, 2 * F))
-                du = (gp_r[s][...].astype(f32) * dh).astype(bf16)
-                dus.append(du)
-                t = mm(du, weight(w_s, s, 0, F), NT)
+            wait_all(copies)
+            odd = scal_r[8] == 1
+            part = None
+            for k in range(2):
+                slot = scal_r[8] if k else 1 - scal_r[8]
+                first, second = (gp_r[1][...], gp_r[0][...]) if k else (gp_r[0][...], gp_r[1][...])
+                slope = jnp.where(odd, first, second).astype(f32)
+                du = (slope * mm(g2, weight(w_s, slot, F, 2 * F))).astype(bf16)
+                if k == 0:
+                    swap_o[:, D:] = du
+                    send(swap_o)
+                else:
+                    du_o[...] = du
+                t = mm(du, weight(w_s, slot, 0, F), NT)
                 part = t if part is None else part + t
             part_o[...] = part.astype(bf16)
-            send(part_o)
-            odd = scal_r[8] == 1
-            du_o[...] = jnp.where(odd, dus[1], dus[0])
-            swap_o[:, D:] = jnp.where(odd, dus[0], dus[1])
 
         ins = [grad] if before is None else [Far(b) for b in before[:3]] + list(before[3:])
         ins += [Far(gp[0]), Far(gp[1])]
@@ -712,7 +715,7 @@
             4,
         )
 
-    def attend_back(qa, kvs, da, before=None):
+    def attend_back(qa, kvs, da, before=None, ahead=False):
         K = 2 * R
 
         def kernel(qa_r, kv0, kv1, da_r, *refs):
@@ -754,7 +757,9 @@
             if before is not None:
                 dq_o[...] = jnp.concatenate([dq_s[0][j][:, :HD] for j in range(2 * H)], 1)
 
-        ins = [Far(qa)] + [Far(a) for a in kvs] + [da] if before is None else [qa] + list(kvs) + [da]
+        ins = [qa] + list(kvs) + [da]
+        if before is None and not ahead:
+            ins = [Far(a) for a in ins[:3]] + [da]
         outs = [((R, 4 * A), bf16), ((R, 4 * A), bf16, FAR)]
         scratch = [pltpu.VMEM((2 * H, K, WIDE), bf16)] * 4
         if before is None:
@@ -1088,7 +1093,7 @@
             if layer == 0:
                 part_b_sum = scatter(after(grad_b, da))
             g1_r = core_swap(g1)
-            dqt, own, snd = k["attend_back"](qa, kvs[2:], da)
+            dqt, own, snd = k["attend_back"](qa, kvs[2:], da, ahead=layer > 0)
             cross = k["cross_sum"](own, core_swap(snd))
             dqt = after(dqt, cross, g1_r, *([part_a_sum] if layer == 0 else []))
             cross = y_swap(cross)

time: 414 us -> 411 us (level)
    unnamed x147 -> x155, local copies, waits for them, and re-layouts: 19.3 us -> 19.5 us
where the time goes in v5:
time: 411 us; the launch traced here: 405 us
  Pallas kernels  181 us (44%)
  waiting for transfers between devices  144 us (35%)
  starting transfers between devices  39.5 us (10%)
  local copies, waits for them, and re-layouts  23 us (6%)
  between operations  15.6 us (4%)
    pallas_call x35, Pallas kernels, run(): pl.pallas_call(wrapped, out_shape=shapes, in_specs=specs, out_specs=[any_...  181 us
    all_gather x3, waiting for transfers between devices, __init__(): whole = lax.all_gather(x, ('shard', 'tc'), axis=0, tiled=False)  36.7 us
    ppermute x9, waiting for transfers between devices, x_swap(): return lax.ppermute(x, 'tx', [(0, 1), (1, 0)])  32.9 us
    ppermute x8, waiting for transfers between devices, y_swap(): return lax.ppermute(x, 'ctx', [(0, 1), (1, 0)])  32.7 us
    ppermute x30, waiting for transfers between devices, core_swap(): return lax.ppermute(x, 'tc', [(0, 1), (1, 0)])  21.9 us
    unnamed x155, local copies, waits for them, and re-layouts  19.5 us
    ppermute x3, waiting for transfers between devices, __init__(): self.mine = [x] + [lax.ppermute(x, 'shard', ring(s)) for s in (1, 3, 2)]  18.3 us
    ppermute x9, starting transfers between devices, x_swap(): return lax.ppermute(x, 'tx', [(0, 1), (1, 0)])  13.8 us
  transfers between devices with their start and end apart: 60, of which 39 were waited for; matrix products, arithmetic and copies ran while one was open for 1% of the time, Pallas kernels for 39%

profile of v5, /device:TPU:0, one launch (start us, length us, event | category | flops | bytes accessed | tf_op | source)
XLA Modules:
  0.0 405.2 jit_solution(8435323122924323906)
XLA Ops:
  7.3 2.6 pack_first.1.refs_2_.refs_5_.refs_8_.refs_6_
  9.8 4.1 %collective-permute-start.2 = (bf16[208,768]{1,0:T(8,128)(2,1)}, bf16[208,768]{1,0:T(8,128)(2,1)S(1)}, u32[]{:S(2)}, u32[]{:S(2)}) collective-permute-start(bf16[208,768]{1,0:T(8,128)(2,1)} %pack_first.1.refs_2_.refs_5_.refs_8_.refs_6_), channel_id=1, source_target_pairs={{0,16},{8,24},{16,0},{24,8},{1,17},{9,25},{17,1},{25,9},{2,18},{10... | collective-permute-start | bytes 958472 | tf_op jit(solution)/shard_map/ppermute | solution.py:75
  18.3 11.9 %collective-permute-done.2.refs_5_.refs_8_.refs_11_.refs_9_ = bf16[208,768]{1,0:T(8,128)(2,1)S(1)} collective-permute-done((bf16[208,768]{1,0:T(8,128)(2,1)}, bf16[208,768]{1,0:T(8,128)(2,1)S(1)}, u32[]{:S(2)}, u32[]{:S(2)}) %collective-permute-start.2) | collective-permute-done | bytes 319520 | tf_op jit(solution)/shard_map/ppermute | solution.py:75
  30.3 6.3 %collective-permute-done.refs_3_.refs_6_.refs_9_.refs_7_ = bf16[208,768]{1,0:T(8,128)(2,1)S(1)} collective-permute-done((bf16[208,768]{1,0:T(8,128)(2,1)}, bf16[208,768]{1,0:T(8,128)(2,1)S(1)}, u32[]{:S(2)}, u32[]{:S(2)}) %collective-permute-start) | collective-permute-done | bytes 319520 | tf_op jit(solution)/shard_map/ppermute | solution.py:75
  39.9 5.2 %project.2 = (bf16[384,768]{1,0:T(8,128)(2,1)}, bf16[384,384]{1,0:T(8,128)(2,1)S(1)}, bf16[384,768]{1,0:T(8,128)(2,1)}, f32[16,768]{1,0:T(8,128)S(1)}, f32[4,576...) custom-call(s32[16]{0:T(128)S(1)} %stack.23.refs_0_, ...), custom_call_target="tpu_custom_call" | custom-call | flops 700000000 | bytes 1000 | tf_op jit(solution)/shard_map/project/pallas_call | solution.py:226
  50.0 5.7 %attend_near.2.refs_4_ = f32[6,384,128]{2,1,0:T(8,128)S(1)} custom-call(bf16[384,384]{1,0:T(8,128)(2,1)S(1)} %get-tuple-element.143.refs_0_.refs_1_, bf16[384,768]{1,0:T(8,128)(2,1)S(1)} %copy-done.15, bf16[384,768]{1,0:T(8,128)(2,1)S(1)} %collective-permute-done.9.refs_2_), custom_call_target="tpu_custom_call" | custom-call | flops 1200000000 | bytes 1000 | tf_op jit(solution)/shard_map/attend_near/pallas_call | solution.py:226
  56.7 7.1 %collective-permute-done.8.refs_2_.refs_1_ = bf16[384,768]{1,0:T(8,128)(2,1)S(1)} collective-permute-done((bf16[384,768]{1,0:T(8,128)(2,1)S(1)}, bf16[384,768]{1,0:T(8,128)(2,1)S(1)}, u32[]{:S(2)}, u32[]{:S(2)}) %collective-permute-start.8) | collective-permute-done | bytes 589856 | tf_op jit(solution)/shard_map/ppermute | solution.py:54
  67.2 10.7 %attend_far.2 = (bf16[384,192]{1,0:T(8,128)(2,1)}, bf16[384,192]{1,0:T(8,128)(2,1)}, bf16[6,384,128]{2,1,0:T(8,128)(2,1)}, bf16[384,192]{1,0:T(8,128)(2,1)}, bf1...) custom-call(s32[16]{0:T(128)S(1)} %stack.23.refs_0_, bf16[384,384]{1,0:T(8,128)(2,1)S(1)} %get-tuple-element.143.refs_0_.refs_1_, ...), custom_call_target="tpu_custom_call" | custom-call | flops 1600000000 | bytes 1000 | tf_op jit(solution)/shard_map/attend_far/pallas_call | solution.py:226
  81.7 12.5 %collective-permute-done.12.refs_3_ = bf16[384,768]{1,0:T(8,128)(2,1)S(1)} collective-permute-done((bf16[384,768]{1,0:T(8,128)(2,1)}, bf16[384,768]{1,0:T(8,128)(2,1)S(1)}, u32[]{:S(2)}, u32[]{:S(2)}) %collective-permute-start.12) | collective-permute-done | bytes 589856 | tf_op jit(solution)/shard_map/ppermute | solution.py:50
  94.5 7.9 %feed.2 = (f32[384,768]{1,0:T(8,128)}, bf16[384,768]{1,0:T(8,128)(2,1)}, bf16[384,768]{1,0:T(8,128)(2,1)}, bf16[384,768]{1,0:T(8,128)(2,1)}, bf16[384,768]{1,0:T...) custom-call(s32[16]{0:T(128)S(1)} %stack.23.refs_0_, ...), custom_call_target="tpu_custom_call" | custom-call | flops 1200000000 | bytes 1000 | tf_op jit(solution)/shard_map/feed/pallas_call | solution.py:226
  105.8 20.7 %all-gather.9.cloned.1.call-done = bf16[1536,768]{1,0:T(8,128)(2,1)} async-done(((bf16[192,768]{1,0:T(8,128)(2,1)}), bf16[1536,768]{1,0:T(8,128)(2,1)}) %all-gather.9.cloned.1.call-update) | async-done | bytes 2359312 | tf_op jit(solution)/shard_map/all_gather | solution.py:98
  126.5 5.0 %project.3 = (bf16[384,768]{1,0:T(8,128)(2,1)}, bf16[384,384]{1,0:T(8,128)(2,1)S(1)}, bf16[384,768]{1,0:T(8,128)(2,1)}, f32[384,768]{1,0:T(8,128)}) custom-call(s32[16]{0:T(128)S(1)} %stack.23.refs_0_, f32[384,768]{1,0:T(8,128)} %get-tuple-element.216.refs_1_, f32[16,768]{1,0:T(8,128)S(1)} %get-tuple-element.149.refs_4_.refs_2_.refs_5_.refs_3_, ...), custom_call_target="tpu_custom_call" | custom-call | flops 700000000 | bytes 1000 | tf_op jit(solution)/shard_map/project/pallas_call | solution.py:226
  134.9 5.7 %attend_near.3.refs_4_ = f32[6,384,128]{2,1,0:T(8,128)S(1)} custom-call(bf16[384,384]{1,0:T(8,128)(2,1)S(1)} %get-tuple-element.165.refs_0_.refs_1_, bf16[384,768]{1,0:T(8,128)(2,1)S(1)} %copy-done.20, bf16[384,768]{1,0:T(8,128)(2,1)S(1)} %collective-permute-done.18.refs_2_), custom_call_target="tpu_custom_call" | custom-call | flops 1200000000 | bytes 1000 | tf_op jit(solution)/shard_map/attend_near/pallas_call | solution.py:226
  140.7 6.9 %collective-permute-done.17.refs_2_.refs_1_ = bf16[384,768]{1,0:T(8,128)(2,1)S(1)} collective-permute-done((bf16[384,768]{1,0:T(8,128)(2,1)}, bf16[384,768]{1,0:T(8,128)(2,1)S(1)}, u32[]{:S(2)}, u32[]{:S(2)}) %collective-permute-start.17) | collective-permute-done | bytes 589856 | tf_op jit(solution)/shard_map/ppermute | solution.py:54
  149.6 11.1 %attend_far.3 = (bf16[384,192]{1,0:T(8,128)(2,1)}, bf16[384,192]{1,0:T(8,128)(2,1)}, bf16[6,384,128]{2,1,0:T(8,128)(2,1)}, bf16[384,192]{1,0:T(8,128)(2,1)}, bf1...) custom-call(s32[16]{0:T(128)S(1)} %stack.23.refs_0_, bf16[384,384]{1,0:T(8,128)(2,1)S(1)} %get-tuple-element.165.refs_0_.refs_1_, ...), custom_call_target="tpu_custom_call" | custom-call | flops 1600000000 | bytes 1000 | tf_op jit(solution)/shard_map/attend_far/pallas_call | solution.py:226
  163.9 15.8 %all-gather.11.cloned.1.call-done = bf16[1536,1536]{1,0:T(8,128)(2,1)} async-done(((bf16[192,1536]{1,0:T(8,128)(2,1)}), bf16[1536,1536]{1,0:T(8,128)(2,1)}) %all-gather.11.cloned.1.call-update) | async-done | bytes 4718608 | tf_op jit(solution)/shard_map/all_gather | solution.py:98
  179.6 8.1 %feed.3 = (f32[384,768]{1,0:T(8,128)}, bf16[384,768]{1,0:T(8,128)(2,1)}, bf16[384,768]{1,0:T(8,128)(2,1)}, bf16[384,768]{1,0:T(8,128)(2,1)}, bf16[384,768]{1,0:T...) custom-call(s32[16]{0:T(128)S(1)} %stack.23.refs_0_, f32[384,768]{1,0:T(8,128)} %get-tuple-element.169.refs_1_, ...), custom_call_target="tpu_custom_call" | custom-call | flops 1200000000 | bytes 1000 | tf_op jit(solution)/shard_map/feed/pallas_call | solution.py:226
  187.8 6.8 %feed_back.2 = (bf16[384,1536]{1,0:T(8,128)(2,1)}, bf16[384,768]{1,0:T(8,128)(2,1)S(1)}, bf16[384,768]{1,0:T(8,128)(2,1)}, f32[1,768]{1,0:T(1,128)S(1)}) custom-call(s32[16]{0:T(128)S(1)} %stack.23.refs_0_, bf16[384,768]{1,0:T(8,128)(2,1)S(1)} %dynamic-slice_bitcast_fusion.refs_1_.refs_2_, bf16[384,768]{1,0:T(8,128)(2,1)} %get-tuple-element.181.refs_2_, ...), custom_call_target="tpu_custom_call" | custom-call | flops 1200000000 | bytes 1000 | tf_op jit(solution)/shard_map/feed_back/pallas_call | solution.py:226
  200.4 8.4 %feed_grads.2 = (bf16[768,1536]{1,0:T(8,128)(2,1)}, f32[2,768]{1,0:T(2,128)S(1)}) custom-call(s32[16]{0:T(128)S(1)} %stack.23.refs_0_, bf16[384,768]{1,0:T(8,128)(2,1)} %get-tuple-element.178.refs_1_, bf16[384,768]{1,0:T(8,128)(2,1)} %copy-done.59, bf16[384,768]{1,0:T(8,128)(2,1)} %get-tuple-element.179.refs_3_, bf16[384,768]{1,0:T(8,128)(2,1)} %copy-done.58, ...), custom_call_target="tpu_custom_call" | custom-call | flops 600000000 | bytes 1000 | tf_op jit(solution)/shard_map/feed_grads/pallas_call | solution.py:226
  208.8 2.3 collective-permute-done.25.refs_4_
  211.4 4.8 %middle_back.2 = (f32[384,768]{1,0:T(8,128)}, bf16[384,768]{1,0:T(8,128)(2,1)}, bf16[6,384,128]{2,1,0:T(8,128)(2,1)S(1)}, f32[3,768]{1,0:T(4,128)S(1)}) custom-call(s32[16]{0:T(128)S(1)} %stack.23.refs_0_, f32[384,768]{1,0:T(8,128)} %get-tuple-element.186.refs_1_.refs_0_, bf16[384,768]{1,0:T(8,128)(2,1)S(1)} %dynamic-slice_bitcast_fusion.refs_1_.refs_2_, ...), custom_call_target="tpu_custom_call" | custom-call | flops 800000000 | bytes 1000 | tf_op jit(solution)/shard_map/middle_back/pallas_call | solution.py:226
  216.2 6.9 %attend_back.4 = (f32[6,128,384]{2,1,0:T(8,128)S(1)}, bf16[384,768]{1,0:T(8,128)(2,1)S(1)}, bf16[384,768]{1,0:T(8,128)(2,1)}) custom-call(bf16[6,384,128]{2,1,0:T(8,128)(2,1)S(1)} %copy-done.31, bf16[384,768]{1,0:T(8,128)(2,1)S(1)} %copy-done.23, bf16[384,768]{1,0:T(8,128)(2,1)S(1)} %copy-done.25, bf16[6,384,128]{2,1,0:T(8,128)(2,1)S(1)} %get-tuple-element.192.refs_3_), custom_call_target="tpu_custom_call" | custom-call | flops 1600000000 | bytes 1000 | tf_op jit(solution)/shard_map/attend_back/pallas_call | solution.py:226
  227.9 7.6 %attend_back.5 = (bf16[384,384]{1,0:T(8,128)(2,1)S(1)}, bf16[384,768]{1,0:T(8,128)(2,1)S(1)}, bf16[384,768]{1,0:T(8,128)(2,1)}) custom-call(bf16[6,384,128]{2,1,0:T(8,128)(2,1)S(1)} %copy-done.31, bf16[384,768]{1,0:T(8,128)(2,1)S(1)} %copy-done.21, bf16[384,768]{1,0:T(8,128)(2,1)S(1)} %collective-permute-done.18.refs_2_, ...), custom_call_target="tpu_custom_call" | custom-call | flops 1600000000 | bytes 1000 | tf_op jit(solution)/shard_map/attend_back/pallas_call | solution.py:226
  235.5 6.5 %collective-permute-done.28.refs_4_ = bf16[384,768]{1,0:T(8,128)(2,1)S(1)} collective-permute-done((bf16[384,768]{1,0:T(8,128)(2,1)}, bf16[384,768]{1,0:T(8,128)(2,1)S(1)}, u32[]{:S(2)}, u32[]{:S(2)}) %collective-permute-start.28) | collective-permute-done | bytes 589856 | tf_op jit(solution)/shard_map/ppermute | solution.py:54
  242.0 2.2 collective-permute-done.29.refs_3_
  244.2 4.3 %project_back.2 = (bf16[384,576]{1,0:T(8,128)(2,1)S(1)}, bf16[384,576]{1,0:T(8,128)(2,1)}, bf16[384,768]{1,0:T(8,128)(2,1)}, f32[2,576]{1,0:T(2,128)S(1)}) custom-call(s32[16]{0:T(128)S(1)} %stack.23.refs_0_, bf16[384,384]{1,0:T(8,128)(2,1)S(1)} %get-tuple-element.198.refs_1_, bf16[384,768]{1,0:T(8,128)(2,1)S(1)} %get-tuple-element.199.refs_2_, ...), custom_call_target="tpu_custom_call" | custom-call | flops 800000000 | bytes 1000 | tf_op jit(solution)/shard_map/project_back/pallas_call | solution.py:226
  253.0 5.0 %own_grads.1 = bf16[4,192,768]{2,1,0:T(8,128)(2,1)} custom-call(bf16[384,768]{1,0:T(8,128)(2,1)} %get-tuple-element.164.refs_0_, bf16[384,768]{1,0:T(8,128)(2,1)} %copy-done.46, bf16[384,576]{1,0:T(8,128)(2,1)S(1)} %get-tuple-element.204.refs_2_, bf16[384,576]{1,0:T(8,128)(2,1)} %copy-done.61, bf16[384,768]{1,0:T(8,128)(2,1)} %get-tuple-element.196.refs_4_, ...), custom_call_target="tpu_custom_call" | custom-call | flops 600000000 | bytes 1000 | tf_op jit(solution)/shard_map/own_grads/pallas_call | solution.py:226
  258.0 6.2 %collective-permute-done.30.refs_4_ = bf16[384,768]{1,0:T(8,128)(2,1)S(1)} collective-permute-done((bf16[384,768]{1,0:T(8,128)(2,1)}, bf16[384,768]{1,0:T(8,128)(2,1)S(1)}, u32[]{:S(2)}, u32[]{:S(2)}) %collective-permute-start.30) | collective-permute-done | bytes 589856 | tf_op jit(solution)/shard_map/ppermute | solution.py:50
  264.5 7.7 %feed_back.3 = (bf16[384,1536]{1,0:T(8,128)(2,1)}, bf16[384,768]{1,0:T(8,128)(2,1)S(1)}, bf16[384,768]{1,0:T(8,128)(2,1)}, f32[1,768]{1,0:T(1,128)S(1)}, f32[384,768]{1,0:T(8,128)S(1)}, /*index=5*/f32[2,768]{1,0:T(2,128)S(1)}) custom-call(s32[16]{0:T(128)S(1)} %stack.23.refs_0_, f32[384,768]{1,0:T(8,128)} %get-tuple-element.169.refs_1_, ...), custom_call_target="tpu_custom_call" | custom-call | flops 1200000000 | bytes 1000 | tf_op jit(solution)/shard_map/feed_back/pallas_call | solution.py:226
  276.5 8.4 %feed_grads.3 = (bf16[768,1536]{1,0:T(8,128)(2,1)}, f32[2,768]{1,0:T(2,128)S(1)}) custom-call(s32[16]{0:T(128)S(1)} %stack.23.refs_0_, bf16[384,768]{1,0:T(8,128)(2,1)} %get-tuple-element.156.refs_1_, bf16[384,768]{1,0:T(8,128)(2,1)} %collective-permute-done.14.refs_2_, bf16[384,768]{1,0:T(8,128)(2,1)} %get-tuple-element.177.refs_3_, ...), custom_call_target="tpu_custom_call" | custom-call | flops 600000000 | bytes 1000 | tf_op jit(solution)/shard_map/feed_grads/pallas_call | solution.py:226
  285.6 3.8 collective-permute-done.33.refs_3_
  290.5 5.0 %middle_back.3 = (f32[384,768]{1,0:T(8,128)}, bf16[384,768]{1,0:T(8,128)(2,1)}, bf16[6,384,128]{2,1,0:T(8,128)(2,1)S(1)}, f32[3,768]{1,0:T(4,128)S(1)}) custom-call(s32[16]{0:T(128)S(1)} %stack.23.refs_0_, f32[384,768]{1,0:T(8,128)} %get-tuple-element.216.refs_1_, f32[384,768]{1,0:T(8,128)S(1)} %get-tuple-element.217.refs_2_, ...), custom_call_target="tpu_custom_call" | custom-call | flops 800000000 | bytes 1000 | tf_op jit(solution)/shard_map/middle_back/pallas_call | solution.py:226
  297.4 8.4 %attend_back.6 = (f32[6,128,384]{2,1,0:T(8,128)S(1)}, bf16[384,768]{1,0:T(8,128)(2,1)S(1)}, bf16[384,768]{1,0:T(8,128)(2,1)}) custom-call(bf16[6,384,128]{2,1,0:T(8,128)(2,1)} %get-tuple-element.176.refs_0_, bf16[384,768]{1,0:T(8,128)(2,1)} %copy-done.18, bf16[384,768]{1,0:T(8,128)(2,1)} %copy-done.19, bf16[6,384,128]{2,1,0:T(8,128)(2,1)S(1)} %copy-done.27), custom_call_target="tpu_custom_call" | custom-call | flops 1600000000 | bytes 1000 | tf_op jit(solution)/shard_map/attend_back/pallas_call | solution.py:226
  311.2 7.6 %attend_back.7 = (bf16[384,384]{1,0:T(8,128)(2,1)S(1)}, bf16[384,768]{1,0:T(8,128)(2,1)S(1)}, bf16[384,768]{1,0:T(8,128)(2,1)}) custom-call(bf16[6,384,128]{2,1,0:T(8,128)(2,1)S(1)} %copy-done.30, bf16[384,768]{1,0:T(8,128)(2,1)S(1)} %copy-done.15, bf16[384,768]{1,0:T(8,128)(2,1)S(1)} %copy-done.17, bf16[6,384,128]{2,1,0:T(8,128)(2,1)S(1)} %copy-done.27, ...), custom_call_target="tpu_custom_call" | custom-call | flops 1600000000 | bytes 1000 | tf_op jit(solution)/shard_map/attend_back/pallas_call | solution.py:226
  318.8 6.1 %collective-permute-done.37.refs_4_ = bf16[384,768]{1,0:T(8,128)(2,1)S(1)} collective-permute-done((bf16[384,768]{1,0:T(8,128)(2,1)}, bf16[384,768]{1,0:T(8,128)(2,1)S(1)}, u32[]{:S(2)}, u32[]{:S(2)}) %collective-permute-start.37) | collective-permute-done | bytes 589856 | tf_op jit(solution)/shard_map/ppermute | solution.py:54
  324.9 2.2 collective-permute-done.38.refs_3_
  327.1 4.8 %project_back.3 = (bf16[384,576]{1,0:T(8,128)(2,1)S(1)}, bf16[384,576]{1,0:T(8,128)(2,1)}, bf16[384,768]{1,0:T(8,128)(2,1)}, f32[2,576]{1,0:T(2,128)S(1)}, f32[2,768]{1,0:T(2,128)S(1)}) custom-call(s32[16]{0:T(128)S(1)} %stack.23.refs_0_, bf16[384,384]{1,0:T(8,128)(2,1)S(1)} %get-tuple-element.227.refs_1_, bf16[384,768]{1,0:T(8,128)(2,1)S(1)} %get-tuple-element.228.refs_2_, ...), custom_call_target="tpu_custom_call" | custom-call | flops 800000000 | bytes 1000 | tf_op jit(solution)/shard_map/project_back/pallas_call | solution.py:226
  335.0 6.8 %project_grads.1 = (bf16[208,768]{1,0:T(8,128)(2,1)}, bf16[208,768]{1,0:T(8,128)(2,1)}, bf16[208,768]{1,0:T(8,128)(2,1)}, bf16[96,768]{1,0:T(8,128)(2,1)}, bf16[112,768]{1,0:T(8,128)(2,1)}) custom-call(s32[16]{0:T(128)S(1)} %stack.23.refs_0_, bf16[384,768]{1,0:T(8,128)(2,1)} %get-tuple-element.142.refs_1_, bf16[384,768]{1,0:T(8,128)(2,1)} %copy-done.53, ...), custom_call_target="tpu_custom_call" | custom-call | flops 600000000 | bytes 1000 | tf_op jit(solution)/shard_map/project_grads/pallas_call | solution.py:226
  343.9 4.1 %collective-permute-done.40.refs_3_ = bf16[384,768]{1,0:T(8,128)(2,1)S(1)} collective-permute-done((bf16[384,768]{1,0:T(8,128)(2,1)}, bf16[384,768]{1,0:T(8,128)(2,1)S(1)}, u32[]{:S(2)}, u32[]{:S(2)}) %collective-permute-start.40) | collective-permute-done | bytes 589856 | tf_op jit(solution)/shard_map/ppermute | solution.py:50
  348.0 2.4 input_back.1
  359.9 2.9 join_rows.2
  362.8 6.7 %collective-permute-done.44.refs_2_ = bf16[384,768]{1,0:T(8,128)(2,1)S(1)} collective-permute-done((bf16[384,768]{1,0:T(8,128)(2,1)S(1)}, bf16[384,768]{1,0:T(8,128)(2,1)S(1)}, u32[]{:S(2)}, u32[]{:S(2)}) %collective-permute-start.44) | collective-permute-done | bytes 589856 | tf_op jit(solution)/shard_map/ppermute | solution.py:50
  370.3 2.6 finish.1.refs_1_
  377.5 3.1 feed_out.1
  381.5 2.9 join_rows.3
  384.3 2.4 collective-permute-done.50.refs_1_
  390.9 2.7 project_out.1
  395.8 2.1 small_out.1
  (282 shorter events, 88.6 us)
Async XLA Ops:
  7.2 87.3 %all-gather.7.cloned.1.call-start = ((), (), s32[]{:S(2)}) async-start(), calls=%async_computation.6 | async-start | bytes 5308416 | tf_op jit(solution)/shard_map/all_gather | solution.py:98
  9.8 20.4 %collective-permute-start.2 = (bf16[208,768]{1,0:T(8,128)(2,1)}, bf16[208,768]{1,0:T(8,128)(2,1)S(1)}, u32[]{:S(2)}, u32[]{:S(2)}) collective-permute-start(bf16[208,768]{1,0:T(8,128)(2,1)} %pack_first.1.refs_2_.refs_5_.refs_8_.refs_6_), channel_id=1, source_target_pairs={{0,16},{8,24},{16,0},{24,8},{1,17},{9,25},{17,1},{25,9},{2,18},{10... | collective-permute-start | bytes 958472 | tf_op jit(solution)/shard_map/ppermute | solution.py:75
  13.9 16.3 %collective-permute-start.1 = (bf16[208,768]{1,0:T(8,128)(2,1)}, bf16[208,768]{1,0:T(8,128)(2,1)S(1)}, u32[]{:S(2)}, u32[]{:S(2)}) collective-permute-start(bf16[208,768]{1,0:T(8,128)(2,1)} %pack_first.1.refs_2_.refs_5_.refs_8_.refs_6_), channel_id=1, source_target_pairs={{0,24},{8,0},{16,8},{24,16},{1,25},{9,1},{17,9},{25,17},{2,26},{10... | collective-permute-start | bytes 958472 | tf_op jit(solution)/shard_map/ppermute | solution.py:75
  15.3 21.3 %collective-permute-start = (bf16[208,768]{1,0:T(8,128)(2,1)}, bf16[208,768]{1,0:T(8,128)(2,1)S(1)}, u32[]{:S(2)}, u32[]{:S(2)}) collective-permute-start(bf16[208,768]{1,0:T(8,128)(2,1)} %pack_first.1.refs_2_.refs_5_.refs_8_.refs_6_), channel_id=1, source_target_pairs={{0,8},{8,16},{16,24},{24,0},{1,9},{9,17},{17,25},{25,1},{2,10},{10... | collective-permute-start | bytes 958472 | tf_op jit(solution)/shard_map/ppermute | solution.py:75
  36.6 89.9 %all-gather.9.cloned.1.call-start = ((), (), s32[]{:S(2)}) async-start(), calls=%async_computation.7 | async-start | bytes 2654208 | tf_op jit(solution)/shard_map/all_gather | solution.py:98
  37.3 2.5 collective-permute-start.4
  45.1 2.3 collective-permute-start.9
  48.3 131.3 %all-gather.11.cloned.1.call-start = ((), (), s32[]{:S(2)}) async-start(), calls=%async_computation.8 | async-start | bytes 5308416 | tf_op jit(solution)/shard_map/all_gather | solution.py:98
  48.4 15.4 %collective-permute-start.8 = (bf16[384,768]{1,0:T(8,128)(2,1)S(1)}, bf16[384,768]{1,0:T(8,128)(2,1)S(1)}, u32[]{:S(2)}, u32[]{:S(2)}) collective-permute-start(bf16[384,768]{1,0:T(8,128)(2,1)S(1)} %copy-done.15), channel_id=1, source_target_pairs={{0,4},{4,0},{1,5},{5,1},{2,6},{6,2},{3,7},{7,3},{8,12},{12,8},{9,1... | collective-permute-start | bytes 1769480 | tf_op jit(solution)/shard_map/ppermute | solution.py:54
  77.9 195.4 %reduce-scatter.4.cloned.1.call-start = ((), (), s32[]{:S(2)}) async-start(), calls=%async_computation.3 | async-start | bytes 2949120 | tf_op jit(solution)/shard_map/reduce_scatter | solution.py:1065
  78.2 2.3 collective-permute-start.7
  78.4 15.8 %collective-permute-start.12 = (bf16[384,768]{1,0:T(8,128)(2,1)}, bf16[384,768]{1,0:T(8,128)(2,1)S(1)}, u32[]{:S(2)}, u32[]{:S(2)}) collective-permute-start(bf16[384,768]{1,0:T(8,128)(2,1)} %get-tuple-element.148.refs_2_), channel_id=1, source_target_pairs={{0,2},{2,0},{1,3},{3,1},{4,6},{6,4},{5,7},{7,5},{8,10},{10,8},{9,1... | collective-permute-start | bytes 1769480 | tf_op jit(solution)/shard_map/ppermute | solution.py:50
  102.4 2.6 collective-permute-start.13
  102.7 3.1 collective-permute-start.14
  103.0 23.6 %collective-permute-start.15 = (bf16[384,768]{1,0:T(8,128)(2,1)}, bf16[384,768]{1,0:T(8,128)(2,1)S(1)}, u32[]{:S(2)}, u32[]{:S(2)}) collective-permute-start(bf16[384,768]{1,0:T(8,128)(2,1)} %get-tuple-element.159.refs_4_), channel_id=1, source_target_pairs={{0,2},{2,0},{1,3},{3,1},{4,6},{6,4},{5,7},{7,5},{8,10},{10,8},{9,1... | collective-permute-start | bytes 1769480 | tf_op jit(solution)/shard_map/ppermute | solution.py:50
  131.5 2.3 collective-permute-start.18
  131.8 15.7 %collective-permute-start.17 = (bf16[384,768]{1,0:T(8,128)(2,1)}, bf16[384,768]{1,0:T(8,128)(2,1)S(1)}, u32[]{:S(2)}, u32[]{:S(2)}) collective-permute-start(bf16[384,768]{1,0:T(8,128)(2,1)} %get-tuple-element.166.refs_1_), channel_id=1, source_target_pairs={{0,4},{4,0},{1,5},{5,1},{2,6},{6,2},{3,7},{7,3},{8,12},{12,8},{9,1... | collective-permute-start | bytes 1769480 | tf_op jit(solution)/shard_map/ppermute | solution.py:54
  147.6 14.7 %collective-permute-start.16 = (bf16[384,768]{1,0:T(8,128)(2,1)S(1)}, bf16[384,768]{1,0:T(8,128)(2,1)S(1)}, u32[]{:S(2)}, u32[]{:S(2)}) collective-permute-start(bf16[384,768]{1,0:T(8,128)(2,1)S(1)} %copy-done.45), channel_id=1, source_target_pairs={{0,1},{1,0},{2,3},{3,2},{4,5},{5,4},{6,7},{7,6},{8,9},{9,8},{10,11... | collective-permute-start | bytes 1769480 | tf_op jit(solution)/shard_map/ppermute | solution.py:46
  160.7 18.9 %collective-permute-start.21 = (bf16[384,768]{1,0:T(8,128)(2,1)}, bf16[384,768]{1,0:T(8,128)(2,1)S(1)}, u32[]{:S(2)}, u32[]{:S(2)}) collective-permute-start(bf16[384,768]{1,0:T(8,128)(2,1)} %get-tuple-element.170.refs_2_), channel_id=1, source_target_pairs={{0,2},{2,0},{1,3},{3,1},{4,6},{6,4},{5,7},{7,5},{8,10},{10,8},{9,1... | collective-permute-start | bytes 1769480 | tf_op jit(solution)/shard_map/ppermute | solution.py:50
  194.6 4.6 %collective-permute-start.24 = (bf16[384,1536]{1,0:T(8,128)(2,1)}, bf16[384,1536]{1,0:T(8,128)(2,1)S(1)}, u32[]{:S(2)}, u32[]{:S(2)}) collective-permute-start(bf16[384,1536]{1,0:T(8,128)(2,1)} %get-tuple-element.183.refs_5_), channel_id=1, source_target_pairs={{0,1},{1,0},{2,3},{3,2},{4,5},{5,4},{6,7},{7,6},{8,9},{9,8},{10,11... | collective-permute-start | bytes 3538952 | tf_op jit(solution)/shard_map/ppermute | solution.py:46
  194.9 3.4 collective-permute-start.23
  195.2 4.0 collective-permute-start.22
  195.4 15.7 %collective-permute-start.25 = (bf16[384,768]{1,0:T(8,128)(2,1)}, bf16[384,768]{1,0:T(8,128)(2,1)S(1)}, u32[]{:S(2)}, u32[]{:S(2)}) collective-permute-start(bf16[384,768]{1,0:T(8,128)(2,1)} %get-tuple-element.187.refs_3_), channel_id=1, source_target_pairs={{0,2},{2,0},{1,3},{3,1},{4,6},{6,4},{5,7},{7,5},{8,10},{10,8},{9,1... | collective-permute-start | bytes 1769480 | tf_op jit(solution)/shard_map/ppermute | solution.py:50
  211.2 98.7 %reduce-scatter.6.cloned.1.call-start = ((), (), s32[]{:S(2)}) async-start(), calls=%async_computation.4 | async-start | bytes 1474560 | tf_op jit(solution)/shard_map/reduce_scatter | solution.py:1065
  223.1 2.3 collective-permute-start.26
  223.2 4.7 %collective-permute-start.27 = (bf16[384,768]{1,0:T(8,128)(2,1)S(1)}, bf16[384,768]{1,0:T(8,128)(2,1)S(1)}, u32[]{:S(2)}, u32[]{:S(2)}) collective-permute-start(bf16[384,768]{1,0:T(8,128)(2,1)S(1)} %copy-done.47), channel_id=1, source_target_pairs={{0,1},{1,0},{2,3},{3,2},{4,5},{5,4},{6,7},{7,6},{8,9},{9,8},{10,11... | collective-permute-start | bytes 1769480 | tf_op jit(solution)/shard_map/ppermute | solution.py:46
  226.4 15.6 %collective-permute-start.28 = (bf16[384,768]{1,0:T(8,128)(2,1)}, bf16[384,768]{1,0:T(8,128)(2,1)S(1)}, u32[]{:S(2)}, u32[]{:S(2)}) collective-permute-start(bf16[384,768]{1,0:T(8,128)(2,1)} %cross_sum.2), channel_id=1, source_target_pairs={{0,4},{4,0},{1,5},{5,1},{2,6},{6,2},{3,7},{7,3},{8,12},{12,8},{9,1... | collective-permute-start | bytes 1769480 | tf_op jit(solution)/shard_map/ppermute | solution.py:54
  248.6 15.6 %collective-permute-start.30 = (bf16[384,768]{1,0:T(8,128)(2,1)}, bf16[384,768]{1,0:T(8,128)(2,1)S(1)}, u32[]{:S(2)}, u32[]{:S(2)}) collective-permute-start(bf16[384,768]{1,0:T(8,128)(2,1)} %get-tuple-element.202.refs_3_), channel_id=1, source_target_pairs={{0,2},{2,0},{1,3},{3,1},{4,6},{6,4},{5,7},{7,5},{8,10},{10,8},{9,1... | collective-permute-start | bytes 1769480 | tf_op jit(solution)/shard_map/ppermute | solution.py:50
  264.2 92.3 %reduce-scatter.8.cloned.1.call-start = ((), (), s32[]{:S(2)}) async-start(), calls=%async_computation.5 | async-start | bytes 2949120 | tf_op jit(solution)/shard_map/reduce_scatter | solution.py:1065
  273.4 3.2 collective-permute-start.32
  273.4 16.1 %collective-permute-start.33 = (bf16[192,1536]{1,0:T(8,128)(2,1)}, bf16[192,1536]{1,0:T(8,128)(2,1)}, u32[]{:S(2)}, u32[]{:S(2)}) collective-permute-start(bf16[192,1536]{1,0:T(8,128)(2,1)} %reduce-scatter.4.cloned.1.call-done.refs_2_), channel_id=1, source_target_pairs={{0,4},{4,0},{1,5},{5,1},{2,6},{6,2},{3,7},{7,3},{8,12},{12,8},{9,1... | collective-permute-start | bytes 1769480 | tf_op jit(solution)/shard_map/ppermute | solution.py:54
  274.8 15.7 %collective-permute-start.34 = (bf16[384,768]{1,0:T(8,128)(2,1)}, bf16[384,768]{1,0:T(8,128)(2,1)S(1)}, u32[]{:S(2)}, u32[]{:S(2)}) collective-permute-start(bf16[384,768]{1,0:T(8,128)(2,1)} %get-tuple-element.214.refs_3_), channel_id=1, source_target_pairs={{0,2},{2,0},{1,3},{3,1},{4,6},{6,4},{5,7},{7,5},{8,10},{10,8},{9,1... | collective-permute-start | bytes 1769480 | tf_op jit(solution)/shard_map/ppermute | solution.py:50
  305.9 2.3 collective-permute-start.35
  306.0 3.9 collective-permute-start.36
  309.2 15.6 %collective-permute-start.37 = (bf16[384,768]{1,0:T(8,128)(2,1)}, bf16[384,768]{1,0:T(8,128)(2,1)S(1)}, u32[]{:S(2)}, u32[]{:S(2)}) collective-permute-start(bf16[384,768]{1,0:T(8,128)(2,1)} %cross_sum.3), channel_id=1, source_target_pairs={{0,4},{4,0},{1,5},{5,1},{2,6},{6,2},{3,7},{7,3},{8,12},{12,8},{9,1... | collective-permute-start | bytes 1769480 | tf_op jit(solution)/shard_map/ppermute | solution.py:54
  332.2 15.8 %collective-permute-start.40 = (bf16[384,768]{1,0:T(8,128)(2,1)}, bf16[384,768]{1,0:T(8,128)(2,1)S(1)}, u32[]{:S(2)}, u32[]{:S(2)}) collective-permute-start(bf16[384,768]{1,0:T(8,128)(2,1)} %get-tuple-element.248.refs_2_), channel_id=1, source_target_pairs={{0,2},{2,0},{1,3},{3,1},{4,6},{6,4},{5,7},{7,5},{8,10},{10,8},{9,1... | collective-permute-start | bytes 1769480 | tf_op jit(solution)/shard_map/ppermute | solution.py:50
  333.7 16.8 %collective-permute-start.41 = (bf16[192,768]{1,0:T(8,128)(2,1)S(1)}, bf16[192,768]{1,0:T(8,128)(2,1)S(1)}, u32[]{:S(2)}, u32[]{:S(2)}) collective-permute-start(bf16[192,768]{1,0:T(8,128)(2,1)S(1)} %copy-done.67), channel_id=1, source_target_pairs={{0,4},{4,0},{1,5},{5,1},{2,6},{6,2},{3,7},{7,3},{8,12},{12,8},{9,1... | collective-permute-start | bytes 884744 | tf_op jit(solution)/shard_map/ppermute | solution.py:54
  341.9 10.4 %collective-permute-start.43 = (bf16[112,768]{1,0:T(8,128)(2,1)}, bf16[112,768]{1,0:T(8,128)(2,1)S(1)}, u32[]{:S(2)}, u32[]{:S(2)}) collective-permute-start(bf16[112,768]{1,0:T(8,128)(2,1)} %get-tuple-element.254), channel_id=1, source_target_pairs={{0,24},{8,0},{16,8},{24,16},{1,25},{9,1},{17,9},{25,17},{2,26},{10... | collective-permute-start | bytes 516104 | tf_op jit(solution)/shard_map/ppermute | solution.py:1120
  343.0 9.2 %collective-permute-start.42 = (bf16[96,768]{1,0:T(8,128)(2,1)}, bf16[96,768]{1,0:T(8,128)(2,1)S(1)}, u32[]{:S(2)}, u32[]{:S(2)}) collective-permute-start(bf16[96,768]{1,0:T(8,128)(2,1)} %get-tuple-element.253), channel_id=1, source_target_pairs={{0,8},{8,16},{16,24},{24,0},{1,9},{9,17},{17,25},{25,1},{2,10},{10... | collective-permute-start | bytes 442376 | tf_op jit(solution)/shard_map/ppermute | solution.py:1120
  350.4 8.7 %collective-permute-start.46 = (bf16[384,768]{1,0:T(8,128)(2,1)}, bf16[384,768]{1,0:T(8,128)(2,1)S(1)}, u32[]{:S(2)}, u32[]{:S(2)}) collective-permute-start(bf16[384,768]{1,0:T(8,128)(2,1)} %get-tuple-element.249.refs_1_), channel_id=1, source_target_pairs={{0,1},{1,0},{2,3},{3,2},{4,5},{5,4},{6,7},{7,6},{8,9},{9,8},{10,11... | collective-permute-start | bytes 1769480 | tf_op jit(solution)/shard_map/ppermute | solution.py:46
  355.0 14.5 %collective-permute-start.44 = (bf16[384,768]{1,0:T(8,128)(2,1)S(1)}, bf16[384,768]{1,0:T(8,128)(2,1)S(1)}, u32[]{:S(2)}, u32[]{:S(2)}) collective-permute-start(bf16[384,768]{1,0:T(8,128)(2,1)S(1)} %copy-done.54), channel_id=1, source_target_pairs={{0,2},{2,0},{1,3},{3,1},{4,6},{6,4},{5,7},{7,5},{8,10},{10,8},{9,1... | collective-permute-start | bytes 1769480 | tf_op jit(solution)/shard_map/ppermute | solution.py:50
  356.5 16.5 %collective-permute-start.45 = (bf16[192,1536]{1,0:T(8,128)(2,1)}, bf16[192,1536]{1,0:T(8,128)(2,1)S(1)}, u32[]{:S(2)}, u32[]{:S(2)}) collective-permute-start(bf16[192,1536]{1,0:T(8,128)(2,1)} %reduce-scatter.8.cloned.1.call-done.refs_0_), channel_id=1, source_target_pairs={{0,4},{4,0},{1,5},{5,1},{2,6},{6,2},{3,7},{7,3},{8,12},{12,8},{9,1... | collective-permute-start | bytes 1769480 | tf_op jit(solution)/shard_map/ppermute | solution.py:54
  357.1 16.0 %collective-permute-start.48 = (bf16[208,768]{1,0:T(8,128)(2,1)}, bf16[208,768]{1,0:T(8,128)(2,1)S(1)}, u32[]{:S(2)}, u32[]{:S(2)}) collective-permute-start(bf16[208,768]{1,0:T(8,128)(2,1)} %get-tuple-element.260), channel_id=1, source_target_pairs={{0,24},{8,0},{16,8},{24,16},{1,25},{9,1},{17,9},{25,17},{2,26},{10... | collective-permute-start | bytes 958472 | tf_op jit(solution)/shard_map/ppermute | solution.py:1123
  358.8 14.2 %collective-permute-start.47 = (bf16[208,768]{1,0:T(8,128)(2,1)}, bf16[208,768]{1,0:T(8,128)(2,1)S(1)}, u32[]{:S(2)}, u32[]{:S(2)}) collective-permute-start(bf16[208,768]{1,0:T(8,128)(2,1)} %get-tuple-element.255), channel_id=1, source_target_pairs={{0,8},{8,16},{16,24},{24,0},{1,9},{9,17},{17,25},{25,1},{2,10},{10... | collective-permute-start | bytes 958472 | tf_op jit(solution)/shard_map/ppermute | solution.py:1123
  376.5 4.2 %collective-permute-start.49 = (bf16[384,768]{1,0:T(8,128)(2,1)S(1)}, bf16[384,768]{1,0:T(8,128)(2,1)S(1)}, u32[]{:S(2)}, u32[]{:S(2)}) collective-permute-start(bf16[384,768]{1,0:T(8,128)(2,1)S(1)} %copy-done.40), channel_id=1, source_target_pairs={{0,1},{1,0},{2,3},{3,2},{4,5},{5,4},{6,7},{7,6},{8,9},{9,8},{10,11... | collective-permute-start | bytes 1769480 | tf_op jit(solution)/shard_map/ppermute | solution.py:46
  376.6 10.2 %collective-permute-start.50 = (bf16[208,768]{1,0:T(8,128)(2,1)}, bf16[208,768]{1,0:T(8,128)(2,1)S(1)}, u32[]{:S(2)}, u32[]{:S(2)}) collective-permute-start(bf16[208,768]{1,0:T(8,128)(2,1)} %sum_blocks.1.refs_0_), channel_id=1, source_target_pairs={{0,4},{4,0},{1,5},{5,1},{2,6},{6,2},{3,7},{7,3},{8,12},{12,8},{9,1... | collective-permute-start | bytes 958472 | tf_op jit(solution)/shard_map/ppermute | solution.py:54
  389.3 4.4 %collective-permute-start.51 = (f32[16,768]{1,0:T(8,128)}, f32[16,768]{1,0:T(8,128)S(1)}, u32[]{:S(2)}, u32[]{:S(2)}) collective-permute-start(f32[16,768]{1,0:T(8,128)} %small_sum.1.refs_1_), channel_id=1, source_target_pairs={{0,2},{2,0},{1,3},{3,1},{4,6},{6,4},{5,7},{7,5},{8,10},{10,8},{9,1... | collective-permute-start | bytes 147464 | tf_op jit(solution)/shard_map/ppermute | solution.py:50
  390.9 3.3 collective-permute-start.52
  (89 other events, 491.9 us)
Sparse Core Ops, SparseCore 0:
  36.7 57.6 all-gather.6
  96.1 30.3 all-gather.8
  128.8 50.8 all-gather.10
  211.3 46.8 reduce-scatter.3
  264.3 27.9 reduce-scatter.5
  296.5 45.9 reduce-scatter.7

commit v6 on v5

--- a/solution.py
+++ b/solution.py
@@ -587,7 +587,7 @@
             v = y_r[...] + (pa_r[...].astype(f32) + pb_r[...].astype(f32) + vec_r[at : at + 1, :])
             o[...] = v.astype(bf16)
 
-        return run(kernel, [Far(y), Far(pa), Far(pb), vec], [((R, D), bf16, FAR)], name="finish")
+        return run(kernel, [Far(y), Far(pa), pb, vec], [((R, D), bf16, FAR)], name="finish")
 
     def feed_back(scal, grad, gp, layer, w, before=None):
         n = len(w.arrays)
@@ -863,7 +863,7 @@
             outs += [((half, z.a_cols), bf16, FAR), ((M + TAIL - half, z.a_cols), bf16, FAR)]
         return run(
             kernel,
-            [Far(n1), Far(n1_r), dp, Far(dp_r), Far(g1), Far(g1_r), Far(o), Far(o_r)] + [Far(a) for a in flat],
+            [Far(n1), Far(n1_r), dp, dp_r, Far(g1), Far(g1_r), Far(o), Far(o_r)] + [Far(a) for a in flat],
             outs,
             [pltpu.VMEM((S,) + block, bf16)],
             scalars=scal,
@@ -880,7 +880,7 @@
 
         return run(
             kernel,
-            [Far(n1), Far(n1_r), dp, Far(dp_r), Far(g1), Far(g1_r), Far(o), Far(o_r)],
+            [Far(n1), Far(n1_r), dp, dp_r, Far(g1), Far(g1_r), Far(o), Far(o_r)],
             [((S, M, z.a_cols), bf16, FAR)],
             name="own_grads",
             us=3,
@@ -959,7 +959,7 @@
         def kernel(a_r, b_r, o):
             o[...] = a_r[M:, :].astype(f32) + b_r[M:, :].astype(f32)
 
-        return run(kernel, [Far(mine), Far(theirs)], [((TAIL, z.a_cols), f32, FAR)], name="small_sum")[0]
+        return run(kernel, [Far(mine), theirs], [((TAIL, z.a_cols), f32, FAR)], name="small_sum")[0]
 
     def small_out(scal, mine, x_side, core_side, far_side):
         def kernel(scal_r, a_r, x_r, c_r, f_r, qvb_o, upb_o, gain_o, shift_o):

time: 411 us -> 409 us (level)
    unnamed x155 -> x149, local copies, waits for them, and re-layouts: 19.5 us -> 15.7 us
  transfers between devices with their start and end apart: 60 -> 60, of which waited for: 39 -> 41; matrix products, arithmetic and copies ran while one was open for 1% -> 1% of each run, Pallas kernels for 39% -> 39%
where the time goes in v6:
time: 409 us; the launch traced here: 403 us
  Pallas kernels  180 us (44%)
  waiting for transfers between devices  147 us (36%)
  starting transfers between devices  39.4 us (10%)
  local copies, waits for them, and re-layouts  19.2 us (5%)
  between operations  15.6 us (4%)
    pallas_call x35, Pallas kernels, run(): pl.pallas_call(wrapped, out_shape=shapes, in_specs=specs, out_specs=[any_...  180 us
    all_gather x3, waiting for transfers between devices, __init__(): whole = lax.all_gather(x, ('shard', 'tc'), axis=0, tiled=False)  36.8 us
    ppermute x9, waiting for transfers between devices, x_swap(): return lax.ppermute(x, 'tx', [(0, 1), (1, 0)])  35.5 us
    ppermute x8, waiting for transfers between devices, y_swap(): return lax.ppermute(x, 'ctx', [(0, 1), (1, 0)])  32.3 us
    ppermute x30, waiting for transfers between devices, core_swap(): return lax.ppermute(x, 'tc', [(0, 1), (1, 0)])  21.9 us
    ppermute x3, waiting for transfers between devices, __init__(): self.mine = [x] + [lax.ppermute(x, 'shard', ring(s)) for s in (1, 3, 2)]  18.3 us
    unnamed x149, local copies, waits for them, and re-layouts  15.7 us
    ppermute x9, starting transfers between devices, x_swap(): return lax.ppermute(x, 'tx', [(0, 1), (1, 0)])  13.4 us
  transfers between devices with their start and end apart: 60, of which 41 were waited for; matrix products, arithmetic and copies ran while one was open for 1% of the time, Pallas kernels for 39%

profile of v6, /device:TPU:0, one launch (start us, length us, event | category | flops | bytes accessed | tf_op | source)
XLA Modules:
  0.0 402.9 jit_solution(6518378250769632953)
XLA Ops:
  7.3 2.6 pack_first.1.refs_2_.refs_5_.refs_8_.refs_6_
  9.8 4.1 %collective-permute-start.2 = (bf16[208,768]{1,0:T(8,128)(2,1)}, bf16[208,768]{1,0:T(8,128)(2,1)S(1)}, u32[]{:S(2)}, u32[]{:S(2)}) collective-permute-start(bf16[208,768]{1,0:T(8,128)(2,1)} %pack_first.1.refs_2_.refs_5_.refs_8_.refs_6_), channel_id=1, source_target_pairs={{0,16},{8,24},{16,0},{24,8},{1,17},{9,25},{17,1},{25,9},{2,18},{10... | collective-permute-start | bytes 958472 | tf_op jit(solution)/shard_map/ppermute | solution.py:75
  18.3 11.9 %collective-permute-done.2.refs_5_.refs_8_.refs_11_.refs_9_ = bf16[208,768]{1,0:T(8,128)(2,1)S(1)} collective-permute-done((bf16[208,768]{1,0:T(8,128)(2,1)}, bf16[208,768]{1,0:T(8,128)(2,1)S(1)}, u32[]{:S(2)}, u32[]{:S(2)}) %collective-permute-start.2) | collective-permute-done | bytes 319520 | tf_op jit(solution)/shard_map/ppermute | solution.py:75
  30.3 6.3 %collective-permute-done.refs_3_.refs_6_.refs_9_.refs_7_ = bf16[208,768]{1,0:T(8,128)(2,1)S(1)} collective-permute-done((bf16[208,768]{1,0:T(8,128)(2,1)}, bf16[208,768]{1,0:T(8,128)(2,1)S(1)}, u32[]{:S(2)}, u32[]{:S(2)}) %collective-permute-start) | collective-permute-done | bytes 319520 | tf_op jit(solution)/shard_map/ppermute | solution.py:75
  39.9 5.2 %project.2 = (bf16[384,768]{1,0:T(8,128)(2,1)}, bf16[384,384]{1,0:T(8,128)(2,1)S(1)}, bf16[384,768]{1,0:T(8,128)(2,1)}, f32[16,768]{1,0:T(8,128)S(1)}, f32[4,576...) custom-call(s32[16]{0:T(128)S(1)} %stack.23.refs_0_, ...), custom_call_target="tpu_custom_call" | custom-call | flops 700000000 | bytes 1000 | tf_op jit(solution)/shard_map/project/pallas_call | solution.py:226
  50.0 5.7 %attend_near.2.refs_4_ = f32[6,384,128]{2,1,0:T(8,128)S(1)} custom-call(bf16[384,384]{1,0:T(8,128)(2,1)S(1)} %get-tuple-element.143.refs_0_.refs_1_, bf16[384,768]{1,0:T(8,128)(2,1)S(1)} %copy-done.16, bf16[384,768]{1,0:T(8,128)(2,1)S(1)} %collective-permute-done.9.refs_2_), custom_call_target="tpu_custom_call" | custom-call | flops 1200000000 | bytes 1000 | tf_op jit(solution)/shard_map/attend_near/pallas_call | solution.py:226
  56.7 7.1 %collective-permute-done.8.refs_2_.refs_1_ = bf16[384,768]{1,0:T(8,128)(2,1)S(1)} collective-permute-done((bf16[384,768]{1,0:T(8,128)(2,1)S(1)}, bf16[384,768]{1,0:T(8,128)(2,1)S(1)}, u32[]{:S(2)}, u32[]{:S(2)}) %collective-permute-start.8) | collective-permute-done | bytes 589856 | tf_op jit(solution)/shard_map/ppermute | solution.py:54
  67.2 10.7 %attend_far.2 = (bf16[384,192]{1,0:T(8,128)(2,1)}, bf16[384,192]{1,0:T(8,128)(2,1)}, bf16[6,384,128]{2,1,0:T(8,128)(2,1)}, bf16[384,192]{1,0:T(8,128)(2,1)}, bf1...) custom-call(s32[16]{0:T(128)S(1)} %stack.23.refs_0_, bf16[384,384]{1,0:T(8,128)(2,1)S(1)} %get-tuple-element.143.refs_0_.refs_1_, ...), custom_call_target="tpu_custom_call" | custom-call | flops 1600000000 | bytes 1000 | tf_op jit(solution)/shard_map/attend_far/pallas_call | solution.py:226
  81.7 12.5 %collective-permute-done.12.refs_3_ = bf16[384,768]{1,0:T(8,128)(2,1)S(1)} collective-permute-done((bf16[384,768]{1,0:T(8,128)(2,1)}, bf16[384,768]{1,0:T(8,128)(2,1)S(1)}, u32[]{:S(2)}, u32[]{:S(2)}) %collective-permute-start.12) | collective-permute-done | bytes 589856 | tf_op jit(solution)/shard_map/ppermute | solution.py:50
  94.5 7.9 %feed.2 = (f32[384,768]{1,0:T(8,128)}, bf16[384,768]{1,0:T(8,128)(2,1)}, bf16[384,768]{1,0:T(8,128)(2,1)}, bf16[384,768]{1,0:T(8,128)(2,1)}, bf16[384,768]{1,0:T...) custom-call(s32[16]{0:T(128)S(1)} %stack.23.refs_0_, ...), custom_call_target="tpu_custom_call" | custom-call | flops 1200000000 | bytes 1000 | tf_op jit(solution)/shard_map/feed/pallas_call | solution.py:226
  105.8 20.7 %all-gather.9.cloned.1.call-done = bf16[1536,768]{1,0:T(8,128)(2,1)} async-done(((bf16[192,768]{1,0:T(8,128)(2,1)}), bf16[1536,768]{1,0:T(8,128)(2,1)}) %all-gather.9.cloned.1.call-update) | async-done | bytes 2359312 | tf_op jit(solution)/shard_map/all_gather | solution.py:98
  126.5 5.0 %project.3 = (bf16[384,768]{1,0:T(8,128)(2,1)}, bf16[384,384]{1,0:T(8,128)(2,1)S(1)}, bf16[384,768]{1,0:T(8,128)(2,1)}, f32[384,768]{1,0:T(8,128)}) custom-call(s32[16]{0:T(128)S(1)} %stack.23.refs_0_, f32[384,768]{1,0:T(8,128)} %get-tuple-element.216.refs_1_, f32[16,768]{1,0:T(8,128)S(1)} %get-tuple-element.149.refs_4_.refs_2_.refs_5_.refs_3_, ...), custom_call_target="tpu_custom_call" | custom-call | flops 700000000 | bytes 1000 | tf_op jit(solution)/shard_map/project/pallas_call | solution.py:226
  134.9 5.7 %attend_near.3.refs_4_ = f32[6,384,128]{2,1,0:T(8,128)S(1)} custom-call(bf16[384,384]{1,0:T(8,128)(2,1)S(1)} %get-tuple-element.165.refs_0_.refs_1_, bf16[384,768]{1,0:T(8,128)(2,1)S(1)} %copy-done.21, bf16[384,768]{1,0:T(8,128)(2,1)S(1)} %collective-permute-done.18.refs_2_), custom_call_target="tpu_custom_call" | custom-call | flops 1200000000 | bytes 1000 | tf_op jit(solution)/shard_map/attend_near/pallas_call | solution.py:226
  140.7 6.9 %collective-permute-done.17.refs_2_.refs_1_ = bf16[384,768]{1,0:T(8,128)(2,1)S(1)} collective-permute-done((bf16[384,768]{1,0:T(8,128)(2,1)}, bf16[384,768]{1,0:T(8,128)(2,1)S(1)}, u32[]{:S(2)}, u32[]{:S(2)}) %collective-permute-start.17) | collective-permute-done | bytes 589856 | tf_op jit(solution)/shard_map/ppermute | solution.py:54
  149.6 11.1 %attend_far.3 = (bf16[384,192]{1,0:T(8,128)(2,1)}, bf16[384,192]{1,0:T(8,128)(2,1)}, bf16[6,384,128]{2,1,0:T(8,128)(2,1)}, bf16[384,192]{1,0:T(8,128)(2,1)}, bf1...) custom-call(s32[16]{0:T(128)S(1)} %stack.23.refs_0_, bf16[384,384]{1,0:T(8,128)(2,1)S(1)} %get-tuple-element.165.refs_0_.refs_1_, ...), custom_call_target="tpu_custom_call" | custom-call | flops 1600000000 | bytes 1000 | tf_op jit(solution)/shard_map/attend_far/pallas_call | solution.py:226
  163.9 15.8 %all-gather.11.cloned.1.call-done = bf16[1536,1536]{1,0:T(8,128)(2,1)} async-done(((bf16[192,1536]{1,0:T(8,128)(2,1)}), bf16[1536,1536]{1,0:T(8,128)(2,1)}) %all-gather.11.cloned.1.call-update) | async-done | bytes 4718608 | tf_op jit(solution)/shard_map/all_gather | solution.py:98
  179.6 8.1 %feed.3 = (f32[384,768]{1,0:T(8,128)}, bf16[384,768]{1,0:T(8,128)(2,1)}, bf16[384,768]{1,0:T(8,128)(2,1)}, bf16[384,768]{1,0:T(8,128)(2,1)}, bf16[384,768]{1,0:T...) custom-call(s32[16]{0:T(128)S(1)} %stack.23.refs_0_, f32[384,768]{1,0:T(8,128)} %get-tuple-element.169.refs_1_, ...), custom_call_target="tpu_custom_call" | custom-call | flops 1200000000 | bytes 1000 | tf_op jit(solution)/shard_map/feed/pallas_call | solution.py:226
  187.8 6.8 %feed_back.2 = (bf16[384,1536]{1,0:T(8,128)(2,1)}, bf16[384,768]{1,0:T(8,128)(2,1)S(1)}, bf16[384,768]{1,0:T(8,128)(2,1)}, f32[1,768]{1,0:T(1,128)S(1)}) custom-call(s32[16]{0:T(128)S(1)} %stack.23.refs_0_, bf16[384,768]{1,0:T(8,128)(2,1)S(1)} %dynamic-slice_bitcast_fusion.refs_1_.refs_2_, bf16[384,768]{1,0:T(8,128)(2,1)} %get-tuple-element.181.refs_2_, ...), custom_call_target="tpu_custom_call" | custom-call | flops 1200000000 | bytes 1000 | tf_op jit(solution)/shard_map/feed_back/pallas_call | solution.py:226
  200.4 8.4 %feed_grads.2 = (bf16[768,1536]{1,0:T(8,128)(2,1)}, f32[2,768]{1,0:T(2,128)S(1)}) custom-call(s32[16]{0:T(128)S(1)} %stack.23.refs_0_, bf16[384,768]{1,0:T(8,128)(2,1)} %get-tuple-element.178.refs_1_, bf16[384,768]{1,0:T(8,128)(2,1)} %copy-done.59, bf16[384,768]{1,0:T(8,128)(2,1)} %get-tuple-element.179.refs_3_, bf16[384,768]{1,0:T(8,128)(2,1)} %copy-done.58, ...), custom_call_target="tpu_custom_call" | custom-call | flops 600000000 | bytes 1000 | tf_op jit(solution)/shard_map/feed_grads/pallas_call | solution.py:226
  208.8 2.3 collective-permute-done.25.refs_4_
  211.4 4.8 %middle_back.2 = (f32[384,768]{1,0:T(8,128)}, bf16[384,768]{1,0:T(8,128)(2,1)}, bf16[6,384,128]{2,1,0:T(8,128)(2,1)S(1)}, f32[3,768]{1,0:T(4,128)S(1)}) custom-call(s32[16]{0:T(128)S(1)} %stack.23.refs_0_, f32[384,768]{1,0:T(8,128)} %get-tuple-element.186.refs_1_.refs_0_, bf16[384,768]{1,0:T(8,128)(2,1)S(1)} %dynamic-slice_bitcast_fusion.refs_1_.refs_2_, ...), custom_call_target="tpu_custom_call" | custom-call | flops 800000000 | bytes 1000 | tf_op jit(solution)/shard_map/middle_back/pallas_call | solution.py:226
  216.2 6.9 %attend_back.4 = (f32[6,128,384]{2,1,0:T(8,128)S(1)}, bf16[384,768]{1,0:T(8,128)(2,1)S(1)}, bf16[384,768]{1,0:T(8,128)(2,1)}) custom-call(bf16[6,384,128]{2,1,0:T(8,128)(2,1)S(1)} %copy-done.32, bf16[384,768]{1,0:T(8,128)(2,1)S(1)} %copy-done.24, bf16[384,768]{1,0:T(8,128)(2,1)S(1)} %copy-done.26, bf16[6,384,128]{2,1,0:T(8,128)(2,1)S(1)} %get-tuple-element.192.refs_3_), custom_call_target="tpu_custom_call" | custom-call | flops 1600000000 | bytes 1000 | tf_op jit(solution)/shard_map/attend_back/pallas_call | solution.py:226
  227.9 7.6 %attend_back.5 = (bf16[384,384]{1,0:T(8,128)(2,1)S(1)}, bf16[384,768]{1,0:T(8,128)(2,1)S(1)}, bf16[384,768]{1,0:T(8,128)(2,1)}) custom-call(bf16[6,384,128]{2,1,0:T(8,128)(2,1)S(1)} %copy-done.32, bf16[384,768]{1,0:T(8,128)(2,1)S(1)} %copy-done.22, bf16[384,768]{1,0:T(8,128)(2,1)S(1)} %collective-permute-done.18.refs_2_, ...), custom_call_target="tpu_custom_call" | custom-call | flops 1600000000 | bytes 1000 | tf_op jit(solution)/shard_map/attend_back/pallas_call | solution.py:226
  235.5 6.5 %collective-permute-done.28.refs_4_ = bf16[384,768]{1,0:T(8,128)(2,1)S(1)} collective-permute-done((bf16[384,768]{1,0:T(8,128)(2,1)}, bf16[384,768]{1,0:T(8,128)(2,1)S(1)}, u32[]{:S(2)}, u32[]{:S(2)}) %collective-permute-start.28) | collective-permute-done | bytes 589856 | tf_op jit(solution)/shard_map/ppermute | solution.py:54
  242.0 2.2 collective-permute-done.29.refs_3_
  244.2 4.3 %project_back.2 = (bf16[384,576]{1,0:T(8,128)(2,1)S(1)}, bf16[384,576]{1,0:T(8,128)(2,1)}, bf16[384,768]{1,0:T(8,128)(2,1)}, f32[2,576]{1,0:T(2,128)S(1)}) custom-call(s32[16]{0:T(128)S(1)} %stack.23.refs_0_, bf16[384,384]{1,0:T(8,128)(2,1)S(1)} %get-tuple-element.198.refs_1_, bf16[384,768]{1,0:T(8,128)(2,1)S(1)} %get-tuple-element.199.refs_2_, ...), custom_call_target="tpu_custom_call" | custom-call | flops 800000000 | bytes 1000 | tf_op jit(solution)/shard_map/project_back/pallas_call | solution.py:226
  250.1 2.1 collective-permute-done.31.refs_3_
  252.2 4.8 %own_grads.1 = bf16[4,192,768]{2,1,0:T(8,128)(2,1)} custom-call(bf16[384,768]{1,0:T(8,128)(2,1)} %get-tuple-element.164.refs_0_, bf16[384,768]{1,0:T(8,128)(2,1)} %copy-done.47, bf16[384,576]{1,0:T(8,128)(2,1)S(1)} %get-tuple-element.204.refs_2_, bf16[384,576]{1,0:T(8,128)(2,1)S(1)} %collective-permute-done.31.refs_3_, ...), custom_call_target="tpu_custom_call" | custom-call | flops 600000000 | bytes 1000 | tf_op jit(solution)/shard_map/own_grads/pallas_call | solution.py:226
  257.0 7.2 %collective-permute-done.30.refs_4_ = bf16[384,768]{1,0:T(8,128)(2,1)S(1)} collective-permute-done((bf16[384,768]{1,0:T(8,128)(2,1)}, bf16[384,768]{1,0:T(8,128)(2,1)S(1)}, u32[]{:S(2)}, u32[]{:S(2)}) %collective-permute-start.30) | collective-permute-done | bytes 589856 | tf_op jit(solution)/shard_map/ppermute | solution.py:50
  264.5 7.7 %feed_back.3 = (bf16[384,1536]{1,0:T(8,128)(2,1)}, bf16[384,768]{1,0:T(8,128)(2,1)S(1)}, bf16[384,768]{1,0:T(8,128)(2,1)}, f32[1,768]{1,0:T(1,128)S(1)}, f32[384,768]{1,0:T(8,128)S(1)}, /*index=5*/f32[2,768]{1,0:T(2,128)S(1)}) custom-call(s32[16]{0:T(128)S(1)} %stack.23.refs_0_, f32[384,768]{1,0:T(8,128)} %get-tuple-element.169.refs_1_, ...), custom_call_target="tpu_custom_call" | custom-call | flops 1200000000 | bytes 1000 | tf_op jit(solution)/shard_map/feed_back/pallas_call | solution.py:226
  276.6 8.4 %feed_grads.3 = (bf16[768,1536]{1,0:T(8,128)(2,1)}, f32[2,768]{1,0:T(2,128)S(1)}) custom-call(s32[16]{0:T(128)S(1)} %stack.23.refs_0_, bf16[384,768]{1,0:T(8,128)(2,1)} %get-tuple-element.156.refs_1_, bf16[384,768]{1,0:T(8,128)(2,1)} %collective-permute-done.14.refs_2_, bf16[384,768]{1,0:T(8,128)(2,1)} %get-tuple-element.177.refs_3_, ...), custom_call_target="tpu_custom_call" | custom-call | flops 600000000 | bytes 1000 | tf_op jit(solution)/shard_map/feed_grads/pallas_call | solution.py:226
  285.6 3.9 collective-permute-done.33.refs_3_
  290.5 5.0 %middle_back.3 = (f32[384,768]{1,0:T(8,128)}, bf16[384,768]{1,0:T(8,128)(2,1)}, bf16[6,384,128]{2,1,0:T(8,128)(2,1)S(1)}, f32[3,768]{1,0:T(4,128)S(1)}) custom-call(s32[16]{0:T(128)S(1)} %stack.23.refs_0_, f32[384,768]{1,0:T(8,128)} %get-tuple-element.216.refs_1_, f32[384,768]{1,0:T(8,128)S(1)} %get-tuple-element.217.refs_2_, ...), custom_call_target="tpu_custom_call" | custom-call | flops 800000000 | bytes 1000 | tf_op jit(solution)/shard_map/middle_back/pallas_call | solution.py:226
  297.4 8.4 %attend_back.6 = (f32[6,128,384]{2,1,0:T(8,128)S(1)}, bf16[384,768]{1,0:T(8,128)(2,1)S(1)}, bf16[384,768]{1,0:T(8,128)(2,1)}) custom-call(bf16[6,384,128]{2,1,0:T(8,128)(2,1)} %get-tuple-element.176.refs_0_, bf16[384,768]{1,0:T(8,128)(2,1)} %copy-done.19, bf16[384,768]{1,0:T(8,128)(2,1)} %copy-done.20, bf16[6,384,128]{2,1,0:T(8,128)(2,1)S(1)} %copy-done.28), custom_call_target="tpu_custom_call" | custom-call | flops 1600000000 | bytes 1000 | tf_op jit(solution)/shard_map/attend_back/pallas_call | solution.py:226
  311.2 7.6 %attend_back.7 = (bf16[384,384]{1,0:T(8,128)(2,1)S(1)}, bf16[384,768]{1,0:T(8,128)(2,1)S(1)}, bf16[384,768]{1,0:T(8,128)(2,1)}) custom-call(bf16[6,384,128]{2,1,0:T(8,128)(2,1)S(1)} %copy-done.31, bf16[384,768]{1,0:T(8,128)(2,1)S(1)} %copy-done.16, bf16[384,768]{1,0:T(8,128)(2,1)S(1)} %copy-done.18, bf16[6,384,128]{2,1,0:T(8,128)(2,1)S(1)} %copy-done.28, ...), custom_call_target="tpu_custom_call" | custom-call | flops 1600000000 | bytes 1000 | tf_op jit(solution)/shard_map/attend_back/pallas_call | solution.py:226
  318.8 6.1 %collective-permute-done.37.refs_4_ = bf16[384,768]{1,0:T(8,128)(2,1)S(1)} collective-permute-done((bf16[384,768]{1,0:T(8,128)(2,1)}, bf16[384,768]{1,0:T(8,128)(2,1)S(1)}, u32[]{:S(2)}, u32[]{:S(2)}) %collective-permute-start.37) | collective-permute-done | bytes 589856 | tf_op jit(solution)/shard_map/ppermute | solution.py:54
  324.9 2.2 collective-permute-done.38.refs_3_
  327.1 4.8 %project_back.3 = (bf16[384,576]{1,0:T(8,128)(2,1)S(1)}, bf16[384,576]{1,0:T(8,128)(2,1)}, bf16[384,768]{1,0:T(8,128)(2,1)}, f32[2,576]{1,0:T(2,128)S(1)}, f32[2,768]{1,0:T(2,128)S(1)}) custom-call(s32[16]{0:T(128)S(1)} %stack.23.refs_0_, bf16[384,384]{1,0:T(8,128)(2,1)S(1)} %get-tuple-element.227.refs_1_, bf16[384,768]{1,0:T(8,128)(2,1)S(1)} %get-tuple-element.228.refs_2_, ...), custom_call_target="tpu_custom_call" | custom-call | flops 800000000 | bytes 1000 | tf_op jit(solution)/shard_map/project_back/pallas_call | solution.py:226
  334.3 6.6 %project_grads.1 = (bf16[208,768]{1,0:T(8,128)(2,1)}, bf16[208,768]{1,0:T(8,128)(2,1)}, bf16[208,768]{1,0:T(8,128)(2,1)}, bf16[96,768]{1,0:T(8,128)(2,1)}, bf16[112,768]{1,0:T(8,128)(2,1)}) custom-call(s32[16]{0:T(128)S(1)} %stack.23.refs_0_, bf16[384,768]{1,0:T(8,128)(2,1)} %get-tuple-element.142.refs_1_, bf16[384,768]{1,0:T(8,128)(2,1)} %copy-done.54, ...), custom_call_target="tpu_custom_call" | custom-call | flops 600000000 | bytes 1000 | tf_op jit(solution)/shard_map/project_grads/pallas_call | solution.py:226
  343.0 5.0 %collective-permute-done.40.refs_3_ = bf16[384,768]{1,0:T(8,128)(2,1)S(1)} collective-permute-done((bf16[384,768]{1,0:T(8,128)(2,1)}, bf16[384,768]{1,0:T(8,128)(2,1)S(1)}, u32[]{:S(2)}, u32[]{:S(2)}) %collective-permute-start.40) | collective-permute-done | bytes 589856 | tf_op jit(solution)/shard_map/ppermute | solution.py:50
  348.0 2.4 input_back.1
  359.0 2.9 join_rows.2
  361.9 7.2 %collective-permute-done.44.refs_2_ = bf16[384,768]{1,0:T(8,128)(2,1)S(1)} collective-permute-done((bf16[384,768]{1,0:T(8,128)(2,1)S(1)}, bf16[384,768]{1,0:T(8,128)(2,1)S(1)}, u32[]{:S(2)}, u32[]{:S(2)}) %collective-permute-start.44) | collective-permute-done | bytes 589856 | tf_op jit(solution)/shard_map/ppermute | solution.py:50
  369.1 2.5 finish.1.refs_1_
  376.8 3.1 feed_out.1
  380.7 2.9 join_rows.3
  388.6 2.7 project_out.1
  393.5 2.1 small_out.1
  (276 shorter events, 84.8 us)
Async XLA Ops:
  7.2 87.3 %all-gather.7.cloned.1.call-start = ((), (), s32[]{:S(2)}) async-start(), calls=%async_computation.6 | async-start | bytes 5308416 | tf_op jit(solution)/shard_map/all_gather | solution.py:98
  9.8 20.4 %collective-permute-start.2 = (bf16[208,768]{1,0:T(8,128)(2,1)}, bf16[208,768]{1,0:T(8,128)(2,1)S(1)}, u32[]{:S(2)}, u32[]{:S(2)}) collective-permute-start(bf16[208,768]{1,0:T(8,128)(2,1)} %pack_first.1.refs_2_.refs_5_.refs_8_.refs_6_), channel_id=1, source_target_pairs={{0,16},{8,24},{16,0},{24,8},{1,17},{9,25},{17,1},{25,9},{2,18},{10... | collective-permute-start | bytes 958472 | tf_op jit(solution)/shard_map/ppermute | solution.py:75
  13.9 16.3 %collective-permute-start.1 = (bf16[208,768]{1,0:T(8,128)(2,1)}, bf16[208,768]{1,0:T(8,128)(2,1)S(1)}, u32[]{:S(2)}, u32[]{:S(2)}) collective-permute-start(bf16[208,768]{1,0:T(8,128)(2,1)} %pack_first.1.refs_2_.refs_5_.refs_8_.refs_6_), channel_id=1, source_target_pairs={{0,24},{8,0},{16,8},{24,16},{1,25},{9,1},{17,9},{25,17},{2,26},{10... | collective-permute-start | bytes 958472 | tf_op jit(solution)/shard_map/ppermute | solution.py:75
  15.3 21.3 %collective-permute-start = (bf16[208,768]{1,0:T(8,128)(2,1)}, bf16[208,768]{1,0:T(8,128)(2,1)S(1)}, u32[]{:S(2)}, u32[]{:S(2)}) collective-permute-start(bf16[208,768]{1,0:T(8,128)(2,1)} %pack_first.1.refs_2_.refs_5_.refs_8_.refs_6_), channel_id=1, source_target_pairs={{0,8},{8,16},{16,24},{24,0},{1,9},{9,17},{17,25},{25,1},{2,10},{10... | collective-permute-start | bytes 958472 | tf_op jit(solution)/shard_map/ppermute | solution.py:75
  36.6 89.9 %all-gather.9.cloned.1.call-start = ((), (), s32[]{:S(2)}) async-start(), calls=%async_computation.7 | async-start | bytes 2654208 | tf_op jit(solution)/shard_map/all_gather | solution.py:98
  37.3 2.5 collective-permute-start.4
  45.1 2.3 collective-permute-start.9
  48.3 131.3 %all-gather.11.cloned.1.call-start = ((), (), s32[]{:S(2)}) async-start(), calls=%async_computation.8 | async-start | bytes 5308416 | tf_op jit(solution)/shard_map/all_gather | solution.py:98
  48.4 15.4 %collective-permute-start.8 = (bf16[384,768]{1,0:T(8,128)(2,1)S(1)}, bf16[384,768]{1,0:T(8,128)(2,1)S(1)}, u32[]{:S(2)}, u32[]{:S(2)}) collective-permute-start(bf16[384,768]{1,0:T(8,128)(2,1)S(1)} %copy-done.16), channel_id=1, source_target_pairs={{0,4},{4,0},{1,5},{5,1},{2,6},{6,2},{3,7},{7,3},{8,12},{12,8},{9,1... | collective-permute-start | bytes 1769480 | tf_op jit(solution)/shard_map/ppermute | solution.py:54
  77.9 195.5 %reduce-scatter.4.cloned.1.call-start = ((), (), s32[]{:S(2)}) async-start(), calls=%async_computation.3 | async-start | bytes 2949120 | tf_op jit(solution)/shard_map/reduce_scatter | solution.py:1065
  78.2 2.3 collective-permute-start.7
  78.4 15.8 %collective-permute-start.12 = (bf16[384,768]{1,0:T(8,128)(2,1)}, bf16[384,768]{1,0:T(8,128)(2,1)S(1)}, u32[]{:S(2)}, u32[]{:S(2)}) collective-permute-start(bf16[384,768]{1,0:T(8,128)(2,1)} %get-tuple-element.148.refs_2_), channel_id=1, source_target_pairs={{0,2},{2,0},{1,3},{3,1},{4,6},{6,4},{5,7},{7,5},{8,10},{10,8},{9,1... | collective-permute-start | bytes 1769480 | tf_op jit(solution)/shard_map/ppermute | solution.py:50
  102.4 2.6 collective-permute-start.13
  102.7 3.1 collective-permute-start.14
  103.0 23.6 %collective-permute-start.15 = (bf16[384,768]{1,0:T(8,128)(2,1)}, bf16[384,768]{1,0:T(8,128)(2,1)S(1)}, u32[]{:S(2)}, u32[]{:S(2)}) collective-permute-start(bf16[384,768]{1,0:T(8,128)(2,1)} %get-tuple-element.159.refs_4_), channel_id=1, source_target_pairs={{0,2},{2,0},{1,3},{3,1},{4,6},{6,4},{5,7},{7,5},{8,10},{10,8},{9,1... | collective-permute-start | bytes 1769480 | tf_op jit(solution)/shard_map/ppermute | solution.py:50
  131.5 2.3 collective-permute-start.18
  131.8 15.7 %collective-permute-start.17 = (bf16[384,768]{1,0:T(8,128)(2,1)}, bf16[384,768]{1,0:T(8,128)(2,1)S(1)}, u32[]{:S(2)}, u32[]{:S(2)}) collective-permute-start(bf16[384,768]{1,0:T(8,128)(2,1)} %get-tuple-element.166.refs_1_), channel_id=1, source_target_pairs={{0,4},{4,0},{1,5},{5,1},{2,6},{6,2},{3,7},{7,3},{8,12},{12,8},{9,1... | collective-permute-start | bytes 1769480 | tf_op jit(solution)/shard_map/ppermute | solution.py:54
  147.6 14.7 %collective-permute-start.16 = (bf16[384,768]{1,0:T(8,128)(2,1)S(1)}, bf16[384,768]{1,0:T(8,128)(2,1)S(1)}, u32[]{:S(2)}, u32[]{:S(2)}) collective-permute-start(bf16[384,768]{1,0:T(8,128)(2,1)S(1)} %copy-done.46), channel_id=1, source_target_pairs={{0,1},{1,0},{2,3},{3,2},{4,5},{5,4},{6,7},{7,6},{8,9},{9,8},{10,11... | collective-permute-start | bytes 1769480 | tf_op jit(solution)/shard_map/ppermute | solution.py:46
  160.7 18.9 %collective-permute-start.21 = (bf16[384,768]{1,0:T(8,128)(2,1)}, bf16[384,768]{1,0:T(8,128)(2,1)S(1)}, u32[]{:S(2)}, u32[]{:S(2)}) collective-permute-start(bf16[384,768]{1,0:T(8,128)(2,1)} %get-tuple-element.170.refs_2_), channel_id=1, source_target_pairs={{0,2},{2,0},{1,3},{3,1},{4,6},{6,4},{5,7},{7,5},{8,10},{10,8},{9,1... | collective-permute-start | bytes 1769480 | tf_op jit(solution)/shard_map/ppermute | solution.py:50
  194.6 4.6 %collective-permute-start.24 = (bf16[384,1536]{1,0:T(8,128)(2,1)}, bf16[384,1536]{1,0:T(8,128)(2,1)S(1)}, u32[]{:S(2)}, u32[]{:S(2)}) collective-permute-start(bf16[384,1536]{1,0:T(8,128)(2,1)} %get-tuple-element.183.refs_5_), channel_id=1, source_target_pairs={{0,1},{1,0},{2,3},{3,2},{4,5},{5,4},{6,7},{7,6},{8,9},{9,8},{10,11... | collective-permute-start | bytes 3538952 | tf_op jit(solution)/shard_map/ppermute | solution.py:46
  194.9 3.4 collective-permute-start.23
  195.1 4.0 collective-permute-start.22
  195.4 15.7 %collective-permute-start.25 = (bf16[384,768]{1,0:T(8,128)(2,1)}, bf16[384,768]{1,0:T(8,128)(2,1)S(1)}, u32[]{:S(2)}, u32[]{:S(2)}) collective-permute-start(bf16[384,768]{1,0:T(8,128)(2,1)} %get-tuple-element.187.refs_3_), channel_id=1, source_target_pairs={{0,2},{2,0},{1,3},{3,1},{4,6},{6,4},{5,7},{7,5},{8,10},{10,8},{9,1... | collective-permute-start | bytes 1769480 | tf_op jit(solution)/shard_map/ppermute | solution.py:50
  211.1 98.7 %reduce-scatter.6.cloned.1.call-start = ((), (), s32[]{:S(2)}) async-start(), calls=%async_computation.4 | async-start | bytes 1474560 | tf_op jit(solution)/shard_map/reduce_scatter | solution.py:1065
  223.1 2.3 collective-permute-start.26
  223.2 4.7 %collective-permute-start.27 = (bf16[384,768]{1,0:T(8,128)(2,1)S(1)}, bf16[384,768]{1,0:T(8,128)(2,1)S(1)}, u32[]{:S(2)}, u32[]{:S(2)}) collective-permute-start(bf16[384,768]{1,0:T(8,128)(2,1)S(1)} %copy-done.48), channel_id=1, source_target_pairs={{0,1},{1,0},{2,3},{3,2},{4,5},{5,4},{6,7},{7,6},{8,9},{9,8},{10,11... | collective-permute-start | bytes 1769480 | tf_op jit(solution)/shard_map/ppermute | solution.py:46
  226.4 15.6 %collective-permute-start.28 = (bf16[384,768]{1,0:T(8,128)(2,1)}, bf16[384,768]{1,0:T(8,128)(2,1)S(1)}, u32[]{:S(2)}, u32[]{:S(2)}) collective-permute-start(bf16[384,768]{1,0:T(8,128)(2,1)} %cross_sum.2), channel_id=1, source_target_pairs={{0,4},{4,0},{1,5},{5,1},{2,6},{6,2},{3,7},{7,3},{8,12},{12,8},{9,1... | collective-permute-start | bytes 1769480 | tf_op jit(solution)/shard_map/ppermute | solution.py:54
  248.6 15.6 %collective-permute-start.30 = (bf16[384,768]{1,0:T(8,128)(2,1)}, bf16[384,768]{1,0:T(8,128)(2,1)S(1)}, u32[]{:S(2)}, u32[]{:S(2)}) collective-permute-start(bf16[384,768]{1,0:T(8,128)(2,1)} %get-tuple-element.202.refs_3_), channel_id=1, source_target_pairs={{0,2},{2,0},{1,3},{3,1},{4,6},{6,4},{5,7},{7,5},{8,10},{10,8},{9,1... | collective-permute-start | bytes 1769480 | tf_op jit(solution)/shard_map/ppermute | solution.py:50
  264.2 91.3 %reduce-scatter.8.cloned.1.call-start = ((), (), s32[]{:S(2)}) async-start(), calls=%async_computation.5 | async-start | bytes 2949120 | tf_op jit(solution)/shard_map/reduce_scatter | solution.py:1065
  273.4 3.2 collective-permute-start.32
  273.4 16.1 %collective-permute-start.33 = (bf16[192,1536]{1,0:T(8,128)(2,1)}, bf16[192,1536]{1,0:T(8,128)(2,1)}, u32[]{:S(2)}, u32[]{:S(2)}) collective-permute-start(bf16[192,1536]{1,0:T(8,128)(2,1)} %reduce-scatter.4.cloned.1.call-done.refs_2_), channel_id=1, source_target_pairs={{0,4},{4,0},{1,5},{5,1},{2,6},{6,2},{3,7},{7,3},{8,12},{12,8},{9,1... | collective-permute-start | bytes 1769480 | tf_op jit(solution)/shard_map/ppermute | solution.py:54
  274.9 15.7 %collective-permute-start.34 = (bf16[384,768]{1,0:T(8,128)(2,1)}, bf16[384,768]{1,0:T(8,128)(2,1)S(1)}, u32[]{:S(2)}, u32[]{:S(2)}) collective-permute-start(bf16[384,768]{1,0:T(8,128)(2,1)} %get-tuple-element.214.refs_3_), channel_id=1, source_target_pairs={{0,2},{2,0},{1,3},{3,1},{4,6},{6,4},{5,7},{7,5},{8,10},{10,8},{9,1... | collective-permute-start | bytes 1769480 | tf_op jit(solution)/shard_map/ppermute | solution.py:50
  305.9 2.3 collective-permute-start.35
  306.0 3.9 collective-permute-start.36
  309.2 15.6 %collective-permute-start.37 = (bf16[384,768]{1,0:T(8,128)(2,1)}, bf16[384,768]{1,0:T(8,128)(2,1)S(1)}, u32[]{:S(2)}, u32[]{:S(2)}) collective-permute-start(bf16[384,768]{1,0:T(8,128)(2,1)} %cross_sum.3), channel_id=1, source_target_pairs={{0,4},{4,0},{1,5},{5,1},{2,6},{6,2},{3,7},{7,3},{8,12},{12,8},{9,1... | collective-permute-start | bytes 1769480 | tf_op jit(solution)/shard_map/ppermute | solution.py:54
  332.2 15.8 %collective-permute-start.40 = (bf16[384,768]{1,0:T(8,128)(2,1)}, bf16[384,768]{1,0:T(8,128)(2,1)S(1)}, u32[]{:S(2)}, u32[]{:S(2)}) collective-permute-start(bf16[384,768]{1,0:T(8,128)(2,1)} %get-tuple-element.248.refs_2_), channel_id=1, source_target_pairs={{0,2},{2,0},{1,3},{3,1},{4,6},{6,4},{5,7},{7,5},{8,10},{10,8},{9,1... | collective-permute-start | bytes 1769480 | tf_op jit(solution)/shard_map/ppermute | solution.py:50
  333.7 16.8 %collective-permute-start.41 = (bf16[192,768]{1,0:T(8,128)(2,1)S(1)}, bf16[192,768]{1,0:T(8,128)(2,1)S(1)}, u32[]{:S(2)}, u32[]{:S(2)}) collective-permute-start(bf16[192,768]{1,0:T(8,128)(2,1)S(1)} %copy-done.64), channel_id=1, source_target_pairs={{0,4},{4,0},{1,5},{5,1},{2,6},{6,2},{3,7},{7,3},{8,12},{12,8},{9,1... | collective-permute-start | bytes 884744 | tf_op jit(solution)/shard_map/ppermute | solution.py:54
  340.9 10.4 %collective-permute-start.43 = (bf16[112,768]{1,0:T(8,128)(2,1)}, bf16[112,768]{1,0:T(8,128)(2,1)S(1)}, u32[]{:S(2)}, u32[]{:S(2)}) collective-permute-start(bf16[112,768]{1,0:T(8,128)(2,1)} %get-tuple-element.254), channel_id=1, source_target_pairs={{0,24},{8,0},{16,8},{24,16},{1,25},{9,1},{17,9},{25,17},{2,26},{10... | collective-permute-start | bytes 516104 | tf_op jit(solution)/shard_map/ppermute | solution.py:1120
  342.1 9.2 %collective-permute-start.42 = (bf16[96,768]{1,0:T(8,128)(2,1)}, bf16[96,768]{1,0:T(8,128)(2,1)S(1)}, u32[]{:S(2)}, u32[]{:S(2)}) collective-permute-start(bf16[96,768]{1,0:T(8,128)(2,1)} %get-tuple-element.253), channel_id=1, source_target_pairs={{0,8},{8,16},{16,24},{24,0},{1,9},{9,17},{17,25},{25,1},{2,10},{10... | collective-permute-start | bytes 442376 | tf_op jit(solution)/shard_map/ppermute | solution.py:1120
  350.4 7.8 %collective-permute-start.46 = (bf16[384,768]{1,0:T(8,128)(2,1)}, bf16[384,768]{1,0:T(8,128)(2,1)S(1)}, u32[]{:S(2)}, u32[]{:S(2)}) collective-permute-start(bf16[384,768]{1,0:T(8,128)(2,1)} %get-tuple-element.249.refs_1_), channel_id=1, source_target_pairs={{0,1},{1,0},{2,3},{3,2},{4,5},{5,4},{6,7},{7,6},{8,9},{9,8},{10,11... | collective-permute-start | bytes 1769480 | tf_op jit(solution)/shard_map/ppermute | solution.py:46
  354.1 15.0 %collective-permute-start.44 = (bf16[384,768]{1,0:T(8,128)(2,1)S(1)}, bf16[384,768]{1,0:T(8,128)(2,1)S(1)}, u32[]{:S(2)}, u32[]{:S(2)}) collective-permute-start(bf16[384,768]{1,0:T(8,128)(2,1)S(1)} %copy-done.55), channel_id=1, source_target_pairs={{0,2},{2,0},{1,3},{3,1},{4,6},{6,4},{5,7},{7,5},{8,10},{10,8},{9,1... | collective-permute-start | bytes 1769480 | tf_op jit(solution)/shard_map/ppermute | solution.py:50
  355.6 16.0 %collective-permute-start.45 = (bf16[192,1536]{1,0:T(8,128)(2,1)}, bf16[192,1536]{1,0:T(8,128)(2,1)S(1)}, u32[]{:S(2)}, u32[]{:S(2)}) collective-permute-start(bf16[192,1536]{1,0:T(8,128)(2,1)} %reduce-scatter.8.cloned.1.call-done.refs_0_), channel_id=1, source_target_pairs={{0,4},{4,0},{1,5},{5,1},{2,6},{6,2},{3,7},{7,3},{8,12},{12,8},{9,1... | collective-permute-start | bytes 1769480 | tf_op jit(solution)/shard_map/ppermute | solution.py:54
  356.2 15.4 %collective-permute-start.48 = (bf16[208,768]{1,0:T(8,128)(2,1)}, bf16[208,768]{1,0:T(8,128)(2,1)S(1)}, u32[]{:S(2)}, u32[]{:S(2)}) collective-permute-start(bf16[208,768]{1,0:T(8,128)(2,1)} %get-tuple-element.260), channel_id=1, source_target_pairs={{0,24},{8,0},{16,8},{24,16},{1,25},{9,1},{17,9},{25,17},{2,26},{10... | collective-permute-start | bytes 958472 | tf_op jit(solution)/shard_map/ppermute | solution.py:1123
  357.9 14.6 %collective-permute-start.47 = (bf16[208,768]{1,0:T(8,128)(2,1)}, bf16[208,768]{1,0:T(8,128)(2,1)S(1)}, u32[]{:S(2)}, u32[]{:S(2)}) collective-permute-start(bf16[208,768]{1,0:T(8,128)(2,1)} %get-tuple-element.255), channel_id=1, source_target_pairs={{0,8},{8,16},{16,24},{24,0},{1,9},{9,17},{17,25},{25,1},{2,10},{10... | collective-permute-start | bytes 958472 | tf_op jit(solution)/shard_map/ppermute | solution.py:1123
  375.2 4.7 %collective-permute-start.49 = (bf16[384,768]{1,0:T(8,128)(2,1)S(1)}, bf16[384,768]{1,0:T(8,128)(2,1)S(1)}, u32[]{:S(2)}, u32[]{:S(2)}) collective-permute-start(bf16[384,768]{1,0:T(8,128)(2,1)S(1)} %copy-done.41), channel_id=1, source_target_pairs={{0,1},{1,0},{2,3},{3,2},{4,5},{5,4},{6,7},{7,6},{8,9},{9,8},{10,11... | collective-permute-start | bytes 1769480 | tf_op jit(solution)/shard_map/ppermute | solution.py:46
  375.3 10.2 %collective-permute-start.50 = (bf16[208,768]{1,0:T(8,128)(2,1)}, bf16[208,768]{1,0:T(8,128)(2,1)S(1)}, u32[]{:S(2)}, u32[]{:S(2)}) collective-permute-start(bf16[208,768]{1,0:T(8,128)(2,1)} %sum_blocks.1.refs_0_), channel_id=1, source_target_pairs={{0,4},{4,0},{1,5},{5,1},{2,6},{6,2},{3,7},{7,3},{8,12},{12,8},{9,1... | collective-permute-start | bytes 958472 | tf_op jit(solution)/shard_map/ppermute | solution.py:54
  387.2 4.4 %collective-permute-start.51 = (f32[16,768]{1,0:T(8,128)}, f32[16,768]{1,0:T(8,128)S(1)}, u32[]{:S(2)}, u32[]{:S(2)}) collective-permute-start(f32[16,768]{1,0:T(8,128)} %small_sum.1.refs_1_), channel_id=1, source_target_pairs={{0,2},{2,0},{1,3},{3,1},{4,6},{6,4},{5,7},{7,5},{8,10},{10,8},{9,1... | collective-permute-start | bytes 147464 | tf_op jit(solution)/shard_map/ppermute | solution.py:50
  388.6 3.3 collective-permute-start.52
  (86 other events, 492.6 us)
Sparse Core Ops, SparseCore 0:
  36.7 57.6 all-gather.6
  96.1 30.3 all-gather.8
  128.8 50.8 all-gather.10
  211.2 46.8 reduce-scatter.3
  264.4 27.9 reduce-scatter.5
  296.5 45.9 reduce-scatter.7
